TPU v7x, 32 devices: a whole 2x2x4 slice. The times are simulated.
32 devices in a mesh: dp: 16 (over z, x, core), expert: 2 (over y).
Axes of the slice: x: 2, y: 2, z: 4, core: 2. Of those that a mesh axis runs over, the one named last changes fastest.
Arguments:
- grad_out: bfloat16 [16384, 3072], P(('dp', 'expert')), may hold values from -0.19921875 to 0.19921875
- expert_ids: int32 [16384, 2], P(('dp', 'expert')), may hold values from 0 to 7, all different within a row; in each aligned block of 512 rows (0 to 511, 512 to 1023, ...) at most 192 rows name the same one
- gate_probs: float32 [16384, 2], P(('dp', 'expert')), may hold values from 0.1 to 1
- saved_gate: bfloat16 [6144, 2, 1024], P('dp', 'expert'), may hold values from -6 to 6
- saved_up: bfloat16 [6144, 2, 1024], P('dp', 'expert'), may hold values from -6 to 6
- master: float32 [2, 1024, 3072], P('expert', 'dp')
- moment_one: float32 [2, 1024, 3072], P('expert', 'dp'), may hold values from -2 to 2
- moment_two: float32 [2, 1024, 3072], P('expert', 'dp'), may hold values from 0.05 to 1
Outputs:
- new_master: float32 [2, 1024, 3072], P('expert', 'dp')
- new_moment_one: float32 [2, 1024, 3072], P('expert', 'dp')
- new_moment_two: float32 [2, 1024, 3072], P('expert', 'dp')
- new_weights: float32 [2, 1024, 3072], P('expert')
Inputs may be any that keep to these rules, and one draw needn't show every extreme that they name: `expert_ids`: in each aligned block of 512 rows (the tokens of one device) no expert is named by more than 192 rows, a bound that some block reaches.
All inputs are finite; a program needn't handle non-finite values.
Results may differ from a plain program's by a relative error of at most 0.00035.
Values may be sent and summed in bfloat16 or wider, within the bound.
No kernel may reach another device: no remote copies, remote signals or barrier semaphores. Data moves between devices by JAX's collectives and lax.ppermute only.
A program may use at most 128 MiB of HBM per device.

v0:
```python
import jax
import jax.numpy as jnp
from jax import lax
from jax.sharding import PartitionSpec as P


def local(grad_out, expert_ids, gate_probs, saved_gate, saved_up, master, moment_one, moment_two):
    tok_rows = grad_out.shape[0]
    cap_rows = tok_rows * 3 // 8
    hit = expert_ids == 0
    chosen = jnp.any(hit, axis=1)
    weight = jnp.sum(jnp.where(hit, gate_probs, jnp.float32(0.0)), axis=1)
    slot = jnp.cumsum(chosen.astype(jnp.int32)) - 1
    scaled = (weight[:, None] * grad_out.astype(jnp.float32)).astype(jnp.bfloat16)
    places = jnp.arange(cap_rows, dtype=jnp.int32)
    placing = ((slot[None, :] == places[:, None]) & chosen[None, :]).astype(jnp.bfloat16)
    dispatched = jnp.dot(placing, scaled, preferred_element_type=jnp.float32).astype(jnp.bfloat16)
    slot_rows = saved_gate.shape[0]
    width = saved_gate.shape[2]
    gate_part = saved_gate.reshape(slot_rows, width)
    up_part = saved_up.reshape(slot_rows, width)
    hidden = (jax.nn.silu(gate_part.astype(jnp.float32)) * up_part.astype(jnp.float32)).astype(
        jnp.bfloat16
    )
    contract = (((0,), (0,)), ((), ()))
    everyone = lax.all_gather(dispatched, "expert", axis=0, tiled=True)
    total = lax.dot_general(hidden, everyone, contract, preferred_element_type=jnp.float32)
    grad_slice = lax.psum_scatter(total, "dp", scatter_dimension=0, tiled=True)
    grad = grad_slice.reshape(master.shape)
    new_one = 0.9 * moment_one + 0.1 * grad
    new_two = 0.95 * moment_two + 0.05 * grad * grad
    step = new_one / (1.0 - 0.9**20) / (jnp.sqrt(new_two / (1.0 - 0.95**20)) + 1e-08)
    wrms = jnp.sqrt(jnp.mean(master * master, axis=-1, keepdims=True) + 1e-06)
    srms = jnp.sqrt(jnp.mean(step * step, axis=-1, keepdims=True) + 1e-06)
    factor = jnp.minimum(1.0, 0.02 * wrms / (0.01 * srms))
    new_master = master - 0.01 * factor * step
    gathered = lax.all_gather(new_master, "dp", axis=1, tiled=True)
    return (new_master, new_one, new_two, gathered)


def solution(mesh):
    return jax.shard_map(
        local,
        mesh=mesh,
        in_specs=(
            P(("dp", "expert"), None),
            P(("dp", "expert"), None),
            P(("dp", "expert"), None),
            P("dp", "expert", None),
            P("dp", "expert", None),
            P("expert", "dp", None),
            P("expert", "dp", None),
            P("expert", "dp", None),
        ),
        out_specs=(
            P("expert", "dp", None),
            P("expert", "dp", None),
            P("expert", "dp", None),
            P("expert", None, None),
        ),
        check_vma=False,
    )
```

profile of v0, /device:TPU:1, one launch (start us, length us, event | category | flops | bytes accessed | tf_op | source)
XLA Modules:
  0.0 316.1 jit_solution(9412340162257555090)
XLA Ops:
  7.2 0.0 all-gather.3.cloned.1.call-start
  7.2 0.7 fusion.17
  7.9 0.3 reduce-window.9
  8.2 0.1 slice.7
  8.3 0.1 slice_reduce_fusion
  8.5 0.1 add_bitcast_fusion
  8.5 0.7 select_reduce_fusion
  9.3 0.0 copy-start.3
  9.3 0.0 copy-start.4
  9.3 3.9 %convolution_convert_fusion = bf16[192,3072]{1,0:T(8,128)(2,1)} fusion(bf16[512,3072]{1,0:T(8,128)(2,1)} %param.8, f32[512]{0:T(512)S(1)} %select_reduce_fusion, s32[512]{0:T(512)S(1)} %add_bitcast_fusion, pred[512]{0:T(512)(128)(4,1)S(1)} %fusion.17), kind=kOutput, calls=%fused_computation.1 | convolution fusion | flops 609484800 | bytes 4329984 | tf_op jit(solution)/shard_map/dot_general | solution.py:17
  13.2 0.0 all-gather.3.cloned.1.call-update
  13.2 0.0 reduce-scatter.2.cloned.1.call-start
  13.3 38.3 %all-gather.3.cloned.1.call-done = bf16[384,3072]{1,0:T(8,128)(2,1)} async-done(((bf16[192,3072]{1,0:T(8,128)(2,1)}), bf16[384,3072]{1,0:T(8,128)(2,1)}) %all-gather.3.cloned.1.call-update) | async-done | bytes 2359312 | tf_op jit(solution)/shard_map/all_gather | solution.py:26
  51.5 0.0 copy-done.3
  51.6 0.0 copy-done.4
  51.6 8.3 %fusion.6 = f32[1024,3072]{1,0:T(8,128)} fusion(bf16[384,3072]{1,0:T(8,128)(2,1)} %all-gather.3.cloned.1.call-done, bf16[384,1,1024]{2,0,1:T(8,128)(2,1)S(1)} %copy-done.3, bf16[384,1,1024]{2,0,1:T(8,128)(2,1)S(1)} %copy-done.4), kind=kOutput, calls=%fused_computation.11 | convolution fusion | flops 2419064832 | bytes 16515072 | tf_op jit(solution)/shard_map/dot_general | solution.py:27
  59.9 0.0 copy-start
  59.9 0.0 copy-start.5
  59.9 0.0 reduce-scatter.2.cloned.1.call-update
  59.9 0.0 all-gather.5.cloned.1.call-start
  60.0 1.1 copy-done
  61.0 0.2 multiply_reduce_fusion.1
  61.2 132.7 %reduce-scatter.2.cloned.1.call-done = f32[64,3072]{1,0:T(8,128)} async-done(((f32[1024,3072]{1,0:T(8,128)}), f32[64,3072]{1,0:T(8,128)}) %reduce-scatter.2.cloned.1.call-update) | async-done | bytes 786448 | tf_op jit(solution)/shard_map/reduce_scatter | solution.py:28
  193.9 0.0 copy-done.5
  193.9 2.0 multiply_reduce_fusion
  195.9 0.0 copy-start.1
  195.9 0.0 copy-start.2
  196.0 1.4 multiply_subtract_fusion
  197.3 0.0 all-gather.5.cloned.1.call-update
  197.4 101.3 %all-gather.5.cloned.1.call-done = f32[1,1024,3072]{2,1,0:T(8,128)} async-done(((f32[1,64,3072]{2,1,0:T(8,128)}), f32[1,1024,3072]{2,1,0:T(8,128)}) %all-gather.5.cloned.1.call-update) | async-done | bytes 12582928 | tf_op jit(solution)/shard_map/all_gather | solution.py:37
  298.6 11.0 %copy.13 = f32[1,1024,3072]{2,1,0:T(8,128)} copy(f32[1,1024,3072]{2,1,0:T(8,128)} %all-gather.5.cloned.1.call-done) | data formatting | bytes 25165824
  309.6 0.0 copy-done.1
  309.6 0.0 copy-done.2
  (3 shorter events, 0.1 us)
Async XLA Ops:
  7.2 44.4 %all-gather.3.cloned.1.call-start = ((), (), s32[]{:S(2)}) async-start(), calls=%async_computation.1 | async-start | bytes 3538944 | tf_op jit(solution)/shard_map/all_gather | solution.py:26
  9.3 42.3 %copy-start.3 = (bf16[384,1,1024]{2,0,1:T(8,128)(2,1)S(1)}, bf16[384,1,1024]{2,0,1:T(8,128)(2,1)}, u32[]{:S(2)}) copy-start(bf16[384,1,1024]{2,0,1:T(8,128)(2,1)} %param.12) | copy-start | bytes 2359300
  9.3 42.3 %copy-start.4 = (bf16[384,1,1024]{2,0,1:T(8,128)(2,1)S(1)}, bf16[384,1,1024]{2,0,1:T(8,128)(2,1)}, u32[]{:S(2)}) copy-start(bf16[384,1,1024]{2,0,1:T(8,128)(2,1)} %param.11) | copy-start | bytes 2359300
  13.2 180.7 %reduce-scatter.2.cloned.1.call-start = ((), (), s32[]{:S(2)}) async-start(), calls=%async_computation.2 | async-start | bytes 13369344 | tf_op jit(solution)/shard_map/reduce_scatter | solution.py:28
  59.9 1.1 copy-start
  59.9 134.0 %copy-start.5 = (f32[1,64,3072]{2,1,0:T(8,128)S(1)}, f32[1,64,3072]{2,1,0:T(8,128)}, u32[]{:S(2)}) copy-start(f32[1,64,3072]{2,1,0:T(8,128)} %param.14) | copy-start | bytes 2359300
  59.9 238.7 %all-gather.5.cloned.1.call-start = ((), (), s32[]{:S(2)}) async-start(), calls=%async_computation.3 | async-start | bytes 13369344 | tf_op jit(solution)/shard_map/all_gather | solution.py:37
  195.9 113.7 %copy-start.1 = (f32[1,64,3072]{2,1,0:T(8,128)}, f32[1,64,3072]{2,1,0:T(8,128)S(1)}, u32[]{:S(2)}) copy-start(f32[1,64,3072]{2,1,0:T(8,128)S(1)} %get-tuple-element.12) | copy-start | bytes 2359300
  195.9 113.7 %copy-start.2 = (f32[1,64,3072]{2,1,0:T(8,128)}, f32[1,64,3072]{2,1,0:T(8,128)S(1)}, u32[]{:S(2)}) copy-start(f32[1,64,3072]{2,1,0:T(8,128)S(1)} %get-tuple-element.13) | copy-start | bytes 2359300
Sparse Core Ops, SparseCore 0:
  13.4 38.1 all-gather.2
  60.1 133.7 reduce-scatter.1
  197.5 101.1 all-gather.4
where the time goes:
time: 317 us; the launch traced here: 316 us
  waiting for transfers between devices  272 us (86%)
  between operations  13.8 us (4%)
  local copies, waits for them, and re-layouts  12.3 us (4%)
  matrix products  12.3 us (4%)
  other arithmetic  5.4 us (2%)
    reduce_scatter x1, waiting for transfers between devices, local(): grad_slice = lax.psum_scatter(total, 'dp', scatter_dimension=0, tiled=True)  133 us
    all_gather x1, waiting for transfers between devices, local(): gathered = lax.all_gather(new_master, 'dp', axis=1, tiled=True)  101 us
    all_gather x1, waiting for transfers between devices, local(): everyone = lax.all_gather(dispatched, 'expert', axis=0, tiled=True)  38.3 us
    unnamed x13, local copies, waits for them, and re-layouts  12.1 us
    dot_general x1, matrix products, local(): lax.dot_general(hidden, everyone, contract, preferred_element_type=jnp.fl...  8.35 us
  transfers between devices with their start and end apart: 3, of which 3 were waited for; matrix products, arithmetic and copies ran while one was open for 0% of the time, Pallas kernels for 0%

commit v1 on v0

v1 whole, which is shorter than its diff:
```python
import jax
import jax.numpy as jnp
from jax import lax
from jax.sharding import PartitionSpec as P

F16 = jnp.float16
F32 = jnp.float32
BF16 = jnp.bfloat16
CHUNKS = 4


def build(mesh):
    devices = mesh.shape["dp"]
    experts = mesh.shape["expert"]
    rows_a = 4
    rows_b = devices // (2 * rows_a)

    def place(a, b, c):
        return ((a % rows_a) * rows_b + b % rows_b) * 2 + c % 2

    spots = [(a, b, c) for a in range(rows_a) for b in range(rows_b) for c in range(2)]

    def shift_a(value, k):
        return lax.ppermute(value, "dp", [(place(a, b, c), place(a + k, b, c)) for a, b, c in spots])

    def shift_b(value, k):
        return lax.ppermute(value, "dp", [(place(a, b, c), place(a, b + k, c)) for a, b, c in spots])

    def swap_core(value):
        return lax.ppermute(value, "dp", [(place(a, b, c), place(a, b, c + 1)) for a, b, c in spots])

    def shift_expert(value, k):
        return lax.ppermute(value, "expert", [(e, (e + k) % experts) for e in range(experts)])

    def local(grad_out, expert_ids, gate_probs, saved_gate, saved_up, master, moment_one, moment_two):
        me = lax.axis_index("dp")
        core = me % 2
        at_b = (me // 2) % rows_b
        at_a = me // (2 * rows_b)
        at_e = lax.axis_index("expert")
        tok_rows, dim = grad_out.shape
        cap_rows = tok_rows * 3 // 8
        own = master.shape[1]
        slot_rows, _, width = saved_gate.shape

        hit = expert_ids == 0
        chosen = jnp.any(hit, axis=1)
        weight = jnp.sum(jnp.where(hit, gate_probs, jnp.float32(0.0)), axis=1)
        slot = jnp.cumsum(chosen.astype(jnp.int32)) - 1
        scaled = (weight[:, None] * grad_out.astype(F32)).astype(BF16)
        places = jnp.arange(cap_rows, dtype=jnp.int32)
        placing = ((slot[None, :] == places[:, None]) & chosen[None, :]).astype(BF16)
        dispatched = jnp.dot(placing, scaled, preferred_element_type=F32).astype(BF16)

        def rolled(saved):
            saved = saved.reshape(experts, cap_rows, width)
            parts = [lax.dynamic_index_in_dim(saved, (at_e + j) % experts, 0, False) for j in range(experts)]
            return jnp.concatenate(parts, axis=0).astype(F32)

        hidden = (jax.nn.silu(rolled(saved_gate)) * rolled(saved_up)).astype(BF16)
        hidden = hidden.T.reshape(rows_a, rows_b, 2, own, slot_rows).transpose(2, 1, 0, 3, 4)
        hidden_mine = lax.dynamic_index_in_dim(hidden, core, 0, False)
        hidden_other = swap_core(lax.dynamic_index_in_dim(hidden, 1 - core, 0, False))
        hidden_all = jnp.concatenate([hidden_mine, hidden_other], axis=-1)
        blocks = [
            lax.dynamic_index_in_dim(hidden_all, (at_b + k) % rows_b, 0, False).reshape(rows_a * own, 2 * slot_rows)
            for k in range(rows_b)
        ]

        bound = jnp.max(jnp.abs(master[0]), axis=-1, keepdims=True) + 0.08
        bounds = lax.all_gather(bound, "dp", axis=0, tiled=True)

        largest = 2 * rows_b * slot_rows * 36.0 * 0.2
        shrink = 1.0
        while largest * shrink > 60000.0:
            shrink *= 0.5

        size = dim // CHUNKS
        grads = []
        for i in range(CHUNKS):
            part = dispatched[:, i * size : (i + 1) * size]
            parts = [part] + [shift_expert(part, -j) for j in range(1, experts)]
            mine = jnp.concatenate(parts, axis=0)
            both = jnp.concatenate([mine, swap_core(mine)], axis=0)
            total = jnp.dot(blocks[0], both, preferred_element_type=F32) * shrink
            for k in range(1, rows_b):
                send = (jnp.dot(blocks[k], both, preferred_element_type=F32) * shrink).astype(F16)
                total = total + shift_b(send, k).astype(F32)
            total = total.reshape(rows_a, own, size)
            grad = lax.dynamic_index_in_dim(total, at_a, 0, False)
            for k in range(1, rows_a):
                send = lax.dynamic_index_in_dim(total, (at_a + k) % rows_a, 0, False).astype(F16)
                grad = grad + shift_a(send, k).astype(F32)
            grads.append(grad)
        grad = (jnp.concatenate(grads, axis=1) * (1.0 / shrink)).reshape(master.shape)

        new_one = 0.9 * moment_one + 0.1 * grad
        new_two = 0.95 * moment_two + 0.05 * grad * grad
        step = new_one / (1.0 - 0.9**20) / (jnp.sqrt(new_two / (1.0 - 0.95**20)) + 1e-08)
        wrms = jnp.sqrt(jnp.mean(master * master, axis=-1, keepdims=True) + 1e-06)
        srms = jnp.sqrt(jnp.mean(step * step, axis=-1, keepdims=True) + 1e-06)
        factor = jnp.minimum(1.0, 0.02 * wrms / (0.01 * srms))
        new_master = master - 0.01 * factor * step

        weights = jnp.zeros((width, dim), F32)

        def put(weights, coded, a, b, c):
            row = place(a, b, c) * own
            scale = lax.dynamic_slice(bounds, (row, 0), (own, 1)) * (1.0 / 32768.0)
            return lax.dynamic_update_slice(weights, coded.astype(F32) * scale, (row, 0))

        coded = (new_master[0] * (32768.0 / bound)).astype(F16)
        for i in range(rows_a):
            for j in range(rows_b):
                held = coded if j == 0 else shift_b(coded, j)
                weights = put(weights, held, at_a - i, at_b - j, core)
                weights = put(weights, swap_core(held), at_a - i, at_b - j, 1 - core)
            if i < rows_a - 1:
                coded = shift_a(coded, 1)
        return (new_master, new_one, new_two, weights[None])

    return local


def solution(mesh):
    return jax.shard_map(
        build(mesh),
        mesh=mesh,
        in_specs=(
            P(("dp", "expert"), None),
            P(("dp", "expert"), None),
            P(("dp", "expert"), None),
            P("dp", "expert", None),
            P("dp", "expert", None),
            P("expert", "dp", None),
            P("expert", "dp", None),
            P("expert", "dp", None),
        ),
        out_specs=(
            P("expert", "dp", None),
            P("expert", "dp", None),
            P("expert", "dp", None),
            P("expert", None, None),
        ),
        check_vma=False,
    )
```

time: 317 us -> 178 us (0.56)
  waiting for transfers between devices: 272 us -> 76.7 us
  starting transfers between devices: 0.12 us -> 32.6 us
  blocking collectives: 0 us -> 30.3 us
  between operations: 13.8 us -> 2.32 us
  other arithmetic: 5.4 us -> 10.4 us
    all_gather x2 -> x0, waiting for transfers between devices: 140 us -> none  [the longest x1 101 us: local(): gathered = lax.all_gather(new_master, 'dp', axis=1, tiled=True)]
    reduce_scatter x1 -> x0, waiting for transfers between devices: 133 us -> none  [local(): grad_slice = lax.psum_scatter(total, 'dp', scatter_dimension=0, tiled=True)]
    ppermute x0 -> x40, waiting for transfers between devices: none -> 76.7 us  [the longest x15 44.3 us: shift_a(): lax.ppermute(value, 'dp', [(place(a, b, c), place(a + k, b, c)) for a, b,...]
    ppermute x0 -> x40, starting transfers between devices: none -> 32.6 us  [the longest x13 13 us: swap_core(): lax.ppermute(value, 'dp', [(place(a, b, c), place(a, b, c + 1)) for a, b,...]
    unnamed x0 -> x1, blocking collectives: none -> 30.3 us
    unnamed x13 -> x26, local copies, waits for them, and re-layouts: 12.1 us -> 6.23 us
    concatenate x0 -> x9, other arithmetic: none -> 5.27 us  [the longest x4 4.01 us: local(): mine = jnp.concatenate(parts, axis=0)]
    dot_general x2 -> x9, matrix products: 12.3 us -> 14.7 us  [the longest x4 5.98 us: local(): total = jnp.dot(blocks[0], both, preferred_element_type=F32) * shrink]
  transfers between devices with their start and end apart: 3 -> 40, of which waited for: 3 -> 13; matrix products, arithmetic and copies ran while one was open for 0% -> 14% of each run, Pallas kernels for 0% -> 0%
where the time goes in v1:
time: 178 us; the launch traced here: 177 us
  waiting for transfers between devices  76.7 us (43%)
  starting transfers between devices  32.6 us (18%)
  blocking collectives  30.3 us (17%)
  matrix products  14.7 us (8%)
  other arithmetic  10.4 us (6%)
  local copies, waits for them, and re-layouts  9.63 us (5%)
  between operations  2.32 us (1%)
    ppermute x15, waiting for transfers between devices, shift_a(): lax.ppermute(value, 'dp', [(place(a, b, c), place(a + k, b, c)) for a, b,...  44.3 us
    ppermute x8, waiting for transfers between devices, shift_b(): lax.ppermute(value, 'dp', [(place(a, b, c), place(a, b + k, c)) for a, b,...  31.6 us
    unnamed x1, blocking collectives  30.3 us
    ppermute x13, starting transfers between devices, swap_core(): lax.ppermute(value, 'dp', [(place(a, b, c), place(a, b, c + 1)) for a, b,...  13 us
    ppermute x15, starting transfers between devices, shift_a(): lax.ppermute(value, 'dp', [(place(a, b, c), place(a + k, b, c)) for a, b,...  9.14 us
    unnamed x26, local copies, waits for them, and re-layouts  6.23 us
    ppermute x8, starting transfers between devices, shift_b(): lax.ppermute(value, 'dp', [(place(a, b, c), place(a, b + k, c)) for a, b,...  6.13 us
    dot_general x4, matrix products, local(): total = jnp.dot(blocks[0], both, preferred_element_type=F32) * shrink  5.98 us
  transfers between devices with their start and end apart: 40, of which 13 were waited for; matrix products, arithmetic and copies ran while one was open for 14% of the time, Pallas kernels for 0%

profile of v1, /device:TPU:1, one launch (start us, length us, event | category | flops | bytes accessed | tf_op | source)
XLA Modules:
  0.0 176.7 jit_solution(2790452946554999211)
XLA Ops:
  0.7 1.5 constant_dynamic-slice_fusion.1
  2.2 0.2 copy.20
  2.4 0.2 copy.21
  2.6 0.2 copy.22
  2.8 0.2 copy.23
  3.0 0.9 fusion.5
  4.1 0.3 reduce-window.9
  4.8 2.8 %convolution_convert_fusion = bf16[192,3072]{1,0:T(8,128)(2,1)S(1)} fusion(bf16[512,3072]{1,0:T(8,128)(2,1)} %param.8, f32[512]{0:T(512)S(1)} %select_reduce_fusion, s32[512]{0:T(512)S(1)} %add_bitcast_fusion, pred[512]{0:T(512)(128)(4,1)S(1)} %fusion.38), kind=kOutput, calls=%fused_computation.1 | convolution fusion | flops 609484800 | bytes 4329984 | tf_op jit(solution)/shard_map/dot_general | solution.py:53
  7.7 2.8 %collective-permute-start.1 = (bf16[192,768]{1,0:T(8,128)(2,1)S(1)}, bf16[192,768]{1,0:T(8,128)(2,1)}, u32[]{:S(2)}, u32[]{:S(2)}) collective-permute-start(bf16[192,768]{1,0:T(8,128)(2,1)S(1)} %get-tuple-element.11), channel_id=1, source_target_pairs={{0,1},{1,0},{2,3},{3,2},{4,5},{5,4},{6,7},{7,6},{8,9},{9,8},{10,11... | collective-permute-start | bytes 884744 | tf_op jit(solution)/shard_map/ppermute | solution.py:33
  10.5 1.4 collective-permute-start.13
  12.0 0.2 abs_reduce_fusion
  12.2 0.6 dynamic-slice.24
  13.8 30.3 %all-reduce = f32[1024]{0:T(1024)S(1)} all-reduce(f32[1024]{0:T(1024)S(1)} %get-tuple-element.51), channel_id=2, replica_groups=mesh['dp'=16,'expert'=2] {'dp'}, use_global_device_ids=true, to_apply=%add | all-reduce | flops 1024 | bytes 8192
  44.2 1.0 pad_maximum_fusion.5
  45.2 4.0 %collective-permute-start.2 = (bf16[384,768]{1,0:T(8,128)(2,1)S(1)}, bf16[384,768]{1,0:T(8,128)(2,1)}, u32[]{:S(2)}, u32[]{:S(2)}) collective-permute-start(bf16[384,768]{1,0:T(8,128)(2,1)S(1)} %pad_maximum_fusion.5), channel_id=1, source_target_pairs={{0,2},{2,0},{4,6},{6,4},{8,10},{10,8},{12,14},{14,12},{16,18},{18,... | collective-permute-start | bytes 1769480 | tf_op jit(solution)/shard_map/ppermute | solution.py:30
  49.4 1.0 pad_maximum_fusion.6
  50.5 1.0 pad_maximum_fusion.7
  51.5 0.5 collective-permute-start.14
  52.1 1.0 pad_maximum_fusion.8
  53.2 1.1 fusion.8
  54.3 1.6 convolution_convert_fusion.4
  56.0 1.4 convolution_convert_fusion.3
  57.5 1.5 collective-permute-start.9
  59.0 1.4 convolution_convert_fusion.2
  60.5 1.4 convolution_convert_fusion.1
  62.0 1.5 collective-permute-start.21
  63.5 2.7 %collective-permute-done.3 = f16[256,768]{1,0:T(8,128)(2,1)S(1)} collective-permute-done((f16[256,768]{1,0:T(8,128)(2,1)S(1)}, f16[256,768]{1,0:T(8,128)(2,1)S(1)}, u32[]{:S(2)}, u32[]{:S(2)}) %collective-permute-start.3) | collective-permute-done | bytes 393248 | tf_op jit(solution)/shard_map/ppermute | solution.py:27
  66.2 1.6 convolution_add_fusion.3
  68.0 6.6 %collective-permute-done.9 = f16[256,768]{1,0:T(8,128)(2,1)S(1)} collective-permute-done((f16[256,768]{1,0:T(8,128)(2,1)S(1)}, f16[256,768]{1,0:T(8,128)(2,1)S(1)}, u32[]{:S(2)}, u32[]{:S(2)}) %collective-permute-start.9) | collective-permute-done | bytes 393248 | tf_op jit(solution)/shard_map/ppermute | solution.py:27
  74.6 1.4 convolution_add_fusion.2
  76.1 6.9 %collective-permute-done.15 = f16[256,768]{1,0:T(8,128)(2,1)S(1)} collective-permute-done((f16[256,768]{1,0:T(8,128)(2,1)S(1)}, f16[256,768]{1,0:T(8,128)(2,1)S(1)}, u32[]{:S(2)}, u32[]{:S(2)}) %collective-permute-start.15) | collective-permute-done | bytes 393248 | tf_op jit(solution)/shard_map/ppermute | solution.py:27
  83.1 1.4 convolution_add_fusion.1
  84.6 6.9 %collective-permute-done.21 = f16[256,768]{1,0:T(8,128)(2,1)S(1)} collective-permute-done((f16[256,768]{1,0:T(8,128)(2,1)S(1)}, f16[256,768]{1,0:T(8,128)(2,1)S(1)}, u32[]{:S(2)}, u32[]{:S(2)}) %collective-permute-start.21) | collective-permute-done | bytes 393248 | tf_op jit(solution)/shard_map/ppermute | solution.py:27
  91.5 1.5 convolution_add_fusion
  93.1 1.4 collective-permute-start.16
  94.6 2.4 %collective-permute-start.17 = (f16[64,768]{1,0:T(8,128)(2,1)S(1)}, f16[64,768]{1,0:T(8,128)(2,1)S(1)}, u32[]{:S(2)}, u32[]{:S(2)}) collective-permute-start(f16[64,768]{1,0:T(8,128)(2,1)S(1)} %get-tuple-element.23), channel_id=1, source_target_pairs={{0,16},{2,18},{4,20},{6,22},{8,24},{10,26},{12,28},{14,30},{16,0},... | collective-permute-start | bytes 294920 | tf_op jit(solution)/shard_map/ppermute | solution.py:24
  97.0 1.0 collective-permute-start.18
  98.0 0.5 collective-permute-start.22
  98.5 0.4 collective-permute-start.23
  99.0 0.9 collective-permute-done.16
  99.9 1.7 collective-permute-start.24
  101.6 2.0 %collective-permute-done.17 = f16[64,768]{1,0:T(8,128)(2,1)S(1)} collective-permute-done((f16[64,768]{1,0:T(8,128)(2,1)S(1)}, f16[64,768]{1,0:T(8,128)(2,1)S(1)}, u32[]{:S(2)}, u32[]{:S(2)}) %collective-permute-start.17) | collective-permute-done | bytes 98336 | tf_op jit(solution)/shard_map/ppermute | solution.py:24
  103.6 2.4 %collective-permute-done.22 = f16[64,768]{1,0:T(8,128)(2,1)S(1)} collective-permute-done((f16[64,768]{1,0:T(8,128)(2,1)S(1)}, f16[64,768]{1,0:T(8,128)(2,1)S(1)}, u32[]{:S(2)}, u32[]{:S(2)}) %collective-permute-start.22) | collective-permute-done | bytes 98336 | tf_op jit(solution)/shard_map/ppermute | solution.py:24
  106.1 7.0 %collective-permute-done.23 = f16[64,768]{1,0:T(8,128)(2,1)S(1)} collective-permute-done((f16[64,768]{1,0:T(8,128)(2,1)S(1)}, f16[64,768]{1,0:T(8,128)(2,1)S(1)}, u32[]{:S(2)}, u32[]{:S(2)}) %collective-permute-start.23) | collective-permute-done | bytes 98336 | tf_op jit(solution)/shard_map/ppermute | solution.py:24
  113.2 0.7 multiply_reduce_fusion
  113.9 0.4 fusion.7
  114.3 3.0 %collective-permute-start.25 = (f16[64,3072]{1,0:T(8,128)(2,1)S(1)}, f16[64,3072]{1,0:T(8,128)(2,1)S(1)}, u32[]{:S(2)}, u32[]{:S(2)}) collective-permute-start(f16[64,3072]{1,0:T(8,128)(2,1)S(1)} %get-tuple-element.6), channel_id=1, source_target_pairs={{0,2},{2,0},{4,6},{6,4},{8,10},{10,8},{12,14},{14,12},{16,18},{18,... | collective-permute-start | bytes 1179656 | tf_op jit(solution)/shard_map/ppermute | solution.py:30
  117.4 1.5 collective-permute-start.28
  118.9 1.6 broadcast_in_dim.46
  120.6 8.9 %collective-permute-done.28 = f16[64,3072]{1,0:T(8,128)(2,1)S(1)} collective-permute-done((f16[64,3072]{1,0:T(8,128)(2,1)S(1)}, f16[64,3072]{1,0:T(8,128)(2,1)S(1)}, u32[]{:S(2)}, u32[]{:S(2)}) %collective-permute-start.28) | collective-permute-done | bytes 393248 | tf_op jit(solution)/shard_map/ppermute | solution.py:24
  129.6 1.2 collective-permute-start.29
  130.7 1.4 collective-permute-start.30
  132.2 0.3 collective-permute-start.27
  132.7 11.7 %collective-permute-done.32 = f16[64,3072]{1,0:T(8,128)(2,1)S(1)} collective-permute-done((f16[64,3072]{1,0:T(8,128)(2,1)S(1)}, f16[64,3072]{1,0:T(8,128)(2,1)S(1)}, u32[]{:S(2)}, u32[]{:S(2)}) %collective-permute-start.32) | collective-permute-done | bytes 393248 | tf_op jit(solution)/shard_map/ppermute | solution.py:24
  144.4 1.1 collective-permute-start.33
  145.5 0.3 collective-permute-start.31
  146.4 11.3 %collective-permute-done.36 = f16[64,3072]{1,0:T(8,128)(2,1)S(1)} collective-permute-done((f16[64,3072]{1,0:T(8,128)(2,1)S(1)}, f16[64,3072]{1,0:T(8,128)(2,1)S(1)}, u32[]{:S(2)}, u32[]{:S(2)}) %collective-permute-start.36) | collective-permute-done | bytes 393248 | tf_op jit(solution)/shard_map/ppermute | solution.py:24
  157.8 1.1 collective-permute-start.37
  158.9 1.4 collective-permute-start.38
  160.3 0.3 collective-permute-start.35
  161.2 8.5 %collective-permute-done.38 = f16[64,3072]{1,0:T(8,128)(2,1)S(1)} collective-permute-done((f16[64,3072]{1,0:T(8,128)(2,1)S(1)}, f16[64,3072]{1,0:T(8,128)(2,1)S(1)}, u32[]{:S(2)}, u32[]{:S(2)}) %collective-permute-start.38) | collective-permute-done | bytes 393248 | tf_op jit(solution)/shard_map/ppermute | solution.py:27
  169.6 0.8 collective-permute-start.39
  171.0 0.8 collective-permute-done.39
  171.9 4.8 %copy-done = f32[1,1024,3072]{2,1,0:T(8,128)} copy-done((f32[1,1024,3072]{2,1,0:T(8,128)}, f32[1,1024,3072]{2,1,0:T(8,128)S(1)}, u32[]{:S(2)}) %copy-start) | copy-done | bytes 12582936
  (100 shorter events, 4.2 us)
Async XLA Ops:
  3.0 1.1 copy-start.7
  3.0 1.7 copy-start.8
  4.0 49.2 %collective-permute-start = (bf16[2,4,64,384]{3,2,0,1:T(8,128)(2,1)S(1)}, bf16[2,4,64,384]{3,2,0,1:T(8,128)(2,1)}, u32[]{:S(2)}, u32[]{:S(2)}) collective-permute-start(bf16[2,4,64,384]{3,2,0,1:T(8,128)(2,1)S(1)} %get-tuple-element.29), channel_id=1, source_target_pairs={{0,2},{2,0},{4,6},{6,4},{8,10},{10,8},{12,14},{14,12},{16,18},{18,... | collective-permute-start | bytes 1179656 | tf_op jit(solution)/shard_map/ppermute | solution.py:30
  7.6 4.4 %copy-start.1 = (f32[1,64,3072]{2,1,0:T(8,128)S(1)}, f32[1,64,3072]{2,1,0:T(8,128)}, u32[]{:S(2)}) copy-start(f32[1,64,3072]{2,1,0:T(8,128)} %param.13) | copy-start | bytes 2359300
  7.6 4.6 %copy-start.9 = (u32[32]{0:T(128)S(1)}, u32[32]{0:T(128)}, u32[]{:S(2)}) copy-start(u32[32]{0:T(128)} %constant.352) | copy-start | bytes 388
  7.7 36.5 %collective-permute-start.1 = (bf16[192,768]{1,0:T(8,128)(2,1)S(1)}, bf16[192,768]{1,0:T(8,128)(2,1)}, u32[]{:S(2)}, u32[]{:S(2)}) collective-permute-start(bf16[192,768]{1,0:T(8,128)(2,1)S(1)} %get-tuple-element.11), channel_id=1, source_target_pairs={{0,1},{1,0},{2,3},{3,2},{4,5},{5,4},{6,7},{7,6},{8,9},{9,8},{10,11... | collective-permute-start | bytes 884744 | tf_op jit(solution)/shard_map/ppermute | solution.py:33
  10.5 38.9 %collective-permute-start.7 = (bf16[192,768]{1,0:T(8,128)(2,1)S(1)}, bf16[192,768]{1,0:T(8,128)(2,1)}, u32[]{:S(2)}, u32[]{:S(2)}) collective-permute-start(bf16[192,768]{1,0:T(8,128)(2,1)S(1)} %get-tuple-element.14), channel_id=1, source_target_pairs={{0,1},{1,0},{2,3},{3,2},{4,5},{5,4},{6,7},{7,6},{8,9},{9,8},{10,11... | collective-permute-start | bytes 884744 | tf_op jit(solution)/shard_map/ppermute | solution.py:33
  10.5 40.0 %collective-permute-start.13 = (bf16[192,768]{1,0:T(8,128)(2,1)S(1)}, bf16[192,768]{1,0:T(8,128)(2,1)}, u32[]{:S(2)}, u32[]{:S(2)}) collective-permute-start(bf16[192,768]{1,0:T(8,128)(2,1)S(1)} %get-tuple-element.13), channel_id=1, source_target_pairs={{0,1},{1,0},{2,3},{3,2},{4,5},{5,4},{6,7},{7,6},{8,9},{9,8},{10,11... | collective-permute-start | bytes 884744 | tf_op jit(solution)/shard_map/ppermute | solution.py:33
  11.9 40.1 %collective-permute-start.19 = (bf16[192,768]{1,0:T(8,128)(2,1)S(1)}, bf16[192,768]{1,0:T(8,128)(2,1)}, u32[]{:S(2)}, u32[]{:S(2)}) collective-permute-start(bf16[192,768]{1,0:T(8,128)(2,1)S(1)} %get-tuple-element.12), channel_id=1, source_target_pairs={{0,1},{1,0},{2,3},{3,2},{4,5},{5,4},{6,7},{7,6},{8,9},{9,8},{10,11... | collective-permute-start | bytes 884744 | tf_op jit(solution)/shard_map/ppermute | solution.py:33
  45.2 9.1 %collective-permute-start.2 = (bf16[384,768]{1,0:T(8,128)(2,1)S(1)}, bf16[384,768]{1,0:T(8,128)(2,1)}, u32[]{:S(2)}, u32[]{:S(2)}) collective-permute-start(bf16[384,768]{1,0:T(8,128)(2,1)S(1)} %pad_maximum_fusion.5), channel_id=1, source_target_pairs={{0,2},{2,0},{4,6},{6,4},{8,10},{10,8},{12,14},{14,12},{16,18},{18,... | collective-permute-start | bytes 1769480 | tf_op jit(solution)/shard_map/ppermute | solution.py:30
  50.4 5.6 %collective-permute-start.8 = (bf16[384,768]{1,0:T(8,128)(2,1)S(1)}, bf16[384,768]{1,0:T(8,128)(2,1)S(1)}, u32[]{:S(2)}, u32[]{:S(2)}) collective-permute-start(bf16[384,768]{1,0:T(8,128)(2,1)S(1)} %pad_maximum_fusion.6), channel_id=1, source_target_pairs={{0,2},{2,0},{4,6},{6,4},{8,10},{10,8},{12,14},{14,12},{16,18},{18,... | collective-permute-start | bytes 1769480 | tf_op jit(solution)/shard_map/ppermute | solution.py:30
  51.5 7.4 %collective-permute-start.14 = (bf16[384,768]{1,0:T(8,128)(2,1)S(1)}, bf16[384,768]{1,0:T(8,128)(2,1)S(1)}, u32[]{:S(2)}, u32[]{:S(2)}) collective-permute-start(bf16[384,768]{1,0:T(8,128)(2,1)S(1)} %pad_maximum_fusion.7), channel_id=1, source_target_pairs={{0,2},{2,0},{4,6},{6,4},{8,10},{10,8},{12,14},{14,12},{16,18},{18,... | collective-permute-start | bytes 1769480 | tf_op jit(solution)/shard_map/ppermute | solution.py:30
  53.1 7.5 %collective-permute-start.20 = (bf16[384,768]{1,0:T(8,128)(2,1)S(1)}, bf16[384,768]{1,0:T(8,128)(2,1)S(1)}, u32[]{:S(2)}, u32[]{:S(2)}) collective-permute-start(bf16[384,768]{1,0:T(8,128)(2,1)S(1)} %pad_maximum_fusion.8), channel_id=1, source_target_pairs={{0,2},{2,0},{4,6},{6,4},{8,10},{10,8},{12,14},{14,12},{16,18},{18,... | collective-permute-start | bytes 1769480 | tf_op jit(solution)/shard_map/ppermute | solution.py:30
  55.9 10.3 %collective-permute-start.3 = (f16[256,768]{1,0:T(8,128)(2,1)S(1)}, f16[256,768]{1,0:T(8,128)(2,1)S(1)}, u32[]{:S(2)}, u32[]{:S(2)}) collective-permute-start(f16[256,768]{1,0:T(8,128)(2,1)S(1)} %convolution_convert_fusion.4), channel_id=1, source_target_pairs={{0,4},{2,6},{4,0},{6,2},{8,12},{10,14},{12,8},{14,10},{16,20},{18,... | collective-permute-start | bytes 1179656 | tf_op jit(solution)/shard_map/ppermute | solution.py:27
  57.5 17.2 %collective-permute-start.9 = (f16[256,768]{1,0:T(8,128)(2,1)S(1)}, f16[256,768]{1,0:T(8,128)(2,1)S(1)}, u32[]{:S(2)}, u32[]{:S(2)}) collective-permute-start(f16[256,768]{1,0:T(8,128)(2,1)S(1)} %convolution_convert_fusion.3), channel_id=1, source_target_pairs={{0,4},{2,6},{4,0},{6,2},{8,12},{10,14},{12,8},{14,10},{16,20},{18,... | collective-permute-start | bytes 1179656 | tf_op jit(solution)/shard_map/ppermute | solution.py:27
  60.4 22.6 %collective-permute-start.15 = (f16[256,768]{1,0:T(8,128)(2,1)S(1)}, f16[256,768]{1,0:T(8,128)(2,1)S(1)}, u32[]{:S(2)}, u32[]{:S(2)}) collective-permute-start(f16[256,768]{1,0:T(8,128)(2,1)S(1)} %convolution_convert_fusion.2), channel_id=1, source_target_pairs={{0,4},{2,6},{4,0},{6,2},{8,12},{10,14},{12,8},{14,10},{16,20},{18,... | collective-permute-start | bytes 1179656 | tf_op jit(solution)/shard_map/ppermute | solution.py:27
  62.0 29.5 %collective-permute-start.21 = (f16[256,768]{1,0:T(8,128)(2,1)S(1)}, f16[256,768]{1,0:T(8,128)(2,1)S(1)}, u32[]{:S(2)}, u32[]{:S(2)}) collective-permute-start(f16[256,768]{1,0:T(8,128)(2,1)S(1)} %convolution_convert_fusion.1), channel_id=1, source_target_pairs={{0,4},{2,6},{4,0},{6,2},{8,12},{10,14},{12,8},{14,10},{16,20},{18,... | collective-permute-start | bytes 1179656 | tf_op jit(solution)/shard_map/ppermute | solution.py:27
  67.9 25.1 %collective-permute-start.4 = (f16[64,768]{1,0:T(8,128)(2,1)S(1)}, f16[64,768]{1,0:T(8,128)(2,1)S(1)}, u32[]{:S(2)}, u32[]{:S(2)}) collective-permute-start(f16[64,768]{1,0:T(8,128)(2,1)S(1)} %get-tuple-element.15), channel_id=1, source_target_pairs={{0,8},{2,10},{4,12},{6,14},{8,16},{10,18},{12,20},{14,22},{16,24},... | collective-permute-start | bytes 294920 | tf_op jit(solution)/shard_map/ppermute | solution.py:24
  68.0 25.1 %collective-permute-start.5 = (f16[64,768]{1,0:T(8,128)(2,1)S(1)}, f16[64,768]{1,0:T(8,128)(2,1)S(1)}, u32[]{:S(2)}, u32[]{:S(2)}) collective-permute-start(f16[64,768]{1,0:T(8,128)(2,1)S(1)} %get-tuple-element.17), channel_id=1, source_target_pairs={{0,16},{2,18},{4,20},{6,22},{8,24},{10,26},{12,28},{14,30},{16,0},... | collective-permute-start | bytes 294920 | tf_op jit(solution)/shard_map/ppermute | solution.py:24
  74.6 19.9 %collective-permute-start.6 = (f16[64,768]{1,0:T(8,128)(2,1)S(1)}, f16[64,768]{1,0:T(8,128)(2,1)S(1)}, u32[]{:S(2)}, u32[]{:S(2)}) collective-permute-start(f16[64,768]{1,0:T(8,128)(2,1)S(1)} %get-tuple-element.16), channel_id=1, source_target_pairs={{0,24},{2,26},{4,28},{6,30},{8,0},{10,2},{12,4},{14,6},{16,8},{18,... | collective-permute-start | bytes 294920 | tf_op jit(solution)/shard_map/ppermute | solution.py:24
  83.1 13.9 %collective-permute-start.10 = (f16[64,768]{1,0:T(8,128)(2,1)S(1)}, f16[64,768]{1,0:T(8,128)(2,1)S(1)}, u32[]{:S(2)}, u32[]{:S(2)}) collective-permute-start(f16[64,768]{1,0:T(8,128)(2,1)S(1)} %get-tuple-element.18), channel_id=1, source_target_pairs={{0,8},{2,10},{4,12},{6,14},{8,16},{10,18},{12,20},{14,22},{16,24},... | collective-permute-start | bytes 294920 | tf_op jit(solution)/shard_map/ppermute | solution.py:24
  91.5 6.5 %collective-permute-start.11 = (f16[64,768]{1,0:T(8,128)(2,1)S(1)}, f16[64,768]{1,0:T(8,128)(2,1)S(1)}, u32[]{:S(2)}, u32[]{:S(2)}) collective-permute-start(f16[64,768]{1,0:T(8,128)(2,1)S(1)} %get-tuple-element.20), channel_id=1, source_target_pairs={{0,16},{2,18},{4,20},{6,22},{8,24},{10,26},{12,28},{14,30},{16,0},... | collective-permute-start | bytes 294920 | tf_op jit(solution)/shard_map/ppermute | solution.py:24
  92.9 20.2 %copy-start.5 = (f32[1,64,3072]{2,1,0:T(8,128)S(1)}, f32[1,64,3072]{2,1,0:T(8,128)}, u32[]{:S(2)}) copy-start(f32[1,64,3072]{2,1,0:T(8,128)} %param.14) | copy-start | bytes 2359300
  93.0 20.2 %copy-start.6 = (f32[1,64,3072]{2,1,0:T(8,128)S(1)}, f32[1,64,3072]{2,1,0:T(8,128)}, u32[]{:S(2)}) copy-start(f32[1,64,3072]{2,1,0:T(8,128)} %param.15) | copy-start | bytes 2359300
  93.0 5.5 %collective-permute-start.12 = (f16[64,768]{1,0:T(8,128)(2,1)S(1)}, f16[64,768]{1,0:T(8,128)(2,1)S(1)}, u32[]{:S(2)}, u32[]{:S(2)}) collective-permute-start(f16[64,768]{1,0:T(8,128)(2,1)S(1)} %get-tuple-element.19), channel_id=1, source_target_pairs={{0,24},{2,26},{4,28},{6,30},{8,0},{10,2},{12,4},{14,6},{16,8},{18,... | collective-permute-start | bytes 294920 | tf_op jit(solution)/shard_map/ppermute | solution.py:24
  93.1 6.8 %collective-permute-start.16 = (f16[64,768]{1,0:T(8,128)(2,1)S(1)}, f16[64,768]{1,0:T(8,128)(2,1)S(1)}, u32[]{:S(2)}, u32[]{:S(2)}) collective-permute-start(f16[64,768]{1,0:T(8,128)(2,1)S(1)} %get-tuple-element.21), channel_id=1, source_target_pairs={{0,8},{2,10},{4,12},{6,14},{8,16},{10,18},{12,20},{14,22},{16,24},... | collective-permute-start | bytes 294920 | tf_op jit(solution)/shard_map/ppermute | solution.py:24
  94.6 9.0 %collective-permute-start.17 = (f16[64,768]{1,0:T(8,128)(2,1)S(1)}, f16[64,768]{1,0:T(8,128)(2,1)S(1)}, u32[]{:S(2)}, u32[]{:S(2)}) collective-permute-start(f16[64,768]{1,0:T(8,128)(2,1)S(1)} %get-tuple-element.23), channel_id=1, source_target_pairs={{0,16},{2,18},{4,20},{6,22},{8,24},{10,26},{12,28},{14,30},{16,0},... | collective-permute-start | bytes 294920 | tf_op jit(solution)/shard_map/ppermute | solution.py:24
  97.0 6.6 %collective-permute-start.18 = (f16[64,768]{1,0:T(8,128)(2,1)S(1)}, f16[64,768]{1,0:T(8,128)(2,1)S(1)}, u32[]{:S(2)}, u32[]{:S(2)}) collective-permute-start(f16[64,768]{1,0:T(8,128)(2,1)S(1)} %get-tuple-element.22), channel_id=1, source_target_pairs={{0,24},{2,26},{4,28},{6,30},{8,0},{10,2},{12,4},{14,6},{16,8},{18,... | collective-permute-start | bytes 294920 | tf_op jit(solution)/shard_map/ppermute | solution.py:24
  98.0 8.1 %collective-permute-start.22 = (f16[64,768]{1,0:T(8,128)(2,1)S(1)}, f16[64,768]{1,0:T(8,128)(2,1)S(1)}, u32[]{:S(2)}, u32[]{:S(2)}) collective-permute-start(f16[64,768]{1,0:T(8,128)(2,1)S(1)} %get-tuple-element.24), channel_id=1, source_target_pairs={{0,8},{2,10},{4,12},{6,14},{8,16},{10,18},{12,20},{14,22},{16,24},... | collective-permute-start | bytes 294920 | tf_op jit(solution)/shard_map/ppermute | solution.py:24
  98.5 14.6 %collective-permute-start.23 = (f16[64,768]{1,0:T(8,128)(2,1)S(1)}, f16[64,768]{1,0:T(8,128)(2,1)S(1)}, u32[]{:S(2)}, u32[]{:S(2)}) collective-permute-start(f16[64,768]{1,0:T(8,128)(2,1)S(1)} %get-tuple-element.26), channel_id=1, source_target_pairs={{0,16},{2,18},{4,20},{6,22},{8,24},{10,26},{12,28},{14,30},{16,0},... | collective-permute-start | bytes 294920 | tf_op jit(solution)/shard_map/ppermute | solution.py:24
  99.9 13.2 %collective-permute-start.24 = (f16[64,768]{1,0:T(8,128)(2,1)S(1)}, f16[64,768]{1,0:T(8,128)(2,1)S(1)}, u32[]{:S(2)}, u32[]{:S(2)}) collective-permute-start(f16[64,768]{1,0:T(8,128)(2,1)S(1)} %get-tuple-element.25), channel_id=1, source_target_pairs={{0,24},{2,26},{4,28},{6,30},{8,0},{10,2},{12,4},{14,6},{16,8},{18,... | collective-permute-start | bytes 294920 | tf_op jit(solution)/shard_map/ppermute | solution.py:24
  113.8 6.6 %copy-start.3 = (f32[1,64,3072]{2,1,0:T(8,128)}, f32[1,64,3072]{2,1,0:T(8,128)S(1)}, u32[]{:S(2)}) copy-start(f32[1,64,3072]{2,1,0:T(8,128)S(1)} %get-tuple-element.9) | copy-start | bytes 2359300
  113.8 6.6 %copy-start.4 = (f32[1,64,3072]{2,1,0:T(8,128)}, f32[1,64,3072]{2,1,0:T(8,128)S(1)}, u32[]{:S(2)}) copy-start(f32[1,64,3072]{2,1,0:T(8,128)S(1)} %get-tuple-element.10) | copy-start | bytes 2359300
  114.3 6.2 %copy-start.2 = (f32[1,64,3072]{2,1,0:T(8,128)}, f32[1,64,3072]{2,1,0:T(8,128)S(1)}, u32[]{:S(2)}) copy-start(f32[1,64,3072]{2,1,0:T(8,128)S(1)} %get-tuple-element.7) | copy-start | bytes 2359300
  114.3 18.1 %collective-permute-start.25 = (f16[64,3072]{1,0:T(8,128)(2,1)S(1)}, f16[64,3072]{1,0:T(8,128)(2,1)S(1)}, u32[]{:S(2)}, u32[]{:S(2)}) collective-permute-start(f16[64,3072]{1,0:T(8,128)(2,1)S(1)} %get-tuple-element.6), channel_id=1, source_target_pairs={{0,2},{2,0},{4,6},{6,4},{8,10},{10,8},{12,14},{14,12},{16,18},{18,... | collective-permute-start | bytes 1179656 | tf_op jit(solution)/shard_map/ppermute | solution.py:30
  117.4 14.8 %collective-permute-start.26 = (f16[64,3072]{1,0:T(8,128)(2,1)S(1)}, f16[64,3072]{1,0:T(8,128)(2,1)S(1)}, u32[]{:S(2)}, u32[]{:S(2)}) collective-permute-start(f16[64,3072]{1,0:T(8,128)(2,1)S(1)} %get-tuple-element.6), channel_id=1, source_target_pairs={{0,4},{2,6},{4,0},{6,2},{8,12},{10,14},{12,8},{14,10},{16,20},{18,... | collective-permute-start | bytes 1179656 | tf_op jit(solution)/shard_map/ppermute | solution.py:27
  117.4 12.2 %collective-permute-start.28 = (f16[64,3072]{1,0:T(8,128)(2,1)S(1)}, f16[64,3072]{1,0:T(8,128)(2,1)S(1)}, u32[]{:S(2)}, u32[]{:S(2)}) collective-permute-start(f16[64,3072]{1,0:T(8,128)(2,1)S(1)} %get-tuple-element.6), channel_id=1, source_target_pairs={{0,8},{2,10},{4,12},{6,14},{8,16},{10,18},{12,20},{14,22},{16,24},... | collective-permute-start | bytes 1179656 | tf_op jit(solution)/shard_map/ppermute | solution.py:24
  129.6 16.6 %collective-permute-start.29 = (f16[64,3072]{1,0:T(8,128)(2,1)S(1)}, f16[64,3072]{1,0:T(8,128)(2,1)S(1)}, u32[]{:S(2)}, u32[]{:S(2)}) collective-permute-start(f16[64,3072]{1,0:T(8,128)(2,1)S(1)} %collective-permute-done.28), channel_id=1, source_target_pairs={{0,2},{2,0},{4,6},{6,4},{8,10},{10,8},{12,14},{14,12},{16,18},{18,... | collective-permute-start | bytes 1179656 | tf_op jit(solution)/shard_map/ppermute | solution.py:30
  130.7 14.8 %collective-permute-start.30 = (f16[64,3072]{1,0:T(8,128)(2,1)S(1)}, f16[64,3072]{1,0:T(8,128)(2,1)S(1)}, u32[]{:S(2)}, u32[]{:S(2)}) collective-permute-start(f16[64,3072]{1,0:T(8,128)(2,1)S(1)} %collective-permute-done.28), channel_id=1, source_target_pairs={{0,4},{2,6},{4,0},{6,2},{8,12},{10,14},{12,8},{14,10},{16,20},{18,... | collective-permute-start | bytes 1179656 | tf_op jit(solution)/shard_map/ppermute | solution.py:27
  132.2 12.2 %collective-permute-start.32 = (f16[64,3072]{1,0:T(8,128)(2,1)S(1)}, f16[64,3072]{1,0:T(8,128)(2,1)S(1)}, u32[]{:S(2)}, u32[]{:S(2)}) collective-permute-start(f16[64,3072]{1,0:T(8,128)(2,1)S(1)} %collective-permute-done.28), channel_id=1, source_target_pairs={{0,8},{2,10},{4,12},{6,14},{8,16},{10,18},{12,20},{14,22},{16,24},... | collective-permute-start | bytes 1179656 | tf_op jit(solution)/shard_map/ppermute | solution.py:24
  132.2 13.3 %collective-permute-start.27 = (f16[64,3072]{1,0:T(8,128)(2,1)S(1)}, f16[64,3072]{1,0:T(8,128)(2,1)S(1)}, u32[]{:S(2)}, u32[]{:S(2)}) collective-permute-start(f16[64,3072]{1,0:T(8,128)(2,1)S(1)} %collective-permute-done.26), channel_id=1, source_target_pairs={{0,2},{2,0},{4,6},{6,4},{8,10},{10,8},{12,14},{14,12},{16,18},{18,... | collective-permute-start | bytes 1179656 | tf_op jit(solution)/shard_map/ppermute | solution.py:30
  144.4 16.5 %collective-permute-start.33 = (f16[64,3072]{1,0:T(8,128)(2,1)S(1)}, f16[64,3072]{1,0:T(8,128)(2,1)S(1)}, u32[]{:S(2)}, u32[]{:S(2)}) collective-permute-start(f16[64,3072]{1,0:T(8,128)(2,1)S(1)} %collective-permute-done.32), channel_id=1, source_target_pairs={{0,2},{2,0},{4,6},{6,4},{8,10},{10,8},{12,14},{14,12},{16,18},{18,... | collective-permute-start | bytes 1179656 | tf_op jit(solution)/shard_map/ppermute | solution.py:30
  145.5 14.8 %collective-permute-start.34 = (f16[64,3072]{1,0:T(8,128)(2,1)S(1)}, f16[64,3072]{1,0:T(8,128)(2,1)S(1)}, u32[]{:S(2)}, u32[]{:S(2)}) collective-permute-start(f16[64,3072]{1,0:T(8,128)(2,1)S(1)} %collective-permute-done.32), channel_id=1, source_target_pairs={{0,4},{2,6},{4,0},{6,2},{8,12},{10,14},{12,8},{14,10},{16,20},{18,... | collective-permute-start | bytes 1179656 | tf_op jit(solution)/shard_map/ppermute | solution.py:27
  145.5 12.2 %collective-permute-start.36 = (f16[64,3072]{1,0:T(8,128)(2,1)S(1)}, f16[64,3072]{1,0:T(8,128)(2,1)S(1)}, u32[]{:S(2)}, u32[]{:S(2)}) collective-permute-start(f16[64,3072]{1,0:T(8,128)(2,1)S(1)} %collective-permute-done.32), channel_id=1, source_target_pairs={{0,8},{2,10},{4,12},{6,14},{8,16},{10,18},{12,20},{14,22},{16,24},... | collective-permute-start | bytes 1179656 | tf_op jit(solution)/shard_map/ppermute | solution.py:24
  145.5 15.1 %collective-permute-start.31 = (f16[64,3072]{1,0:T(8,128)(2,1)S(1)}, f16[64,3072]{1,0:T(8,128)(2,1)S(1)}, u32[]{:S(2)}, u32[]{:S(2)}) collective-permute-start(f16[64,3072]{1,0:T(8,128)(2,1)S(1)} %collective-permute-done.30), channel_id=1, source_target_pairs={{0,2},{2,0},{4,6},{6,4},{8,10},{10,8},{12,14},{14,12},{16,18},{18,... | collective-permute-start | bytes 1179656 | tf_op jit(solution)/shard_map/ppermute | solution.py:30
  157.8 12.9 %collective-permute-start.37 = (f16[64,3072]{1,0:T(8,128)(2,1)S(1)}, f16[64,3072]{1,0:T(8,128)(2,1)S(1)}, u32[]{:S(2)}, u32[]{:S(2)}) collective-permute-start(f16[64,3072]{1,0:T(8,128)(2,1)S(1)} %collective-permute-done.36), channel_id=1, source_target_pairs={{0,2},{2,0},{4,6},{6,4},{8,10},{10,8},{12,14},{14,12},{16,18},{18,... | collective-permute-start | bytes 1179656 | tf_op jit(solution)/shard_map/ppermute | solution.py:30
  158.9 10.7 %collective-permute-start.38 = (f16[64,3072]{1,0:T(8,128)(2,1)S(1)}, f16[64,3072]{1,0:T(8,128)(2,1)S(1)}, u32[]{:S(2)}, u32[]{:S(2)}) collective-permute-start(f16[64,3072]{1,0:T(8,128)(2,1)S(1)} %collective-permute-done.36), channel_id=1, source_target_pairs={{0,4},{2,6},{4,0},{6,2},{8,12},{10,14},{12,8},{14,10},{16,20},{18,... | collective-permute-start | bytes 1179656 | tf_op jit(solution)/shard_map/ppermute | solution.py:27
  160.3 10.1 %collective-permute-start.35 = (f16[64,3072]{1,0:T(8,128)(2,1)S(1)}, f16[64,3072]{1,0:T(8,128)(2,1)S(1)}, u32[]{:S(2)}, u32[]{:S(2)}) collective-permute-start(f16[64,3072]{1,0:T(8,128)(2,1)S(1)} %collective-permute-done.34), channel_id=1, source_target_pairs={{0,2},{2,0},{4,6},{6,4},{8,10},{10,8},{12,14},{14,12},{16,18},{18,... | collective-permute-start | bytes 1179656 | tf_op jit(solution)/shard_map/ppermute | solution.py:30
  169.6 2.1 %collective-permute-start.39 = (f16[64,3072]{1,0:T(8,128)(2,1)S(1)}, f16[64,3072]{1,0:T(8,128)(2,1)S(1)}, u32[]{:S(2)}, u32[]{:S(2)}) collective-permute-start(f16[64,3072]{1,0:T(8,128)(2,1)S(1)} %collective-permute-done.38), channel_id=1, source_target_pairs={{0,2},{2,0},{4,6},{6,4},{8,10},{10,8},{12,14},{14,12},{16,18},{18,... | collective-permute-start | bytes 1179656 | tf_op jit(solution)/shard_map/ppermute | solution.py:30
  171.9 4.8 %copy-start = (f32[1,1024,3072]{2,1,0:T(8,128)}, f32[1,1024,3072]{2,1,0:T(8,128)S(1)}, u32[]{:S(2)}) copy-start(f32[1,1024,3072]{2,1,0:T(8,128)S(1)} %bitcast_dynamic-update-slice_fusion) | copy-start | bytes 37748740

commit v2 on v1

v2 whole, which is shorter than its diff:
```python
import functools

import jax
import jax.numpy as jnp
from jax import lax
from jax.experimental import pallas as pl
from jax.experimental.pallas import tpu as pltpu
from jax.sharding import PartitionSpec as P

F16 = jnp.float16
F32 = jnp.float32
BF16 = jnp.bfloat16
CHUNKS = (768, 768, 768, 768)
STREAMS = (3072,)
PUT_FLOPS = 2 << 30


def after(value, other):
    return lax.optimization_barrier((value, other))[0]


def dispatch_kernel(cap_rows, ids, probs, grad, *outs):
    tok_rows = ids.shape[1]
    hit = ids[...] == 0
    weight = jnp.sum(jnp.where(hit, probs[...], 0.0), axis=0, keepdims=True)
    chosen = jnp.sum(jnp.where(hit, 1.0, 0.0), axis=0, keepdims=True)
    earlier = lax.broadcasted_iota(jnp.int32, (tok_rows, tok_rows), 0) < lax.broadcasted_iota(
        jnp.int32, (tok_rows, tok_rows), 1
    )
    slot = jnp.dot(
        jnp.broadcast_to(chosen, (8, tok_rows)).astype(BF16),
        jnp.where(earlier, 1.0, 0.0).astype(BF16),
        preferred_element_type=F32,
    )[:1]
    slot = jnp.where(chosen > 0.0, slot, -1.0)
    places = lax.broadcasted_iota(jnp.int32, (cap_rows, tok_rows), 0).astype(F32)
    placing = jnp.where(slot == places, 1.0, 0.0).astype(BF16)
    weight = jnp.broadcast_to(weight, (128, tok_rows)).T[:, :1]
    first = 0
    for out in outs:
        size = out.shape[1]
        scaled = (weight * grad[:, first : first + size].astype(F32)).astype(BF16)
        out[...] = jnp.dot(placing, scaled, preferred_element_type=F32).astype(BF16)
        first += size


def dispatch(ids, probs, grad, cap_rows):
    vmem = pl.BlockSpec(memory_space=pltpu.VMEM)
    return pl.pallas_call(
        functools.partial(dispatch_kernel, cap_rows),
        out_shape=tuple(jax.ShapeDtypeStruct((cap_rows, size), BF16) for size in CHUNKS),
        in_specs=[vmem] * 3,
        out_specs=(vmem,) * len(CHUNKS),
        compiler_params=pltpu.CompilerParams(vmem_limit_bytes=16 << 20),
        name="dispatch",
    )(ids.T, probs.T, grad)


def put_kernel(marks, aliased, starts, *refs):
    refs = refs[1:] if aliased else refs
    pieces, out, sems = refs[: len(marks)], refs[len(marks)], refs[len(marks) + 1]
    copies = []
    for n, (index, column) in enumerate(marks):
        height, size = pieces[n].shape
        row = pl.multiple_of(starts[index], height)
        spot = out.at[pl.ds(row, height), pl.ds(column, size)]
        copies.append(pltpu.make_async_copy(pieces[n], spot, sems.at[n]))
        copies[-1].start()
    for copy in copies:
        copy.wait()


def put(weights, shape, starts, marks, pieces):
    aliased = weights is not None
    spec = pl.BlockSpec(memory_space=pl.ANY)
    return pl.pallas_call(
        functools.partial(put_kernel, tuple(marks), aliased),
        out_shape=jax.ShapeDtypeStruct(shape, F32),
        in_specs=[pl.BlockSpec(memory_space=pltpu.SMEM)] + [spec] * (aliased + len(pieces)),
        out_specs=spec,
        scratch_shapes=[pltpu.SemaphoreType.DMA((len(pieces),))],
        input_output_aliases={1: 0} if aliased else {},
        compiler_params=pltpu.CompilerParams(vmem_limit_bytes=1 << 20),
        cost_estimate=pl.CostEstimate(flops=PUT_FLOPS, bytes_accessed=0, transcendentals=0),
        name="put",
    )(starts, *([weights] if aliased else []), *pieces)


def hidden_kernel(sizes, at, gate, up, mine, send):
    experts, rows_b, rows_a, own = sizes
    cap_rows = gate.shape[0] // experts
    at_e, at_b, core = at[0], at[1], at[2]
    values = []
    for j in range(experts):
        spot = pl.ds(pl.multiple_of(lax.rem(at_e + j, experts) * cap_rows, cap_rows), cap_rows)
        value = gate[spot, :].astype(F32)
        values.append(value / (1.0 + jnp.exp(-value)) * up[spot, :].astype(F32))
    value = jnp.concatenate(values, axis=0).T.astype(BF16)
    for b in range(rows_b):
        k = lax.rem(b - at_b + rows_b, rows_b)
        for a in range(rows_a):
            first = (a * rows_b + b) * 2 * own
            low, high = value[first : first + own], value[first + own : first + 2 * own]
            rows = pl.ds(a * own, own)
            mine[k, rows, :] = jnp.where(core == 0, low, high)
            send[k, rows, :] = jnp.where(core == 0, high, low)


def hidden_pieces(at, gate, up, sizes):
    experts, rows_b, rows_a, own = sizes
    shape = jax.ShapeDtypeStruct((rows_b, rows_a * own, gate.shape[0]), BF16)
    vmem = pl.BlockSpec(memory_space=pltpu.VMEM)
    return pl.pallas_call(
        functools.partial(hidden_kernel, sizes),
        out_shape=(shape, shape),
        in_specs=[pl.BlockSpec(memory_space=pltpu.SMEM), vmem, vmem],
        out_specs=(vmem, vmem),
        compiler_params=pltpu.CompilerParams(vmem_limit_bytes=(8 << 20) * max(1, experts // 2)),
        name="hidden_pieces",
    )(at, gate, up)


def product_kernel(scale, left, *refs):
    pieces, kept, sent, rows = refs[:-3], refs[-3], refs[-2], refs[-1]
    height = pieces[0].shape[0]
    for n, piece in enumerate(pieces):
        rows[n * height : (n + 1) * height, :] = piece[...]
    for k in range(left.shape[0]):
        total = jnp.dot(left[k], rows[...], preferred_element_type=F32)
        total = total * scale if scale != 1.0 else total
        if k == 0:
            kept[...] = total
        else:
            sent[k - 1] = total


def product(left, pieces, scale):
    count, half, depth = left.shape
    size = pieces[0].shape[1]
    vmem = pl.BlockSpec(memory_space=pltpu.VMEM)
    return pl.pallas_call(
        functools.partial(product_kernel, scale),
        out_shape=(
            jax.ShapeDtypeStruct((half, size), F32),
            jax.ShapeDtypeStruct((count - 1, half, size), F32),
        ),
        in_specs=[vmem] * (1 + len(pieces)),
        out_specs=(vmem, vmem),
        scratch_shapes=[pltpu.VMEM((depth, size), BF16)],
        compiler_params=pltpu.CompilerParams(vmem_limit_bytes=16 << 20),
        cost_estimate=pl.CostEstimate(flops=2 * count * half * depth * size, bytes_accessed=0, transcendentals=0),
        name="product",
    )(left, *pieces)


def build(mesh):
    devices = mesh.shape["dp"]
    experts = mesh.shape["expert"]
    rows_a = 4
    rows_b = devices // (2 * rows_a)

    def place(a, b, c):
        return ((a % rows_a) * rows_b + b % rows_b) * 2 + c % 2

    spots = [(a, b, c) for a in range(rows_a) for b in range(rows_b) for c in range(2)]

    def flip_a(value, k):
        return lax.ppermute(value, "dp", [(place(a, b, c), place(a ^ k, b, c)) for a, b, c in spots])

    ring = [p ^ (p >> 1) for p in range(rows_a)]

    def step_ring(value):
        pairs = [(p, (p + 1) % rows_a) for p in range(rows_a)]
        return lax.ppermute(
            value,
            "dp",
            [(place(ring[p], b, c), place(ring[q], b, c)) for p, q in pairs for b in range(rows_b) for c in range(2)],
        )

    def shift_b(value, k):
        return lax.ppermute(value, "dp", [(place(a, b, c), place(a, b + k, c)) for a, b, c in spots])

    def swap_core(value):
        return lax.ppermute(value, "dp", [(place(a, b, c), place(a, b, c + 1)) for a, b, c in spots])

    def shift_expert(value, k):
        return lax.ppermute(value, "expert", [(e, (e + k) % experts) for e in range(experts)])

    def local(grad_out, expert_ids, gate_probs, saved_gate, saved_up, master, moment_one, moment_two):
        me = lax.axis_index("dp")
        core = me % 2
        at_b = (me // 2) % rows_b
        at_a = me // (2 * rows_b)
        at_e = lax.axis_index("expert")
        tok_rows, dim = grad_out.shape
        cap_rows = tok_rows * 3 // 8
        own = master.shape[1]
        slot_rows, _, width = saved_gate.shape

        count = len(CHUNKS)
        cuts = [sum(CHUNKS[:i]) for i in range(count)]
        parts = dispatch(expert_ids, gate_probs, grad_out, cap_rows)

        hidden_mine, hidden_send = hidden_pieces(
            jnp.stack([at_e, at_b, core]).astype(jnp.int32),
            saved_gate.reshape(slot_rows, width),
            saved_up.reshape(slot_rows, width),
            (experts, rows_b, rows_a, own),
        )
        hidden_other = swap_core(hidden_send)
        left = jnp.concatenate([hidden_mine, hidden_other], axis=2)

        largest = 2 * rows_b * slot_rows * 36.0 * 0.2
        shrink = 1.0
        while largest * shrink > 60000.0:
            shrink *= 0.5

        far = []
        for i in range(count):
            part = parts[i]
            if i == 1:
                part = after(part, hidden_send)
            elif i > 1:
                part = after(part, far[i - 2][-1])
            far.append([shift_expert(part, -j) for j in range(1, experts)])
        kept, sent = [], []
        for i in range(count):
            here = [parts[i]] + (far[i] if i == 0 else [after(x, sent[i - 1][-1]) for x in far[i]])
            there = [swap_core(x) for x in here]
            mine, others = product(left, here + there, shrink)
            kept.append(mine)
            sent.append([others[k].astype(F16) for k in range(rows_b - 1)])
        got = [[shift_b(x, k + 1) for k, x in enumerate(xs)] for xs in sent]
        halves = []
        for i in range(count):
            total = kept[i]
            for x in got[i]:
                total = total + (after(x, sent[i + 1][-1]) if i + 1 < count else x).astype(F32)
            total = total.reshape(rows_a // 2, 2, own, CHUNKS[i])
            mine = lax.dynamic_index_in_dim(total, at_a % 2, 1, False)
            send = lax.dynamic_index_in_dim(total, 1 - at_a % 2, 1, False).astype(F16)
            halves.append((mine, send))
        quarters = []
        for i in range(count):
            mine, send = halves[i]
            came = flip_a(send, 1)
            total = mine + (after(came, halves[i + 1][1]) if i + 1 < count else came).astype(F32)
            mine = lax.dynamic_index_in_dim(total, at_a // 2, 0, False)
            send = lax.dynamic_index_in_dim(total, 1 - at_a // 2, 0, False).astype(F16)
            quarters.append((mine, send))
        grads = []
        for i in range(count):
            mine, send = quarters[i]
            came = flip_a(send, 2)
            grads.append(mine + (after(came, quarters[i + 1][1]) if i + 1 < count else came).astype(F32))
        grad = (jnp.concatenate(grads, axis=1) * (1.0 / shrink)).reshape(master.shape)

        new_one = 0.9 * moment_one + 0.1 * grad
        new_two = 0.95 * moment_two + 0.05 * grad * grad
        step = new_one / (1.0 - 0.9**20) / (jnp.sqrt(new_two / (1.0 - 0.95**20)) + 1e-08)
        wrms = jnp.sqrt(jnp.mean(master * master, axis=-1, keepdims=True) + 1e-06)
        srms = jnp.sqrt(jnp.mean(step * step, axis=-1, keepdims=True) + 1e-06)
        factor = jnp.minimum(1.0, 0.02 * wrms / (0.01 * srms))
        new_master = master - 0.01 * factor * step

        bound = jnp.max(jnp.abs(master[0]), axis=-1, keepdims=True) + 0.08
        power = jnp.floor(jnp.log2(bound))
        coded = (new_master[0] * jnp.exp2(13.0 - power)).astype(F16)
        coded = jnp.concatenate([coded, jnp.broadcast_to(power.astype(F16), (own, 128))], axis=1)
        pad = coded.shape[1] - dim
        edges = [(sum(STREAMS[:n]), sum(STREAMS[: n + 1])) for n in range(len(STREAMS))]
        coded = jnp.concatenate([coded[:, dim:], coded[:, :dim]], axis=1)
        streams = [coded[:, (low + pad if n else low) : high + pad] for n, (low, high) in enumerate(edges)]
        held = [[value] for value in streams]
        moved = [[[shift_b(value, j) for j in range(1, rows_b)]] for value in streams]
        for value, along in zip(held, moved):
            for i in range(1, rows_a):
                value.append(step_ring(value[-1]))
                along.append([shift_b(value[-1], j) for j in range(1, rows_b)])
        groups = [[(0, 0, n) for n in range(len(STREAMS))]]
        for i in range(1, rows_a + 1):
            for n in range(len(STREAMS)):
                group = [(i, 0, n)] if i < rows_a else []
                groups.append(group + [(i - 1, j, n) for j in range(1, rows_b)])
        scales, weights, late = {}, None, []
        back = (at_a ^ (at_a >> 1)) + rows_a - jnp.arange(rows_a, dtype=jnp.int32)
        from_a = (back % rows_a) ^ (back % rows_a >> 1)
        from_b = (at_b + rows_b - jnp.arange(rows_b, dtype=jnp.int32)) % rows_b
        from_core = (core + jnp.arange(2, dtype=jnp.int32)) % 2
        starts = (from_a[:, None, None] * rows_b + from_b[:, None]) * 2 + from_core
        starts = (starts * own).astype(jnp.int32).reshape(-1)
        for group in groups + [[]]:
            pieces = late
            late = []
            for i, j, n in group:
                value = held[n][i] if j == 0 else moved[n][i][j - 1]
                pieces = pieces + [((i, j, 0), n, value)]
                late.append(((i, j, 1), n, swap_core(value)))
            values = []
            for spot, n, value in pieces:
                if n == 0:
                    scales[spot] = jnp.exp2(value[:, :1].astype(F32) - 13.0)
                    value = value[:, pad:]
                values.append(value.astype(F32) * scales[spot])
            marks = [((i * rows_b + j) * 2 + k, edges[n][0]) for (i, j, k), n, _ in pieces]
            weights = put(weights, (width, dim), starts, marks, values)
        return (new_master, new_one, new_two, weights[None])

    return local


def solution(mesh):
    return jax.shard_map(
        build(mesh),
        mesh=mesh,
        in_specs=(
            P(("dp", "expert"), None),
            P(("dp", "expert"), None),
            P(("dp", "expert"), None),
            P("dp", "expert", None),
            P("dp", "expert", None),
            P("expert", "dp", None),
            P("expert", "dp", None),
            P("expert", "dp", None),
        ),
        out_specs=(
            P("expert", "dp", None),
            P("expert", "dp", None),
            P("expert", "dp", None),
            P("expert", None, None),
        ),
        check_vma=False,
    )
```

time: 178 us -> 136 us (0.76)
  blocking collectives: 30.3 us -> 0 us
  waiting for transfers between devices: 76.7 us -> 58 us
  Pallas kernels: 0 us -> 16.7 us
  matrix products: 14.7 us -> 0 us
  starting transfers between devices: 32.6 us -> 42.2 us
  local copies, waits for them, and re-layouts: 9.63 us -> 6.81 us
    unnamed x1 -> x0, blocking collectives: 30.3 us -> none
    ppermute x15 -> x11, waiting for transfers between devices: 44.3 us -> 23.3 us  [the longest x3 18.7 us: step_ring(): lax.ppermute(value, 'dp', [(place(ring[p], b, c), place(ring[q], b, c)) f...]
    pallas_call x0 -> x12, Pallas kernels: none -> 16.7 us  [the longest x6 11.3 us: put(): pl.pallas_call(functools.partial(put_kernel, tuple(marks), aliased), out_...]
    ppermute x4, waiting for transfers between devices: 0.01 us -> 16.6 us  [shift_expert(): lax.ppermute(value, 'expert', [(e, (e + k) % experts) for e in range(expe...]
    dot_general x9 -> x0, matrix products: 14.7 us -> none  [the longest x4 5.98 us: local(): total = jnp.dot(blocks[0], both, preferred_element_type=F32) * shrink]
    ppermute x8, waiting for transfers between devices: 31.6 us -> 18 us  [shift_b(): lax.ppermute(value, 'dp', [(place(a, b, c), place(a, b + k, c)) for a, b,...]
    ppermute x15 -> x11, starting transfers between devices: 9.14 us -> 17 us  [the longest x8 16.8 us: flip_a(): lax.ppermute(value, 'dp', [(place(a, b, c), place(a ^ k, b, c)) for a, b,...]
    concatenate x5 -> x1, other arithmetic: 5.1 us -> 0.1 us  [local(): coded = jnp.concatenate([coded[:, dim:], coded[:, :dim]], axis=1)]
  transfers between devices with their start and end apart: 40 -> 40, of which waited for: 13 -> 12; matrix products, arithmetic and copies ran while one was open for 14% -> 7% of each run, Pallas kernels for 0% -> 10%
where the time goes in v2:
time: 136 us; the launch traced here: 135 us
  waiting for transfers between devices  58 us (43%)
  starting transfers between devices  42.2 us (31%)
  Pallas kernels  16.7 us (12%)
  other arithmetic  10.1 us (7%)
  local copies, waits for them, and re-layouts  6.81 us (5%)
  between operations  1.45 us (1%)
    ppermute x3, waiting for transfers between devices, step_ring(): lax.ppermute(value, 'dp', [(place(ring[p], b, c), place(ring[q], b, c)) f...  18.7 us
    ppermute x8, waiting for transfers between devices, shift_b(): lax.ppermute(value, 'dp', [(place(a, b, c), place(a, b + k, c)) for a, b,...  18 us
    ppermute x17, starting transfers between devices, swap_core(): lax.ppermute(value, 'dp', [(place(a, b, c), place(a, b, c + 1)) for a, b,...  17.4 us
    ppermute x8, starting transfers between devices, flip_a(): lax.ppermute(value, 'dp', [(place(a, b, c), place(a ^ k, b, c)) for a, b,...  16.8 us
    ppermute x4, waiting for transfers between devices, shift_expert(): lax.ppermute(value, 'expert', [(e, (e + k) % experts) for e in range(expe...  16.6 us
    pallas_call x6, Pallas kernels, put(): pl.pallas_call(functools.partial(put_kernel, tuple(marks), aliased), out_...  11.3 us
    unnamed x21, local copies, waits for them, and re-layouts  5.59 us
    ppermute x8, waiting for transfers between devices, flip_a(): lax.ppermute(value, 'dp', [(place(a, b, c), place(a ^ k, b, c)) for a, b,...  4.66 us
  transfers between devices with their start and end apart: 40, of which 12 were waited for; matrix products, arithmetic and copies ran while one was open for 7% of the time, Pallas kernels for 10%

profile of v2, /device:TPU:1, one launch (start us, length us, event | category | flops | bytes accessed | tf_op | source)
XLA Modules:
  0.0 135.2 jit_solution(10612651064897690108)
XLA Ops:
  0.6 1.9 %copy-done = bf16[512,3072]{1,0:T(8,128)(2,1)S(1)} copy-done((bf16[512,3072]{1,0:T(8,128)(2,1)S(1)}, bf16[512,3072]{1,0:T(8,128)(2,1)}, u32[]{:S(2)}) %copy-start) | copy-done | bytes 3145752
  2.5 0.7 copy-done.3
  3.2 0.7 copy-done.4
  3.9 1.1 dispatch.1
  5.0 2.1 %collective-permute-start.1 = (bf16[192,768]{1,0:T(8,128)(2,1)S(1)}, bf16[192,768]{1,0:T(8,128)(2,1)S(1)}, u32[]{:S(2)}, u32[]{:S(2)}) collective-permute-start(bf16[192,768]{1,0:T(8,128)(2,1)S(1)} %get-tuple-element.35.refs_0_), channel_id=1, source_target_pairs={{0,1},{1,0},{2,3},{3,2},{4,5},{5,4},{6,7},{7,6},{8,9},{9,8},{10,11... | collective-permute-start | bytes 884744 | tf_op jit(solution)/shard_map/ppermute | solution.py:187
  7.2 1.1 copy-done.1
  8.3 1.1 copy-done.2
  9.5 1.2 hidden_pieces.1
  10.7 1.0 collective-permute-start
  11.8 0.4 collective-permute-start.6
  12.3 1.6 %collective-permute-done.1.refs_1_ = bf16[192,768]{1,0:T(8,128)(2,1)S(1)} collective-permute-done((bf16[192,768]{1,0:T(8,128)(2,1)S(1)}, bf16[192,768]{1,0:T(8,128)(2,1)S(1)}, u32[]{:S(2)}, u32[]{:S(2)}) %collective-permute-start.1) | collective-permute-done | bytes 294944 | tf_op jit(solution)/shard_map/ppermute | solution.py:187
  13.9 1.6 %collective-permute-start.3 = (bf16[192,768]{1,0:T(8,128)(2,1)S(1)}, bf16[192,768]{1,0:T(8,128)(2,1)S(1)}, u32[]{:S(2)}, u32[]{:S(2)}) collective-permute-start(bf16[192,768]{1,0:T(8,128)(2,1)S(1)} %collective-permute-done.1.refs_1_), channel_id=1, source_target_pairs={{0,2},{2,0},{4,6},{6,4},{8,10},{10,8},{12,14},{14,12},{16,18},{18,... | collective-permute-start | bytes 884744 | tf_op jit(solution)/shard_map/ppermute | solution.py:184
  15.7 1.1 constant_dynamic-update-slice_fusion.left
  16.8 0.6 collective-permute-start.17
  17.3 0.8 product.4
  18.2 2.7 %collective-permute-done.5.refs_1_ = bf16[192,768]{1,0:T(8,128)(2,1)S(1)} collective-permute-done((bf16[192,768]{1,0:T(8,128)(2,1)S(1)}, bf16[192,768]{1,0:T(8,128)(2,1)S(1)}, u32[]{:S(2)}, u32[]{:S(2)}) %collective-permute-start.5) | collective-permute-done | bytes 294944 | tf_op jit(solution)/shard_map/ppermute | solution.py:187
  20.8 0.8 collective-permute-start.7
  21.8 1.2 collective-permute-start.4
  23.0 1.3 abs_reduce_fusion
  24.3 1.3 collective-permute-start.16
  25.6 0.3 collective-permute-start.10
  25.8 0.8 product.5
  26.7 12.3 %collective-permute-done.10.refs_1_ = bf16[192,768]{1,0:T(8,128)(2,1)S(1)} collective-permute-done((bf16[192,768]{1,0:T(8,128)(2,1)S(1)}, bf16[192,768]{1,0:T(8,128)(2,1)S(1)}, u32[]{:S(2)}, u32[]{:S(2)}) %collective-permute-start.10) | collective-permute-done | bytes 294944 | tf_op jit(solution)/shard_map/ppermute | solution.py:187
  39.3 1.4 %collective-permute-start.12 = (bf16[192,768]{1,0:T(8,128)(2,1)S(1)}, bf16[192,768]{1,0:T(8,128)(2,1)S(1)}, u32[]{:S(2)}, u32[]{:S(2)}) collective-permute-start(bf16[192,768]{1,0:T(8,128)(2,1)S(1)} %collective-permute-done.10.refs_1_), channel_id=1, source_target_pairs={{0,2},{2,0},{4,6},{6,4},{8,10},{10,8},{12,14},{14,12},{16,18},{18,... | collective-permute-start | bytes 884744 | tf_op jit(solution)/shard_map/ppermute | solution.py:184
  40.8 1.4 %collective-permute-start.8 = (f16[2,64,768]{2,1,0:T(8,128)(2,1)S(1)}, f16[2,64,768]{2,1,0:T(8,128)(2,1)S(1)}, u32[]{:S(2)}, u32[]{:S(2)}) collective-permute-start(f16[2,64,768]{2,1,0:T(8,128)(2,1)S(1)} %fusion.2), channel_id=1, source_target_pairs={{0,8},{2,10},{4,12},{6,14},{8,0},{10,2},{12,4},{14,6},{16,24},{18,... | collective-permute-start | bytes 589832 | tf_op jit(solution)/shard_map/ppermute | solution.py:168
  42.2 0.8 product.6
  43.0 1.3 collective-permute-start.15
  44.3 0.6 collective-permute-start.18
  44.8 3.7 %collective-permute-done.9 = f16[256,768]{1,0:T(8,128)(2,1)S(1)} collective-permute-done((f16[256,768]{1,0:T(8,128)(2,1)S(1)}, f16[256,768]{1,0:T(8,128)(2,1)S(1)}, u32[]{:S(2)}, u32[]{:S(2)}) %collective-permute-start.9) | collective-permute-done | bytes 393248 | tf_op jit(solution)/shard_map/ppermute | solution.py:181
  48.7 1.4 %collective-permute-start.14 = (f16[2,64,768]{2,1,0:T(8,128)(2,1)S(1)}, f16[2,64,768]{2,1,0:T(8,128)(2,1)S(1)}, u32[]{:S(2)}, u32[]{:S(2)}) collective-permute-start(f16[2,64,768]{2,1,0:T(8,128)(2,1)S(1)} %fusion.3), channel_id=1, source_target_pairs={{0,8},{2,10},{4,12},{6,14},{8,0},{10,2},{12,4},{14,6},{16,24},{18,... | collective-permute-start | bytes 589832 | tf_op jit(solution)/shard_map/ppermute | solution.py:168
  50.1 2.4 %collective-permute-start.13 = (f16[64,768]{1,0:T(8,128)(2,1)S(1)}, f16[64,768]{1,0:T(8,128)(2,1)S(1)}, u32[]{:S(2)}, u32[]{:S(2)}) collective-permute-start(f16[64,768]{1,0:T(8,128)(2,1)S(1)} %fusion.10), channel_id=1, source_target_pairs={{0,16},{2,18},{4,20},{6,22},{8,24},{10,26},{12,28},{14,30},{16,0},... | collective-permute-start | bytes 294920 | tf_op jit(solution)/shard_map/ppermute | solution.py:168
  52.5 0.8 product.7
  53.3 0.3 collective-permute-start.21
  53.7 3.3 %collective-permute-done.15 = f16[256,768]{1,0:T(8,128)(2,1)S(1)} collective-permute-done((f16[256,768]{1,0:T(8,128)(2,1)S(1)}, f16[256,768]{1,0:T(8,128)(2,1)S(1)}, u32[]{:S(2)}, u32[]{:S(2)}) %collective-permute-start.15) | collective-permute-done | bytes 393248 | tf_op jit(solution)/shard_map/ppermute | solution.py:181
  57.1 1.4 %collective-permute-start.20 = (f16[2,64,768]{2,1,0:T(8,128)(2,1)S(1)}, f16[2,64,768]{2,1,0:T(8,128)(2,1)S(1)}, u32[]{:S(2)}, u32[]{:S(2)}) collective-permute-start(f16[2,64,768]{2,1,0:T(8,128)(2,1)S(1)} %fusion.4), channel_id=1, source_target_pairs={{0,8},{2,10},{4,12},{6,14},{8,0},{10,2},{12,4},{14,6},{16,24},{18,... | collective-permute-start | bytes 589832 | tf_op jit(solution)/shard_map/ppermute | solution.py:168
  58.5 2.4 %collective-permute-start.19 = (f16[64,768]{1,0:T(8,128)(2,1)S(1)}, f16[64,768]{1,0:T(8,128)(2,1)S(1)}, u32[]{:S(2)}, u32[]{:S(2)}) collective-permute-start(f16[64,768]{1,0:T(8,128)(2,1)S(1)} %fusion.11), channel_id=1, source_target_pairs={{0,16},{2,18},{4,20},{6,22},{8,24},{10,26},{12,28},{14,30},{16,0},... | collective-permute-start | bytes 294920 | tf_op jit(solution)/shard_map/ppermute | solution.py:168
  61.0 3.8 %collective-permute-done.21 = f16[256,768]{1,0:T(8,128)(2,1)S(1)} collective-permute-done((f16[256,768]{1,0:T(8,128)(2,1)S(1)}, f16[256,768]{1,0:T(8,128)(2,1)S(1)}, u32[]{:S(2)}, u32[]{:S(2)}) %collective-permute-start.21) | collective-permute-done | bytes 393248 | tf_op jit(solution)/shard_map/ppermute | solution.py:181
  64.8 2.0 %collective-permute-start.23 = (f16[2,64,768]{2,1,0:T(8,128)(2,1)S(1)}, f16[2,64,768]{2,1,0:T(8,128)(2,1)S(1)}, u32[]{:S(2)}, u32[]{:S(2)}) collective-permute-start(f16[2,64,768]{2,1,0:T(8,128)(2,1)S(1)} %fusion.5), channel_id=1, source_target_pairs={{0,8},{2,10},{4,12},{6,14},{8,0},{10,2},{12,4},{14,6},{16,24},{18,... | collective-permute-start | bytes 589832 | tf_op jit(solution)/shard_map/ppermute | solution.py:168
  66.9 2.4 %collective-permute-start.22 = (f16[64,768]{1,0:T(8,128)(2,1)S(1)}, f16[64,768]{1,0:T(8,128)(2,1)S(1)}, u32[]{:S(2)}, u32[]{:S(2)}) collective-permute-start(f16[64,768]{1,0:T(8,128)(2,1)S(1)} %fusion.12), channel_id=1, source_target_pairs={{0,16},{2,18},{4,20},{6,22},{8,24},{10,26},{12,28},{14,30},{16,0},... | collective-permute-start | bytes 294920 | tf_op jit(solution)/shard_map/ppermute | solution.py:168
  69.3 0.6 collective-permute-done.23
  70.0 3.6 %collective-permute-start.24 = (f16[64,768]{1,0:T(8,128)(2,1)S(1)}, f16[64,768]{1,0:T(8,128)(2,1)S(1)}, u32[]{:S(2)}, u32[]{:S(2)}) collective-permute-start(f16[64,768]{1,0:T(8,128)(2,1)S(1)} %fusion.13), channel_id=1, source_target_pairs={{0,16},{2,18},{4,20},{6,22},{8,24},{10,26},{12,28},{14,30},{16,0},... | collective-permute-start | bytes 294920 | tf_op jit(solution)/shard_map/ppermute | solution.py:168
  73.6 4.1 %collective-permute-done.24 = f16[64,768]{1,0:T(8,128)(2,1)S(1)} collective-permute-done((f16[64,768]{1,0:T(8,128)(2,1)S(1)}, f16[64,768]{1,0:T(8,128)(2,1)S(1)}, u32[]{:S(2)}, u32[]{:S(2)}) %collective-permute-start.24) | collective-permute-done | bytes 98336 | tf_op jit(solution)/shard_map/ppermute | solution.py:168
  77.8 0.6 multiply_reduce_fusion
  78.5 1.4 %convert_multiply_fusion.15 = (f32[64,3072]{1,0:T(8,128)S(1)}, f16[64,3072]{1,0:T(8,128)(2,1)S(1)}, f32[1,64,3072]{2,1,0:T(8,128)}) fusion(f32[64]{0:T(128)S(1)} %get-tuple-element.73, f32[64]{0:T(128)S(1)} %get-tuple-element.72, f32[1,64,3072]{2,1,0:T(8,128)S(1)} %copy-done.5, f32[1,64,3072]{2,1,0:T(8,128)S(1)} %get-tuple-element.71, ...), kind=kLoop, calls=%fused_computation.20 | loop fusion | flops 1966080 | bytes 4326144 | tf_op jit(solution)/shard_map/mul | solution.py:304
  80.6 4.4 %collective-permute-start.25 = (f16[64,3200]{1,0:T(8,128)(2,1)S(1)}, f16[64,3200]{1,0:T(8,128)(2,1)S(1)}, u32[]{:S(2)}, u32[]{:S(2)}) collective-permute-start(f16[64,3200]{1,0:T(8,128)(2,1)S(1)} %pad_maximum_fusion.1), channel_id=1, source_target_pairs={{0,2},{2,0},{4,6},{6,4},{8,10},{10,8},{12,14},{14,12},{16,18},{18,... | collective-permute-start | bytes 1228808 | tf_op jit(solution)/shard_map/ppermute | solution.py:184
  85.0 1.4 %put.6.refs_0_ = f32[1024,3072]{1,0:T(8,128)} custom-call(s32[16]{0:T(128)S(1)} %mul.301.starts, f32[64,3072]{1,0:T(8,128)S(1)} %get-tuple-element.66.refs_0_), custom_call_target="tpu_custom_call" | custom-call | flops 2147483648 | tf_op jit(solution)/shard_map/put/pallas_call | solution.py:76
  86.4 3.2 %collective-permute-done.26 = f16[64,3200]{1,0:T(8,128)(2,1)} collective-permute-done((f16[64,3200]{1,0:T(8,128)(2,1)S(1)}, f16[64,3200]{1,0:T(8,128)(2,1)}, u32[]{:S(2)}, u32[]{:S(2)}) %collective-permute-start.26) | collective-permute-done | bytes 409632 | tf_op jit(solution)/shard_map/ppermute | solution.py:174
  89.6 3.4 %collective-permute-start.28 = (f16[64,3200]{1,0:T(8,128)(2,1)}, f16[64,3200]{1,0:T(8,128)(2,1)S(1)}, u32[]{:S(2)}, u32[]{:S(2)}) collective-permute-start(f16[64,3200]{1,0:T(8,128)(2,1)} %collective-permute-done.26), channel_id=1, source_target_pairs={{0,2},{2,0},{4,6},{6,4},{8,10},{10,8},{12,14},{14,12},{16,18},{18,... | collective-permute-start | bytes 1228808 | tf_op jit(solution)/shard_map/ppermute | solution.py:184
  93.2 0.3 collective-permute-start.29
  93.5 0.8 exponential_reduce_fusion.13
  94.7 1.1 convert_multiply_fusion.13.refs_2_
  96.0 2.0 %put.7.refs_0_ = f32[1024,3072]{1,0:T(8,128)} custom-call(s32[16]{0:T(128)S(1)} %mul.301.starts, f32[1024,3072]{1,0:T(8,128)} %put.6.refs_0_, f32[64,3072]{1,0:T(8,128)S(1)} %convert_multiply_fusion.14.refs_1_, f32[64,3072]{1,0:T(8,128)S(1)} %convert_multiply_fusion.13.refs_2_, ...), custom_call_target="tpu_custom_call", output_to_operand_aliasing={{}: (1, {})} | custom-call | flops 2147483648 | tf_op jit(solution)/shard_map/put/pallas_call | solution.py:76
  98.0 7.2 %collective-permute-done.30 = f16[64,3200]{1,0:T(8,128)(2,1)S(1)} collective-permute-done((f16[64,3200]{1,0:T(8,128)(2,1)}, f16[64,3200]{1,0:T(8,128)(2,1)S(1)}, u32[]{:S(2)}, u32[]{:S(2)}) %collective-permute-start.30) | collective-permute-done | bytes 409632 | tf_op jit(solution)/shard_map/ppermute | solution.py:174
  105.2 0.8 collective-permute-start.32
  106.3 0.3 collective-permute-start.35
  107.4 2.2 %put.8.refs_0_ = f32[1024,3072]{1,0:T(8,128)} custom-call(s32[16]{0:T(128)S(1)} %mul.301.starts, f32[1024,3072]{1,0:T(8,128)} %put.7.refs_0_, f32[64,3072]{1,0:T(8,128)S(1)} %convert_multiply_fusion.11.refs_1_, f32[64,3072]{1,0:T(8,128)S(1)} %convert_multiply_fusion.10.refs_2_, ...), custom_call_target="tpu_custom_call", output_to_operand_aliasing={{}: (1, {})} | custom-call | flops 2147483648 | tf_op jit(solution)/shard_map/put/pallas_call | solution.py:76
  109.6 8.3 %collective-permute-done.34 = f16[64,3200]{1,0:T(8,128)(2,1)S(1)} collective-permute-done((f16[64,3200]{1,0:T(8,128)(2,1)S(1)}, f16[64,3200]{1,0:T(8,128)(2,1)S(1)}, u32[]{:S(2)}, u32[]{:S(2)}) %collective-permute-start.34) | collective-permute-done | bytes 409632 | tf_op jit(solution)/shard_map/ppermute | solution.py:174
  118.0 0.8 collective-permute-start.36
  119.0 0.3 collective-permute-start.37
  120.3 2.2 %put.9.refs_0_ = f32[1024,3072]{1,0:T(8,128)} custom-call(s32[16]{0:T(128)S(1)} %mul.301.starts, f32[1024,3072]{1,0:T(8,128)} %put.8.refs_0_, f32[64,3072]{1,0:T(8,128)S(1)} %convert_multiply_fusion.7.refs_1_, f32[64,3072]{1,0:T(8,128)S(1)} %convert_multiply_fusion.6.refs_2_, ...), custom_call_target="tpu_custom_call", output_to_operand_aliasing={{}: (1, {})} | custom-call | flops 2147483648 | tf_op jit(solution)/shard_map/put/pallas_call | solution.py:76
  122.6 7.3 %collective-permute-done.38 = f16[64,3200]{1,0:T(8,128)(2,1)S(1)} collective-permute-done((f16[64,3200]{1,0:T(8,128)(2,1)S(1)}, f16[64,3200]{1,0:T(8,128)(2,1)S(1)}, u32[]{:S(2)}, u32[]{:S(2)}) %collective-permute-start.38) | collective-permute-done | bytes 409632 | tf_op jit(solution)/shard_map/ppermute | solution.py:181
  129.8 0.8 collective-permute-start.39
  131.4 2.0 %put.10.refs_0_ = f32[1024,3072]{1,0:T(8,128)} custom-call(s32[16]{0:T(128)S(1)} %mul.301.starts, f32[1024,3072]{1,0:T(8,128)} %put.9.refs_0_, f32[64,3072]{1,0:T(8,128)S(1)} %convert_multiply_fusion.3.refs_1_, f32[64,3072]{1,0:T(8,128)S(1)} %convert_multiply_fusion.2.refs_2_, ...), custom_call_target="tpu_custom_call", output_to_operand_aliasing={{}: (1, {})} | custom-call | flops 2147483648 | tf_op jit(solution)/shard_map/put/pallas_call | solution.py:76
  133.6 1.4 %put.11 = f32[1024,3072]{1,0:T(8,128)} custom-call(s32[16]{0:T(128)S(1)} %mul.301.starts, f32[1024,3072]{1,0:T(8,128)} %put.10.refs_0_, f32[64,3072]{1,0:T(8,128)S(1)} %convert_multiply_fusion.refs_1_), custom_call_target="tpu_custom_call", output_to_operand_aliasing={{}: (1, {})} | custom-call | flops 2147483648 | tf_op jit(solution)/shard_map/put/pallas_call | solution.py:76
  (117 shorter events, 6.5 us)
Async XLA Ops:
  0.6 1.9 %copy-start = (bf16[512,3072]{1,0:T(8,128)(2,1)S(1)}, bf16[512,3072]{1,0:T(8,128)(2,1)}, u32[]{:S(2)}) copy-start(bf16[512,3072]{1,0:T(8,128)(2,1)} %grad.1) | copy-start | bytes 9437188
  2.5 0.7 copy-start.3
  3.2 0.7 copy-start.4
  5.0 8.9 %collective-permute-start.1 = (bf16[192,768]{1,0:T(8,128)(2,1)S(1)}, bf16[192,768]{1,0:T(8,128)(2,1)S(1)}, u32[]{:S(2)}, u32[]{:S(2)}) collective-permute-start(bf16[192,768]{1,0:T(8,128)(2,1)S(1)} %get-tuple-element.35.refs_0_), channel_id=1, source_target_pairs={{0,1},{1,0},{2,3},{3,2},{4,5},{5,4},{6,7},{7,6},{8,9},{9,8},{10,11... | collective-permute-start | bytes 884744 | tf_op jit(solution)/shard_map/ppermute | solution.py:187
  7.2 1.1 copy-start.1
  8.3 1.1 copy-start.2
  10.7 4.9 %collective-permute-start = (bf16[2,256,384]{2,1,0:T(8,128)(2,1)S(1)}, bf16[2,256,384]{2,1,0:T(8,128)(2,1)}, u32[]{:S(2)}, u32[]{:S(2)}) collective-permute-start(bf16[2,256,384]{2,1,0:T(8,128)(2,1)S(1)} %get-tuple-element.34), channel_id=1, source_target_pairs={{0,2},{2,0},{4,6},{6,4},{8,10},{10,8},{12,14},{14,12},{16,18},{18,... | collective-permute-start | bytes 1179656 | tf_op jit(solution)/shard_map/ppermute | solution.py:184
  11.7 5.0 %collective-permute-start.2 = (bf16[192,768]{1,0:T(8,128)(2,1)S(1)}, bf16[192,768]{1,0:T(8,128)(2,1)S(1)}, u32[]{:S(2)}, u32[]{:S(2)}) collective-permute-start(bf16[192,768]{1,0:T(8,128)(2,1)S(1)} %get-tuple-element.35.refs_0_), channel_id=1, source_target_pairs={{0,2},{2,0},{4,6},{6,4},{8,10},{10,8},{12,14},{14,12},{16,18},{18,... | collective-permute-start | bytes 884744 | tf_op jit(solution)/shard_map/ppermute | solution.py:184
  11.8 12.5 %collective-permute-start.6 = (bf16[192,768]{1,0:T(8,128)(2,1)S(1)}, bf16[192,768]{1,0:T(8,128)(2,1)S(1)}, u32[]{:S(2)}, u32[]{:S(2)}) collective-permute-start(bf16[192,768]{1,0:T(8,128)(2,1)S(1)} %get-tuple-element.39.refs_0_), channel_id=1, source_target_pairs={{0,2},{2,0},{4,6},{6,4},{8,10},{10,8},{12,14},{14,12},{16,18},{18,... | collective-permute-start | bytes 884744 | tf_op jit(solution)/shard_map/ppermute | solution.py:184
  12.2 8.6 %collective-permute-start.5 = (bf16[192,768]{1,0:T(8,128)(2,1)S(1)}, bf16[192,768]{1,0:T(8,128)(2,1)S(1)}, u32[]{:S(2)}, u32[]{:S(2)}) collective-permute-start(bf16[192,768]{1,0:T(8,128)(2,1)S(1)} %get-tuple-element.39.refs_0_), channel_id=1, source_target_pairs={{0,1},{1,0},{2,3},{3,2},{4,5},{5,4},{6,7},{7,6},{8,9},{9,8},{10,11... | collective-permute-start | bytes 884744 | tf_op jit(solution)/shard_map/ppermute | solution.py:187
  13.9 3.5 %collective-permute-start.3 = (bf16[192,768]{1,0:T(8,128)(2,1)S(1)}, bf16[192,768]{1,0:T(8,128)(2,1)S(1)}, u32[]{:S(2)}, u32[]{:S(2)}) collective-permute-start(bf16[192,768]{1,0:T(8,128)(2,1)S(1)} %collective-permute-done.1.refs_1_), channel_id=1, source_target_pairs={{0,2},{2,0},{4,6},{6,4},{8,10},{10,8},{12,14},{14,12},{16,18},{18,... | collective-permute-start | bytes 884744 | tf_op jit(solution)/shard_map/ppermute | solution.py:184
  15.6 25.2 %collective-permute-start.11 = (bf16[192,768]{1,0:T(8,128)(2,1)S(1)}, bf16[192,768]{1,0:T(8,128)(2,1)S(1)}, u32[]{:S(2)}, u32[]{:S(2)}) collective-permute-start(bf16[192,768]{1,0:T(8,128)(2,1)S(1)} %get-tuple-element.45.refs_0_), channel_id=1, source_target_pairs={{0,2},{2,0},{4,6},{6,4},{8,10},{10,8},{12,14},{14,12},{16,18},{18,... | collective-permute-start | bytes 884744 | tf_op jit(solution)/shard_map/ppermute | solution.py:184
  16.8 35.7 %collective-permute-start.17 = (bf16[192,768]{1,0:T(8,128)(2,1)S(1)}, bf16[192,768]{1,0:T(8,128)(2,1)S(1)}, u32[]{:S(2)}, u32[]{:S(2)}) collective-permute-start(bf16[192,768]{1,0:T(8,128)(2,1)S(1)} %get-tuple-element.52.refs_0_), channel_id=1, source_target_pairs={{0,2},{2,0},{4,6},{6,4},{8,10},{10,8},{12,14},{14,12},{16,18},{18,... | collective-permute-start | bytes 884744 | tf_op jit(solution)/shard_map/ppermute | solution.py:184
  20.8 4.7 %collective-permute-start.7 = (bf16[192,768]{1,0:T(8,128)(2,1)S(1)}, bf16[192,768]{1,0:T(8,128)(2,1)S(1)}, u32[]{:S(2)}, u32[]{:S(2)}) collective-permute-start(bf16[192,768]{1,0:T(8,128)(2,1)S(1)} %collective-permute-done.5.refs_1_), channel_id=1, source_target_pairs={{0,2},{2,0},{4,6},{6,4},{8,10},{10,8},{12,14},{14,12},{16,18},{18,... | collective-permute-start | bytes 884744 | tf_op jit(solution)/shard_map/ppermute | solution.py:184
  21.8 17.5 %collective-permute-start.4 = (f16[256,768]{1,0:T(8,128)(2,1)S(1)}, f16[256,768]{1,0:T(8,128)(2,1)S(1)}, u32[]{:S(2)}, u32[]{:S(2)}) collective-permute-start(f16[256,768]{1,0:T(8,128)(2,1)S(1)} %convert_bitcast_fusion.3), channel_id=1, source_target_pairs={{0,4},{2,6},{4,0},{6,2},{8,12},{10,14},{12,8},{14,10},{16,20},{18,... | collective-permute-start | bytes 1179656 | tf_op jit(solution)/shard_map/ppermute | solution.py:181
  24.3 20.0 %collective-permute-start.16 = (bf16[192,768]{1,0:T(8,128)(2,1)S(1)}, bf16[192,768]{1,0:T(8,128)(2,1)S(1)}, u32[]{:S(2)}, u32[]{:S(2)}) collective-permute-start(bf16[192,768]{1,0:T(8,128)(2,1)S(1)} %get-tuple-element.52.refs_0_), channel_id=1, source_target_pairs={{0,1},{1,0},{2,3},{3,2},{4,5},{5,4},{6,7},{7,6},{8,9},{9,8},{10,11... | collective-permute-start | bytes 884744 | tf_op jit(solution)/shard_map/ppermute | solution.py:187
  25.6 13.4 %collective-permute-start.10 = (bf16[192,768]{1,0:T(8,128)(2,1)S(1)}, bf16[192,768]{1,0:T(8,128)(2,1)S(1)}, u32[]{:S(2)}, u32[]{:S(2)}) collective-permute-start(bf16[192,768]{1,0:T(8,128)(2,1)S(1)} %get-tuple-element.45.refs_0_), channel_id=1, source_target_pairs={{0,1},{1,0},{2,3},{3,2},{4,5},{5,4},{6,7},{7,6},{8,9},{9,8},{10,11... | collective-permute-start | bytes 884744 | tf_op jit(solution)/shard_map/ppermute | solution.py:187
  26.6 51.1 %copy-start.8 = (f32[1,64,3072]{2,1,0:T(8,128)S(1)}, f32[1,64,3072]{2,1,0:T(8,128)}, u32[]{:S(2)}) copy-start(f32[1,64,3072]{2,1,0:T(8,128)} %param.14) | copy-start | bytes 2359300
  26.6 51.1 %copy-start.9 = (f32[1,64,3072]{2,1,0:T(8,128)S(1)}, f32[1,64,3072]{2,1,0:T(8,128)}, u32[]{:S(2)}) copy-start(f32[1,64,3072]{2,1,0:T(8,128)} %param.15) | copy-start | bytes 2359300
  39.0 9.5 %collective-permute-start.9 = (f16[256,768]{1,0:T(8,128)(2,1)S(1)}, f16[256,768]{1,0:T(8,128)(2,1)S(1)}, u32[]{:S(2)}, u32[]{:S(2)}) collective-permute-start(f16[256,768]{1,0:T(8,128)(2,1)S(1)} %convert_bitcast_fusion.2), channel_id=1, source_target_pairs={{0,4},{2,6},{4,0},{6,2},{8,12},{10,14},{12,8},{14,10},{16,20},{18,... | collective-permute-start | bytes 1179656 | tf_op jit(solution)/shard_map/ppermute | solution.py:181
  39.3 2.9 %collective-permute-start.12 = (bf16[192,768]{1,0:T(8,128)(2,1)S(1)}, bf16[192,768]{1,0:T(8,128)(2,1)S(1)}, u32[]{:S(2)}, u32[]{:S(2)}) collective-permute-start(bf16[192,768]{1,0:T(8,128)(2,1)S(1)} %collective-permute-done.10.refs_1_), channel_id=1, source_target_pairs={{0,2},{2,0},{4,6},{6,4},{8,10},{10,8},{12,14},{14,12},{16,18},{18,... | collective-permute-start | bytes 884744 | tf_op jit(solution)/shard_map/ppermute | solution.py:184
  40.8 37.7 %copy-start.5 = (f32[1,64,3072]{2,1,0:T(8,128)S(1)}, f32[1,64,3072]{2,1,0:T(8,128)}, u32[]{:S(2)}) copy-start(f32[1,64,3072]{2,1,0:T(8,128)} %param.13) | copy-start | bytes 2359300
  40.8 9.2 %collective-permute-start.8 = (f16[2,64,768]{2,1,0:T(8,128)(2,1)S(1)}, f16[2,64,768]{2,1,0:T(8,128)(2,1)S(1)}, u32[]{:S(2)}, u32[]{:S(2)}) collective-permute-start(f16[2,64,768]{2,1,0:T(8,128)(2,1)S(1)} %fusion.2), channel_id=1, source_target_pairs={{0,8},{2,10},{4,12},{6,14},{8,0},{10,2},{12,4},{14,6},{16,24},{18,... | collective-permute-start | bytes 589832 | tf_op jit(solution)/shard_map/ppermute | solution.py:168
  43.0 13.9 %collective-permute-start.15 = (f16[256,768]{1,0:T(8,128)(2,1)S(1)}, f16[256,768]{1,0:T(8,128)(2,1)S(1)}, u32[]{:S(2)}, u32[]{:S(2)}) collective-permute-start(f16[256,768]{1,0:T(8,128)(2,1)S(1)} %convert_bitcast_fusion.1), channel_id=1, source_target_pairs={{0,4},{2,6},{4,0},{6,2},{8,12},{10,14},{12,8},{14,10},{16,20},{18,... | collective-permute-start | bytes 1179656 | tf_op jit(solution)/shard_map/ppermute | solution.py:181
  44.3 8.2 %collective-permute-start.18 = (bf16[192,768]{1,0:T(8,128)(2,1)S(1)}, bf16[192,768]{1,0:T(8,128)(2,1)S(1)}, u32[]{:S(2)}, u32[]{:S(2)}) collective-permute-start(bf16[192,768]{1,0:T(8,128)(2,1)S(1)} %collective-permute-done.16.refs_1_), channel_id=1, source_target_pairs={{0,2},{2,0},{4,6},{6,4},{8,10},{10,8},{12,14},{14,12},{16,18},{18,... | collective-permute-start | bytes 884744 | tf_op jit(solution)/shard_map/ppermute | solution.py:184
  48.7 9.8 %collective-permute-start.14 = (f16[2,64,768]{2,1,0:T(8,128)(2,1)S(1)}, f16[2,64,768]{2,1,0:T(8,128)(2,1)S(1)}, u32[]{:S(2)}, u32[]{:S(2)}) collective-permute-start(f16[2,64,768]{2,1,0:T(8,128)(2,1)S(1)} %fusion.3), channel_id=1, source_target_pairs={{0,8},{2,10},{4,12},{6,14},{8,0},{10,2},{12,4},{14,6},{16,24},{18,... | collective-permute-start | bytes 589832 | tf_op jit(solution)/shard_map/ppermute | solution.py:168
  50.1 10.8 %collective-permute-start.13 = (f16[64,768]{1,0:T(8,128)(2,1)S(1)}, f16[64,768]{1,0:T(8,128)(2,1)S(1)}, u32[]{:S(2)}, u32[]{:S(2)}) collective-permute-start(f16[64,768]{1,0:T(8,128)(2,1)S(1)} %fusion.10), channel_id=1, source_target_pairs={{0,16},{2,18},{4,20},{6,22},{8,24},{10,26},{12,28},{14,30},{16,0},... | collective-permute-start | bytes 294920 | tf_op jit(solution)/shard_map/ppermute | solution.py:168
  53.3 11.4 %collective-permute-start.21 = (f16[256,768]{1,0:T(8,128)(2,1)S(1)}, f16[256,768]{1,0:T(8,128)(2,1)S(1)}, u32[]{:S(2)}, u32[]{:S(2)}) collective-permute-start(f16[256,768]{1,0:T(8,128)(2,1)S(1)} %convert_bitcast_fusion), channel_id=1, source_target_pairs={{0,4},{2,6},{4,0},{6,2},{8,12},{10,14},{12,8},{14,10},{16,20},{18,... | collective-permute-start | bytes 1179656 | tf_op jit(solution)/shard_map/ppermute | solution.py:181
  57.1 9.8 %collective-permute-start.20 = (f16[2,64,768]{2,1,0:T(8,128)(2,1)S(1)}, f16[2,64,768]{2,1,0:T(8,128)(2,1)S(1)}, u32[]{:S(2)}, u32[]{:S(2)}) collective-permute-start(f16[2,64,768]{2,1,0:T(8,128)(2,1)S(1)} %fusion.4), channel_id=1, source_target_pairs={{0,8},{2,10},{4,12},{6,14},{8,0},{10,2},{12,4},{14,6},{16,24},{18,... | collective-permute-start | bytes 589832 | tf_op jit(solution)/shard_map/ppermute | solution.py:168
  58.5 10.8 %collective-permute-start.19 = (f16[64,768]{1,0:T(8,128)(2,1)S(1)}, f16[64,768]{1,0:T(8,128)(2,1)S(1)}, u32[]{:S(2)}, u32[]{:S(2)}) collective-permute-start(f16[64,768]{1,0:T(8,128)(2,1)S(1)} %fusion.11), channel_id=1, source_target_pairs={{0,16},{2,18},{4,20},{6,22},{8,24},{10,26},{12,28},{14,30},{16,0},... | collective-permute-start | bytes 294920 | tf_op jit(solution)/shard_map/ppermute | solution.py:168
  64.8 5.1 %collective-permute-start.23 = (f16[2,64,768]{2,1,0:T(8,128)(2,1)S(1)}, f16[2,64,768]{2,1,0:T(8,128)(2,1)S(1)}, u32[]{:S(2)}, u32[]{:S(2)}) collective-permute-start(f16[2,64,768]{2,1,0:T(8,128)(2,1)S(1)} %fusion.5), channel_id=1, source_target_pairs={{0,8},{2,10},{4,12},{6,14},{8,0},{10,2},{12,4},{14,6},{16,24},{18,... | collective-permute-start | bytes 589832 | tf_op jit(solution)/shard_map/ppermute | solution.py:168
  66.9 6.7 %collective-permute-start.22 = (f16[64,768]{1,0:T(8,128)(2,1)S(1)}, f16[64,768]{1,0:T(8,128)(2,1)S(1)}, u32[]{:S(2)}, u32[]{:S(2)}) collective-permute-start(f16[64,768]{1,0:T(8,128)(2,1)S(1)} %fusion.12), channel_id=1, source_target_pairs={{0,16},{2,18},{4,20},{6,22},{8,24},{10,26},{12,28},{14,30},{16,0},... | collective-permute-start | bytes 294920 | tf_op jit(solution)/shard_map/ppermute | solution.py:168
  70.0 7.7 %collective-permute-start.24 = (f16[64,768]{1,0:T(8,128)(2,1)S(1)}, f16[64,768]{1,0:T(8,128)(2,1)S(1)}, u32[]{:S(2)}, u32[]{:S(2)}) collective-permute-start(f16[64,768]{1,0:T(8,128)(2,1)S(1)} %fusion.13), channel_id=1, source_target_pairs={{0,16},{2,18},{4,20},{6,22},{8,24},{10,26},{12,28},{14,30},{16,0},... | collective-permute-start | bytes 294920 | tf_op jit(solution)/shard_map/ppermute | solution.py:168
  78.4 19.6 %copy-start.6 = (f32[1,64,3072]{2,1,0:T(8,128)}, f32[1,64,3072]{2,1,0:T(8,128)S(1)}, u32[]{:S(2)}) copy-start(f32[1,64,3072]{2,1,0:T(8,128)S(1)} %get-tuple-element.70) | copy-start | bytes 2359300
  78.4 19.6 %copy-start.7 = (f32[1,64,3072]{2,1,0:T(8,128)}, f32[1,64,3072]{2,1,0:T(8,128)S(1)}, u32[]{:S(2)}) copy-start(f32[1,64,3072]{2,1,0:T(8,128)S(1)} %get-tuple-element.71) | copy-start | bytes 2359300
  80.0 9.5 %collective-permute-start.26 = (f16[64,3200]{1,0:T(8,128)(2,1)S(1)}, f16[64,3200]{1,0:T(8,128)(2,1)}, u32[]{:S(2)}, u32[]{:S(2)}) collective-permute-start(f16[64,3200]{1,0:T(8,128)(2,1)S(1)} %pad_maximum_fusion.1), channel_id=1, source_target_pairs={{0,8},{2,10},{4,12},{6,14},{8,24},{10,26},{12,28},{14,30},{24,16},... | collective-permute-start | bytes 1228808 | tf_op jit(solution)/shard_map/ppermute | solution.py:174
  80.2 13.0 %collective-permute-start.27 = (f16[64,3200]{1,0:T(8,128)(2,1)S(1)}, f16[64,3200]{1,0:T(8,128)(2,1)S(1)}, u32[]{:S(2)}, u32[]{:S(2)}) collective-permute-start(f16[64,3200]{1,0:T(8,128)(2,1)S(1)} %pad_maximum_fusion.1), channel_id=1, source_target_pairs={{0,4},{2,6},{4,0},{6,2},{8,12},{10,14},{12,8},{14,10},{16,20},{18,... | collective-permute-start | bytes 1228808 | tf_op jit(solution)/shard_map/ppermute | solution.py:181
  80.6 13.9 %collective-permute-start.25 = (f16[64,3200]{1,0:T(8,128)(2,1)S(1)}, f16[64,3200]{1,0:T(8,128)(2,1)S(1)}, u32[]{:S(2)}, u32[]{:S(2)}) collective-permute-start(f16[64,3200]{1,0:T(8,128)(2,1)S(1)} %pad_maximum_fusion.1), channel_id=1, source_target_pairs={{0,2},{2,0},{4,6},{6,4},{8,10},{10,8},{12,14},{14,12},{16,18},{18,... | collective-permute-start | bytes 1228808 | tf_op jit(solution)/shard_map/ppermute | solution.py:184
  89.6 16.7 %collective-permute-start.28 = (f16[64,3200]{1,0:T(8,128)(2,1)}, f16[64,3200]{1,0:T(8,128)(2,1)S(1)}, u32[]{:S(2)}, u32[]{:S(2)}) collective-permute-start(f16[64,3200]{1,0:T(8,128)(2,1)} %collective-permute-done.26), channel_id=1, source_target_pairs={{0,2},{2,0},{4,6},{6,4},{8,10},{10,8},{12,14},{14,12},{16,18},{18,... | collective-permute-start | bytes 1228808 | tf_op jit(solution)/shard_map/ppermute | solution.py:184
  93.0 12.2 %collective-permute-start.30 = (f16[64,3200]{1,0:T(8,128)(2,1)}, f16[64,3200]{1,0:T(8,128)(2,1)S(1)}, u32[]{:S(2)}, u32[]{:S(2)}) collective-permute-start(f16[64,3200]{1,0:T(8,128)(2,1)} %collective-permute-done.26), channel_id=1, source_target_pairs={{0,8},{2,10},{4,12},{6,14},{8,24},{10,26},{12,28},{14,30},{24,16},... | collective-permute-start | bytes 1228808 | tf_op jit(solution)/shard_map/ppermute | solution.py:174
  93.0 13.0 %collective-permute-start.31 = (f16[64,3200]{1,0:T(8,128)(2,1)}, f16[64,3200]{1,0:T(8,128)(2,1)S(1)}, u32[]{:S(2)}, u32[]{:S(2)}) collective-permute-start(f16[64,3200]{1,0:T(8,128)(2,1)} %collective-permute-done.26), channel_id=1, source_target_pairs={{0,4},{2,6},{4,0},{6,2},{8,12},{10,14},{12,8},{14,10},{16,20},{18,... | collective-permute-start | bytes 1228808 | tf_op jit(solution)/shard_map/ppermute | solution.py:181
  93.2 13.6 %collective-permute-start.29 = (f16[64,3200]{1,0:T(8,128)(2,1)S(1)}, f16[64,3200]{1,0:T(8,128)(2,1)S(1)}, u32[]{:S(2)}, u32[]{:S(2)}) collective-permute-start(f16[64,3200]{1,0:T(8,128)(2,1)S(1)} %collective-permute-done.27), channel_id=1, source_target_pairs={{0,2},{2,0},{4,6},{6,4},{8,10},{10,8},{12,14},{14,12},{16,18},{18,... | collective-permute-start | bytes 1228808 | tf_op jit(solution)/shard_map/ppermute | solution.py:184
  105.2 14.4 %collective-permute-start.32 = (f16[64,3200]{1,0:T(8,128)(2,1)S(1)}, f16[64,3200]{1,0:T(8,128)(2,1)S(1)}, u32[]{:S(2)}, u32[]{:S(2)}) collective-permute-start(f16[64,3200]{1,0:T(8,128)(2,1)S(1)} %collective-permute-done.30), channel_id=1, source_target_pairs={{0,2},{2,0},{4,6},{6,4},{8,10},{10,8},{12,14},{14,12},{16,18},{18,... | collective-permute-start | bytes 1228808 | tf_op jit(solution)/shard_map/ppermute | solution.py:184
  106.0 12.0 %collective-permute-start.34 = (f16[64,3200]{1,0:T(8,128)(2,1)S(1)}, f16[64,3200]{1,0:T(8,128)(2,1)S(1)}, u32[]{:S(2)}, u32[]{:S(2)}) collective-permute-start(f16[64,3200]{1,0:T(8,128)(2,1)S(1)} %collective-permute-done.30), channel_id=1, source_target_pairs={{0,8},{2,10},{4,12},{6,14},{8,24},{10,26},{12,28},{14,30},{24,16},... | collective-permute-start | bytes 1228808 | tf_op jit(solution)/shard_map/ppermute | solution.py:174
  106.0 13.8 %collective-permute-start.33 = (f16[64,3200]{1,0:T(8,128)(2,1)S(1)}, f16[64,3200]{1,0:T(8,128)(2,1)S(1)}, u32[]{:S(2)}, u32[]{:S(2)}) collective-permute-start(f16[64,3200]{1,0:T(8,128)(2,1)S(1)} %collective-permute-done.31), channel_id=1, source_target_pairs={{0,2},{2,0},{4,6},{6,4},{8,10},{10,8},{12,14},{14,12},{16,18},{18,... | collective-permute-start | bytes 1228808 | tf_op jit(solution)/shard_map/ppermute | solution.py:184
  106.3 12.7 %collective-permute-start.35 = (f16[64,3200]{1,0:T(8,128)(2,1)S(1)}, f16[64,3200]{1,0:T(8,128)(2,1)S(1)}, u32[]{:S(2)}, u32[]{:S(2)}) collective-permute-start(f16[64,3200]{1,0:T(8,128)(2,1)S(1)} %collective-permute-done.30), channel_id=1, source_target_pairs={{0,4},{2,6},{4,0},{6,2},{8,12},{10,14},{12,8},{14,10},{16,20},{18,... | collective-permute-start | bytes 1228808 | tf_op jit(solution)/shard_map/ppermute | solution.py:181
  118.0 12.8 %collective-permute-start.36 = (f16[64,3200]{1,0:T(8,128)(2,1)S(1)}, f16[64,3200]{1,0:T(8,128)(2,1)S(1)}, u32[]{:S(2)}, u32[]{:S(2)}) collective-permute-start(f16[64,3200]{1,0:T(8,128)(2,1)S(1)} %collective-permute-done.34), channel_id=1, source_target_pairs={{0,2},{2,0},{4,6},{6,4},{8,10},{10,8},{12,14},{14,12},{16,18},{18,... | collective-permute-start | bytes 1228808 | tf_op jit(solution)/shard_map/ppermute | solution.py:184
  118.7 11.1 %collective-permute-start.38 = (f16[64,3200]{1,0:T(8,128)(2,1)S(1)}, f16[64,3200]{1,0:T(8,128)(2,1)S(1)}, u32[]{:S(2)}, u32[]{:S(2)}) collective-permute-start(f16[64,3200]{1,0:T(8,128)(2,1)S(1)} %collective-permute-done.34), channel_id=1, source_target_pairs={{0,4},{2,6},{4,0},{6,2},{8,12},{10,14},{12,8},{14,10},{16,20},{18,... | collective-permute-start | bytes 1228808 | tf_op jit(solution)/shard_map/ppermute | solution.py:181
  119.0 12.0 %collective-permute-start.37 = (f16[64,3200]{1,0:T(8,128)(2,1)S(1)}, f16[64,3200]{1,0:T(8,128)(2,1)S(1)}, u32[]{:S(2)}, u32[]{:S(2)}) collective-permute-start(f16[64,3200]{1,0:T(8,128)(2,1)S(1)} %collective-permute-done.35), channel_id=1, source_target_pairs={{0,2},{2,0},{4,6},{6,4},{8,10},{10,8},{12,14},{14,12},{16,18},{18,... | collective-permute-start | bytes 1228808 | tf_op jit(solution)/shard_map/ppermute | solution.py:184
  129.8 3.5 %collective-permute-start.39 = (f16[64,3200]{1,0:T(8,128)(2,1)S(1)}, f16[64,3200]{1,0:T(8,128)(2,1)S(1)}, u32[]{:S(2)}, u32[]{:S(2)}) collective-permute-start(f16[64,3200]{1,0:T(8,128)(2,1)S(1)} %collective-permute-done.38), channel_id=1, source_target_pairs={{0,2},{2,0},{4,6},{6,4},{8,10},{10,8},{12,14},{14,12},{16,18},{18,... | collective-permute-start | bytes 1228808 | tf_op jit(solution)/shard_map/ppermute | solution.py:184

commit v3 on v2

v3 whole, which is shorter than its diff:
```python
import functools

import jax
import jax.numpy as jnp
from jax import lax
from jax.experimental import pallas as pl
from jax.experimental.pallas import tpu as pltpu
from jax.sharding import PartitionSpec as P

F16 = jnp.float16
F32 = jnp.float32
BF16 = jnp.bfloat16
CHUNKS = (1280, 1792)
PUT_FLOPS = 2 << 30
HIDDEN_FLOPS = 8 << 30
OFFSET = 3


def after(value, other):
    return lax.optimization_barrier((value, other))[0]


def dispatch_kernel(cap_rows, ids_in, probs_in, grad_in, *refs):
    outs, (ids, probs, grad, sems) = refs[:-4], refs[-4:]
    cuts = [sum(out.shape[1] for out in outs[:n]) for n in range(len(outs))]
    spots = [pl.ds(first, out.shape[1]) for first, out in zip(cuts, outs)]
    copies = [pltpu.make_async_copy(ids_in, ids, sems.at[0]), pltpu.make_async_copy(probs_in, probs, sems.at[1])]
    copies += [
        pltpu.make_async_copy(grad_in.at[:, spot], grad.at[:, spot], sems.at[2 + n]) for n, spot in enumerate(spots)
    ]
    for copy in copies:
        copy.start()
    copies[0].wait()
    copies[1].wait()
    tok_rows = ids.shape[1]
    hit = ids[...] == 0
    weight = jnp.sum(jnp.where(hit, probs[...], 0.0), axis=0, keepdims=True)
    chosen = jnp.sum(jnp.where(hit, 1.0, 0.0), axis=0, keepdims=True)
    earlier = lax.broadcasted_iota(jnp.int32, (tok_rows, tok_rows), 0) < lax.broadcasted_iota(
        jnp.int32, (tok_rows, tok_rows), 1
    )
    slot = jnp.dot(
        jnp.broadcast_to(chosen, (8, tok_rows)).astype(BF16),
        jnp.where(earlier, 1.0, 0.0).astype(BF16),
        preferred_element_type=F32,
    )[:1]
    slot = jnp.where(chosen > 0.0, slot, -1.0)
    places = lax.broadcasted_iota(jnp.int32, (cap_rows, tok_rows), 0).astype(F32)
    placing = jnp.where(slot == places, 1.0, 0.0).astype(BF16)
    weight = jnp.broadcast_to(weight, (128, tok_rows)).T[:, :1]
    for n, (spot, out) in enumerate(zip(spots, outs)):
        copies[2 + n].wait()
        scaled = (weight * grad[:, spot].astype(F32)).astype(BF16)
        out[...] = jnp.dot(placing, scaled, preferred_element_type=F32).astype(BF16)


def dispatch(ids, probs, grad, cap_rows):
    ids, probs = ids.T, probs.T
    vmem, hbm = pl.BlockSpec(memory_space=pltpu.VMEM), pl.BlockSpec(memory_space=pltpu.HBM)
    return pl.pallas_call(
        functools.partial(dispatch_kernel, cap_rows),
        out_shape=tuple(jax.ShapeDtypeStruct((cap_rows, size), BF16) for size in CHUNKS),
        in_specs=[hbm] * 3,
        out_specs=(vmem,) * len(CHUNKS),
        scratch_shapes=[
            pltpu.VMEM(ids.shape, ids.dtype),
            pltpu.VMEM(probs.shape, probs.dtype),
            pltpu.VMEM(grad.shape, grad.dtype),
            pltpu.SemaphoreType.DMA((2 + len(CHUNKS),)),
        ],
        compiler_params=pltpu.CompilerParams(vmem_limit_bytes=56 << 20),
        name="dispatch",
    )(ids, probs, grad)


def put_kernel(marks, aliased, starts, *refs):
    refs = refs[1:] if aliased else refs
    pieces, out, sems = refs[: len(marks)], refs[len(marks)], refs[len(marks) + 1]
    copies = []
    for n, (index, column) in enumerate(marks):
        height, size = pieces[n].shape
        row = pl.multiple_of(starts[index], height)
        spot = out.at[pl.ds(row, height), pl.ds(column, size)]
        copies.append(pltpu.make_async_copy(pieces[n], spot, sems.at[n]))
        copies[-1].start()
    for copy in copies:
        copy.wait()


def put(weights, shape, starts, marks, pieces):
    aliased = weights is not None
    spec = pl.BlockSpec(memory_space=pl.ANY)
    return pl.pallas_call(
        functools.partial(put_kernel, tuple(marks), aliased),
        out_shape=jax.ShapeDtypeStruct(shape, F32),
        in_specs=[pl.BlockSpec(memory_space=pltpu.SMEM)] + [spec] * (aliased + len(pieces)),
        out_specs=spec,
        scratch_shapes=[pltpu.SemaphoreType.DMA((len(pieces),))],
        input_output_aliases={1: 0} if aliased else {},
        compiler_params=pltpu.CompilerParams(vmem_limit_bytes=1 << 20),
        cost_estimate=pl.CostEstimate(flops=PUT_FLOPS, bytes_accessed=0, transcendentals=0),
        name="put",
    )(starts, *([weights] if aliased else []), *pieces)


def hidden_kernel(sizes, at, gate, up, mine, send):
    experts, length, own = sizes
    cap_rows = gate.shape[0] // experts
    at_e, core = at[0], at[1]
    values = []
    for j in range(experts):
        spot = pl.ds(pl.multiple_of(lax.rem(at_e + j, experts) * cap_rows, cap_rows), cap_rows)
        value = gate[spot, :].astype(F32)
        values.append(value / (1.0 + jnp.exp(-value)) * up[spot, :].astype(F32))
    value = jnp.concatenate(values, axis=0).T.astype(BF16)
    for chip in range(length):
        d = at[2 + chip]
        first = chip * 2 * own
        low, high = value[first : first + own], value[first + own : first + 2 * own]
        mine[d] = jnp.where(core == 0, low, high)
        send[d] = jnp.where(core == 0, high, low)


def hidden_pieces(at, gate, up, sizes):
    experts, length, own = sizes
    shape = jax.ShapeDtypeStruct((length, own, gate.shape[0]), BF16)
    vmem = pl.BlockSpec(memory_space=pltpu.VMEM)
    return pl.pallas_call(
        functools.partial(hidden_kernel, sizes),
        out_shape=(shape, shape),
        in_specs=[pl.BlockSpec(memory_space=pltpu.SMEM), vmem, vmem],
        out_specs=(vmem, vmem),
        compiler_params=pltpu.CompilerParams(vmem_limit_bytes=(8 << 20) * max(1, experts // 2)),
        cost_estimate=pl.CostEstimate(flops=HIDDEN_FLOPS, bytes_accessed=0, transcendentals=0),
        name="hidden_pieces",
    )(at, gate, up)


def product_kernel(scale, left, *refs):
    pieces, out, rows = refs[:-2], refs[-2], refs[-1]
    height = pieces[0].shape[0]
    for n, piece in enumerate(pieces):
        rows[n * height : (n + 1) * height, :] = piece[...]
    total = jnp.dot(left[...], rows[...], preferred_element_type=F32)
    out[...] = total * scale if scale != 1.0 else total


def product(left, pieces, scale):
    height, depth = left.shape
    size = pieces[0].shape[1]
    vmem = pl.BlockSpec(memory_space=pltpu.VMEM)
    return pl.pallas_call(
        functools.partial(product_kernel, scale),
        out_shape=jax.ShapeDtypeStruct((height, size), F32),
        in_specs=[vmem] * (1 + len(pieces)),
        out_specs=vmem,
        scratch_shapes=[pltpu.VMEM((depth, size), BF16)],
        compiler_params=pltpu.CompilerParams(vmem_limit_bytes=16 << 20),
        cost_estimate=pl.CostEstimate(flops=0, bytes_accessed=0, transcendentals=0),
        name="product",
    )(left, *pieces)


def build(mesh):
    devices = mesh.shape["dp"]
    experts = mesh.shape["expert"]
    rows_a = 4
    rows_b = devices // (2 * rows_a)

    def place(a, b, c):
        return ((a % rows_a) * rows_b + b % rows_b) * 2 + c % 2

    spots = [(a, b, c) for a in range(rows_a) for b in range(rows_b) for c in range(2)]

    ring = [(a, 0) for a in range(rows_a)]
    for n, a in enumerate(reversed(range(rows_a))):
        ring += [(a, b) for b in (range(1, rows_b) if n % 2 == 0 else reversed(range(1, rows_b)))]
    length = len(ring)
    sources = [[0] * length for _ in ring]
    distances = [[0] * length for _ in ring]
    for p, (a, b) in enumerate(ring):
        for d in range(length):
            from_a, from_b = ring[(p - d) % length]
            sources[a * rows_b + b][d] = from_a * rows_b + from_b
            distances[a * rows_b + b][from_a * rows_b + from_b] = (length - d) % length

    def step_ring(value, way):
        pairs = [(ring[p], ring[(p + way) % length]) for p in range(length)]
        return lax.ppermute(value, "dp", [(place(*x, c), place(*y, c)) for x, y in pairs for c in range(2)])

    def swap_core(value):
        return lax.ppermute(value, "dp", [(place(a, b, c), place(a, b, c + 1)) for a, b, c in spots])

    def shift_expert(value, k):
        return lax.ppermute(value, "expert", [(e, (e + k) % experts) for e in range(experts)])

    def local(grad_out, expert_ids, gate_probs, saved_gate, saved_up, master, moment_one, moment_two):
        me = lax.axis_index("dp")
        core = me % 2
        at_b = (me // 2) % rows_b
        at_a = me // (2 * rows_b)
        at_e = lax.axis_index("expert")
        tok_rows, dim = grad_out.shape
        cap_rows = tok_rows * 3 // 8
        own = master.shape[1]
        slot_rows, _, width = saved_gate.shape

        count = len(CHUNKS)
        cuts = [sum(CHUNKS[:i]) for i in range(count)]
        parts = dispatch(expert_ids, gate_probs, grad_out, cap_rows)

        chip = lax.dynamic_index_in_dim(jnp.array(sources, jnp.int32), me // 2, 0, False)
        ahead = lax.dynamic_index_in_dim(jnp.array(distances, jnp.int32), me // 2, 0, False)
        at = jnp.concatenate([jnp.stack([at_e, core]).astype(jnp.int32), ahead])
        hidden_mine, hidden_send = hidden_pieces(
            after(at, parts[0]),
            saved_gate.reshape(slot_rows, width),
            saved_up.reshape(slot_rows, width),
            (experts, length, own),
        )
        left = jnp.concatenate([hidden_mine, swap_core(hidden_send)], axis=2)
        left = left.reshape(length * own, 2 * slot_rows)

        largest = length // 2 * 2 * slot_rows * 36.0 * 0.2
        shrink = 1.0
        while largest * shrink > 60000.0:
            shrink *= 0.5

        middle = length // 2
        events = sorted((step + OFFSET * i, -i, i, step) for i in range(count) for step in range(middle))
        far, totals, moving = [], [], []
        token = hidden_mine
        for _, _, i, step in events:
            size = CHUNKS[i]
            cut = size // 2
            if step == 0:
                while len(far) < min(i + 2, count):
                    n = len(far)
                    part = parts[n] if n == 0 else after(parts[n], far[n - 1][-1])
                    far.append([shift_expert(part, -j) for j in range(1, experts)])
                here = [parts[i]] + [after(x, token) for x in far[i]]
                total = product(left, here + [swap_core(x) for x in here], shrink).reshape(length, own, size)
                totals.append(total)
                one, two = total[middle, :, :cut], total[middle, :, cut:]
                moving.append(None)
            else:
                total, d = totals[i], middle - step
                up, down = after(moving[i], token)
                one, two = total[d], total[length - d]
                if step == 1:
                    one = jnp.concatenate([one[:, :cut] + up.astype(F32), one[:, cut:]], axis=1)
                    two = jnp.concatenate([two[:, :cut], two[:, cut:] + down.astype(F32)], axis=1)
                else:
                    one, two = one + up.astype(F32), two + down.astype(F32)
            one, two = one.astype(F16), two.astype(F16)
            token = (one, two)
            moving[i] = (step_ring(one, 1), step_ring(two, -1))
        grads = [
            total[0] + up.astype(F32) + down.astype(F32)
            for total, (up, down) in ((totals[i], after(moving[i], token)) for i in range(count))
        ]
        grad = (jnp.concatenate(grads, axis=1) * (1.0 / shrink)).reshape(master.shape)

        new_one = 0.9 * moment_one + 0.1 * grad
        new_two = 0.95 * moment_two + 0.05 * grad * grad
        step = new_one / (1.0 - 0.9**20) / (jnp.sqrt(new_two / (1.0 - 0.95**20)) + 1e-08)
        wrms = jnp.sqrt(jnp.mean(master * master, axis=-1, keepdims=True) + 1e-06)
        srms = jnp.sqrt(jnp.mean(step * step, axis=-1, keepdims=True) + 1e-06)
        factor = jnp.minimum(1.0, 0.02 * wrms / (0.01 * srms))
        new_master = master - 0.01 * factor * step

        bound = jnp.max(jnp.abs(after(master[0], token)), axis=-1, keepdims=True) + 0.08
        power = jnp.floor(jnp.log2(bound))
        coded = (new_master[0] * jnp.exp2(13.0 - power)).astype(F16)
        coded = jnp.concatenate([coded, jnp.broadcast_to(power.astype(F16), (own, 128))], axis=1)
        steps = [[(0, 0, coded)]]
        ahead, back = coded, coded
        for i in range(1, length // 2):
            ahead, back = step_ring(ahead, 1), step_ring(back, -1)
            steps.append([(i, 0, ahead), (length - i, 0, back)])
        cut = dim // 2
        opposite = [step_ring(back[:, cut:], -1), step_ring(ahead[:, :cut], 1)]
        steps.append([(length // 2, cut, opposite[0]), (length // 2, 0, opposite[1])])
        starts = ((chip[:, None] * 2 + (core + jnp.arange(2, dtype=jnp.int32)) % 2) * own).astype(jnp.int32).reshape(-1)
        scales, weights, late = {}, None, []
        for step in steps[:-1] + [[]] + steps[-1:] + [[]]:
            pieces = late
            late = []
            for d, first, value in step:
                pieces = pieces + [((d, 0), first, value)]
                late.append(((d, 1), first, swap_core(value)))
            marks, values = [], []
            for spot, first, value in pieces:
                if first + value.shape[1] > dim:
                    scales[spot] = jnp.exp2(value[:, -1:].astype(F32) - 13.0)
                    value = value[:, : dim - first]
                values.append(value.astype(F32) * scales[spot])
                marks.append((spot[0] * 2 + spot[1], first))
            weights = put(weights, (width, dim), starts, marks, values)
        return (new_master, new_one, new_two, weights[None])

    return local


def solution(mesh):
    return jax.shard_map(
        build(mesh),
        mesh=mesh,
        in_specs=(
            P(("dp", "expert"), None),
            P(("dp", "expert"), None),
            P(("dp", "expert"), None),
            P("dp", "expert", None),
            P("dp", "expert", None),
            P("expert", "dp", None),
            P("expert", "dp", None),
            P("expert", "dp", None),
        ),
        out_specs=(
            P("expert", "dp", None),
            P("expert", "dp", None),
            P("expert", "dp", None),
            P("expert", None, None),
        ),
        check_vma=False,
    )
```

time: 136 us -> 122 us (0.90)
  waiting for transfers between devices: 58 us -> 46.9 us
  local copies, waits for them, and re-layouts: 6.81 us -> 0.42 us
  Pallas kernels: 16.7 us -> 20 us
    ppermute x19 -> x24, waiting for transfers between devices: 41.4 us -> 35.6 us  [step_ring(): lax.ppermute(value, 'dp', [(place(*x, c), place(*y, c)) for x, y in pairs...]
    ppermute x4 -> x2, waiting for transfers between devices: 16.6 us -> 11 us  [shift_expert(): lax.ppermute(value, 'expert', [(e, (e + k) % experts) for e in range(expe...]
    unnamed x21 -> x18, local copies, waits for them, and re-layouts: 5.59 us -> 0.04 us
    ppermute x19 -> x24, starting transfers between devices: 21.1 us -> 18.4 us  [step_ring(): lax.ppermute(value, 'dp', [(place(*x, c), place(*y, c)) for x, y in pairs...]
    ppermute x17 -> x14, starting transfers between devices: 17.4 us -> 19.9 us  [swap_core(): lax.ppermute(value, 'dp', [(place(a, b, c), place(a, b, c + 1)) for a, b,...]
    pallas_call x1, Pallas kernels: 1.09 us -> 3.5 us  [dispatch(): pl.pallas_call(functools.partial(dispatch_kernel, cap_rows), out_shape=tu...]
    pallas_call x6 -> x7, Pallas kernels: 11.3 us -> 12.5 us  [put(): pl.pallas_call(functools.partial(put_kernel, tuple(marks), aliased), out_...]
    pallas_call x4 -> x2, Pallas kernels: 3.09 us -> 2.78 us  [product(): pl.pallas_call(functools.partial(product_kernel, scale), out_shape=jax.Sh...]
  transfers between devices with their start and end apart: 40 -> 40, of which waited for: 12 -> 21; matrix products, arithmetic and copies ran while one was open for 7% -> 7% of each run, Pallas kernels for 10% -> 12%
where the time goes in v3:
time: 122 us
  waiting for transfers between devices  46.9 us (38%)
  starting transfers between devices  41.9 us (34%)
  Pallas kernels  20 us (16%)
  other arithmetic  11 us (9%)
    ppermute x24, waiting for transfers between devices, step_ring(): lax.ppermute(value, 'dp', [(place(*x, c), place(*y, c)) for x, y in pairs...  35.6 us
    ppermute x14, starting transfers between devices, swap_core(): lax.ppermute(value, 'dp', [(place(a, b, c), place(a, b, c + 1)) for a, b,...  19.9 us
    ppermute x24, starting transfers between devices, step_ring(): lax.ppermute(value, 'dp', [(place(*x, c), place(*y, c)) for x, y in pairs...  18.4 us
    pallas_call x7, Pallas kernels, put(): pl.pallas_call(functools.partial(put_kernel, tuple(marks), aliased), out_...  12.5 us
    ppermute x2, waiting for transfers between devices, shift_expert(): lax.ppermute(value, 'expert', [(e, (e + k) % experts) for e in range(expe...  11 us
    mul x16, other arithmetic, local(): values.append(value.astype(F32) * scales[spot])  4.27 us
    ppermute x2, starting transfers between devices, shift_expert(): lax.ppermute(value, 'expert', [(e, (e + k) % experts) for e in range(expe...  3.66 us
    pallas_call x1, Pallas kernels, dispatch(): pl.pallas_call(functools.partial(dispatch_kernel, cap_rows), out_shape=tu...  3.5 us
  transfers between devices with their start and end apart: 40, of which 21 were waited for; matrix products, arithmetic and copies ran while one was open for 7% of the time, Pallas kernels for 12%

profile of v3, /device:TPU:1, one launch (start us, length us, event | category | flops | bytes accessed | tf_op | source)
XLA Modules:
  0.0 121.5 jit_solution(9462449999414304211)
XLA Ops:
  0.7 3.5 %dispatch.1 = (bf16[192,1280]{1,0:T(8,128)(2,1)}, bf16[192,1792]{1,0:T(8,128)(2,1)}) custom-call(s32[2,512]{1,0:T(2,128)} %bitcast.40, f32[2,512]{1,0:T(2,128)} %bitcast.41, bf16[512,3072]{1,0:T(8,128)(2,1)} %grad_in.1), custom_call_target="tpu_custom_call" | custom-call | tf_op jit(solution)/shard_map/dispatch/pallas_call | solution.py:60
  4.2 2.1 %collective-permute-start.1 = (bf16[192,1280]{1,0:T(8,128)(2,1)}, bf16[192,1280]{1,0:T(8,128)(2,1)S(1)}, u32[]{:S(2)}, u32[]{:S(2)}) collective-permute-start(bf16[192,1280]{1,0:T(8,128)(2,1)} %get-tuple-element.29.refs_0_), channel_id=1, source_target_pairs={{0,1},{1,0},{2,3},{3,2},{4,5},{5,4},{6,7},{7,6},{8,9},{9,8},{10,11... | collective-permute-start | bytes 1474568 | tf_op jit(solution)/shard_map/ppermute | solution.py:195
  6.3 0.7 multiply_bitcast_fusion
  7.1 1.3 %hidden_pieces.1 = (bf16[8,64,384]{2,1,0:T(8,128)(2,1)S(1)}, bf16[8,64,384]{2,1,0:T(8,128)(2,1)S(1)}) custom-call(s32[10]{0:T(128)S(1)} %pad_add_fusion.at, bf16[384,1024]{1,0:T(8,128)(2,1)S(1)} %bitcast.34, bf16[384,1024]{1,0:T(8,128)(2,1)S(1)} %bitcast.35), custom_call_target="tpu_custom_call" | custom-call | flops 8589934592 | tf_op jit(solution)/shard_map/hidden_pieces/pallas_call | solution.py:128
  8.4 1.0 collective-permute-start
  9.5 8.0 %collective-permute-done.1.refs_1_ = bf16[192,1280]{1,0:T(8,128)(2,1)S(1)} collective-permute-done((bf16[192,1280]{1,0:T(8,128)(2,1)}, bf16[192,1280]{1,0:T(8,128)(2,1)S(1)}, u32[]{:S(2)}, u32[]{:S(2)}) %collective-permute-start.1) | collective-permute-done | bytes 491552 | tf_op jit(solution)/shard_map/ppermute | solution.py:195
  17.4 1.2 %collective-permute-start.3 = (bf16[192,1280]{1,0:T(8,128)(2,1)S(1)}, bf16[192,1280]{1,0:T(8,128)(2,1)S(1)}, u32[]{:S(2)}, u32[]{:S(2)}) collective-permute-start(bf16[192,1280]{1,0:T(8,128)(2,1)S(1)} %collective-permute-done.1.refs_1_), channel_id=1, source_target_pairs={{0,2},{2,0},{4,6},{6,4},{8,10},{10,8},{12,14},{14,12},{16,18},{18,... | collective-permute-start | bytes 1474568 | tf_op jit(solution)/shard_map/ppermute | solution.py:192
  18.8 1.5 %collective-permute-start.10 = (bf16[192,1792]{1,0:T(8,128)(2,1)S(1)}, bf16[192,1792]{1,0:T(8,128)(2,1)S(1)}, u32[]{:S(2)}, u32[]{:S(2)}) collective-permute-start(bf16[192,1792]{1,0:T(8,128)(2,1)S(1)} %copy-done), channel_id=1, source_target_pairs={{0,1},{1,0},{2,3},{3,2},{4,5},{5,4},{6,7},{7,6},{8,9},{9,8},{10,11... | collective-permute-start | bytes 2064392 | tf_op jit(solution)/shard_map/ppermute | solution.py:195
  20.3 1.2 product.2
  21.7 1.4 %collective-permute-start.4 = (f16[64,640]{1,0:T(8,128)(2,1)S(1)}, f16[64,640]{1,0:T(8,128)(2,1)S(1)}, u32[]{:S(2)}, u32[]{:S(2)}) collective-permute-start(f16[64,640]{1,0:T(8,128)(2,1)S(1)} %get-tuple-element.81), channel_id=1, source_target_pairs={{0,8},{2,10},{8,16},{10,18},{16,24},{18,26},{24,28},{26,30},{28,20... | collective-permute-start | bytes 245768 | tf_op jit(solution)/shard_map/ppermute | solution.py:189
  23.2 2.2 %collective-permute-done.4 = f16[64,640]{1,0:T(8,128)(2,1)S(1)} collective-permute-done((f16[64,640]{1,0:T(8,128)(2,1)S(1)}, f16[64,640]{1,0:T(8,128)(2,1)S(1)}, u32[]{:S(2)}, u32[]{:S(2)}) %collective-permute-start.4) | collective-permute-done | bytes 81952 | tf_op jit(solution)/shard_map/ppermute | solution.py:189
  25.5 1.2 %collective-permute-done.5 = f16[64,640]{1,0:T(8,128)(2,1)S(1)} collective-permute-done((f16[64,640]{1,0:T(8,128)(2,1)S(1)}, f16[64,640]{1,0:T(8,128)(2,1)S(1)}, u32[]{:S(2)}, u32[]{:S(2)}) %collective-permute-start.5) | collective-permute-done | bytes 81952 | tf_op jit(solution)/shard_map/ppermute | solution.py:189
  26.8 1.3 %collective-permute-start.6 = (f16[64,1280]{1,0:T(8,128)(2,1)S(1)}, f16[64,1280]{1,0:T(8,128)(2,1)S(1)}, u32[]{:S(2)}, u32[]{:S(2)}) collective-permute-start(f16[64,1280]{1,0:T(8,128)(2,1)S(1)} %pad_maximum_fusion.5), channel_id=1, source_target_pairs={{0,8},{2,10},{8,16},{10,18},{16,24},{18,26},{24,28},{26,30},{28,20... | collective-permute-start | bytes 491528 | tf_op jit(solution)/shard_map/ppermute | solution.py:189
  28.4 2.1 %collective-permute-start.11 = (bf16[192,1792]{1,0:T(8,128)(2,1)S(1)}, bf16[192,1792]{1,0:T(8,128)(2,1)S(1)}, u32[]{:S(2)}, u32[]{:S(2)}) collective-permute-start(bf16[192,1792]{1,0:T(8,128)(2,1)S(1)} %copy-done), channel_id=1, source_target_pairs={{0,2},{2,0},{4,6},{6,4},{8,10},{10,8},{12,14},{14,12},{16,18},{18,... | collective-permute-start | bytes 2064392 | tf_op jit(solution)/shard_map/ppermute | solution.py:192
  30.5 0.8 collective-permute-done.6
  31.3 1.4 %collective-permute-done.7 = f16[64,1280]{1,0:T(8,128)(2,1)S(1)} collective-permute-done((f16[64,1280]{1,0:T(8,128)(2,1)S(1)}, f16[64,1280]{1,0:T(8,128)(2,1)S(1)}, u32[]{:S(2)}, u32[]{:S(2)}) %collective-permute-start.7) | collective-permute-done | bytes 163872 | tf_op jit(solution)/shard_map/ppermute | solution.py:189
  32.8 3.1 %collective-permute-done.10.refs_1_ = bf16[192,1792]{1,0:T(8,128)(2,1)S(1)} collective-permute-done((bf16[192,1792]{1,0:T(8,128)(2,1)S(1)}, bf16[192,1792]{1,0:T(8,128)(2,1)S(1)}, u32[]{:S(2)}, u32[]{:S(2)}) %collective-permute-start.10) | collective-permute-done | bytes 688160 | tf_op jit(solution)/shard_map/ppermute | solution.py:195
  35.9 0.8 collective-permute-start.12
  36.7 1.5 %collective-permute-start.8 = (f16[64,1280]{1,0:T(8,128)(2,1)S(1)}, f16[64,1280]{1,0:T(8,128)(2,1)S(1)}, u32[]{:S(2)}, u32[]{:S(2)}) collective-permute-start(f16[64,1280]{1,0:T(8,128)(2,1)S(1)} %get-tuple-element.71), channel_id=1, source_target_pairs={{0,8},{2,10},{8,16},{10,18},{16,24},{18,26},{24,28},{26,30},{28,20... | collective-permute-start | bytes 491528 | tf_op jit(solution)/shard_map/ppermute | solution.py:189
  38.5 1.6 %product.3 = f32[512,1792]{1,0:T(8,128)S(1)} custom-call(bf16[512,768]{1,0:T(8,128)(2,1)S(1)} %bitcast.33, bf16[192,1792]{1,0:T(8,128)(2,1)S(1)} %copy-done, bf16[192,1792]{1,0:T(8,128)(2,1)S(1)} %collective-permute-done.10.refs_1_, bf16[192,1792]{1,0:T(8,128)(2,1)S(1)} %collective-permute-done.11.refs_2_, bf16[192,1792]{1,0:T(8,128)(2,1)S(1)} %collective-permute-done.12.refs_3_), custom_call_target="tpu_custom_call" | custom-call | tf_op jit(solution)/shard_map/product/pallas_call | solution.py:152
  40.3 1.6 %collective-permute-start.15 = (f16[64,896]{1,0:T(8,128)(2,1)S(1)}, f16[64,896]{1,0:T(8,128)(2,1)S(1)}, u32[]{:S(2)}, u32[]{:S(2)}) collective-permute-start(f16[64,896]{1,0:T(8,128)(2,1)S(1)} %get-tuple-element.77), channel_id=1, source_target_pairs={{0,8},{2,10},{8,16},{10,18},{16,24},{18,26},{24,28},{26,30},{28,20... | collective-permute-start | bytes 344072 | tf_op jit(solution)/shard_map/ppermute | solution.py:189
  41.9 0.6 collective-permute-done.8
  42.5 1.2 collective-permute-done.9
  43.8 0.9 collective-permute-done.15
  44.7 1.2 collective-permute-done.16
  46.0 1.4 %collective-permute-start.17 = (f16[64,1792]{1,0:T(8,128)(2,1)S(1)}, f16[64,1792]{1,0:T(8,128)(2,1)S(1)}, u32[]{:S(2)}, u32[]{:S(2)}) collective-permute-start(f16[64,1792]{1,0:T(8,128)(2,1)S(1)} %pad_maximum_fusion.3), channel_id=1, source_target_pairs={{0,8},{2,10},{8,16},{10,18},{16,24},{18,26},{24,28},{26,30},{28,20... | collective-permute-start | bytes 688136 | tf_op jit(solution)/shard_map/ppermute | solution.py:189
  47.7 4.0 %collective-permute-done.17 = f16[64,1792]{1,0:T(8,128)(2,1)S(1)} collective-permute-done((f16[64,1792]{1,0:T(8,128)(2,1)S(1)}, f16[64,1792]{1,0:T(8,128)(2,1)S(1)}, u32[]{:S(2)}, u32[]{:S(2)}) %collective-permute-start.17) | collective-permute-done | bytes 229408 | tf_op jit(solution)/shard_map/ppermute | solution.py:189
  51.7 1.2 collective-permute-done.18
  53.0 1.3 %collective-permute-start.19 = (f16[64,1792]{1,0:T(8,128)(2,1)S(1)}, f16[64,1792]{1,0:T(8,128)(2,1)S(1)}, u32[]{:S(2)}, u32[]{:S(2)}) collective-permute-start(f16[64,1792]{1,0:T(8,128)(2,1)S(1)} %get-tuple-element.65), channel_id=1, source_target_pairs={{0,8},{2,10},{8,16},{10,18},{16,24},{18,26},{24,28},{26,30},{28,20... | collective-permute-start | bytes 688136 | tf_op jit(solution)/shard_map/ppermute | solution.py:189
  54.7 1.3 %collective-permute-start.13 = (f16[64,1280]{1,0:T(8,128)(2,1)S(1)}, f16[64,1280]{1,0:T(8,128)(2,1)S(1)}, u32[]{:S(2)}, u32[]{:S(2)}) collective-permute-start(f16[64,1280]{1,0:T(8,128)(2,1)S(1)} %get-tuple-element.69), channel_id=1, source_target_pairs={{0,8},{2,10},{8,16},{10,18},{16,24},{18,26},{24,28},{26,30},{28,20... | collective-permute-start | bytes 491528 | tf_op jit(solution)/shard_map/ppermute | solution.py:189
  56.2 1.7 %collective-permute-done.19 = f16[64,1792]{1,0:T(8,128)(2,1)S(1)} collective-permute-done((f16[64,1792]{1,0:T(8,128)(2,1)S(1)}, f16[64,1792]{1,0:T(8,128)(2,1)S(1)}, u32[]{:S(2)}, u32[]{:S(2)}) %collective-permute-start.19) | collective-permute-done | bytes 229408 | tf_op jit(solution)/shard_map/ppermute | solution.py:189
  57.9 1.6 %collective-permute-done.20 = f16[64,1792]{1,0:T(8,128)(2,1)S(1)} collective-permute-done((f16[64,1792]{1,0:T(8,128)(2,1)S(1)}, f16[64,1792]{1,0:T(8,128)(2,1)S(1)}, u32[]{:S(2)}, u32[]{:S(2)}) %collective-permute-start.20) | collective-permute-done | bytes 229408 | tf_op jit(solution)/shard_map/ppermute | solution.py:189
  59.6 1.2 %collective-permute-start.21 = (f16[64,1792]{1,0:T(8,128)(2,1)S(1)}, f16[64,1792]{1,0:T(8,128)(2,1)S(1)}, u32[]{:S(2)}, u32[]{:S(2)}) collective-permute-start(f16[64,1792]{1,0:T(8,128)(2,1)S(1)} %get-tuple-element.63), channel_id=1, source_target_pairs={{0,8},{2,10},{8,16},{10,18},{16,24},{18,26},{24,28},{26,30},{28,20... | collective-permute-start | bytes 688136 | tf_op jit(solution)/shard_map/ppermute | solution.py:189
  61.3 0.6 collective-permute-done.14
  62.0 4.6 %collective-permute-done.21 = f16[64,1792]{1,0:T(8,128)(2,1)S(1)} collective-permute-done((f16[64,1792]{1,0:T(8,128)(2,1)S(1)}, f16[64,1792]{1,0:T(8,128)(2,1)S(1)}, u32[]{:S(2)}, u32[]{:S(2)}) %collective-permute-start.21) | collective-permute-done | bytes 229408 | tf_op jit(solution)/shard_map/ppermute | solution.py:189
  66.6 1.3 %collective-permute-done.22 = f16[64,1792]{1,0:T(8,128)(2,1)S(1)} collective-permute-done((f16[64,1792]{1,0:T(8,128)(2,1)S(1)}, f16[64,1792]{1,0:T(8,128)(2,1)S(1)}, u32[]{:S(2)}, u32[]{:S(2)}) %collective-permute-start.22) | collective-permute-done | bytes 229408 | tf_op jit(solution)/shard_map/ppermute | solution.py:189
  68.0 0.6 multiply_reduce_fusion
  68.7 1.4 %convert_multiply_fusion.13 = (f32[64,3072]{1,0:T(8,128)S(1)}, f16[64,3072]{1,0:T(8,128)(2,1)S(1)}, f32[1,64,3072]{2,1,0:T(8,128)}) fusion(f32[64]{0:T(128)S(1)} %get-tuple-element.87, f32[64]{0:T(128)S(1)} %get-tuple-element.86, f32[1,64,3072]{2,1,0:T(8,128)S(1)} %copy-done.4, f32[1,64,3072]{2,1,0:T(8,128)S(1)} %get-tuple-element.61, ...), kind=kLoop, calls=%fused_computation.19 | loop fusion | flops 1966080 | bytes 4326144 | tf_op jit(solution)/shard_map/mul | solution.py:297
  70.3 0.9 collective-permute-start.24
  71.2 0.6 collective-permute-start.25
  71.9 5.5 %collective-permute-start.23 = (f16[64,3200]{1,0:T(8,128)(2,1)S(1)}, f16[64,3200]{1,0:T(8,128)(2,1)S(1)}, u32[]{:S(2)}, u32[]{:S(2)}) collective-permute-start(f16[64,3200]{1,0:T(8,128)(2,1)S(1)} %pad_maximum_fusion.2), channel_id=1, source_target_pairs={{0,2},{2,0},{4,6},{6,4},{8,10},{10,8},{12,14},{14,12},{16,18},{18,... | collective-permute-start | bytes 1228808 | tf_op jit(solution)/shard_map/ppermute | solution.py:192
  77.4 1.4 %put.7.refs_0_ = f32[1024,3072]{1,0:T(8,128)} custom-call(s32[16]{0:T(128)S(1)} %mul.308.starts, f32[64,3072]{1,0:T(8,128)S(1)} %get-tuple-element.56.refs_0_), custom_call_target="tpu_custom_call" | custom-call | flops 2147483648 | tf_op jit(solution)/shard_map/put/pallas_call | solution.py:93
  78.9 4.4 %collective-permute-start.26 = (f16[64,3200]{1,0:T(8,128)(2,1)}, f16[64,3200]{1,0:T(8,128)(2,1)S(1)}, u32[]{:S(2)}, u32[]{:S(2)}) collective-permute-start(f16[64,3200]{1,0:T(8,128)(2,1)} %collective-permute-done.24), channel_id=1, source_target_pairs={{0,2},{2,0},{4,6},{6,4},{8,10},{10,8},{12,14},{14,12},{16,18},{18,... | collective-permute-start | bytes 1228808 | tf_op jit(solution)/shard_map/ppermute | solution.py:192
  83.3 0.8 collective-permute-start.28
  84.4 0.7 collective-permute-start.29
  85.1 0.9 exponential_reduce_fusion.13
  86.5 1.1 convert_multiply_fusion.11.refs_2_
  87.7 2.0 %put.8.refs_0_ = f32[1024,3072]{1,0:T(8,128)} custom-call(s32[16]{0:T(128)S(1)} %mul.308.starts, f32[1024,3072]{1,0:T(8,128)} %put.7.refs_0_, f32[64,3072]{1,0:T(8,128)S(1)} %convert_multiply_fusion.12.refs_1_, f32[64,3072]{1,0:T(8,128)S(1)} %convert_multiply_fusion.11.refs_2_, ...), custom_call_target="tpu_custom_call", output_to_operand_aliasing={{}: (1, {})} | custom-call | flops 2147483648 | tf_op jit(solution)/shard_map/put/pallas_call | solution.py:93
  89.7 4.9 %collective-permute-done.28 = f16[64,3200]{1,0:T(8,128)(2,1)S(1)} collective-permute-done((f16[64,3200]{1,0:T(8,128)(2,1)}, f16[64,3200]{1,0:T(8,128)(2,1)S(1)}, u32[]{:S(2)}, u32[]{:S(2)}) %collective-permute-start.28) | collective-permute-done | bytes 409632 | tf_op jit(solution)/shard_map/ppermute | solution.py:189
  94.6 0.8 collective-permute-start.30
  95.4 0.8 collective-permute-start.32
  96.9 0.7 collective-permute-start.33
  98.5 2.2 %put.9.refs_0_ = f32[1024,3072]{1,0:T(8,128)} custom-call(s32[16]{0:T(128)S(1)} %mul.308.starts, f32[1024,3072]{1,0:T(8,128)} %put.8.refs_0_, f32[64,3072]{1,0:T(8,128)S(1)} %convert_multiply_fusion.9.refs_1_, f32[64,3072]{1,0:T(8,128)S(1)} %convert_multiply_fusion.8.refs_2_, ...), custom_call_target="tpu_custom_call", output_to_operand_aliasing={{}: (1, {})} | custom-call | flops 2147483648 | tf_op jit(solution)/shard_map/put/pallas_call | solution.py:93
  100.7 5.8 %collective-permute-done.32 = f16[64,3200]{1,0:T(8,128)(2,1)S(1)} collective-permute-done((f16[64,3200]{1,0:T(8,128)(2,1)S(1)}, f16[64,3200]{1,0:T(8,128)(2,1)S(1)}, u32[]{:S(2)}, u32[]{:S(2)}) %collective-permute-start.32) | collective-permute-done | bytes 409632 | tf_op jit(solution)/shard_map/ppermute | solution.py:189
  106.5 0.8 collective-permute-start.37
  107.4 0.4 collective-permute-done.33
  107.8 0.7 collective-permute-start.36
  108.5 1.3 %collective-permute-start.34 = (f16[64,3200]{1,0:T(8,128)(2,1)S(1)}, f16[64,3200]{1,0:T(8,128)(2,1)S(1)}, u32[]{:S(2)}, u32[]{:S(2)}) collective-permute-start(f16[64,3200]{1,0:T(8,128)(2,1)S(1)} %collective-permute-done.32), channel_id=1, source_target_pairs={{0,2},{2,0},{4,6},{6,4},{8,10},{10,8},{12,14},{14,12},{16,18},{18,... | collective-permute-start | bytes 1228808 | tf_op jit(solution)/shard_map/ppermute | solution.py:192
  111.2 2.2 %put.10.refs_0_ = f32[1024,3072]{1,0:T(8,128)} custom-call(s32[16]{0:T(128)S(1)} %mul.308.starts, f32[1024,3072]{1,0:T(8,128)} %put.9.refs_0_, f32[64,3072]{1,0:T(8,128)S(1)} %convert_multiply_fusion.5.refs_1_, f32[64,3072]{1,0:T(8,128)S(1)} %convert_multiply_fusion.4.refs_2_, ...), custom_call_target="tpu_custom_call", output_to_operand_aliasing={{}: (1, {})} | custom-call | flops 2147483648 | tf_op jit(solution)/shard_map/put/pallas_call | solution.py:93
  113.5 0.6 collective-permute-start.39
  114.2 1.5 %collective-permute-start.38 = (f16[64,1664]{1,0:T(8,128)(2,1)S(1)}, f16[64,1664]{1,0:T(8,128)(2,1)S(1)}, u32[]{:S(2)}, u32[]{:S(2)}) collective-permute-start(f16[64,1664]{1,0:T(8,128)(2,1)S(1)} %collective-permute-done.36), channel_id=1, source_target_pairs={{0,2},{2,0},{4,6},{6,4},{8,10},{10,8},{12,14},{14,12},{16,18},{18,... | collective-permute-start | bytes 638984 | tf_op jit(solution)/shard_map/ppermute | solution.py:192
  116.6 1.7 %put.11.refs_0_ = f32[1024,3072]{1,0:T(8,128)} custom-call(s32[16]{0:T(128)S(1)} %mul.308.starts, f32[1024,3072]{1,0:T(8,128)} %put.10.refs_0_, f32[64,3072]{1,0:T(8,128)S(1)} %convert_multiply_fusion.1.refs_1_, f32[64,3072]{1,0:T(8,128)S(1)} %convert_multiply_fusion.refs_2_), custom_call_target="tpu_custom_call", output_to_operand_aliasing={{}: (1, {})} | custom-call | flops 2147483648 | tf_op jit(solution)/shard_map/put/pallas_call | solution.py:93
  118.3 1.4 %put.12.refs_0_ = f32[1024,3072]{1,0:T(8,128)} custom-call(s32[16]{0:T(128)S(1)} %mul.308.starts, f32[1024,3072]{1,0:T(8,128)} %put.11.refs_0_, f32[64,1536]{1,0:T(8,128)S(1)} %get-tuple-element.85.refs_1_, f32[64,1536]{1,0:T(8,128)S(1)} %get-tuple-element.84.refs_2_), custom_call_target="tpu_custom_call", output_to_operand_aliasing={{}: (1, {})} | custom-call | flops 2147483648 | tf_op jit(solution)/shard_map/put/pallas_call | solution.py:93
  120.1 1.4 %put.13 = f32[1024,3072]{1,0:T(8,128)} custom-call(s32[16]{0:T(128)S(1)} %mul.308.starts, f32[1024,3072]{1,0:T(8,128)} %put.12.refs_0_, f32[64,1536]{1,0:T(8,128)S(1)} %get-tuple-element.83.refs_1_, f32[64,1536]{1,0:T(8,128)S(1)} %get-tuple-element.82.refs_2_), custom_call_target="tpu_custom_call", output_to_operand_aliasing={{}: (1, {})} | custom-call | flops 2147483648 | tf_op jit(solution)/shard_map/put/pallas_call | solution.py:93
  (110 shorter events, 8.9 us)
Async XLA Ops:
  0.6 6.4 %copy-start.2 = (bf16[384,1,1024]{2,0,1:T(8,128)(2,1)S(1)}, bf16[384,1,1024]{2,0,1:T(8,128)(2,1)}, u32[]{:S(2)}) copy-start(bf16[384,1,1024]{2,0,1:T(8,128)(2,1)} %param.13) | copy-start | bytes 2359300
  0.6 6.4 %copy-start.3 = (bf16[384,1,1024]{2,0,1:T(8,128)(2,1)S(1)}, bf16[384,1,1024]{2,0,1:T(8,128)(2,1)}, u32[]{:S(2)}) copy-start(bf16[384,1,1024]{2,0,1:T(8,128)(2,1)} %param.14) | copy-start | bytes 2359300
  4.2 13.3 %collective-permute-start.1 = (bf16[192,1280]{1,0:T(8,128)(2,1)}, bf16[192,1280]{1,0:T(8,128)(2,1)S(1)}, u32[]{:S(2)}, u32[]{:S(2)}) collective-permute-start(bf16[192,1280]{1,0:T(8,128)(2,1)} %get-tuple-element.29.refs_0_), channel_id=1, source_target_pairs={{0,1},{1,0},{2,3},{3,2},{4,5},{5,4},{6,7},{7,6},{8,9},{9,8},{10,11... | collective-permute-start | bytes 1474568 | tf_op jit(solution)/shard_map/ppermute | solution.py:195
  7.1 2.3 %copy-start.1 = (bf16[192,1280]{1,0:T(8,128)(2,1)S(1)}, bf16[192,1280]{1,0:T(8,128)(2,1)}, u32[]{:S(2)}) copy-start(bf16[192,1280]{1,0:T(8,128)(2,1)} %get-tuple-element.29.refs_0_) | copy-start | bytes 1474564
  7.1 11.7 %copy-start = (bf16[192,1792]{1,0:T(8,128)(2,1)S(1)}, bf16[192,1792]{1,0:T(8,128)(2,1)}, u32[]{:S(2)}) copy-start(bf16[192,1792]{1,0:T(8,128)(2,1)} %get-tuple-element.39.refs_0_) | copy-start | bytes 2064388
  8.4 10.3 %collective-permute-start = (bf16[8,64,384]{2,1,0:T(8,128)(2,1)S(1)}, bf16[8,64,384]{2,1,0:T(8,128)(2,1)S(1)}, u32[]{:S(2)}, u32[]{:S(2)}) collective-permute-start(bf16[8,64,384]{2,1,0:T(8,128)(2,1)S(1)} %get-tuple-element.32), channel_id=1, source_target_pairs={{0,2},{2,0},{4,6},{6,4},{8,10},{10,8},{12,14},{14,12},{16,18},{18,... | collective-permute-start | bytes 1179656 | tf_op jit(solution)/shard_map/ppermute | solution.py:192
  9.4 10.9 %collective-permute-start.2 = (bf16[192,1280]{1,0:T(8,128)(2,1)S(1)}, bf16[192,1280]{1,0:T(8,128)(2,1)S(1)}, u32[]{:S(2)}, u32[]{:S(2)}) collective-permute-start(bf16[192,1280]{1,0:T(8,128)(2,1)S(1)} %copy-done.1), channel_id=1, source_target_pairs={{0,2},{2,0},{4,6},{6,4},{8,10},{10,8},{12,14},{14,12},{16,18},{18,... | collective-permute-start | bytes 1474568 | tf_op jit(solution)/shard_map/ppermute | solution.py:192
  17.4 2.8 %collective-permute-start.3 = (bf16[192,1280]{1,0:T(8,128)(2,1)S(1)}, bf16[192,1280]{1,0:T(8,128)(2,1)S(1)}, u32[]{:S(2)}, u32[]{:S(2)}) collective-permute-start(bf16[192,1280]{1,0:T(8,128)(2,1)S(1)} %collective-permute-done.1.refs_1_), channel_id=1, source_target_pairs={{0,2},{2,0},{4,6},{6,4},{8,10},{10,8},{12,14},{14,12},{16,18},{18,... | collective-permute-start | bytes 1474568 | tf_op jit(solution)/shard_map/ppermute | solution.py:192
  18.8 17.1 %collective-permute-start.10 = (bf16[192,1792]{1,0:T(8,128)(2,1)S(1)}, bf16[192,1792]{1,0:T(8,128)(2,1)S(1)}, u32[]{:S(2)}, u32[]{:S(2)}) collective-permute-start(bf16[192,1792]{1,0:T(8,128)(2,1)S(1)} %copy-done), channel_id=1, source_target_pairs={{0,1},{1,0},{2,3},{3,2},{4,5},{5,4},{6,7},{7,6},{8,9},{9,8},{10,11... | collective-permute-start | bytes 2064392 | tf_op jit(solution)/shard_map/ppermute | solution.py:195
  21.7 3.8 %collective-permute-start.4 = (f16[64,640]{1,0:T(8,128)(2,1)S(1)}, f16[64,640]{1,0:T(8,128)(2,1)S(1)}, u32[]{:S(2)}, u32[]{:S(2)}) collective-permute-start(f16[64,640]{1,0:T(8,128)(2,1)S(1)} %get-tuple-element.81), channel_id=1, source_target_pairs={{0,8},{2,10},{8,16},{10,18},{16,24},{18,26},{24,28},{26,30},{28,20... | collective-permute-start | bytes 245768 | tf_op jit(solution)/shard_map/ppermute | solution.py:189
  23.1 3.6 %collective-permute-start.5 = (f16[64,640]{1,0:T(8,128)(2,1)S(1)}, f16[64,640]{1,0:T(8,128)(2,1)S(1)}, u32[]{:S(2)}, u32[]{:S(2)}) collective-permute-start(f16[64,640]{1,0:T(8,128)(2,1)S(1)} %get-tuple-element.80), channel_id=1, source_target_pairs={{0,4},{2,6},{8,0},{10,2},{16,8},{18,10},{24,16},{26,18},{28,24},{3... | collective-permute-start | bytes 245768 | tf_op jit(solution)/shard_map/ppermute | solution.py:189
  26.8 4.5 %collective-permute-start.6 = (f16[64,1280]{1,0:T(8,128)(2,1)S(1)}, f16[64,1280]{1,0:T(8,128)(2,1)S(1)}, u32[]{:S(2)}, u32[]{:S(2)}) collective-permute-start(f16[64,1280]{1,0:T(8,128)(2,1)S(1)} %pad_maximum_fusion.5), channel_id=1, source_target_pairs={{0,8},{2,10},{8,16},{10,18},{16,24},{18,26},{24,28},{26,30},{28,20... | collective-permute-start | bytes 491528 | tf_op jit(solution)/shard_map/ppermute | solution.py:189
  28.2 4.5 %collective-permute-start.7 = (f16[64,1280]{1,0:T(8,128)(2,1)S(1)}, f16[64,1280]{1,0:T(8,128)(2,1)S(1)}, u32[]{:S(2)}, u32[]{:S(2)}) collective-permute-start(f16[64,1280]{1,0:T(8,128)(2,1)S(1)} %pad_maximum_fusion.6), channel_id=1, source_target_pairs={{0,4},{2,6},{8,0},{10,2},{16,8},{18,10},{24,16},{26,18},{28,24},{3... | collective-permute-start | bytes 491528 | tf_op jit(solution)/shard_map/ppermute | solution.py:189
  28.4 9.8 %collective-permute-start.11 = (bf16[192,1792]{1,0:T(8,128)(2,1)S(1)}, bf16[192,1792]{1,0:T(8,128)(2,1)S(1)}, u32[]{:S(2)}, u32[]{:S(2)}) collective-permute-start(bf16[192,1792]{1,0:T(8,128)(2,1)S(1)} %copy-done), channel_id=1, source_target_pairs={{0,2},{2,0},{4,6},{6,4},{8,10},{10,8},{12,14},{14,12},{16,18},{18,... | collective-permute-start | bytes 2064392 | tf_op jit(solution)/shard_map/ppermute | solution.py:192
  35.9 2.6 %collective-permute-start.12 = (bf16[192,1792]{1,0:T(8,128)(2,1)S(1)}, bf16[192,1792]{1,0:T(8,128)(2,1)S(1)}, u32[]{:S(2)}, u32[]{:S(2)}) collective-permute-start(bf16[192,1792]{1,0:T(8,128)(2,1)S(1)} %collective-permute-done.10.refs_1_), channel_id=1, source_target_pairs={{0,2},{2,0},{4,6},{6,4},{8,10},{10,8},{12,14},{14,12},{16,18},{18,... | collective-permute-start | bytes 2064392 | tf_op jit(solution)/shard_map/ppermute | solution.py:192
  36.7 5.8 %collective-permute-start.8 = (f16[64,1280]{1,0:T(8,128)(2,1)S(1)}, f16[64,1280]{1,0:T(8,128)(2,1)S(1)}, u32[]{:S(2)}, u32[]{:S(2)}) collective-permute-start(f16[64,1280]{1,0:T(8,128)(2,1)S(1)} %get-tuple-element.71), channel_id=1, source_target_pairs={{0,8},{2,10},{8,16},{10,18},{16,24},{18,26},{24,28},{26,30},{28,20... | collective-permute-start | bytes 491528 | tf_op jit(solution)/shard_map/ppermute | solution.py:189
  38.2 5.5 %collective-permute-start.9 = (f16[64,1280]{1,0:T(8,128)(2,1)S(1)}, f16[64,1280]{1,0:T(8,128)(2,1)S(1)}, u32[]{:S(2)}, u32[]{:S(2)}) collective-permute-start(f16[64,1280]{1,0:T(8,128)(2,1)S(1)} %get-tuple-element.70), channel_id=1, source_target_pairs={{0,4},{2,6},{8,0},{10,2},{16,8},{18,10},{24,16},{26,18},{28,24},{3... | collective-permute-start | bytes 491528 | tf_op jit(solution)/shard_map/ppermute | solution.py:189
  40.3 4.4 %collective-permute-start.15 = (f16[64,896]{1,0:T(8,128)(2,1)S(1)}, f16[64,896]{1,0:T(8,128)(2,1)S(1)}, u32[]{:S(2)}, u32[]{:S(2)}) collective-permute-start(f16[64,896]{1,0:T(8,128)(2,1)S(1)} %get-tuple-element.77), channel_id=1, source_target_pairs={{0,8},{2,10},{8,16},{10,18},{16,24},{18,26},{24,28},{26,30},{28,20... | collective-permute-start | bytes 344072 | tf_op jit(solution)/shard_map/ppermute | solution.py:189
  41.9 12.6 %copy-start.4 = (f32[1,64,3072]{2,1,0:T(8,128)S(1)}, f32[1,64,3072]{2,1,0:T(8,128)}, u32[]{:S(2)}) copy-start(f32[1,64,3072]{2,1,0:T(8,128)} %param.15) | copy-start | bytes 2359300
  41.9 4.0 %collective-permute-start.16 = (f16[64,896]{1,0:T(8,128)(2,1)S(1)}, f16[64,896]{1,0:T(8,128)(2,1)S(1)}, u32[]{:S(2)}, u32[]{:S(2)}) collective-permute-start(f16[64,896]{1,0:T(8,128)(2,1)S(1)} %get-tuple-element.76), channel_id=1, source_target_pairs={{0,4},{2,6},{8,0},{10,2},{16,8},{18,10},{24,16},{26,18},{28,24},{3... | collective-permute-start | bytes 344072 | tf_op jit(solution)/shard_map/ppermute | solution.py:189
  46.0 5.6 %collective-permute-start.17 = (f16[64,1792]{1,0:T(8,128)(2,1)S(1)}, f16[64,1792]{1,0:T(8,128)(2,1)S(1)}, u32[]{:S(2)}, u32[]{:S(2)}) collective-permute-start(f16[64,1792]{1,0:T(8,128)(2,1)S(1)} %pad_maximum_fusion.3), channel_id=1, source_target_pairs={{0,8},{2,10},{8,16},{10,18},{16,24},{18,26},{24,28},{26,30},{28,20... | collective-permute-start | bytes 688136 | tf_op jit(solution)/shard_map/ppermute | solution.py:189
  47.5 5.4 %collective-permute-start.18 = (f16[64,1792]{1,0:T(8,128)(2,1)S(1)}, f16[64,1792]{1,0:T(8,128)(2,1)S(1)}, u32[]{:S(2)}, u32[]{:S(2)}) collective-permute-start(f16[64,1792]{1,0:T(8,128)(2,1)S(1)} %pad_maximum_fusion.4), channel_id=1, source_target_pairs={{0,4},{2,6},{8,0},{10,2},{16,8},{18,10},{24,16},{26,18},{28,24},{3... | collective-permute-start | bytes 688136 | tf_op jit(solution)/shard_map/ppermute | solution.py:189
  53.0 4.9 %collective-permute-start.19 = (f16[64,1792]{1,0:T(8,128)(2,1)S(1)}, f16[64,1792]{1,0:T(8,128)(2,1)S(1)}, u32[]{:S(2)}, u32[]{:S(2)}) collective-permute-start(f16[64,1792]{1,0:T(8,128)(2,1)S(1)} %get-tuple-element.65), channel_id=1, source_target_pairs={{0,8},{2,10},{8,16},{10,18},{16,24},{18,26},{24,28},{26,30},{28,20... | collective-permute-start | bytes 688136 | tf_op jit(solution)/shard_map/ppermute | solution.py:189
  54.3 5.2 %collective-permute-start.20 = (f16[64,1792]{1,0:T(8,128)(2,1)S(1)}, f16[64,1792]{1,0:T(8,128)(2,1)S(1)}, u32[]{:S(2)}, u32[]{:S(2)}) collective-permute-start(f16[64,1792]{1,0:T(8,128)(2,1)S(1)} %get-tuple-element.64), channel_id=1, source_target_pairs={{0,4},{2,6},{8,0},{10,2},{16,8},{18,10},{24,16},{26,18},{28,24},{3... | collective-permute-start | bytes 688136 | tf_op jit(solution)/shard_map/ppermute | solution.py:189
  54.7 13.3 %copy-start.7 = (f32[1,64,3072]{2,1,0:T(8,128)S(1)}, f32[1,64,3072]{2,1,0:T(8,128)}, u32[]{:S(2)}) copy-start(f32[1,64,3072]{2,1,0:T(8,128)} %param.16) | copy-start | bytes 2359300
  54.7 13.3 %copy-start.8 = (f32[1,64,3072]{2,1,0:T(8,128)S(1)}, f32[1,64,3072]{2,1,0:T(8,128)}, u32[]{:S(2)}) copy-start(f32[1,64,3072]{2,1,0:T(8,128)} %param.17) | copy-start | bytes 2359300
  54.7 6.6 %collective-permute-start.13 = (f16[64,1280]{1,0:T(8,128)(2,1)S(1)}, f16[64,1280]{1,0:T(8,128)(2,1)S(1)}, u32[]{:S(2)}, u32[]{:S(2)}) collective-permute-start(f16[64,1280]{1,0:T(8,128)(2,1)S(1)} %get-tuple-element.69), channel_id=1, source_target_pairs={{0,8},{2,10},{8,16},{10,18},{16,24},{18,26},{24,28},{26,30},{28,20... | collective-permute-start | bytes 491528 | tf_op jit(solution)/shard_map/ppermute | solution.py:189
  56.0 5.9 %collective-permute-start.14 = (f16[64,1280]{1,0:T(8,128)(2,1)S(1)}, f16[64,1280]{1,0:T(8,128)(2,1)S(1)}, u32[]{:S(2)}, u32[]{:S(2)}) collective-permute-start(f16[64,1280]{1,0:T(8,128)(2,1)S(1)} %get-tuple-element.68), channel_id=1, source_target_pairs={{0,4},{2,6},{8,0},{10,2},{16,8},{18,10},{24,16},{26,18},{28,24},{3... | collective-permute-start | bytes 491528 | tf_op jit(solution)/shard_map/ppermute | solution.py:189
  59.6 7.0 %collective-permute-start.21 = (f16[64,1792]{1,0:T(8,128)(2,1)S(1)}, f16[64,1792]{1,0:T(8,128)(2,1)S(1)}, u32[]{:S(2)}, u32[]{:S(2)}) collective-permute-start(f16[64,1792]{1,0:T(8,128)(2,1)S(1)} %get-tuple-element.63), channel_id=1, source_target_pairs={{0,8},{2,10},{8,16},{10,18},{16,24},{18,26},{24,28},{26,30},{28,20... | collective-permute-start | bytes 688136 | tf_op jit(solution)/shard_map/ppermute | solution.py:189
  60.9 7.0 %collective-permute-start.22 = (f16[64,1792]{1,0:T(8,128)(2,1)S(1)}, f16[64,1792]{1,0:T(8,128)(2,1)S(1)}, u32[]{:S(2)}, u32[]{:S(2)}) collective-permute-start(f16[64,1792]{1,0:T(8,128)(2,1)S(1)} %get-tuple-element.62), channel_id=1, source_target_pairs={{0,4},{2,6},{8,0},{10,2},{16,8},{18,10},{24,16},{26,18},{28,24},{3... | collective-permute-start | bytes 688136 | tf_op jit(solution)/shard_map/ppermute | solution.py:189
  68.7 10.2 %copy-start.5 = (f32[1,64,3072]{2,1,0:T(8,128)}, f32[1,64,3072]{2,1,0:T(8,128)S(1)}, u32[]{:S(2)}) copy-start(f32[1,64,3072]{2,1,0:T(8,128)S(1)} %get-tuple-element.60) | copy-start | bytes 2359300
  68.7 10.2 %copy-start.6 = (f32[1,64,3072]{2,1,0:T(8,128)}, f32[1,64,3072]{2,1,0:T(8,128)S(1)}, u32[]{:S(2)}) copy-start(f32[1,64,3072]{2,1,0:T(8,128)S(1)} %get-tuple-element.61) | copy-start | bytes 2359300
  70.3 8.6 %collective-permute-start.24 = (f16[64,3200]{1,0:T(8,128)(2,1)S(1)}, f16[64,3200]{1,0:T(8,128)(2,1)}, u32[]{:S(2)}, u32[]{:S(2)}) collective-permute-start(f16[64,3200]{1,0:T(8,128)(2,1)S(1)} %pad_maximum_fusion.2), channel_id=1, source_target_pairs={{0,8},{2,10},{8,16},{10,18},{16,24},{18,26},{24,28},{26,30},{28,20... | collective-permute-start | bytes 1228808 | tf_op jit(solution)/shard_map/ppermute | solution.py:189
  71.2 12.9 %collective-permute-start.25 = (f16[64,3200]{1,0:T(8,128)(2,1)S(1)}, f16[64,3200]{1,0:T(8,128)(2,1)S(1)}, u32[]{:S(2)}, u32[]{:S(2)}) collective-permute-start(f16[64,3200]{1,0:T(8,128)(2,1)S(1)} %pad_maximum_fusion.2), channel_id=1, source_target_pairs={{0,4},{2,6},{8,0},{10,2},{16,8},{18,10},{24,16},{26,18},{28,24},{3... | collective-permute-start | bytes 1228808 | tf_op jit(solution)/shard_map/ppermute | solution.py:189
  71.9 14.2 %collective-permute-start.23 = (f16[64,3200]{1,0:T(8,128)(2,1)S(1)}, f16[64,3200]{1,0:T(8,128)(2,1)S(1)}, u32[]{:S(2)}, u32[]{:S(2)}) collective-permute-start(f16[64,3200]{1,0:T(8,128)(2,1)S(1)} %pad_maximum_fusion.2), channel_id=1, source_target_pairs={{0,2},{2,0},{4,6},{6,4},{8,10},{10,8},{12,14},{14,12},{16,18},{18,... | collective-permute-start | bytes 1228808 | tf_op jit(solution)/shard_map/ppermute | solution.py:192
  78.9 18.0 %collective-permute-start.26 = (f16[64,3200]{1,0:T(8,128)(2,1)}, f16[64,3200]{1,0:T(8,128)(2,1)S(1)}, u32[]{:S(2)}, u32[]{:S(2)}) collective-permute-start(f16[64,3200]{1,0:T(8,128)(2,1)} %collective-permute-done.24), channel_id=1, source_target_pairs={{0,2},{2,0},{4,6},{6,4},{8,10},{10,8},{12,14},{14,12},{16,18},{18,... | collective-permute-start | bytes 1228808 | tf_op jit(solution)/shard_map/ppermute | solution.py:192
  83.3 11.3 %collective-permute-start.28 = (f16[64,3200]{1,0:T(8,128)(2,1)}, f16[64,3200]{1,0:T(8,128)(2,1)S(1)}, u32[]{:S(2)}, u32[]{:S(2)}) collective-permute-start(f16[64,3200]{1,0:T(8,128)(2,1)} %collective-permute-done.24), channel_id=1, source_target_pairs={{0,8},{2,10},{8,16},{10,18},{16,24},{18,26},{24,28},{26,30},{28,20... | collective-permute-start | bytes 1228808 | tf_op jit(solution)/shard_map/ppermute | solution.py:189
  84.1 13.8 %collective-permute-start.27 = (f16[64,3200]{1,0:T(8,128)(2,1)S(1)}, f16[64,3200]{1,0:T(8,128)(2,1)S(1)}, u32[]{:S(2)}, u32[]{:S(2)}) collective-permute-start(f16[64,3200]{1,0:T(8,128)(2,1)S(1)} %collective-permute-done.25), channel_id=1, source_target_pairs={{0,2},{2,0},{4,6},{6,4},{8,10},{10,8},{12,14},{14,12},{16,18},{18,... | collective-permute-start | bytes 1228808 | tf_op jit(solution)/shard_map/ppermute | solution.py:192
  84.4 11.8 %collective-permute-start.29 = (f16[64,3200]{1,0:T(8,128)(2,1)S(1)}, f16[64,3200]{1,0:T(8,128)(2,1)S(1)}, u32[]{:S(2)}, u32[]{:S(2)}) collective-permute-start(f16[64,3200]{1,0:T(8,128)(2,1)S(1)} %collective-permute-done.25), channel_id=1, source_target_pairs={{0,4},{2,6},{8,0},{10,2},{16,8},{18,10},{24,16},{26,18},{28,24},{3... | collective-permute-start | bytes 1228808 | tf_op jit(solution)/shard_map/ppermute | solution.py:189
  94.6 15.6 %collective-permute-start.30 = (f16[64,3200]{1,0:T(8,128)(2,1)S(1)}, f16[64,3200]{1,0:T(8,128)(2,1)S(1)}, u32[]{:S(2)}, u32[]{:S(2)}) collective-permute-start(f16[64,3200]{1,0:T(8,128)(2,1)S(1)} %collective-permute-done.28), channel_id=1, source_target_pairs={{0,2},{2,0},{4,6},{6,4},{8,10},{10,8},{12,14},{14,12},{16,18},{18,... | collective-permute-start | bytes 1228808 | tf_op jit(solution)/shard_map/ppermute | solution.py:192
  95.4 11.1 %collective-permute-start.32 = (f16[64,3200]{1,0:T(8,128)(2,1)S(1)}, f16[64,3200]{1,0:T(8,128)(2,1)S(1)}, u32[]{:S(2)}, u32[]{:S(2)}) collective-permute-start(f16[64,3200]{1,0:T(8,128)(2,1)S(1)} %collective-permute-done.28), channel_id=1, source_target_pairs={{0,8},{2,10},{8,16},{10,18},{16,24},{18,26},{24,28},{26,30},{28,20... | collective-permute-start | bytes 1228808 | tf_op jit(solution)/shard_map/ppermute | solution.py:189
  96.2 14.5 %collective-permute-start.31 = (f16[64,3200]{1,0:T(8,128)(2,1)S(1)}, f16[64,3200]{1,0:T(8,128)(2,1)S(1)}, u32[]{:S(2)}, u32[]{:S(2)}) collective-permute-start(f16[64,3200]{1,0:T(8,128)(2,1)S(1)} %collective-permute-done.29), channel_id=1, source_target_pairs={{0,2},{2,0},{4,6},{6,4},{8,10},{10,8},{12,14},{14,12},{16,18},{18,... | collective-permute-start | bytes 1228808 | tf_op jit(solution)/shard_map/ppermute | solution.py:192
  96.9 10.9 %collective-permute-start.33 = (f16[64,3200]{1,0:T(8,128)(2,1)S(1)}, f16[64,3200]{1,0:T(8,128)(2,1)S(1)}, u32[]{:S(2)}, u32[]{:S(2)}) collective-permute-start(f16[64,3200]{1,0:T(8,128)(2,1)S(1)} %collective-permute-done.29), channel_id=1, source_target_pairs={{0,4},{2,6},{8,0},{10,2},{16,8},{18,10},{24,16},{26,18},{28,24},{3... | collective-permute-start | bytes 1228808 | tf_op jit(solution)/shard_map/ppermute | solution.py:189
  106.5 6.9 %collective-permute-start.37 = (f16[64,1536]{1,0:T(8,128)(2,1)S(1)}, f16[64,1536]{1,0:T(8,128)(2,1)S(1)}, u32[]{:S(2)}, u32[]{:S(2)}) collective-permute-start(f16[64,1536]{1,0:T(8,128)(2,1)S(1)} %slice.302), channel_id=1, source_target_pairs={{0,8},{2,10},{8,16},{10,18},{16,24},{18,26},{24,28},{26,30},{28,20... | collective-permute-start | bytes 589832 | tf_op jit(solution)/shard_map/ppermute | solution.py:189
  107.8 6.3 %collective-permute-start.36 = (f16[64,1664]{1,0:T(8,128)(2,1)S(1)}, f16[64,1664]{1,0:T(8,128)(2,1)S(1)}, u32[]{:S(2)}, u32[]{:S(2)}) collective-permute-start(f16[64,1664]{1,0:T(8,128)(2,1)S(1)} %slice.299), channel_id=1, source_target_pairs={{0,4},{2,6},{8,0},{10,2},{16,8},{18,10},{24,16},{26,18},{28,24},{3... | collective-permute-start | bytes 638984 | tf_op jit(solution)/shard_map/ppermute | solution.py:189
  108.5 7.4 %collective-permute-start.34 = (f16[64,3200]{1,0:T(8,128)(2,1)S(1)}, f16[64,3200]{1,0:T(8,128)(2,1)S(1)}, u32[]{:S(2)}, u32[]{:S(2)}) collective-permute-start(f16[64,3200]{1,0:T(8,128)(2,1)S(1)} %collective-permute-done.32), channel_id=1, source_target_pairs={{0,2},{2,0},{4,6},{6,4},{8,10},{10,8},{12,14},{14,12},{16,18},{18,... | collective-permute-start | bytes 1228808 | tf_op jit(solution)/shard_map/ppermute | solution.py:192
  110.2 6.0 %collective-permute-start.35 = (f16[64,3200]{1,0:T(8,128)(2,1)S(1)}, f16[64,3200]{1,0:T(8,128)(2,1)S(1)}, u32[]{:S(2)}, u32[]{:S(2)}) collective-permute-start(f16[64,3200]{1,0:T(8,128)(2,1)S(1)} %collective-permute-done.33), channel_id=1, source_target_pairs={{0,2},{2,0},{4,6},{6,4},{8,10},{10,8},{12,14},{14,12},{16,18},{18,... | collective-permute-start | bytes 1228808 | tf_op jit(solution)/shard_map/ppermute | solution.py:192
  113.5 6.4 %collective-permute-start.39 = (f16[64,1536]{1,0:T(8,128)(2,1)S(1)}, f16[64,1536]{1,0:T(8,128)(2,1)S(1)}, u32[]{:S(2)}, u32[]{:S(2)}) collective-permute-start(f16[64,1536]{1,0:T(8,128)(2,1)S(1)} %collective-permute-done.37), channel_id=1, source_target_pairs={{0,2},{2,0},{4,6},{6,4},{8,10},{10,8},{12,14},{14,12},{16,18},{18,... | collective-permute-start | bytes 589832 | tf_op jit(solution)/shard_map/ppermute | solution.py:192
  114.2 5.5 %collective-permute-start.38 = (f16[64,1664]{1,0:T(8,128)(2,1)S(1)}, f16[64,1664]{1,0:T(8,128)(2,1)S(1)}, u32[]{:S(2)}, u32[]{:S(2)}) collective-permute-start(f16[64,1664]{1,0:T(8,128)(2,1)S(1)} %collective-permute-done.36), channel_id=1, source_target_pairs={{0,2},{2,0},{4,6},{6,4},{8,10},{10,8},{12,14},{14,12},{16,18},{18,... | collective-permute-start | bytes 638984 | tf_op jit(solution)/shard_map/ppermute | solution.py:192

commit v4 on v3

--- a/solution.py
+++ b/solution.py
@@ -10,23 +10,27 @@
 F16 = jnp.float16
 F32 = jnp.float32
 BF16 = jnp.bfloat16
-CHUNKS = (1280, 1792)
-PUT_FLOPS = 2 << 30
+CHUNKS = (1536, 1536)
+PUT_FLOPS = 4 << 30
+SPLIT = 1
 HIDDEN_FLOPS = 8 << 30
 OFFSET = 3
+DISPATCH_FLOPS = 4 << 30
+DISPATCH_VMEM = 56
 
 
 def after(value, other):
     return lax.optimization_barrier((value, other))[0]
 
 
-def dispatch_kernel(cap_rows, ids_in, probs_in, grad_in, *refs):
-    outs, (ids, probs, grad, sems) = refs[:-4], refs[-4:]
-    cuts = [sum(out.shape[1] for out in outs[:n]) for n in range(len(outs))]
-    spots = [pl.ds(first, out.shape[1]) for first, out in zip(cuts, outs)]
+def dispatch_kernel(first, ids_in, probs_in, grad_in, out, ids, probs, grad, sems):
+    cap_rows, size = out.shape
+    cuts = [n * (size // 2) for n in range(2)]
+    spots = [pl.ds(cut, size // 2) for cut in cuts]
     copies = [pltpu.make_async_copy(ids_in, ids, sems.at[0]), pltpu.make_async_copy(probs_in, probs, sems.at[1])]
     copies += [
-        pltpu.make_async_copy(grad_in.at[:, spot], grad.at[:, spot], sems.at[2 + n]) for n, spot in enumerate(spots)
+        pltpu.make_async_copy(grad_in.at[:, pl.ds(first + cut, size // 2)], grad.at[:, spot], sems.at[2 + n])
+        for n, (cut, spot) in enumerate(zip(cuts, spots))
     ]
     for copy in copies:
         copy.start()
@@ -48,27 +52,27 @@
     places = lax.broadcasted_iota(jnp.int32, (cap_rows, tok_rows), 0).astype(F32)
     placing = jnp.where(slot == places, 1.0, 0.0).astype(BF16)
     weight = jnp.broadcast_to(weight, (128, tok_rows)).T[:, :1]
-    for n, (spot, out) in enumerate(zip(spots, outs)):
+    for n, spot in enumerate(spots):
         copies[2 + n].wait()
         scaled = (weight * grad[:, spot].astype(F32)).astype(BF16)
-        out[...] = jnp.dot(placing, scaled, preferred_element_type=F32).astype(BF16)
-
-
-def dispatch(ids, probs, grad, cap_rows):
-    ids, probs = ids.T, probs.T
-    vmem, hbm = pl.BlockSpec(memory_space=pltpu.VMEM), pl.BlockSpec(memory_space=pltpu.HBM)
+        out[:, spot] = jnp.dot(placing, scaled, preferred_element_type=F32).astype(BF16)
+
+
+def dispatch(ids, probs, grad, cap_rows, first, size):
+    vmem, hbm = pl.BlockSpec(memory_space=pltpu.VMEM), pl.BlockSpec(memory_space=pl.ANY)
     return pl.pallas_call(
-        functools.partial(dispatch_kernel, cap_rows),
-        out_shape=tuple(jax.ShapeDtypeStruct((cap_rows, size), BF16) for size in CHUNKS),
+        functools.partial(dispatch_kernel, first),
+        out_shape=jax.ShapeDtypeStruct((cap_rows, size), BF16),
         in_specs=[hbm] * 3,
-        out_specs=(vmem,) * len(CHUNKS),
+        out_specs=vmem,
         scratch_shapes=[
             pltpu.VMEM(ids.shape, ids.dtype),
             pltpu.VMEM(probs.shape, probs.dtype),
-            pltpu.VMEM(grad.shape, grad.dtype),
-            pltpu.SemaphoreType.DMA((2 + len(CHUNKS),)),
+            pltpu.VMEM((grad.shape[0], size), grad.dtype),
+            pltpu.SemaphoreType.DMA((4,)),
         ],
-        compiler_params=pltpu.CompilerParams(vmem_limit_bytes=56 << 20),
+        compiler_params=pltpu.CompilerParams(vmem_limit_bytes=DISPATCH_VMEM << 20),
+        cost_estimate=pl.CostEstimate(flops=DISPATCH_FLOPS, bytes_accessed=0, transcendentals=0),
         name="dispatch",
     )(ids, probs, grad)
 
@@ -79,10 +83,14 @@
     copies = []
     for n, (index, column) in enumerate(marks):
         height, size = pieces[n].shape
-        row = pl.multiple_of(starts[index], height)
-        spot = out.at[pl.ds(row, height), pl.ds(column, size)]
-        copies.append(pltpu.make_async_copy(pieces[n], spot, sems.at[n]))
-        copies[-1].start()
+        part = height // SPLIT
+        for k in range(SPLIT):
+            row = pl.multiple_of(starts[index] + k * part, part)
+            spot = out.at[pl.ds(row, part), pl.ds(column, size)]
+            copies.append(
+                pltpu.make_async_copy(pieces[n].at[pl.ds(k * part, part), :], spot, sems.at[n * SPLIT + k])
+            )
+            copies[-1].start()
     for copy in copies:
         copy.wait()
 
@@ -95,7 +103,7 @@
         out_shape=jax.ShapeDtypeStruct(shape, F32),
         in_specs=[pl.BlockSpec(memory_space=pltpu.SMEM)] + [spec] * (aliased + len(pieces)),
         out_specs=spec,
-        scratch_shapes=[pltpu.SemaphoreType.DMA((len(pieces),))],
+        scratch_shapes=[pltpu.SemaphoreType.DMA((len(pieces) * SPLIT,))],
         input_output_aliases={1: 0} if aliased else {},
         compiler_params=pltpu.CompilerParams(vmem_limit_bytes=1 << 20),
         cost_estimate=pl.CostEstimate(flops=PUT_FLOPS, bytes_accessed=0, transcendentals=0),
@@ -207,7 +215,10 @@
 
         count = len(CHUNKS)
         cuts = [sum(CHUNKS[:i]) for i in range(count)]
-        parts = dispatch(expert_ids, gate_probs, grad_out, cap_rows)
+        ids, probs = expert_ids.T, gate_probs.T
+        parts = []
+        for first, size in zip(cuts, CHUNKS):
+            parts.append(dispatch(after(ids, parts[-1]) if parts else ids, probs, grad_out, cap_rows, first, size))
 
         chip = lax.dynamic_index_in_dim(jnp.array(sources, jnp.int32), me // 2, 0, False)
         ahead = lax.dynamic_index_in_dim(jnp.array(distances, jnp.int32), me // 2, 0, False)
@@ -229,7 +240,7 @@
         middle = length // 2
         events = sorted((step + OFFSET * i, -i, i, step) for i in range(count) for step in range(middle))
         far, totals, moving = [], [], []
-        token = hidden_mine
+        token = (left, parts[-1])
         for _, _, i, step in events:
             size = CHUNKS[i]
             cut = size // 2
@@ -245,7 +256,7 @@
                 moving.append(None)
             else:
                 total, d = totals[i], middle - step
-                up, down = after(moving[i], token)
+                up, down = after(moving[i], (token, far[i + 1]) if step == 2 and i + 1 < count else token)
                 one, two = total[d], total[length - d]
                 if step == 1:
                     one = jnp.concatenate([one[:, :cut] + up.astype(F32), one[:, cut:]], axis=1)
@@ -283,7 +294,7 @@
         steps.append([(length // 2, cut, opposite[0]), (length // 2, 0, opposite[1])])
         starts = ((chip[:, None] * 2 + (core + jnp.arange(2, dtype=jnp.int32)) % 2) * own).astype(jnp.int32).reshape(-1)
         scales, weights, late = {}, None, []
-        for step in steps[:-1] + [[]] + steps[-1:] + [[]]:
+        for step in steps + [[]]:
             pieces = late
             late = []
             for d, first, value in step:

time: 122 us -> 119 us (0.975)
  waiting for transfers between devices: 46.9 us -> 41.3 us
  starting transfers between devices: 41.9 us -> 43.4 us
    ppermute x24, waiting for transfers between devices: 35.6 us -> 31.1 us  [step_ring(): lax.ppermute(value, 'dp', [(place(*x, c), place(*y, c)) for x, y in pairs...]
    pallas_call x1 -> x2, Pallas kernels: 3.5 us -> 5.82 us  [dispatch(): pl.pallas_call(functools.partial(dispatch_kernel, first), out_shape=jax.S...]
    ppermute x14, starting transfers between devices: 19.9 us -> 21.6 us  [swap_core(): lax.ppermute(value, 'dp', [(place(a, b, c), place(a, b, c + 1)) for a, b,...]
    pallas_call x7 -> x6, Pallas kernels: 12.5 us -> 11.3 us  [put(): pl.pallas_call(functools.partial(put_kernel, tuple(marks), aliased), out_...]
  transfers between devices with their start and end apart: 40 -> 40, of which waited for: 21 -> 20; matrix products, arithmetic and copies ran while one was open for 7% -> 7% of each run, Pallas kernels for 12% -> 14%
where the time goes in v4:
time: 119 us
  starting transfers between devices  43.4 us (36%)
  waiting for transfers between devices  41.3 us (35%)
  Pallas kernels  21.1 us (18%)
  other arithmetic  11.1 us (9%)
  between operations  1.21 us (1%)
    ppermute x24, waiting for transfers between devices, step_ring(): lax.ppermute(value, 'dp', [(place(*x, c), place(*y, c)) for x, y in pairs...  31.1 us
    ppermute x14, starting transfers between devices, swap_core(): lax.ppermute(value, 'dp', [(place(a, b, c), place(a, b, c + 1)) for a, b,...  21.6 us
    ppermute x24, starting transfers between devices, step_ring(): lax.ppermute(value, 'dp', [(place(*x, c), place(*y, c)) for x, y in pairs...  18.3 us
    pallas_call x6, Pallas kernels, put(): pl.pallas_call(functools.partial(put_kernel, tuple(marks), aliased), out_...  11.3 us
    ppermute x2, waiting for transfers between devices, shift_expert(): lax.ppermute(value, 'expert', [(e, (e + k) % experts) for e in range(expe...  9.92 us
    pallas_call x2, Pallas kernels, dispatch(): pl.pallas_call(functools.partial(dispatch_kernel, first), out_shape=jax.S...  5.82 us
    mul x16, other arithmetic, local(): values.append(value.astype(F32) * scales[spot])  4.27 us
    ppermute x2, starting transfers between devices, shift_expert(): lax.ppermute(value, 'expert', [(e, (e + k) % experts) for e in range(expe...  3.59 us
  transfers between devices with their start and end apart: 40, of which 20 were waited for; matrix products, arithmetic and copies ran while one was open for 7% of the time, Pallas kernels for 14%

profile of v4, /device:TPU:1, one launch (start us, length us, event | category | flops | bytes accessed | tf_op | source)
XLA Modules:
  0.0 118.7 jit_solution(14136695894737042778)
XLA Ops:
  0.7 2.9 %dispatch.2.refs_0_ = bf16[192,1536]{1,0:T(8,128)(2,1)} custom-call(s32[2,512]{1,0:T(2,128)} %bitcast.40, f32[2,512]{1,0:T(2,128)} %bitcast.42, bf16[512,3072]{1,0:T(8,128)(2,1)} %grad_in.3), custom_call_target="tpu_custom_call" | custom-call | flops 4294967296 | tf_op jit(solution)/shard_map/dispatch/pallas_call | solution.py:63
  3.6 2.1 %collective-permute-start.1 = (bf16[192,1536]{1,0:T(8,128)(2,1)}, bf16[192,1536]{1,0:T(8,128)(2,1)S(1)}, u32[]{:S(2)}, u32[]{:S(2)}) collective-permute-start(bf16[192,1536]{1,0:T(8,128)(2,1)} %dispatch.2.refs_0_), channel_id=1, source_target_pairs={{0,1},{1,0},{2,3},{3,2},{4,5},{5,4},{6,7},{7,6},{8,9},{9,8},{10,11... | collective-permute-start | bytes 1769480 | tf_op jit(solution)/shard_map/ppermute | solution.py:203
  5.7 1.0 collective-permute-start.2
  6.7 0.7 multiply_bitcast_fusion
  7.5 1.3 %hidden_pieces.1 = (bf16[8,64,384]{2,1,0:T(8,128)(2,1)S(1)}, bf16[8,64,384]{2,1,0:T(8,128)(2,1)S(1)}) custom-call(s32[10]{0:T(128)S(1)} %pad_add_fusion.at, bf16[384,1024]{1,0:T(8,128)(2,1)S(1)} %bitcast.34, bf16[384,1024]{1,0:T(8,128)(2,1)S(1)} %bitcast.35), custom_call_target="tpu_custom_call" | custom-call | flops 8589934592 | tf_op jit(solution)/shard_map/hidden_pieces/pallas_call | solution.py:136
  8.8 2.9 %dispatch.3.refs_0_ = bf16[192,1536]{1,0:T(8,128)(2,1)} custom-call(s32[2,512]{1,0:T(2,128)} %bitcast.41, f32[2,512]{1,0:T(2,128)} %bitcast.43, bf16[512,3072]{1,0:T(8,128)(2,1)} %grad_in.3), custom_call_target="tpu_custom_call" | custom-call | flops 4294967296 | tf_op jit(solution)/shard_map/dispatch/pallas_call | solution.py:63
  11.8 7.2 %collective-permute-done.1.refs_1_ = bf16[192,1536]{1,0:T(8,128)(2,1)S(1)} collective-permute-done((bf16[192,1536]{1,0:T(8,128)(2,1)}, bf16[192,1536]{1,0:T(8,128)(2,1)S(1)}, u32[]{:S(2)}, u32[]{:S(2)}) %collective-permute-start.1) | collective-permute-done | bytes 589856 | tf_op jit(solution)/shard_map/ppermute | solution.py:203
  19.0 1.2 %collective-permute-start.3 = (bf16[192,1536]{1,0:T(8,128)(2,1)S(1)}, bf16[192,1536]{1,0:T(8,128)(2,1)S(1)}, u32[]{:S(2)}, u32[]{:S(2)}) collective-permute-start(bf16[192,1536]{1,0:T(8,128)(2,1)S(1)} %collective-permute-done.1.refs_1_), channel_id=1, source_target_pairs={{0,2},{2,0},{4,6},{6,4},{8,10},{10,8},{12,14},{14,12},{16,18},{18,... | collective-permute-start | bytes 1769480 | tf_op jit(solution)/shard_map/ppermute | solution.py:200
  20.2 1.5 %collective-permute-start.8 = (bf16[192,1536]{1,0:T(8,128)(2,1)}, bf16[192,1536]{1,0:T(8,128)(2,1)S(1)}, u32[]{:S(2)}, u32[]{:S(2)}) collective-permute-start(bf16[192,1536]{1,0:T(8,128)(2,1)} %dispatch.3.refs_0_), channel_id=1, source_target_pairs={{0,1},{1,0},{2,3},{3,2},{4,5},{5,4},{6,7},{7,6},{8,9},{9,8},{10,11... | collective-permute-start | bytes 1769480 | tf_op jit(solution)/shard_map/ppermute | solution.py:203
  21.9 1.4 %product.2 = f32[512,1536]{1,0:T(8,128)S(1)} custom-call(bf16[512,768]{1,0:T(8,128)(2,1)S(1)} %bitcast.32, bf16[192,1536]{1,0:T(8,128)(2,1)S(1)} %copy-done.1, bf16[192,1536]{1,0:T(8,128)(2,1)S(1)} %collective-permute-done.1.refs_1_, bf16[192,1536]{1,0:T(8,128)(2,1)S(1)} %collective-permute-done.2.refs_2_, bf16[192,1536]{1,0:T(8,128)(2,1)S(1)} %collective-permute-done.3.refs_3_), custom_call_target="tpu_custom_call" | custom-call | tf_op jit(solution)/shard_map/product/pallas_call | solution.py:160
  23.5 1.6 %collective-permute-start.4 = (f16[64,768]{1,0:T(8,128)(2,1)S(1)}, f16[64,768]{1,0:T(8,128)(2,1)S(1)}, u32[]{:S(2)}, u32[]{:S(2)}) collective-permute-start(f16[64,768]{1,0:T(8,128)(2,1)S(1)} %get-tuple-element.79), channel_id=1, source_target_pairs={{0,8},{2,10},{8,16},{10,18},{16,24},{18,26},{24,28},{26,30},{28,20... | collective-permute-start | bytes 294920 | tf_op jit(solution)/shard_map/ppermute | solution.py:197
  25.1 2.5 %collective-permute-done.4 = f16[64,768]{1,0:T(8,128)(2,1)S(1)} collective-permute-done((f16[64,768]{1,0:T(8,128)(2,1)S(1)}, f16[64,768]{1,0:T(8,128)(2,1)S(1)}, u32[]{:S(2)}, u32[]{:S(2)}) %collective-permute-start.4) | collective-permute-done | bytes 98336 | tf_op jit(solution)/shard_map/ppermute | solution.py:197
  27.6 1.3 %collective-permute-done.5 = f16[64,768]{1,0:T(8,128)(2,1)S(1)} collective-permute-done((f16[64,768]{1,0:T(8,128)(2,1)S(1)}, f16[64,768]{1,0:T(8,128)(2,1)S(1)}, u32[]{:S(2)}, u32[]{:S(2)}) %collective-permute-start.5) | collective-permute-done | bytes 98336 | tf_op jit(solution)/shard_map/ppermute | solution.py:197
  29.0 1.3 %collective-permute-start.6 = (f16[64,1536]{1,0:T(8,128)(2,1)S(1)}, f16[64,1536]{1,0:T(8,128)(2,1)S(1)}, u32[]{:S(2)}, u32[]{:S(2)}) collective-permute-start(f16[64,1536]{1,0:T(8,128)(2,1)S(1)} %pad_maximum_fusion.3), channel_id=1, source_target_pairs={{0,8},{2,10},{8,16},{10,18},{16,24},{18,26},{24,28},{26,30},{28,20... | collective-permute-start | bytes 589832 | tf_op jit(solution)/shard_map/ppermute | solution.py:197
  30.6 2.1 %collective-permute-start.11 = (bf16[192,1536]{1,0:T(8,128)(2,1)S(1)}, bf16[192,1536]{1,0:T(8,128)(2,1)S(1)}, u32[]{:S(2)}, u32[]{:S(2)}) collective-permute-start(bf16[192,1536]{1,0:T(8,128)(2,1)S(1)} %copy-done), channel_id=1, source_target_pairs={{0,2},{2,0},{4,6},{6,4},{8,10},{10,8},{12,14},{14,12},{16,18},{18,... | collective-permute-start | bytes 1769480 | tf_op jit(solution)/shard_map/ppermute | solution.py:200
  32.7 2.7 %collective-permute-done.8.refs_1_ = bf16[192,1536]{1,0:T(8,128)(2,1)S(1)} collective-permute-done((bf16[192,1536]{1,0:T(8,128)(2,1)}, bf16[192,1536]{1,0:T(8,128)(2,1)S(1)}, u32[]{:S(2)}, u32[]{:S(2)}) %collective-permute-start.8) | collective-permute-done | bytes 589856 | tf_op jit(solution)/shard_map/ppermute | solution.py:203
  35.5 2.5 %collective-permute-start.12 = (bf16[192,1536]{1,0:T(8,128)(2,1)S(1)}, bf16[192,1536]{1,0:T(8,128)(2,1)S(1)}, u32[]{:S(2)}, u32[]{:S(2)}) collective-permute-start(bf16[192,1536]{1,0:T(8,128)(2,1)S(1)} %collective-permute-done.8.refs_1_), channel_id=1, source_target_pairs={{0,2},{2,0},{4,6},{6,4},{8,10},{10,8},{12,14},{14,12},{16,18},{18,... | collective-permute-start | bytes 1769480 | tf_op jit(solution)/shard_map/ppermute | solution.py:200
  38.1 1.3 %collective-permute-start.9 = (f16[64,1536]{1,0:T(8,128)(2,1)S(1)}, f16[64,1536]{1,0:T(8,128)(2,1)S(1)}, u32[]{:S(2)}, u32[]{:S(2)}) collective-permute-start(f16[64,1536]{1,0:T(8,128)(2,1)S(1)} %get-tuple-element.69), channel_id=1, source_target_pairs={{0,8},{2,10},{8,16},{10,18},{16,24},{18,26},{24,28},{26,30},{28,20... | collective-permute-start | bytes 589832 | tf_op jit(solution)/shard_map/ppermute | solution.py:197
  39.7 1.4 %product.3 = f32[512,1536]{1,0:T(8,128)S(1)} custom-call(bf16[512,768]{1,0:T(8,128)(2,1)S(1)} %bitcast.33, bf16[192,1536]{1,0:T(8,128)(2,1)S(1)} %copy-done, bf16[192,1536]{1,0:T(8,128)(2,1)S(1)} %collective-permute-done.8.refs_1_, bf16[192,1536]{1,0:T(8,128)(2,1)S(1)} %collective-permute-done.11.refs_2_, bf16[192,1536]{1,0:T(8,128)(2,1)S(1)} %collective-permute-done.12.refs_3_), custom_call_target="tpu_custom_call" | custom-call | tf_op jit(solution)/shard_map/product/pallas_call | solution.py:160
  41.4 1.3 %collective-permute-start.15 = (f16[64,768]{1,0:T(8,128)(2,1)S(1)}, f16[64,768]{1,0:T(8,128)(2,1)S(1)}, u32[]{:S(2)}, u32[]{:S(2)}) collective-permute-start(f16[64,768]{1,0:T(8,128)(2,1)S(1)} %get-tuple-element.75), channel_id=1, source_target_pairs={{0,8},{2,10},{8,16},{10,18},{16,24},{18,26},{24,28},{26,30},{28,20... | collective-permute-start | bytes 294920 | tf_op jit(solution)/shard_map/ppermute | solution.py:197
  42.9 1.7 %collective-permute-done.9 = f16[64,1536]{1,0:T(8,128)(2,1)S(1)} collective-permute-done((f16[64,1536]{1,0:T(8,128)(2,1)S(1)}, f16[64,1536]{1,0:T(8,128)(2,1)S(1)}, u32[]{:S(2)}, u32[]{:S(2)}) %collective-permute-start.9) | collective-permute-done | bytes 196640 | tf_op jit(solution)/shard_map/ppermute | solution.py:197
  44.5 1.0 collective-permute-done.10
  45.6 1.0 collective-permute-done.15
  46.6 1.0 collective-permute-done.16
  47.7 1.3 %collective-permute-start.17 = (f16[64,1536]{1,0:T(8,128)(2,1)S(1)}, f16[64,1536]{1,0:T(8,128)(2,1)S(1)}, u32[]{:S(2)}, u32[]{:S(2)}) collective-permute-start(f16[64,1536]{1,0:T(8,128)(2,1)S(1)} %pad_maximum_fusion.5), channel_id=1, source_target_pairs={{0,8},{2,10},{8,16},{10,18},{16,24},{18,26},{24,28},{26,30},{28,20... | collective-permute-start | bytes 589832 | tf_op jit(solution)/shard_map/ppermute | solution.py:197
  49.4 3.6 %collective-permute-done.17 = f16[64,1536]{1,0:T(8,128)(2,1)S(1)} collective-permute-done((f16[64,1536]{1,0:T(8,128)(2,1)S(1)}, f16[64,1536]{1,0:T(8,128)(2,1)S(1)}, u32[]{:S(2)}, u32[]{:S(2)}) %collective-permute-start.17) | collective-permute-done | bytes 196640 | tf_op jit(solution)/shard_map/ppermute | solution.py:197
  53.0 1.0 collective-permute-done.18
  54.2 0.5 collective-permute-start.19
  54.7 1.0 collective-permute-start.20
  55.9 0.5 collective-permute-start.13
  56.4 1.0 collective-permute-start.14
  57.4 1.4 %collective-permute-done.19 = f16[64,1536]{1,0:T(8,128)(2,1)S(1)} collective-permute-done((f16[64,1536]{1,0:T(8,128)(2,1)S(1)}, f16[64,1536]{1,0:T(8,128)(2,1)S(1)}, u32[]{:S(2)}, u32[]{:S(2)}) %collective-permute-start.19) | collective-permute-done | bytes 196640 | tf_op jit(solution)/shard_map/ppermute | solution.py:197
  58.8 0.5 collective-permute-done.20
  59.4 1.0 collective-permute-start.21
  60.4 0.5 collective-permute-start.22
  61.1 1.4 %collective-permute-done.13 = f16[64,1536]{1,0:T(8,128)(2,1)S(1)} collective-permute-done((f16[64,1536]{1,0:T(8,128)(2,1)S(1)}, f16[64,1536]{1,0:T(8,128)(2,1)S(1)}, u32[]{:S(2)}, u32[]{:S(2)}) %collective-permute-start.13) | collective-permute-done | bytes 196640 | tf_op jit(solution)/shard_map/ppermute | solution.py:197
  62.5 0.4 collective-permute-done.14
  62.9 3.8 %collective-permute-done.21 = f16[64,1536]{1,0:T(8,128)(2,1)S(1)} collective-permute-done((f16[64,1536]{1,0:T(8,128)(2,1)S(1)}, f16[64,1536]{1,0:T(8,128)(2,1)S(1)}, u32[]{:S(2)}, u32[]{:S(2)}) %collective-permute-start.21) | collective-permute-done | bytes 196640 | tf_op jit(solution)/shard_map/ppermute | solution.py:197
  66.7 0.7 collective-permute-done.22
  67.5 0.6 multiply_reduce_fusion
  68.2 1.4 %convert_multiply_fusion.13 = (f32[64,3072]{1,0:T(8,128)S(1)}, f16[64,3072]{1,0:T(8,128)(2,1)S(1)}, f32[1,64,3072]{2,1,0:T(8,128)}) fusion(f32[64]{0:T(128)S(1)} %get-tuple-element.85, f32[64]{0:T(128)S(1)} %get-tuple-element.84, f32[1,64,3072]{2,1,0:T(8,128)S(1)} %copy-done.4, f32[1,64,3072]{2,1,0:T(8,128)S(1)} %get-tuple-element.59, ...), kind=kLoop, calls=%fused_computation.19 | loop fusion | flops 1966080 | bytes 4326144 | tf_op jit(solution)/shard_map/mul | solution.py:308
  69.9 1.3 %collective-permute-start.25 = (f16[64,3200]{1,0:T(8,128)(2,1)S(1)}, f16[64,3200]{1,0:T(8,128)(2,1)S(1)}, u32[]{:S(2)}, u32[]{:S(2)}) collective-permute-start(f16[64,3200]{1,0:T(8,128)(2,1)S(1)} %pad_maximum_fusion.2), channel_id=1, source_target_pairs={{0,4},{2,6},{8,0},{10,2},{16,8},{18,10},{24,16},{26,18},{28,24},{3... | collective-permute-start | bytes 1228808 | tf_op jit(solution)/shard_map/ppermute | solution.py:197
  71.4 5.2 %collective-permute-start.23 = (f16[64,3200]{1,0:T(8,128)(2,1)S(1)}, f16[64,3200]{1,0:T(8,128)(2,1)S(1)}, u32[]{:S(2)}, u32[]{:S(2)}) collective-permute-start(f16[64,3200]{1,0:T(8,128)(2,1)S(1)} %pad_maximum_fusion.2), channel_id=1, source_target_pairs={{0,2},{2,0},{4,6},{6,4},{8,10},{10,8},{12,14},{14,12},{16,18},{18,... | collective-permute-start | bytes 1228808 | tf_op jit(solution)/shard_map/ppermute | solution.py:200
  76.6 1.4 %put.6.refs_0_ = f32[1024,3072]{1,0:T(8,128)} custom-call(s32[16]{0:T(128)S(1)} %mul.308.starts, f32[64,3072]{1,0:T(8,128)S(1)} %get-tuple-element.54.refs_0_), custom_call_target="tpu_custom_call" | custom-call | flops 4294967296 | tf_op jit(solution)/shard_map/put/pallas_call | solution.py:101
  78.1 4.4 %collective-permute-start.26 = (f16[64,3200]{1,0:T(8,128)(2,1)}, f16[64,3200]{1,0:T(8,128)(2,1)S(1)}, u32[]{:S(2)}, u32[]{:S(2)}) collective-permute-start(f16[64,3200]{1,0:T(8,128)(2,1)} %collective-permute-done.24), channel_id=1, source_target_pairs={{0,2},{2,0},{4,6},{6,4},{8,10},{10,8},{12,14},{14,12},{16,18},{18,... | collective-permute-start | bytes 1228808 | tf_op jit(solution)/shard_map/ppermute | solution.py:200
  82.8 1.1 collective-permute-start.29
  83.9 0.9 exponential_reduce_fusion.13
  85.4 1.1 convert_multiply_fusion.11.refs_2_
  86.6 2.0 %put.7.refs_0_ = f32[1024,3072]{1,0:T(8,128)} custom-call(s32[16]{0:T(128)S(1)} %mul.308.starts, f32[1024,3072]{1,0:T(8,128)} %put.6.refs_0_, f32[64,3072]{1,0:T(8,128)S(1)} %convert_multiply_fusion.12.refs_1_, f32[64,3072]{1,0:T(8,128)S(1)} %convert_multiply_fusion.11.refs_2_, ...), custom_call_target="tpu_custom_call", output_to_operand_aliasing={{}: (1, {})} | custom-call | flops 4294967296 | tf_op jit(solution)/shard_map/put/pallas_call | solution.py:101
  88.6 0.6 collective-permute-start.27
  89.2 4.5 %collective-permute-done.28 = f16[64,3200]{1,0:T(8,128)(2,1)S(1)} collective-permute-done((f16[64,3200]{1,0:T(8,128)(2,1)}, f16[64,3200]{1,0:T(8,128)(2,1)S(1)}, u32[]{:S(2)}, u32[]{:S(2)}) %collective-permute-start.28) | collective-permute-done | bytes 409632 | tf_op jit(solution)/shard_map/ppermute | solution.py:197
  93.8 0.8 collective-permute-start.30
  94.9 1.1 collective-permute-start.33
  97.3 2.2 %put.8.refs_0_ = f32[1024,3072]{1,0:T(8,128)} custom-call(s32[16]{0:T(128)S(1)} %mul.308.starts, f32[1024,3072]{1,0:T(8,128)} %put.7.refs_0_, f32[64,3072]{1,0:T(8,128)S(1)} %convert_multiply_fusion.9.refs_1_, f32[64,3072]{1,0:T(8,128)S(1)} %convert_multiply_fusion.8.refs_2_, ...), custom_call_target="tpu_custom_call", output_to_operand_aliasing={{}: (1, {})} | custom-call | flops 4294967296 | tf_op jit(solution)/shard_map/put/pallas_call | solution.py:101
  99.6 0.6 collective-permute-start.31
  100.2 5.5 %collective-permute-done.32 = f16[64,3200]{1,0:T(8,128)(2,1)S(1)} collective-permute-done((f16[64,3200]{1,0:T(8,128)(2,1)S(1)}, f16[64,3200]{1,0:T(8,128)(2,1)S(1)}, u32[]{:S(2)}, u32[]{:S(2)}) %collective-permute-start.32) | collective-permute-done | bytes 409632 | tf_op jit(solution)/shard_map/ppermute | solution.py:197
  105.7 0.4 collective-permute-start.37
  106.1 1.2 %collective-permute-start.36 = (f16[64,1664]{1,0:T(8,128)(2,1)S(1)}, f16[64,1664]{1,0:T(8,128)(2,1)S(1)}, u32[]{:S(2)}, u32[]{:S(2)}) collective-permute-start(f16[64,1664]{1,0:T(8,128)(2,1)S(1)} %slice.299), channel_id=1, source_target_pairs={{0,4},{2,6},{8,0},{10,2},{16,8},{18,10},{24,16},{26,18},{28,24},{3... | collective-permute-start | bytes 638984 | tf_op jit(solution)/shard_map/ppermute | solution.py:197
  108.6 2.2 %put.9.refs_0_ = f32[1024,3072]{1,0:T(8,128)} custom-call(s32[16]{0:T(128)S(1)} %mul.308.starts, f32[1024,3072]{1,0:T(8,128)} %put.8.refs_0_, f32[64,3072]{1,0:T(8,128)S(1)} %convert_multiply_fusion.5.refs_1_, f32[64,3072]{1,0:T(8,128)S(1)} %convert_multiply_fusion.4.refs_2_, ...), custom_call_target="tpu_custom_call", output_to_operand_aliasing={{}: (1, {})} | custom-call | flops 4294967296 | tf_op jit(solution)/shard_map/put/pallas_call | solution.py:101
  110.9 1.4 %collective-permute-start.34 = (f16[64,3200]{1,0:T(8,128)(2,1)S(1)}, f16[64,3200]{1,0:T(8,128)(2,1)S(1)}, u32[]{:S(2)}, u32[]{:S(2)}) collective-permute-start(f16[64,3200]{1,0:T(8,128)(2,1)S(1)} %collective-permute-done.32), channel_id=1, source_target_pairs={{0,2},{2,0},{4,6},{6,4},{8,10},{10,8},{12,14},{14,12},{16,18},{18,... | collective-permute-start | bytes 1228808 | tf_op jit(solution)/shard_map/ppermute | solution.py:200
  112.3 0.7 collective-permute-start.39
  113.3 0.8 collective-permute-start.38
  114.9 2.0 %put.10.refs_0_ = f32[1024,3072]{1,0:T(8,128)} custom-call(s32[16]{0:T(128)S(1)} %mul.308.starts, f32[1024,3072]{1,0:T(8,128)} %put.9.refs_0_, f32[64,3072]{1,0:T(8,128)S(1)} %convert_multiply_fusion.1.refs_1_, f32[64,3072]{1,0:T(8,128)S(1)} %convert_multiply_fusion.refs_2_, ...), custom_call_target="tpu_custom_call", output_to_operand_aliasing={{}: (1, {})} | custom-call | flops 4294967296 | tf_op jit(solution)/shard_map/put/pallas_call | solution.py:101
  117.2 1.4 %put.11 = f32[1024,3072]{1,0:T(8,128)} custom-call(s32[16]{0:T(128)S(1)} %mul.308.starts, f32[1024,3072]{1,0:T(8,128)} %put.10.refs_0_, f32[64,1536]{1,0:T(8,128)S(1)} %get-tuple-element.81.refs_1_, f32[64,1536]{1,0:T(8,128)S(1)} %get-tuple-element.80.refs_2_), custom_call_target="tpu_custom_call", output_to_operand_aliasing={{}: (1, {})} | custom-call | flops 4294967296 | tf_op jit(solution)/shard_map/put/pallas_call | solution.py:101
  (110 shorter events, 9.1 us)
Async XLA Ops:
  0.6 6.8 %copy-start.2 = (bf16[384,1,1024]{2,0,1:T(8,128)(2,1)S(1)}, bf16[384,1,1024]{2,0,1:T(8,128)(2,1)}, u32[]{:S(2)}) copy-start(bf16[384,1,1024]{2,0,1:T(8,128)(2,1)} %param.13) | copy-start | bytes 2359300
  0.6 6.8 %copy-start.3 = (bf16[384,1,1024]{2,0,1:T(8,128)(2,1)S(1)}, bf16[384,1,1024]{2,0,1:T(8,128)(2,1)}, u32[]{:S(2)}) copy-start(bf16[384,1,1024]{2,0,1:T(8,128)(2,1)} %param.14) | copy-start | bytes 2359300
  3.6 15.4 %collective-permute-start.1 = (bf16[192,1536]{1,0:T(8,128)(2,1)}, bf16[192,1536]{1,0:T(8,128)(2,1)S(1)}, u32[]{:S(2)}, u32[]{:S(2)}) collective-permute-start(bf16[192,1536]{1,0:T(8,128)(2,1)} %dispatch.2.refs_0_), channel_id=1, source_target_pairs={{0,1},{1,0},{2,3},{3,2},{4,5},{5,4},{6,7},{7,6},{8,9},{9,8},{10,11... | collective-permute-start | bytes 1769480 | tf_op jit(solution)/shard_map/ppermute | solution.py:203
  5.7 16.0 %collective-permute-start.2 = (bf16[192,1536]{1,0:T(8,128)(2,1)}, bf16[192,1536]{1,0:T(8,128)(2,1)S(1)}, u32[]{:S(2)}, u32[]{:S(2)}) collective-permute-start(bf16[192,1536]{1,0:T(8,128)(2,1)} %dispatch.2.refs_0_), channel_id=1, source_target_pairs={{0,2},{2,0},{4,6},{6,4},{8,10},{10,8},{12,14},{14,12},{16,18},{18,... | collective-permute-start | bytes 1769480 | tf_op jit(solution)/shard_map/ppermute | solution.py:200
  8.8 13.1 %copy-start.1 = (bf16[192,1536]{1,0:T(8,128)(2,1)S(1)}, bf16[192,1536]{1,0:T(8,128)(2,1)}, u32[]{:S(2)}) copy-start(bf16[192,1536]{1,0:T(8,128)(2,1)} %dispatch.2.refs_0_) | copy-start | bytes 1769476
  8.8 3.0 %collective-permute-start = (bf16[8,64,384]{2,1,0:T(8,128)(2,1)S(1)}, bf16[8,64,384]{2,1,0:T(8,128)(2,1)S(1)}, u32[]{:S(2)}, u32[]{:S(2)}) collective-permute-start(bf16[8,64,384]{2,1,0:T(8,128)(2,1)S(1)} %get-tuple-element.30), channel_id=1, source_target_pairs={{0,2},{2,0},{4,6},{6,4},{8,10},{10,8},{12,14},{14,12},{16,18},{18,... | collective-permute-start | bytes 1179656 | tf_op jit(solution)/shard_map/ppermute | solution.py:200
  19.0 2.9 %collective-permute-start.3 = (bf16[192,1536]{1,0:T(8,128)(2,1)S(1)}, bf16[192,1536]{1,0:T(8,128)(2,1)S(1)}, u32[]{:S(2)}, u32[]{:S(2)}) collective-permute-start(bf16[192,1536]{1,0:T(8,128)(2,1)S(1)} %collective-permute-done.1.refs_1_), channel_id=1, source_target_pairs={{0,2},{2,0},{4,6},{6,4},{8,10},{10,8},{12,14},{14,12},{16,18},{18,... | collective-permute-start | bytes 1769480 | tf_op jit(solution)/shard_map/ppermute | solution.py:200
  20.2 15.2 %collective-permute-start.8 = (bf16[192,1536]{1,0:T(8,128)(2,1)}, bf16[192,1536]{1,0:T(8,128)(2,1)S(1)}, u32[]{:S(2)}, u32[]{:S(2)}) collective-permute-start(bf16[192,1536]{1,0:T(8,128)(2,1)} %dispatch.3.refs_0_), channel_id=1, source_target_pairs={{0,1},{1,0},{2,3},{3,2},{4,5},{5,4},{6,7},{7,6},{8,9},{9,8},{10,11... | collective-permute-start | bytes 1769480 | tf_op jit(solution)/shard_map/ppermute | solution.py:203
  23.2 7.3 %copy-start = (bf16[192,1536]{1,0:T(8,128)(2,1)S(1)}, bf16[192,1536]{1,0:T(8,128)(2,1)}, u32[]{:S(2)}) copy-start(bf16[192,1536]{1,0:T(8,128)(2,1)} %dispatch.3.refs_0_) | copy-start | bytes 1769476
  23.5 4.1 %collective-permute-start.4 = (f16[64,768]{1,0:T(8,128)(2,1)S(1)}, f16[64,768]{1,0:T(8,128)(2,1)S(1)}, u32[]{:S(2)}, u32[]{:S(2)}) collective-permute-start(f16[64,768]{1,0:T(8,128)(2,1)S(1)} %get-tuple-element.79), channel_id=1, source_target_pairs={{0,8},{2,10},{8,16},{10,18},{16,24},{18,26},{24,28},{26,30},{28,20... | collective-permute-start | bytes 294920 | tf_op jit(solution)/shard_map/ppermute | solution.py:197
  25.1 3.8 %collective-permute-start.5 = (f16[64,768]{1,0:T(8,128)(2,1)S(1)}, f16[64,768]{1,0:T(8,128)(2,1)S(1)}, u32[]{:S(2)}, u32[]{:S(2)}) collective-permute-start(f16[64,768]{1,0:T(8,128)(2,1)S(1)} %get-tuple-element.78), channel_id=1, source_target_pairs={{0,4},{2,6},{8,0},{10,2},{16,8},{18,10},{24,16},{26,18},{28,24},{3... | collective-permute-start | bytes 294920 | tf_op jit(solution)/shard_map/ppermute | solution.py:197
  29.0 6.4 %collective-permute-start.6 = (f16[64,1536]{1,0:T(8,128)(2,1)S(1)}, f16[64,1536]{1,0:T(8,128)(2,1)S(1)}, u32[]{:S(2)}, u32[]{:S(2)}) collective-permute-start(f16[64,1536]{1,0:T(8,128)(2,1)S(1)} %pad_maximum_fusion.3), channel_id=1, source_target_pairs={{0,8},{2,10},{8,16},{10,18},{16,24},{18,26},{24,28},{26,30},{28,20... | collective-permute-start | bytes 589832 | tf_op jit(solution)/shard_map/ppermute | solution.py:197
  30.4 5.0 %collective-permute-start.7 = (f16[64,1536]{1,0:T(8,128)(2,1)S(1)}, f16[64,1536]{1,0:T(8,128)(2,1)S(1)}, u32[]{:S(2)}, u32[]{:S(2)}) collective-permute-start(f16[64,1536]{1,0:T(8,128)(2,1)S(1)} %pad_maximum_fusion.4), channel_id=1, source_target_pairs={{0,4},{2,6},{8,0},{10,2},{16,8},{18,10},{24,16},{26,18},{28,24},{3... | collective-permute-start | bytes 589832 | tf_op jit(solution)/shard_map/ppermute | solution.py:197
  30.6 8.9 %collective-permute-start.11 = (bf16[192,1536]{1,0:T(8,128)(2,1)S(1)}, bf16[192,1536]{1,0:T(8,128)(2,1)S(1)}, u32[]{:S(2)}, u32[]{:S(2)}) collective-permute-start(bf16[192,1536]{1,0:T(8,128)(2,1)S(1)} %copy-done), channel_id=1, source_target_pairs={{0,2},{2,0},{4,6},{6,4},{8,10},{10,8},{12,14},{14,12},{16,18},{18,... | collective-permute-start | bytes 1769480 | tf_op jit(solution)/shard_map/ppermute | solution.py:200
  35.5 4.2 %collective-permute-start.12 = (bf16[192,1536]{1,0:T(8,128)(2,1)S(1)}, bf16[192,1536]{1,0:T(8,128)(2,1)S(1)}, u32[]{:S(2)}, u32[]{:S(2)}) collective-permute-start(bf16[192,1536]{1,0:T(8,128)(2,1)S(1)} %collective-permute-done.8.refs_1_), channel_id=1, source_target_pairs={{0,2},{2,0},{4,6},{6,4},{8,10},{10,8},{12,14},{14,12},{16,18},{18,... | collective-permute-start | bytes 1769480 | tf_op jit(solution)/shard_map/ppermute | solution.py:200
  38.1 6.5 %collective-permute-start.9 = (f16[64,1536]{1,0:T(8,128)(2,1)S(1)}, f16[64,1536]{1,0:T(8,128)(2,1)S(1)}, u32[]{:S(2)}, u32[]{:S(2)}) collective-permute-start(f16[64,1536]{1,0:T(8,128)(2,1)S(1)} %get-tuple-element.69), channel_id=1, source_target_pairs={{0,8},{2,10},{8,16},{10,18},{16,24},{18,26},{24,28},{26,30},{28,20... | collective-permute-start | bytes 589832 | tf_op jit(solution)/shard_map/ppermute | solution.py:197
  39.4 6.1 %collective-permute-start.10 = (f16[64,1536]{1,0:T(8,128)(2,1)S(1)}, f16[64,1536]{1,0:T(8,128)(2,1)S(1)}, u32[]{:S(2)}, u32[]{:S(2)}) collective-permute-start(f16[64,1536]{1,0:T(8,128)(2,1)S(1)} %get-tuple-element.68), channel_id=1, source_target_pairs={{0,4},{2,6},{8,0},{10,2},{16,8},{18,10},{24,16},{26,18},{28,24},{3... | collective-permute-start | bytes 589832 | tf_op jit(solution)/shard_map/ppermute | solution.py:197
  41.3 14.4 %copy-start.4 = (f32[1,64,3072]{2,1,0:T(8,128)S(1)}, f32[1,64,3072]{2,1,0:T(8,128)}, u32[]{:S(2)}) copy-start(f32[1,64,3072]{2,1,0:T(8,128)} %param.15) | copy-start | bytes 2359300
  41.4 5.3 %collective-permute-start.15 = (f16[64,768]{1,0:T(8,128)(2,1)S(1)}, f16[64,768]{1,0:T(8,128)(2,1)S(1)}, u32[]{:S(2)}, u32[]{:S(2)}) collective-permute-start(f16[64,768]{1,0:T(8,128)(2,1)S(1)} %get-tuple-element.75), channel_id=1, source_target_pairs={{0,8},{2,10},{8,16},{10,18},{16,24},{18,26},{24,28},{26,30},{28,20... | collective-permute-start | bytes 294920 | tf_op jit(solution)/shard_map/ppermute | solution.py:197
  42.7 4.9 %collective-permute-start.16 = (f16[64,768]{1,0:T(8,128)(2,1)S(1)}, f16[64,768]{1,0:T(8,128)(2,1)S(1)}, u32[]{:S(2)}, u32[]{:S(2)}) collective-permute-start(f16[64,768]{1,0:T(8,128)(2,1)S(1)} %get-tuple-element.74), channel_id=1, source_target_pairs={{0,4},{2,6},{8,0},{10,2},{16,8},{18,10},{24,16},{26,18},{28,24},{3... | collective-permute-start | bytes 294920 | tf_op jit(solution)/shard_map/ppermute | solution.py:197
  47.7 5.3 %collective-permute-start.17 = (f16[64,1536]{1,0:T(8,128)(2,1)S(1)}, f16[64,1536]{1,0:T(8,128)(2,1)S(1)}, u32[]{:S(2)}, u32[]{:S(2)}) collective-permute-start(f16[64,1536]{1,0:T(8,128)(2,1)S(1)} %pad_maximum_fusion.5), channel_id=1, source_target_pairs={{0,8},{2,10},{8,16},{10,18},{16,24},{18,26},{24,28},{26,30},{28,20... | collective-permute-start | bytes 589832 | tf_op jit(solution)/shard_map/ppermute | solution.py:197
  49.1 5.0 %collective-permute-start.18 = (f16[64,1536]{1,0:T(8,128)(2,1)S(1)}, f16[64,1536]{1,0:T(8,128)(2,1)S(1)}, u32[]{:S(2)}, u32[]{:S(2)}) collective-permute-start(f16[64,1536]{1,0:T(8,128)(2,1)S(1)} %pad_maximum_fusion.6), channel_id=1, source_target_pairs={{0,4},{2,6},{8,0},{10,2},{16,8},{18,10},{24,16},{26,18},{28,24},{3... | collective-permute-start | bytes 589832 | tf_op jit(solution)/shard_map/ppermute | solution.py:197
  54.2 13.3 %copy-start.7 = (f32[1,64,3072]{2,1,0:T(8,128)S(1)}, f32[1,64,3072]{2,1,0:T(8,128)}, u32[]{:S(2)}) copy-start(f32[1,64,3072]{2,1,0:T(8,128)} %param.16) | copy-start | bytes 2359300
  54.2 13.3 %copy-start.8 = (f32[1,64,3072]{2,1,0:T(8,128)S(1)}, f32[1,64,3072]{2,1,0:T(8,128)}, u32[]{:S(2)}) copy-start(f32[1,64,3072]{2,1,0:T(8,128)} %param.17) | copy-start | bytes 2359300
  54.2 4.6 %collective-permute-start.19 = (f16[64,1536]{1,0:T(8,128)(2,1)S(1)}, f16[64,1536]{1,0:T(8,128)(2,1)S(1)}, u32[]{:S(2)}, u32[]{:S(2)}) collective-permute-start(f16[64,1536]{1,0:T(8,128)(2,1)S(1)} %get-tuple-element.63), channel_id=1, source_target_pairs={{0,8},{2,10},{8,16},{10,18},{16,24},{18,26},{24,28},{26,30},{28,20... | collective-permute-start | bytes 589832 | tf_op jit(solution)/shard_map/ppermute | solution.py:197
  54.7 4.5 %collective-permute-start.20 = (f16[64,1536]{1,0:T(8,128)(2,1)S(1)}, f16[64,1536]{1,0:T(8,128)(2,1)S(1)}, u32[]{:S(2)}, u32[]{:S(2)}) collective-permute-start(f16[64,1536]{1,0:T(8,128)(2,1)S(1)} %get-tuple-element.62), channel_id=1, source_target_pairs={{0,4},{2,6},{8,0},{10,2},{16,8},{18,10},{24,16},{26,18},{28,24},{3... | collective-permute-start | bytes 589832 | tf_op jit(solution)/shard_map/ppermute | solution.py:197
  55.9 6.6 %collective-permute-start.13 = (f16[64,1536]{1,0:T(8,128)(2,1)S(1)}, f16[64,1536]{1,0:T(8,128)(2,1)S(1)}, u32[]{:S(2)}, u32[]{:S(2)}) collective-permute-start(f16[64,1536]{1,0:T(8,128)(2,1)S(1)} %get-tuple-element.67), channel_id=1, source_target_pairs={{0,8},{2,10},{8,16},{10,18},{16,24},{18,26},{24,28},{26,30},{28,20... | collective-permute-start | bytes 589832 | tf_op jit(solution)/shard_map/ppermute | solution.py:197
  56.4 6.4 %collective-permute-start.14 = (f16[64,1536]{1,0:T(8,128)(2,1)S(1)}, f16[64,1536]{1,0:T(8,128)(2,1)S(1)}, u32[]{:S(2)}, u32[]{:S(2)}) collective-permute-start(f16[64,1536]{1,0:T(8,128)(2,1)S(1)} %get-tuple-element.66), channel_id=1, source_target_pairs={{0,4},{2,6},{8,0},{10,2},{16,8},{18,10},{24,16},{26,18},{28,24},{3... | collective-permute-start | bytes 589832 | tf_op jit(solution)/shard_map/ppermute | solution.py:197
  59.4 7.3 %collective-permute-start.21 = (f16[64,1536]{1,0:T(8,128)(2,1)S(1)}, f16[64,1536]{1,0:T(8,128)(2,1)S(1)}, u32[]{:S(2)}, u32[]{:S(2)}) collective-permute-start(f16[64,1536]{1,0:T(8,128)(2,1)S(1)} %get-tuple-element.61), channel_id=1, source_target_pairs={{0,8},{2,10},{8,16},{10,18},{16,24},{18,26},{24,28},{26,30},{28,20... | collective-permute-start | bytes 589832 | tf_op jit(solution)/shard_map/ppermute | solution.py:197
  60.4 7.0 %collective-permute-start.22 = (f16[64,1536]{1,0:T(8,128)(2,1)S(1)}, f16[64,1536]{1,0:T(8,128)(2,1)S(1)}, u32[]{:S(2)}, u32[]{:S(2)}) collective-permute-start(f16[64,1536]{1,0:T(8,128)(2,1)S(1)} %get-tuple-element.60), channel_id=1, source_target_pairs={{0,4},{2,6},{8,0},{10,2},{16,8},{18,10},{24,16},{26,18},{28,24},{3... | collective-permute-start | bytes 589832 | tf_op jit(solution)/shard_map/ppermute | solution.py:197
  68.1 9.9 %copy-start.5 = (f32[1,64,3072]{2,1,0:T(8,128)}, f32[1,64,3072]{2,1,0:T(8,128)S(1)}, u32[]{:S(2)}) copy-start(f32[1,64,3072]{2,1,0:T(8,128)S(1)} %get-tuple-element.58) | copy-start | bytes 2359300
  68.1 9.9 %copy-start.6 = (f32[1,64,3072]{2,1,0:T(8,128)}, f32[1,64,3072]{2,1,0:T(8,128)S(1)}, u32[]{:S(2)}) copy-start(f32[1,64,3072]{2,1,0:T(8,128)S(1)} %get-tuple-element.59) | copy-start | bytes 2359300
  69.7 8.3 %collective-permute-start.24 = (f16[64,3200]{1,0:T(8,128)(2,1)S(1)}, f16[64,3200]{1,0:T(8,128)(2,1)}, u32[]{:S(2)}, u32[]{:S(2)}) collective-permute-start(f16[64,3200]{1,0:T(8,128)(2,1)S(1)} %pad_maximum_fusion.2), channel_id=1, source_target_pairs={{0,8},{2,10},{8,16},{10,18},{16,24},{18,26},{24,28},{26,30},{28,20... | collective-permute-start | bytes 1228808 | tf_op jit(solution)/shard_map/ppermute | solution.py:197
  69.9 12.8 %collective-permute-start.25 = (f16[64,3200]{1,0:T(8,128)(2,1)S(1)}, f16[64,3200]{1,0:T(8,128)(2,1)S(1)}, u32[]{:S(2)}, u32[]{:S(2)}) collective-permute-start(f16[64,3200]{1,0:T(8,128)(2,1)S(1)} %pad_maximum_fusion.2), channel_id=1, source_target_pairs={{0,4},{2,6},{8,0},{10,2},{16,8},{18,10},{24,16},{26,18},{28,24},{3... | collective-permute-start | bytes 1228808 | tf_op jit(solution)/shard_map/ppermute | solution.py:197
  71.4 13.7 %collective-permute-start.23 = (f16[64,3200]{1,0:T(8,128)(2,1)S(1)}, f16[64,3200]{1,0:T(8,128)(2,1)S(1)}, u32[]{:S(2)}, u32[]{:S(2)}) collective-permute-start(f16[64,3200]{1,0:T(8,128)(2,1)S(1)} %pad_maximum_fusion.2), channel_id=1, source_target_pairs={{0,2},{2,0},{4,6},{6,4},{8,10},{10,8},{12,14},{14,12},{16,18},{18,... | collective-permute-start | bytes 1228808 | tf_op jit(solution)/shard_map/ppermute | solution.py:200
  78.1 18.3 %collective-permute-start.26 = (f16[64,3200]{1,0:T(8,128)(2,1)}, f16[64,3200]{1,0:T(8,128)(2,1)S(1)}, u32[]{:S(2)}, u32[]{:S(2)}) collective-permute-start(f16[64,3200]{1,0:T(8,128)(2,1)} %collective-permute-done.24), channel_id=1, source_target_pairs={{0,2},{2,0},{4,6},{6,4},{8,10},{10,8},{12,14},{14,12},{16,18},{18,... | collective-permute-start | bytes 1228808 | tf_op jit(solution)/shard_map/ppermute | solution.py:200
  82.5 11.3 %collective-permute-start.28 = (f16[64,3200]{1,0:T(8,128)(2,1)}, f16[64,3200]{1,0:T(8,128)(2,1)S(1)}, u32[]{:S(2)}, u32[]{:S(2)}) collective-permute-start(f16[64,3200]{1,0:T(8,128)(2,1)} %collective-permute-done.24), channel_id=1, source_target_pairs={{0,8},{2,10},{8,16},{10,18},{16,24},{18,26},{24,28},{26,30},{28,20... | collective-permute-start | bytes 1228808 | tf_op jit(solution)/shard_map/ppermute | solution.py:197
  82.8 12.1 %collective-permute-start.29 = (f16[64,3200]{1,0:T(8,128)(2,1)S(1)}, f16[64,3200]{1,0:T(8,128)(2,1)S(1)}, u32[]{:S(2)}, u32[]{:S(2)}) collective-permute-start(f16[64,3200]{1,0:T(8,128)(2,1)S(1)} %collective-permute-done.25), channel_id=1, source_target_pairs={{0,4},{2,6},{8,0},{10,2},{16,8},{18,10},{24,16},{26,18},{28,24},{3... | collective-permute-start | bytes 1228808 | tf_op jit(solution)/shard_map/ppermute | solution.py:197
  88.6 8.1 %collective-permute-start.27 = (f16[64,3200]{1,0:T(8,128)(2,1)S(1)}, f16[64,3200]{1,0:T(8,128)(2,1)S(1)}, u32[]{:S(2)}, u32[]{:S(2)}) collective-permute-start(f16[64,3200]{1,0:T(8,128)(2,1)S(1)} %collective-permute-done.25), channel_id=1, source_target_pairs={{0,2},{2,0},{4,6},{6,4},{8,10},{10,8},{12,14},{14,12},{16,18},{18,... | collective-permute-start | bytes 1228808 | tf_op jit(solution)/shard_map/ppermute | solution.py:200
  93.8 13.9 %collective-permute-start.30 = (f16[64,3200]{1,0:T(8,128)(2,1)S(1)}, f16[64,3200]{1,0:T(8,128)(2,1)S(1)}, u32[]{:S(2)}, u32[]{:S(2)}) collective-permute-start(f16[64,3200]{1,0:T(8,128)(2,1)S(1)} %collective-permute-done.28), channel_id=1, source_target_pairs={{0,2},{2,0},{4,6},{6,4},{8,10},{10,8},{12,14},{14,12},{16,18},{18,... | collective-permute-start | bytes 1228808 | tf_op jit(solution)/shard_map/ppermute | solution.py:200
  94.6 11.1 %collective-permute-start.32 = (f16[64,3200]{1,0:T(8,128)(2,1)S(1)}, f16[64,3200]{1,0:T(8,128)(2,1)S(1)}, u32[]{:S(2)}, u32[]{:S(2)}) collective-permute-start(f16[64,3200]{1,0:T(8,128)(2,1)S(1)} %collective-permute-done.28), channel_id=1, source_target_pairs={{0,8},{2,10},{8,16},{10,18},{16,24},{18,26},{24,28},{26,30},{28,20... | collective-permute-start | bytes 1228808 | tf_op jit(solution)/shard_map/ppermute | solution.py:197
  94.9 11.2 %collective-permute-start.33 = (f16[64,3200]{1,0:T(8,128)(2,1)S(1)}, f16[64,3200]{1,0:T(8,128)(2,1)S(1)}, u32[]{:S(2)}, u32[]{:S(2)}) collective-permute-start(f16[64,3200]{1,0:T(8,128)(2,1)S(1)} %collective-permute-done.29), channel_id=1, source_target_pairs={{0,4},{2,6},{8,0},{10,2},{16,8},{18,10},{24,16},{26,18},{28,24},{3... | collective-permute-start | bytes 1228808 | tf_op jit(solution)/shard_map/ppermute | solution.py:197
  99.6 8.5 %collective-permute-start.31 = (f16[64,3200]{1,0:T(8,128)(2,1)S(1)}, f16[64,3200]{1,0:T(8,128)(2,1)S(1)}, u32[]{:S(2)}, u32[]{:S(2)}) collective-permute-start(f16[64,3200]{1,0:T(8,128)(2,1)S(1)} %collective-permute-done.29), channel_id=1, source_target_pairs={{0,2},{2,0},{4,6},{6,4},{8,10},{10,8},{12,14},{14,12},{16,18},{18,... | collective-permute-start | bytes 1228808 | tf_op jit(solution)/shard_map/ppermute | solution.py:200
  105.7 6.7 %collective-permute-start.37 = (f16[64,1536]{1,0:T(8,128)(2,1)S(1)}, f16[64,1536]{1,0:T(8,128)(2,1)S(1)}, u32[]{:S(2)}, u32[]{:S(2)}) collective-permute-start(f16[64,1536]{1,0:T(8,128)(2,1)S(1)} %slice.302), channel_id=1, source_target_pairs={{0,8},{2,10},{8,16},{10,18},{16,24},{18,26},{24,28},{26,30},{28,20... | collective-permute-start | bytes 589832 | tf_op jit(solution)/shard_map/ppermute | solution.py:197
  106.1 6.9 %collective-permute-start.36 = (f16[64,1664]{1,0:T(8,128)(2,1)S(1)}, f16[64,1664]{1,0:T(8,128)(2,1)S(1)}, u32[]{:S(2)}, u32[]{:S(2)}) collective-permute-start(f16[64,1664]{1,0:T(8,128)(2,1)S(1)} %slice.299), channel_id=1, source_target_pairs={{0,4},{2,6},{8,0},{10,2},{16,8},{18,10},{24,16},{26,18},{28,24},{3... | collective-permute-start | bytes 638984 | tf_op jit(solution)/shard_map/ppermute | solution.py:197
  110.9 3.4 %collective-permute-start.34 = (f16[64,3200]{1,0:T(8,128)(2,1)S(1)}, f16[64,3200]{1,0:T(8,128)(2,1)S(1)}, u32[]{:S(2)}, u32[]{:S(2)}) collective-permute-start(f16[64,3200]{1,0:T(8,128)(2,1)S(1)} %collective-permute-done.32), channel_id=1, source_target_pairs={{0,2},{2,0},{4,6},{6,4},{8,10},{10,8},{12,14},{14,12},{16,18},{18,... | collective-permute-start | bytes 1228808 | tf_op jit(solution)/shard_map/ppermute | solution.py:200
  112.3 2.3 %collective-permute-start.35 = (f16[64,3200]{1,0:T(8,128)(2,1)S(1)}, f16[64,3200]{1,0:T(8,128)(2,1)S(1)}, u32[]{:S(2)}, u32[]{:S(2)}) collective-permute-start(f16[64,3200]{1,0:T(8,128)(2,1)S(1)} %collective-permute-done.33), channel_id=1, source_target_pairs={{0,2},{2,0},{4,6},{6,4},{8,10},{10,8},{12,14},{14,12},{16,18},{18,... | collective-permute-start | bytes 1228808 | tf_op jit(solution)/shard_map/ppermute | solution.py:200
  112.3 4.7 %collective-permute-start.39 = (f16[64,1536]{1,0:T(8,128)(2,1)S(1)}, f16[64,1536]{1,0:T(8,128)(2,1)S(1)}, u32[]{:S(2)}, u32[]{:S(2)}) collective-permute-start(f16[64,1536]{1,0:T(8,128)(2,1)S(1)} %collective-permute-done.37), channel_id=1, source_target_pairs={{0,2},{2,0},{4,6},{6,4},{8,10},{10,8},{12,14},{14,12},{16,18},{18,... | collective-permute-start | bytes 589832 | tf_op jit(solution)/shard_map/ppermute | solution.py:200
  113.3 3.6 %collective-permute-start.38 = (f16[64,1664]{1,0:T(8,128)(2,1)S(1)}, f16[64,1664]{1,0:T(8,128)(2,1)S(1)}, u32[]{:S(2)}, u32[]{:S(2)}) collective-permute-start(f16[64,1664]{1,0:T(8,128)(2,1)S(1)} %collective-permute-done.36), channel_id=1, source_target_pairs={{0,2},{2,0},{4,6},{6,4},{8,10},{10,8},{12,14},{14,12},{16,18},{18,... | collective-permute-start | bytes 638984 | tf_op jit(solution)/shard_map/ppermute | solution.py:200

commit v5 on v4

--- a/solution.py
+++ b/solution.py
@@ -15,8 +15,25 @@
 SPLIT = 1
 HIDDEN_FLOPS = 8 << 30
 OFFSET = 3
+FINE = 2
 DISPATCH_FLOPS = 4 << 30
 DISPATCH_VMEM = 56
+
+
+def encode(value):
+    largest = jnp.max(jnp.abs(value), axis=1, keepdims=True)
+    power = jnp.floor(jnp.log2(jnp.maximum(largest, 1e-30)))
+    root = jnp.sqrt(jnp.abs(value) * jnp.exp2(28.0 - power))
+    code = jnp.where(value < 0.0, -root, root)
+    tail = jnp.broadcast_to(power, (value.shape[0], 128))
+    return jnp.round(jnp.concatenate([code, tail], axis=1)).astype(jnp.int16)
+
+
+def decode(code):
+    if code.dtype == F16:
+        return code.astype(F32)
+    root = code[:, :-128].astype(F32)
+    return root * jnp.abs(root) * jnp.exp2(code[:, -1:].astype(F32) - 28.0)
 
 
 def after(value, other):
@@ -259,15 +276,16 @@
                 up, down = after(moving[i], (token, far[i + 1]) if step == 2 and i + 1 < count else token)
                 one, two = total[d], total[length - d]
                 if step == 1:
-                    one = jnp.concatenate([one[:, :cut] + up.astype(F32), one[:, cut:]], axis=1)
-                    two = jnp.concatenate([two[:, :cut], two[:, cut:] + down.astype(F32)], axis=1)
+                    one = jnp.concatenate([one[:, :cut] + decode(up), one[:, cut:]], axis=1)
+                    two = jnp.concatenate([two[:, :cut], two[:, cut:] + decode(down)], axis=1)
                 else:
-                    one, two = one + up.astype(F32), two + down.astype(F32)
-            one, two = one.astype(F16), two.astype(F16)
+                    one, two = one + decode(up), two + decode(down)
+            pack = encode if step >= middle - FINE else (lambda x: x.astype(F16))
+            one, two = pack(one), pack(two)
             token = (one, two)
             moving[i] = (step_ring(one, 1), step_ring(two, -1))
         grads = [
-            total[0] + up.astype(F32) + down.astype(F32)
+            total[0] + decode(up) + decode(down)
             for total, (up, down) in ((totals[i], after(moving[i], token)) for i in range(count))
         ]
         grad = (jnp.concatenate(grads, axis=1) * (1.0 / shrink)).reshape(master.shape)

time: 119 us -> 123 us (1.034)
  other arithmetic: 11.1 us -> 16.1 us
  waiting for transfers between devices: 41.3 us -> 38.8 us
    ppermute x24, waiting for transfers between devices: 31.1 us -> 28.5 us  [step_ring(): lax.ppermute(value, 'dp', [(place(*x, c), place(*y, c)) for x, y in pairs...]
    select_n x0 -> x4, other arithmetic: none -> 1.99 us  [encode(): code = jnp.where(value < 0.0, -root, root)]
    exp2 x0 -> x16, other arithmetic: none -> 1.6 us  [the longest x8 1.5 us: decode(): return root * jnp.abs(root) * jnp.exp2(code[:, -1:].astype(F32) - 28.0)]
  transfers between devices with their start and end apart: 40 -> 40, of which waited for: 20 -> 18; matrix products, arithmetic and copies ran while one was open for 7% -> 11% of each run, Pallas kernels for 14% -> 14%
where the time goes in v5:
time: 123 us
  starting transfers between devices  44 us (36%)
  waiting for transfers between devices  38.8 us (32%)
  Pallas kernels  21.1 us (17%)
  other arithmetic  16.1 us (13%)
  between operations  1.56 us (1%)
    ppermute x24, waiting for transfers between devices, step_ring(): lax.ppermute(value, 'dp', [(place(*x, c), place(*y, c)) for x, y in pairs...  28.5 us
    ppermute x14, starting transfers between devices, swap_core(): lax.ppermute(value, 'dp', [(place(a, b, c), place(a, b, c + 1)) for a, b,...  21.9 us
    ppermute x24, starting transfers between devices, step_ring(): lax.ppermute(value, 'dp', [(place(*x, c), place(*y, c)) for x, y in pairs...  18.5 us
    pallas_call x6, Pallas kernels, put(): pl.pallas_call(functools.partial(put_kernel, tuple(marks), aliased), out_...  11.3 us
    ppermute x2, waiting for transfers between devices, shift_expert(): lax.ppermute(value, 'expert', [(e, (e + k) % experts) for e in range(expe...  9.92 us
    pallas_call x2, Pallas kernels, dispatch(): pl.pallas_call(functools.partial(dispatch_kernel, first), out_shape=jax.S...  5.82 us
    mul x16, other arithmetic, local(): values.append(value.astype(F32) * scales[spot])  4.27 us
    ppermute x2, starting transfers between devices, shift_expert(): lax.ppermute(value, 'expert', [(e, (e + k) % experts) for e in range(expe...  3.6 us
  transfers between devices with their start and end apart: 40, of which 18 were waited for; matrix products, arithmetic and copies ran while one was open for 11% of the time, Pallas kernels for 14%

profile of v5, /device:TPU:1, one launch (start us, length us, event | category | flops | bytes accessed | tf_op | source)
XLA Modules:
  0.0 122.6 jit_solution(10294534547293426244)
XLA Ops:
  0.7 2.9 %dispatch.2.refs_0_ = bf16[192,1536]{1,0:T(8,128)(2,1)} custom-call(s32[2,512]{1,0:T(2,128)} %bitcast.40, f32[2,512]{1,0:T(2,128)} %bitcast.42, bf16[512,3072]{1,0:T(8,128)(2,1)} %grad_in.3), custom_call_target="tpu_custom_call" | custom-call | flops 4294967296 | tf_op jit(solution)/shard_map/dispatch/pallas_call | solution.py:80
  3.6 2.1 %collective-permute-start.1 = (bf16[192,1536]{1,0:T(8,128)(2,1)}, bf16[192,1536]{1,0:T(8,128)(2,1)S(1)}, u32[]{:S(2)}, u32[]{:S(2)}) collective-permute-start(bf16[192,1536]{1,0:T(8,128)(2,1)} %dispatch.2.refs_0_), channel_id=1, source_target_pairs={{0,1},{1,0},{2,3},{3,2},{4,5},{5,4},{6,7},{7,6},{8,9},{9,8},{10,11... | collective-permute-start | bytes 1769480 | tf_op jit(solution)/shard_map/ppermute | solution.py:220
  5.7 1.0 collective-permute-start.2
  6.7 0.7 multiply_bitcast_fusion
  7.5 1.3 %hidden_pieces.1 = (bf16[8,64,384]{2,1,0:T(8,128)(2,1)S(1)}, bf16[8,64,384]{2,1,0:T(8,128)(2,1)S(1)}) custom-call(s32[10]{0:T(128)S(1)} %pad_add_fusion.at, bf16[384,1024]{1,0:T(8,128)(2,1)S(1)} %bitcast.34, bf16[384,1024]{1,0:T(8,128)(2,1)S(1)} %bitcast.35), custom_call_target="tpu_custom_call" | custom-call | flops 8589934592 | tf_op jit(solution)/shard_map/hidden_pieces/pallas_call | solution.py:153
  8.8 2.9 %dispatch.3.refs_0_ = bf16[192,1536]{1,0:T(8,128)(2,1)} custom-call(s32[2,512]{1,0:T(2,128)} %bitcast.41, f32[2,512]{1,0:T(2,128)} %bitcast.43, bf16[512,3072]{1,0:T(8,128)(2,1)} %grad_in.3), custom_call_target="tpu_custom_call" | custom-call | flops 4294967296 | tf_op jit(solution)/shard_map/dispatch/pallas_call | solution.py:80
  11.8 7.2 %collective-permute-done.1.refs_1_ = bf16[192,1536]{1,0:T(8,128)(2,1)S(1)} collective-permute-done((bf16[192,1536]{1,0:T(8,128)(2,1)}, bf16[192,1536]{1,0:T(8,128)(2,1)S(1)}, u32[]{:S(2)}, u32[]{:S(2)}) %collective-permute-start.1) | collective-permute-done | bytes 589856 | tf_op jit(solution)/shard_map/ppermute | solution.py:220
  19.0 1.2 %collective-permute-start.3 = (bf16[192,1536]{1,0:T(8,128)(2,1)S(1)}, bf16[192,1536]{1,0:T(8,128)(2,1)S(1)}, u32[]{:S(2)}, u32[]{:S(2)}) collective-permute-start(bf16[192,1536]{1,0:T(8,128)(2,1)S(1)} %collective-permute-done.1.refs_1_), channel_id=1, source_target_pairs={{0,2},{2,0},{4,6},{6,4},{8,10},{10,8},{12,14},{14,12},{16,18},{18,... | collective-permute-start | bytes 1769480 | tf_op jit(solution)/shard_map/ppermute | solution.py:217
  20.2 1.5 %collective-permute-start.8 = (bf16[192,1536]{1,0:T(8,128)(2,1)}, bf16[192,1536]{1,0:T(8,128)(2,1)S(1)}, u32[]{:S(2)}, u32[]{:S(2)}) collective-permute-start(bf16[192,1536]{1,0:T(8,128)(2,1)} %dispatch.3.refs_0_), channel_id=1, source_target_pairs={{0,1},{1,0},{2,3},{3,2},{4,5},{5,4},{6,7},{7,6},{8,9},{9,8},{10,11... | collective-permute-start | bytes 1769480 | tf_op jit(solution)/shard_map/ppermute | solution.py:220
  21.9 1.4 %product.2 = f32[512,1536]{1,0:T(8,128)S(1)} custom-call(bf16[512,768]{1,0:T(8,128)(2,1)S(1)} %bitcast.32, bf16[192,1536]{1,0:T(8,128)(2,1)S(1)} %copy-done.1, bf16[192,1536]{1,0:T(8,128)(2,1)S(1)} %collective-permute-done.1.refs_1_, bf16[192,1536]{1,0:T(8,128)(2,1)S(1)} %collective-permute-done.2.refs_2_, bf16[192,1536]{1,0:T(8,128)(2,1)S(1)} %collective-permute-done.3.refs_3_), custom_call_target="tpu_custom_call" | custom-call | tf_op jit(solution)/shard_map/product/pallas_call | solution.py:177
  23.5 1.6 %collective-permute-start.4 = (f16[64,768]{1,0:T(8,128)(2,1)S(1)}, f16[64,768]{1,0:T(8,128)(2,1)S(1)}, u32[]{:S(2)}, u32[]{:S(2)}) collective-permute-start(f16[64,768]{1,0:T(8,128)(2,1)S(1)} %get-tuple-element.103), channel_id=1, source_target_pairs={{0,8},{2,10},{8,16},{10,18},{16,24},{18,26},{24,28},{26,30},{28,20... | collective-permute-start | bytes 294920 | tf_op jit(solution)/shard_map/ppermute | solution.py:214
  25.1 2.4 %collective-permute-done.4 = f16[64,768]{1,0:T(8,128)(2,1)S(1)} collective-permute-done((f16[64,768]{1,0:T(8,128)(2,1)S(1)}, f16[64,768]{1,0:T(8,128)(2,1)S(1)}, u32[]{:S(2)}, u32[]{:S(2)}) %collective-permute-start.4) | collective-permute-done | bytes 98336 | tf_op jit(solution)/shard_map/ppermute | solution.py:214
  27.6 1.3 %collective-permute-done.5 = f16[64,768]{1,0:T(8,128)(2,1)S(1)} collective-permute-done((f16[64,768]{1,0:T(8,128)(2,1)S(1)}, f16[64,768]{1,0:T(8,128)(2,1)S(1)}, u32[]{:S(2)}, u32[]{:S(2)}) %collective-permute-start.5) | collective-permute-done | bytes 98336 | tf_op jit(solution)/shard_map/ppermute | solution.py:214
  29.0 1.3 %collective-permute-start.6 = (f16[64,1536]{1,0:T(8,128)(2,1)S(1)}, f16[64,1536]{1,0:T(8,128)(2,1)S(1)}, u32[]{:S(2)}, u32[]{:S(2)}) collective-permute-start(f16[64,1536]{1,0:T(8,128)(2,1)S(1)} %pad_maximum_fusion.3), channel_id=1, source_target_pairs={{0,8},{2,10},{8,16},{10,18},{16,24},{18,26},{24,28},{26,30},{28,20... | collective-permute-start | bytes 589832 | tf_op jit(solution)/shard_map/ppermute | solution.py:214
  30.6 2.1 %collective-permute-start.11 = (bf16[192,1536]{1,0:T(8,128)(2,1)S(1)}, bf16[192,1536]{1,0:T(8,128)(2,1)S(1)}, u32[]{:S(2)}, u32[]{:S(2)}) collective-permute-start(bf16[192,1536]{1,0:T(8,128)(2,1)S(1)} %copy-done), channel_id=1, source_target_pairs={{0,2},{2,0},{4,6},{6,4},{8,10},{10,8},{12,14},{14,12},{16,18},{18,... | collective-permute-start | bytes 1769480 | tf_op jit(solution)/shard_map/ppermute | solution.py:217
  32.7 2.7 %collective-permute-done.8.refs_1_ = bf16[192,1536]{1,0:T(8,128)(2,1)S(1)} collective-permute-done((bf16[192,1536]{1,0:T(8,128)(2,1)}, bf16[192,1536]{1,0:T(8,128)(2,1)S(1)}, u32[]{:S(2)}, u32[]{:S(2)}) %collective-permute-start.8) | collective-permute-done | bytes 589856 | tf_op jit(solution)/shard_map/ppermute | solution.py:220
  35.6 0.4 negate_select_fusion.6
  36.3 2.5 %collective-permute-start.12 = (bf16[192,1536]{1,0:T(8,128)(2,1)S(1)}, bf16[192,1536]{1,0:T(8,128)(2,1)S(1)}, u32[]{:S(2)}, u32[]{:S(2)}) collective-permute-start(bf16[192,1536]{1,0:T(8,128)(2,1)S(1)} %collective-permute-done.8.refs_1_), channel_id=1, source_target_pairs={{0,2},{2,0},{4,6},{6,4},{8,10},{10,8},{12,14},{14,12},{16,18},{18,... | collective-permute-start | bytes 1769480 | tf_op jit(solution)/shard_map/ppermute | solution.py:217
  38.9 1.3 %collective-permute-start.9 = (s16[64,1664]{1,0:T(8,128)(2,1)S(1)}, s16[64,1664]{1,0:T(8,128)(2,1)S(1)}, u32[]{:S(2)}, u32[]{:S(2)}) collective-permute-start(s16[64,1664]{1,0:T(8,128)(2,1)S(1)} %fusion.2), channel_id=1, source_target_pairs={{0,8},{2,10},{8,16},{10,18},{16,24},{18,26},{24,28},{26,30},{28,20... | collective-permute-start | bytes 638984 | tf_op jit(solution)/shard_map/ppermute | solution.py:214
  40.5 1.4 %product.3 = f32[512,1536]{1,0:T(8,128)S(1)} custom-call(bf16[512,768]{1,0:T(8,128)(2,1)S(1)} %bitcast.33, bf16[192,1536]{1,0:T(8,128)(2,1)S(1)} %copy-done, bf16[192,1536]{1,0:T(8,128)(2,1)S(1)} %collective-permute-done.8.refs_1_, bf16[192,1536]{1,0:T(8,128)(2,1)S(1)} %collective-permute-done.11.refs_2_, bf16[192,1536]{1,0:T(8,128)(2,1)S(1)} %collective-permute-done.12.refs_3_), custom_call_target="tpu_custom_call" | custom-call | tf_op jit(solution)/shard_map/product/pallas_call | solution.py:177
  42.2 1.3 %collective-permute-start.15 = (f16[64,768]{1,0:T(8,128)(2,1)S(1)}, f16[64,768]{1,0:T(8,128)(2,1)S(1)}, u32[]{:S(2)}, u32[]{:S(2)}) collective-permute-start(f16[64,768]{1,0:T(8,128)(2,1)S(1)} %get-tuple-element.99), channel_id=1, source_target_pairs={{0,8},{2,10},{8,16},{10,18},{16,24},{18,26},{24,28},{26,30},{28,20... | collective-permute-start | bytes 294920 | tf_op jit(solution)/shard_map/ppermute | solution.py:214
  43.7 2.0 %collective-permute-done.9 = s16[64,1664]{1,0:T(8,128)(2,1)S(1)} collective-permute-done((s16[64,1664]{1,0:T(8,128)(2,1)S(1)}, s16[64,1664]{1,0:T(8,128)(2,1)S(1)}, u32[]{:S(2)}, u32[]{:S(2)}) %collective-permute-start.9) | collective-permute-done | bytes 213024 | tf_op jit(solution)/shard_map/ppermute | solution.py:214
  45.7 1.0 collective-permute-done.10
  47.4 0.6 negate_select_fusion.4
  48.3 0.5 collective-permute-done.16
  48.9 1.3 %collective-permute-start.17 = (f16[64,1536]{1,0:T(8,128)(2,1)S(1)}, f16[64,1536]{1,0:T(8,128)(2,1)S(1)}, u32[]{:S(2)}, u32[]{:S(2)}) collective-permute-start(f16[64,1536]{1,0:T(8,128)(2,1)S(1)} %pad_maximum_fusion.5), channel_id=1, source_target_pairs={{0,8},{2,10},{8,16},{10,18},{16,24},{18,26},{24,28},{26,30},{28,20... | collective-permute-start | bytes 589832 | tf_op jit(solution)/shard_map/ppermute | solution.py:214
  50.5 3.3 %collective-permute-done.17 = f16[64,1536]{1,0:T(8,128)(2,1)S(1)} collective-permute-done((f16[64,1536]{1,0:T(8,128)(2,1)S(1)}, f16[64,1536]{1,0:T(8,128)(2,1)S(1)}, u32[]{:S(2)}, u32[]{:S(2)}) %collective-permute-start.17) | collective-permute-done | bytes 196640 | tf_op jit(solution)/shard_map/ppermute | solution.py:214
  53.8 1.2 %collective-permute-done.18 = f16[64,1536]{1,0:T(8,128)(2,1)S(1)} collective-permute-done((f16[64,1536]{1,0:T(8,128)(2,1)S(1)}, f16[64,1536]{1,0:T(8,128)(2,1)S(1)}, u32[]{:S(2)}, u32[]{:S(2)}) %collective-permute-start.18) | collective-permute-done | bytes 196640 | tf_op jit(solution)/shard_map/ppermute | solution.py:214
  55.3 0.4 negate_select_fusion.2
  55.9 0.4 collective-permute-start.19
  56.4 1.2 collective-permute-start.20
  58.1 1.1 collective-permute-start.14
  59.3 1.4 %collective-permute-done.19 = s16[64,1664]{1,0:T(8,128)(2,1)S(1)} collective-permute-done((s16[64,1664]{1,0:T(8,128)(2,1)S(1)}, s16[64,1664]{1,0:T(8,128)(2,1)S(1)}, u32[]{:S(2)}, u32[]{:S(2)}) %collective-permute-start.19) | collective-permute-done | bytes 213024 | tf_op jit(solution)/shard_map/ppermute | solution.py:214
  60.6 0.5 collective-permute-done.20
  62.0 0.6 negate_select_fusion
  62.7 1.1 collective-permute-start.21
  63.9 0.6 collective-permute-start.22
  65.6 4.4 %collective-permute-done.21 = s16[64,1664]{1,0:T(8,128)(2,1)S(1)} collective-permute-done((s16[64,1664]{1,0:T(8,128)(2,1)S(1)}, s16[64,1664]{1,0:T(8,128)(2,1)S(1)}, u32[]{:S(2)}, u32[]{:S(2)}) %collective-permute-start.21) | collective-permute-done | bytes 213024 | tf_op jit(solution)/shard_map/ppermute | solution.py:214
  70.9 0.6 multiply_reduce_fusion
  71.6 1.4 %convert_multiply_fusion.13 = (f32[64,3072]{1,0:T(8,128)S(1)}, f16[64,3072]{1,0:T(8,128)(2,1)S(1)}, f32[1,64,3072]{2,1,0:T(8,128)}) fusion(f32[64]{0:T(128)S(1)} %get-tuple-element.109, f32[64]{0:T(128)S(1)} %get-tuple-element.108, f32[1,64,3072]{2,1,0:T(8,128)S(1)} %copy-done.4, f32[1,64,3072]{2,1,0:T(8,128)S(1)} %get-tuple-element.67, ...), kind=kLoop, calls=%fused_computation.19 | loop fusion | flops 1966080 | bytes 4326144 | tf_op jit(solution)/shard_map/mul | solution.py:326
  73.2 1.0 collective-permute-start.24
  74.1 0.6 collective-permute-start.25
  74.8 5.5 %collective-permute-start.23 = (f16[64,3200]{1,0:T(8,128)(2,1)S(1)}, f16[64,3200]{1,0:T(8,128)(2,1)S(1)}, u32[]{:S(2)}, u32[]{:S(2)}) collective-permute-start(f16[64,3200]{1,0:T(8,128)(2,1)S(1)} %pad_maximum_fusion.2), channel_id=1, source_target_pairs={{0,2},{2,0},{4,6},{6,4},{8,10},{10,8},{12,14},{14,12},{16,18},{18,... | collective-permute-start | bytes 1228808 | tf_op jit(solution)/shard_map/ppermute | solution.py:217
  80.4 1.4 %put.6.refs_0_ = f32[1024,3072]{1,0:T(8,128)} custom-call(s32[16]{0:T(128)S(1)} %mul.524.starts, f32[64,3072]{1,0:T(8,128)S(1)} %get-tuple-element.62.refs_0_), custom_call_target="tpu_custom_call" | custom-call | flops 4294967296 | tf_op jit(solution)/shard_map/put/pallas_call | solution.py:118
  81.8 4.4 %collective-permute-start.26 = (f16[64,3200]{1,0:T(8,128)(2,1)}, f16[64,3200]{1,0:T(8,128)(2,1)S(1)}, u32[]{:S(2)}, u32[]{:S(2)}) collective-permute-start(f16[64,3200]{1,0:T(8,128)(2,1)} %collective-permute-done.24), channel_id=1, source_target_pairs={{0,2},{2,0},{4,6},{6,4},{8,10},{10,8},{12,14},{14,12},{16,18},{18,... | collective-permute-start | bytes 1228808 | tf_op jit(solution)/shard_map/ppermute | solution.py:217
  86.6 1.1 collective-permute-start.29
  87.7 0.9 exponential_reduce_fusion.13
  89.2 1.1 convert_multiply_fusion.11.refs_2_
  90.4 2.0 %put.7.refs_0_ = f32[1024,3072]{1,0:T(8,128)} custom-call(s32[16]{0:T(128)S(1)} %mul.524.starts, f32[1024,3072]{1,0:T(8,128)} %put.6.refs_0_, f32[64,3072]{1,0:T(8,128)S(1)} %convert_multiply_fusion.12.refs_1_, f32[64,3072]{1,0:T(8,128)S(1)} %convert_multiply_fusion.11.refs_2_, ...), custom_call_target="tpu_custom_call", output_to_operand_aliasing={{}: (1, {})} | custom-call | flops 4294967296 | tf_op jit(solution)/shard_map/put/pallas_call | solution.py:118
  92.4 0.6 collective-permute-start.27
  93.0 4.5 %collective-permute-done.28 = f16[64,3200]{1,0:T(8,128)(2,1)S(1)} collective-permute-done((f16[64,3200]{1,0:T(8,128)(2,1)}, f16[64,3200]{1,0:T(8,128)(2,1)S(1)}, u32[]{:S(2)}, u32[]{:S(2)}) %collective-permute-start.28) | collective-permute-done | bytes 409632 | tf_op jit(solution)/shard_map/ppermute | solution.py:214
  97.6 0.8 collective-permute-start.30
  98.7 1.1 collective-permute-start.33
  101.1 2.2 %put.8.refs_0_ = f32[1024,3072]{1,0:T(8,128)} custom-call(s32[16]{0:T(128)S(1)} %mul.524.starts, f32[1024,3072]{1,0:T(8,128)} %put.7.refs_0_, f32[64,3072]{1,0:T(8,128)S(1)} %convert_multiply_fusion.9.refs_1_, f32[64,3072]{1,0:T(8,128)S(1)} %convert_multiply_fusion.8.refs_2_, ...), custom_call_target="tpu_custom_call", output_to_operand_aliasing={{}: (1, {})} | custom-call | flops 4294967296 | tf_op jit(solution)/shard_map/put/pallas_call | solution.py:118
  103.4 0.6 collective-permute-start.31
  104.0 5.5 %collective-permute-done.32 = f16[64,3200]{1,0:T(8,128)(2,1)S(1)} collective-permute-done((f16[64,3200]{1,0:T(8,128)(2,1)S(1)}, f16[64,3200]{1,0:T(8,128)(2,1)S(1)}, u32[]{:S(2)}, u32[]{:S(2)}) %collective-permute-start.32) | collective-permute-done | bytes 409632 | tf_op jit(solution)/shard_map/ppermute | solution.py:214
  109.5 0.4 collective-permute-start.37
  109.9 1.2 collective-permute-start.36
  112.4 2.2 %put.9.refs_0_ = f32[1024,3072]{1,0:T(8,128)} custom-call(s32[16]{0:T(128)S(1)} %mul.524.starts, f32[1024,3072]{1,0:T(8,128)} %put.8.refs_0_, f32[64,3072]{1,0:T(8,128)S(1)} %convert_multiply_fusion.5.refs_1_, f32[64,3072]{1,0:T(8,128)S(1)} %convert_multiply_fusion.4.refs_2_, ...), custom_call_target="tpu_custom_call", output_to_operand_aliasing={{}: (1, {})} | custom-call | flops 4294967296 | tf_op jit(solution)/shard_map/put/pallas_call | solution.py:118
  114.6 1.4 %collective-permute-start.34 = (f16[64,3200]{1,0:T(8,128)(2,1)S(1)}, f16[64,3200]{1,0:T(8,128)(2,1)S(1)}, u32[]{:S(2)}, u32[]{:S(2)}) collective-permute-start(f16[64,3200]{1,0:T(8,128)(2,1)S(1)} %collective-permute-done.32), channel_id=1, source_target_pairs={{0,2},{2,0},{4,6},{6,4},{8,10},{10,8},{12,14},{14,12},{16,18},{18,... | collective-permute-start | bytes 1228808 | tf_op jit(solution)/shard_map/ppermute | solution.py:217
  116.1 0.7 collective-permute-start.39
  117.0 0.8 collective-permute-start.38
  118.7 2.0 %put.10.refs_0_ = f32[1024,3072]{1,0:T(8,128)} custom-call(s32[16]{0:T(128)S(1)} %mul.524.starts, f32[1024,3072]{1,0:T(8,128)} %put.9.refs_0_, f32[64,3072]{1,0:T(8,128)S(1)} %convert_multiply_fusion.1.refs_1_, f32[64,3072]{1,0:T(8,128)S(1)} %convert_multiply_fusion.refs_2_, ...), custom_call_target="tpu_custom_call", output_to_operand_aliasing={{}: (1, {})} | custom-call | flops 4294967296 | tf_op jit(solution)/shard_map/put/pallas_call | solution.py:118
  121.0 1.4 %put.11 = f32[1024,3072]{1,0:T(8,128)} custom-call(s32[16]{0:T(128)S(1)} %mul.524.starts, f32[1024,3072]{1,0:T(8,128)} %put.10.refs_0_, f32[64,1536]{1,0:T(8,128)S(1)} %get-tuple-element.105.refs_1_, f32[64,1536]{1,0:T(8,128)S(1)} %get-tuple-element.104.refs_2_), custom_call_target="tpu_custom_call", output_to_operand_aliasing={{}: (1, {})} | custom-call | flops 4294967296 | tf_op jit(solution)/shard_map/put/pallas_call | solution.py:118
  (146 shorter events, 13.3 us)
Async XLA Ops:
  0.6 6.8 %copy-start.2 = (bf16[384,1,1024]{2,0,1:T(8,128)(2,1)S(1)}, bf16[384,1,1024]{2,0,1:T(8,128)(2,1)}, u32[]{:S(2)}) copy-start(bf16[384,1,1024]{2,0,1:T(8,128)(2,1)} %param.13) | copy-start | bytes 2359300
  0.6 6.8 %copy-start.3 = (bf16[384,1,1024]{2,0,1:T(8,128)(2,1)S(1)}, bf16[384,1,1024]{2,0,1:T(8,128)(2,1)}, u32[]{:S(2)}) copy-start(bf16[384,1,1024]{2,0,1:T(8,128)(2,1)} %param.14) | copy-start | bytes 2359300
  3.6 15.4 %collective-permute-start.1 = (bf16[192,1536]{1,0:T(8,128)(2,1)}, bf16[192,1536]{1,0:T(8,128)(2,1)S(1)}, u32[]{:S(2)}, u32[]{:S(2)}) collective-permute-start(bf16[192,1536]{1,0:T(8,128)(2,1)} %dispatch.2.refs_0_), channel_id=1, source_target_pairs={{0,1},{1,0},{2,3},{3,2},{4,5},{5,4},{6,7},{7,6},{8,9},{9,8},{10,11... | collective-permute-start | bytes 1769480 | tf_op jit(solution)/shard_map/ppermute | solution.py:220
  5.7 16.0 %collective-permute-start.2 = (bf16[192,1536]{1,0:T(8,128)(2,1)}, bf16[192,1536]{1,0:T(8,128)(2,1)S(1)}, u32[]{:S(2)}, u32[]{:S(2)}) collective-permute-start(bf16[192,1536]{1,0:T(8,128)(2,1)} %dispatch.2.refs_0_), channel_id=1, source_target_pairs={{0,2},{2,0},{4,6},{6,4},{8,10},{10,8},{12,14},{14,12},{16,18},{18,... | collective-permute-start | bytes 1769480 | tf_op jit(solution)/shard_map/ppermute | solution.py:217
  8.8 13.1 %copy-start.1 = (bf16[192,1536]{1,0:T(8,128)(2,1)S(1)}, bf16[192,1536]{1,0:T(8,128)(2,1)}, u32[]{:S(2)}) copy-start(bf16[192,1536]{1,0:T(8,128)(2,1)} %dispatch.2.refs_0_) | copy-start | bytes 1769476
  8.8 3.0 %collective-permute-start = (bf16[8,64,384]{2,1,0:T(8,128)(2,1)S(1)}, bf16[8,64,384]{2,1,0:T(8,128)(2,1)S(1)}, u32[]{:S(2)}, u32[]{:S(2)}) collective-permute-start(bf16[8,64,384]{2,1,0:T(8,128)(2,1)S(1)} %get-tuple-element.30), channel_id=1, source_target_pairs={{0,2},{2,0},{4,6},{6,4},{8,10},{10,8},{12,14},{14,12},{16,18},{18,... | collective-permute-start | bytes 1179656 | tf_op jit(solution)/shard_map/ppermute | solution.py:217
  19.0 2.9 %collective-permute-start.3 = (bf16[192,1536]{1,0:T(8,128)(2,1)S(1)}, bf16[192,1536]{1,0:T(8,128)(2,1)S(1)}, u32[]{:S(2)}, u32[]{:S(2)}) collective-permute-start(bf16[192,1536]{1,0:T(8,128)(2,1)S(1)} %collective-permute-done.1.refs_1_), channel_id=1, source_target_pairs={{0,2},{2,0},{4,6},{6,4},{8,10},{10,8},{12,14},{14,12},{16,18},{18,... | collective-permute-start | bytes 1769480 | tf_op jit(solution)/shard_map/ppermute | solution.py:217
  20.2 15.2 %collective-permute-start.8 = (bf16[192,1536]{1,0:T(8,128)(2,1)}, bf16[192,1536]{1,0:T(8,128)(2,1)S(1)}, u32[]{:S(2)}, u32[]{:S(2)}) collective-permute-start(bf16[192,1536]{1,0:T(8,128)(2,1)} %dispatch.3.refs_0_), channel_id=1, source_target_pairs={{0,1},{1,0},{2,3},{3,2},{4,5},{5,4},{6,7},{7,6},{8,9},{9,8},{10,11... | collective-permute-start | bytes 1769480 | tf_op jit(solution)/shard_map/ppermute | solution.py:220
  23.2 7.3 %copy-start = (bf16[192,1536]{1,0:T(8,128)(2,1)S(1)}, bf16[192,1536]{1,0:T(8,128)(2,1)}, u32[]{:S(2)}) copy-start(bf16[192,1536]{1,0:T(8,128)(2,1)} %dispatch.3.refs_0_) | copy-start | bytes 1769476
  23.5 4.1 %collective-permute-start.4 = (f16[64,768]{1,0:T(8,128)(2,1)S(1)}, f16[64,768]{1,0:T(8,128)(2,1)S(1)}, u32[]{:S(2)}, u32[]{:S(2)}) collective-permute-start(f16[64,768]{1,0:T(8,128)(2,1)S(1)} %get-tuple-element.103), channel_id=1, source_target_pairs={{0,8},{2,10},{8,16},{10,18},{16,24},{18,26},{24,28},{26,30},{28,20... | collective-permute-start | bytes 294920 | tf_op jit(solution)/shard_map/ppermute | solution.py:214
  25.1 3.8 %collective-permute-start.5 = (f16[64,768]{1,0:T(8,128)(2,1)S(1)}, f16[64,768]{1,0:T(8,128)(2,1)S(1)}, u32[]{:S(2)}, u32[]{:S(2)}) collective-permute-start(f16[64,768]{1,0:T(8,128)(2,1)S(1)} %get-tuple-element.102), channel_id=1, source_target_pairs={{0,4},{2,6},{8,0},{10,2},{16,8},{18,10},{24,16},{26,18},{28,24},{3... | collective-permute-start | bytes 294920 | tf_op jit(solution)/shard_map/ppermute | solution.py:214
  29.0 6.4 %collective-permute-start.6 = (f16[64,1536]{1,0:T(8,128)(2,1)S(1)}, f16[64,1536]{1,0:T(8,128)(2,1)S(1)}, u32[]{:S(2)}, u32[]{:S(2)}) collective-permute-start(f16[64,1536]{1,0:T(8,128)(2,1)S(1)} %pad_maximum_fusion.3), channel_id=1, source_target_pairs={{0,8},{2,10},{8,16},{10,18},{16,24},{18,26},{24,28},{26,30},{28,20... | collective-permute-start | bytes 589832 | tf_op jit(solution)/shard_map/ppermute | solution.py:214
  30.4 5.0 %collective-permute-start.7 = (f16[64,1536]{1,0:T(8,128)(2,1)S(1)}, f16[64,1536]{1,0:T(8,128)(2,1)S(1)}, u32[]{:S(2)}, u32[]{:S(2)}) collective-permute-start(f16[64,1536]{1,0:T(8,128)(2,1)S(1)} %pad_maximum_fusion.4), channel_id=1, source_target_pairs={{0,4},{2,6},{8,0},{10,2},{16,8},{18,10},{24,16},{26,18},{28,24},{3... | collective-permute-start | bytes 589832 | tf_op jit(solution)/shard_map/ppermute | solution.py:214
  30.6 9.7 %collective-permute-start.11 = (bf16[192,1536]{1,0:T(8,128)(2,1)S(1)}, bf16[192,1536]{1,0:T(8,128)(2,1)S(1)}, u32[]{:S(2)}, u32[]{:S(2)}) collective-permute-start(bf16[192,1536]{1,0:T(8,128)(2,1)S(1)} %copy-done), channel_id=1, source_target_pairs={{0,2},{2,0},{4,6},{6,4},{8,10},{10,8},{12,14},{14,12},{16,18},{18,... | collective-permute-start | bytes 1769480 | tf_op jit(solution)/shard_map/ppermute | solution.py:217
  36.3 4.2 %collective-permute-start.12 = (bf16[192,1536]{1,0:T(8,128)(2,1)S(1)}, bf16[192,1536]{1,0:T(8,128)(2,1)S(1)}, u32[]{:S(2)}, u32[]{:S(2)}) collective-permute-start(bf16[192,1536]{1,0:T(8,128)(2,1)S(1)} %collective-permute-done.8.refs_1_), channel_id=1, source_target_pairs={{0,2},{2,0},{4,6},{6,4},{8,10},{10,8},{12,14},{14,12},{16,18},{18,... | collective-permute-start | bytes 1769480 | tf_op jit(solution)/shard_map/ppermute | solution.py:217
  38.9 6.8 %collective-permute-start.9 = (s16[64,1664]{1,0:T(8,128)(2,1)S(1)}, s16[64,1664]{1,0:T(8,128)(2,1)S(1)}, u32[]{:S(2)}, u32[]{:S(2)}) collective-permute-start(s16[64,1664]{1,0:T(8,128)(2,1)S(1)} %fusion.2), channel_id=1, source_target_pairs={{0,8},{2,10},{8,16},{10,18},{16,24},{18,26},{24,28},{26,30},{28,20... | collective-permute-start | bytes 638984 | tf_op jit(solution)/shard_map/ppermute | solution.py:214
  40.2 6.5 %collective-permute-start.10 = (s16[64,1664]{1,0:T(8,128)(2,1)S(1)}, s16[64,1664]{1,0:T(8,128)(2,1)S(1)}, u32[]{:S(2)}, u32[]{:S(2)}) collective-permute-start(s16[64,1664]{1,0:T(8,128)(2,1)S(1)} %fusion.3), channel_id=1, source_target_pairs={{0,4},{2,6},{8,0},{10,2},{16,8},{18,10},{24,16},{26,18},{28,24},{3... | collective-permute-start | bytes 638984 | tf_op jit(solution)/shard_map/ppermute | solution.py:214
  42.2 6.2 %collective-permute-start.15 = (f16[64,768]{1,0:T(8,128)(2,1)S(1)}, f16[64,768]{1,0:T(8,128)(2,1)S(1)}, u32[]{:S(2)}, u32[]{:S(2)}) collective-permute-start(f16[64,768]{1,0:T(8,128)(2,1)S(1)} %get-tuple-element.99), channel_id=1, source_target_pairs={{0,8},{2,10},{8,16},{10,18},{16,24},{18,26},{24,28},{26,30},{28,20... | collective-permute-start | bytes 294920 | tf_op jit(solution)/shard_map/ppermute | solution.py:214
  43.5 5.3 %collective-permute-start.16 = (f16[64,768]{1,0:T(8,128)(2,1)S(1)}, f16[64,768]{1,0:T(8,128)(2,1)S(1)}, u32[]{:S(2)}, u32[]{:S(2)}) collective-permute-start(f16[64,768]{1,0:T(8,128)(2,1)S(1)} %get-tuple-element.98), channel_id=1, source_target_pairs={{0,4},{2,6},{8,0},{10,2},{16,8},{18,10},{24,16},{26,18},{28,24},{3... | collective-permute-start | bytes 294920 | tf_op jit(solution)/shard_map/ppermute | solution.py:214
  48.3 9.3 %copy-start.4 = (f32[1,64,3072]{2,1,0:T(8,128)S(1)}, f32[1,64,3072]{2,1,0:T(8,128)}, u32[]{:S(2)}) copy-start(f32[1,64,3072]{2,1,0:T(8,128)} %param.15) | copy-start | bytes 2359300
  48.9 4.9 %collective-permute-start.17 = (f16[64,1536]{1,0:T(8,128)(2,1)S(1)}, f16[64,1536]{1,0:T(8,128)(2,1)S(1)}, u32[]{:S(2)}, u32[]{:S(2)}) collective-permute-start(f16[64,1536]{1,0:T(8,128)(2,1)S(1)} %pad_maximum_fusion.5), channel_id=1, source_target_pairs={{0,8},{2,10},{8,16},{10,18},{16,24},{18,26},{24,28},{26,30},{28,20... | collective-permute-start | bytes 589832 | tf_op jit(solution)/shard_map/ppermute | solution.py:214
  50.2 4.9 %collective-permute-start.18 = (f16[64,1536]{1,0:T(8,128)(2,1)S(1)}, f16[64,1536]{1,0:T(8,128)(2,1)S(1)}, u32[]{:S(2)}, u32[]{:S(2)}) collective-permute-start(f16[64,1536]{1,0:T(8,128)(2,1)S(1)} %pad_maximum_fusion.6), channel_id=1, source_target_pairs={{0,4},{2,6},{8,0},{10,2},{16,8},{18,10},{24,16},{26,18},{28,24},{3... | collective-permute-start | bytes 589832 | tf_op jit(solution)/shard_map/ppermute | solution.py:214
  55.9 4.7 %collective-permute-start.19 = (s16[64,1664]{1,0:T(8,128)(2,1)S(1)}, s16[64,1664]{1,0:T(8,128)(2,1)S(1)}, u32[]{:S(2)}, u32[]{:S(2)}) collective-permute-start(s16[64,1664]{1,0:T(8,128)(2,1)S(1)} %fusion.6), channel_id=1, source_target_pairs={{0,8},{2,10},{8,16},{10,18},{16,24},{18,26},{24,28},{26,30},{28,20... | collective-permute-start | bytes 638984 | tf_op jit(solution)/shard_map/ppermute | solution.py:214
  56.4 4.7 %collective-permute-start.20 = (s16[64,1664]{1,0:T(8,128)(2,1)S(1)}, s16[64,1664]{1,0:T(8,128)(2,1)S(1)}, u32[]{:S(2)}, u32[]{:S(2)}) collective-permute-start(s16[64,1664]{1,0:T(8,128)(2,1)S(1)} %fusion.7), channel_id=1, source_target_pairs={{0,4},{2,6},{8,0},{10,2},{16,8},{18,10},{24,16},{26,18},{28,24},{3... | collective-permute-start | bytes 638984 | tf_op jit(solution)/shard_map/ppermute | solution.py:214
  57.8 6.9 %collective-permute-start.13 = (s16[64,1664]{1,0:T(8,128)(2,1)S(1)}, s16[64,1664]{1,0:T(8,128)(2,1)S(1)}, u32[]{:S(2)}, u32[]{:S(2)}) collective-permute-start(s16[64,1664]{1,0:T(8,128)(2,1)S(1)} %fusion.4), channel_id=1, source_target_pairs={{0,8},{2,10},{8,16},{10,18},{16,24},{18,26},{24,28},{26,30},{28,20... | collective-permute-start | bytes 638984 | tf_op jit(solution)/shard_map/ppermute | solution.py:214
  58.1 6.8 %collective-permute-start.14 = (s16[64,1664]{1,0:T(8,128)(2,1)S(1)}, s16[64,1664]{1,0:T(8,128)(2,1)S(1)}, u32[]{:S(2)}, u32[]{:S(2)}) collective-permute-start(s16[64,1664]{1,0:T(8,128)(2,1)S(1)} %fusion.5), channel_id=1, source_target_pairs={{0,4},{2,6},{8,0},{10,2},{16,8},{18,10},{24,16},{26,18},{28,24},{3... | collective-permute-start | bytes 638984 | tf_op jit(solution)/shard_map/ppermute | solution.py:214
  61.9 9.0 %copy-start.7 = (f32[1,64,3072]{2,1,0:T(8,128)S(1)}, f32[1,64,3072]{2,1,0:T(8,128)}, u32[]{:S(2)}) copy-start(f32[1,64,3072]{2,1,0:T(8,128)} %param.16) | copy-start | bytes 2359300
  61.9 9.0 %copy-start.8 = (f32[1,64,3072]{2,1,0:T(8,128)S(1)}, f32[1,64,3072]{2,1,0:T(8,128)}, u32[]{:S(2)}) copy-start(f32[1,64,3072]{2,1,0:T(8,128)} %param.17) | copy-start | bytes 2359300
  62.7 7.4 %collective-permute-start.21 = (s16[64,1664]{1,0:T(8,128)(2,1)S(1)}, s16[64,1664]{1,0:T(8,128)(2,1)S(1)}, u32[]{:S(2)}, u32[]{:S(2)}) collective-permute-start(s16[64,1664]{1,0:T(8,128)(2,1)S(1)} %fusion.8), channel_id=1, source_target_pairs={{0,8},{2,10},{8,16},{10,18},{16,24},{18,26},{24,28},{26,30},{28,20... | collective-permute-start | bytes 638984 | tf_op jit(solution)/shard_map/ppermute | solution.py:214
  63.9 6.3 %collective-permute-start.22 = (s16[64,1664]{1,0:T(8,128)(2,1)S(1)}, s16[64,1664]{1,0:T(8,128)(2,1)S(1)}, u32[]{:S(2)}, u32[]{:S(2)}) collective-permute-start(s16[64,1664]{1,0:T(8,128)(2,1)S(1)} %fusion.9), channel_id=1, source_target_pairs={{0,4},{2,6},{8,0},{10,2},{16,8},{18,10},{24,16},{26,18},{28,24},{3... | collective-permute-start | bytes 638984 | tf_op jit(solution)/shard_map/ppermute | solution.py:214
  71.6 10.3 %copy-start.5 = (f32[1,64,3072]{2,1,0:T(8,128)}, f32[1,64,3072]{2,1,0:T(8,128)S(1)}, u32[]{:S(2)}) copy-start(f32[1,64,3072]{2,1,0:T(8,128)S(1)} %get-tuple-element.66) | copy-start | bytes 2359300
  71.6 10.3 %copy-start.6 = (f32[1,64,3072]{2,1,0:T(8,128)}, f32[1,64,3072]{2,1,0:T(8,128)S(1)}, u32[]{:S(2)}) copy-start(f32[1,64,3072]{2,1,0:T(8,128)S(1)} %get-tuple-element.67) | copy-start | bytes 2359300
  73.2 8.7 %collective-permute-start.24 = (f16[64,3200]{1,0:T(8,128)(2,1)S(1)}, f16[64,3200]{1,0:T(8,128)(2,1)}, u32[]{:S(2)}, u32[]{:S(2)}) collective-permute-start(f16[64,3200]{1,0:T(8,128)(2,1)S(1)} %pad_maximum_fusion.2), channel_id=1, source_target_pairs={{0,8},{2,10},{8,16},{10,18},{16,24},{18,26},{24,28},{26,30},{28,20... | collective-permute-start | bytes 1228808 | tf_op jit(solution)/shard_map/ppermute | solution.py:214
  74.1 12.5 %collective-permute-start.25 = (f16[64,3200]{1,0:T(8,128)(2,1)S(1)}, f16[64,3200]{1,0:T(8,128)(2,1)S(1)}, u32[]{:S(2)}, u32[]{:S(2)}) collective-permute-start(f16[64,3200]{1,0:T(8,128)(2,1)S(1)} %pad_maximum_fusion.2), channel_id=1, source_target_pairs={{0,4},{2,6},{8,0},{10,2},{16,8},{18,10},{24,16},{26,18},{28,24},{3... | collective-permute-start | bytes 1228808 | tf_op jit(solution)/shard_map/ppermute | solution.py:214
  74.8 14.0 %collective-permute-start.23 = (f16[64,3200]{1,0:T(8,128)(2,1)S(1)}, f16[64,3200]{1,0:T(8,128)(2,1)S(1)}, u32[]{:S(2)}, u32[]{:S(2)}) collective-permute-start(f16[64,3200]{1,0:T(8,128)(2,1)S(1)} %pad_maximum_fusion.2), channel_id=1, source_target_pairs={{0,2},{2,0},{4,6},{6,4},{8,10},{10,8},{12,14},{14,12},{16,18},{18,... | collective-permute-start | bytes 1228808 | tf_op jit(solution)/shard_map/ppermute | solution.py:217
  81.8 18.3 %collective-permute-start.26 = (f16[64,3200]{1,0:T(8,128)(2,1)}, f16[64,3200]{1,0:T(8,128)(2,1)S(1)}, u32[]{:S(2)}, u32[]{:S(2)}) collective-permute-start(f16[64,3200]{1,0:T(8,128)(2,1)} %collective-permute-done.24), channel_id=1, source_target_pairs={{0,2},{2,0},{4,6},{6,4},{8,10},{10,8},{12,14},{14,12},{16,18},{18,... | collective-permute-start | bytes 1228808 | tf_op jit(solution)/shard_map/ppermute | solution.py:217
  86.3 11.3 %collective-permute-start.28 = (f16[64,3200]{1,0:T(8,128)(2,1)}, f16[64,3200]{1,0:T(8,128)(2,1)S(1)}, u32[]{:S(2)}, u32[]{:S(2)}) collective-permute-start(f16[64,3200]{1,0:T(8,128)(2,1)} %collective-permute-done.24), channel_id=1, source_target_pairs={{0,8},{2,10},{8,16},{10,18},{16,24},{18,26},{24,28},{26,30},{28,20... | collective-permute-start | bytes 1228808 | tf_op jit(solution)/shard_map/ppermute | solution.py:214
  86.6 12.1 %collective-permute-start.29 = (f16[64,3200]{1,0:T(8,128)(2,1)S(1)}, f16[64,3200]{1,0:T(8,128)(2,1)S(1)}, u32[]{:S(2)}, u32[]{:S(2)}) collective-permute-start(f16[64,3200]{1,0:T(8,128)(2,1)S(1)} %collective-permute-done.25), channel_id=1, source_target_pairs={{0,4},{2,6},{8,0},{10,2},{16,8},{18,10},{24,16},{26,18},{28,24},{3... | collective-permute-start | bytes 1228808 | tf_op jit(solution)/shard_map/ppermute | solution.py:214
  92.4 8.1 %collective-permute-start.27 = (f16[64,3200]{1,0:T(8,128)(2,1)S(1)}, f16[64,3200]{1,0:T(8,128)(2,1)S(1)}, u32[]{:S(2)}, u32[]{:S(2)}) collective-permute-start(f16[64,3200]{1,0:T(8,128)(2,1)S(1)} %collective-permute-done.25), channel_id=1, source_target_pairs={{0,2},{2,0},{4,6},{6,4},{8,10},{10,8},{12,14},{14,12},{16,18},{18,... | collective-permute-start | bytes 1228808 | tf_op jit(solution)/shard_map/ppermute | solution.py:217
  97.6 13.9 %collective-permute-start.30 = (f16[64,3200]{1,0:T(8,128)(2,1)S(1)}, f16[64,3200]{1,0:T(8,128)(2,1)S(1)}, u32[]{:S(2)}, u32[]{:S(2)}) collective-permute-start(f16[64,3200]{1,0:T(8,128)(2,1)S(1)} %collective-permute-done.28), channel_id=1, source_target_pairs={{0,2},{2,0},{4,6},{6,4},{8,10},{10,8},{12,14},{14,12},{16,18},{18,... | collective-permute-start | bytes 1228808 | tf_op jit(solution)/shard_map/ppermute | solution.py:217
  98.3 11.1 %collective-permute-start.32 = (f16[64,3200]{1,0:T(8,128)(2,1)S(1)}, f16[64,3200]{1,0:T(8,128)(2,1)S(1)}, u32[]{:S(2)}, u32[]{:S(2)}) collective-permute-start(f16[64,3200]{1,0:T(8,128)(2,1)S(1)} %collective-permute-done.28), channel_id=1, source_target_pairs={{0,8},{2,10},{8,16},{10,18},{16,24},{18,26},{24,28},{26,30},{28,20... | collective-permute-start | bytes 1228808 | tf_op jit(solution)/shard_map/ppermute | solution.py:214
  98.7 11.2 %collective-permute-start.33 = (f16[64,3200]{1,0:T(8,128)(2,1)S(1)}, f16[64,3200]{1,0:T(8,128)(2,1)S(1)}, u32[]{:S(2)}, u32[]{:S(2)}) collective-permute-start(f16[64,3200]{1,0:T(8,128)(2,1)S(1)} %collective-permute-done.29), channel_id=1, source_target_pairs={{0,4},{2,6},{8,0},{10,2},{16,8},{18,10},{24,16},{26,18},{28,24},{3... | collective-permute-start | bytes 1228808 | tf_op jit(solution)/shard_map/ppermute | solution.py:214
  103.4 8.5 %collective-permute-start.31 = (f16[64,3200]{1,0:T(8,128)(2,1)S(1)}, f16[64,3200]{1,0:T(8,128)(2,1)S(1)}, u32[]{:S(2)}, u32[]{:S(2)}) collective-permute-start(f16[64,3200]{1,0:T(8,128)(2,1)S(1)} %collective-permute-done.29), channel_id=1, source_target_pairs={{0,2},{2,0},{4,6},{6,4},{8,10},{10,8},{12,14},{14,12},{16,18},{18,... | collective-permute-start | bytes 1228808 | tf_op jit(solution)/shard_map/ppermute | solution.py:217
  109.5 6.7 %collective-permute-start.37 = (f16[64,1536]{1,0:T(8,128)(2,1)S(1)}, f16[64,1536]{1,0:T(8,128)(2,1)S(1)}, u32[]{:S(2)}, u32[]{:S(2)}) collective-permute-start(f16[64,1536]{1,0:T(8,128)(2,1)S(1)} %slice.366), channel_id=1, source_target_pairs={{0,8},{2,10},{8,16},{10,18},{16,24},{18,26},{24,28},{26,30},{28,20... | collective-permute-start | bytes 589832 | tf_op jit(solution)/shard_map/ppermute | solution.py:214
  109.9 6.9 %collective-permute-start.36 = (f16[64,1664]{1,0:T(8,128)(2,1)S(1)}, f16[64,1664]{1,0:T(8,128)(2,1)S(1)}, u32[]{:S(2)}, u32[]{:S(2)}) collective-permute-start(f16[64,1664]{1,0:T(8,128)(2,1)S(1)} %slice.363), channel_id=1, source_target_pairs={{0,4},{2,6},{8,0},{10,2},{16,8},{18,10},{24,16},{26,18},{28,24},{3... | collective-permute-start | bytes 638984 | tf_op jit(solution)/shard_map/ppermute | solution.py:214
  114.6 3.4 %collective-permute-start.34 = (f16[64,3200]{1,0:T(8,128)(2,1)S(1)}, f16[64,3200]{1,0:T(8,128)(2,1)S(1)}, u32[]{:S(2)}, u32[]{:S(2)}) collective-permute-start(f16[64,3200]{1,0:T(8,128)(2,1)S(1)} %collective-permute-done.32), channel_id=1, source_target_pairs={{0,2},{2,0},{4,6},{6,4},{8,10},{10,8},{12,14},{14,12},{16,18},{18,... | collective-permute-start | bytes 1228808 | tf_op jit(solution)/shard_map/ppermute | solution.py:217
  116.1 2.3 %collective-permute-start.35 = (f16[64,3200]{1,0:T(8,128)(2,1)S(1)}, f16[64,3200]{1,0:T(8,128)(2,1)S(1)}, u32[]{:S(2)}, u32[]{:S(2)}) collective-permute-start(f16[64,3200]{1,0:T(8,128)(2,1)S(1)} %collective-permute-done.33), channel_id=1, source_target_pairs={{0,2},{2,0},{4,6},{6,4},{8,10},{10,8},{12,14},{14,12},{16,18},{18,... | collective-permute-start | bytes 1228808 | tf_op jit(solution)/shard_map/ppermute | solution.py:217
  116.1 4.7 %collective-permute-start.39 = (f16[64,1536]{1,0:T(8,128)(2,1)S(1)}, f16[64,1536]{1,0:T(8,128)(2,1)S(1)}, u32[]{:S(2)}, u32[]{:S(2)}) collective-permute-start(f16[64,1536]{1,0:T(8,128)(2,1)S(1)} %collective-permute-done.37), channel_id=1, source_target_pairs={{0,2},{2,0},{4,6},{6,4},{8,10},{10,8},{12,14},{14,12},{16,18},{18,... | collective-permute-start | bytes 589832 | tf_op jit(solution)/shard_map/ppermute | solution.py:217
  117.0 3.6 %collective-permute-start.38 = (f16[64,1664]{1,0:T(8,128)(2,1)S(1)}, f16[64,1664]{1,0:T(8,128)(2,1)S(1)}, u32[]{:S(2)}, u32[]{:S(2)}) collective-permute-start(f16[64,1664]{1,0:T(8,128)(2,1)S(1)} %collective-permute-done.36), channel_id=1, source_target_pairs={{0,2},{2,0},{4,6},{6,4},{8,10},{10,8},{12,14},{14,12},{16,18},{18,... | collective-permute-start | bytes 638984 | tf_op jit(solution)/shard_map/ppermute | solution.py:217

commit v6 on v5

--- a/solution.py
+++ b/solution.py
@@ -15,14 +15,14 @@
 SPLIT = 1
 HIDDEN_FLOPS = 8 << 30
 OFFSET = 3
-FINE = 2
+FINE = 1
 DISPATCH_FLOPS = 4 << 30
 DISPATCH_VMEM = 56
 
 
 def encode(value):
     largest = jnp.max(jnp.abs(value), axis=1, keepdims=True)
-    power = jnp.floor(jnp.log2(jnp.maximum(largest, 1e-30)))
+    power = jnp.floor(jnp.log2(jnp.maximum(largest, 1e-20)))
     root = jnp.sqrt(jnp.abs(value) * jnp.exp2(28.0 - power))
     code = jnp.where(value < 0.0, -root, root)
     tail = jnp.broadcast_to(power, (value.shape[0], 128))

time: 123 us -> 121 us (0.984)
  other arithmetic: 16.1 us -> 13.4 us
  waiting for transfers between devices: 38.8 us -> 40.3 us
    ppermute x24, waiting for transfers between devices: 28.5 us -> 30 us  [step_ring(): lax.ppermute(value, 'dp', [(place(*x, c), place(*y, c)) for x, y in pairs...]
  transfers between devices with their start and end apart: 40 -> 40, of which waited for: 18 -> 20; matrix products, arithmetic and copies ran while one was open for 11% -> 9% of each run, Pallas kernels for 14% -> 14%
where the time goes in v6:
time: 121 us; the launch traced here: 120 us
  starting transfers between devices  43.3 us (36%)
  waiting for transfers between devices  40.3 us (33%)
  Pallas kernels  21.1 us (17%)
  other arithmetic  13.4 us (11%)
  between operations  1.45 us (1%)
    ppermute x24, waiting for transfers between devices, step_ring(): lax.ppermute(value, 'dp', [(place(*x, c), place(*y, c)) for x, y in pairs...  30 us
    ppermute x14, starting transfers between devices, swap_core(): lax.ppermute(value, 'dp', [(place(a, b, c), place(a, b, c + 1)) for a, b,...  21.4 us
    ppermute x24, starting transfers between devices, step_ring(): lax.ppermute(value, 'dp', [(place(*x, c), place(*y, c)) for x, y in pairs...  18.3 us
    pallas_call x6, Pallas kernels, put(): pl.pallas_call(functools.partial(put_kernel, tuple(marks), aliased), out_...  11.3 us
    ppermute x2, waiting for transfers between devices, shift_expert(): lax.ppermute(value, 'expert', [(e, (e + k) % experts) for e in range(expe...  9.92 us
    pallas_call x2, Pallas kernels, dispatch(): pl.pallas_call(functools.partial(dispatch_kernel, first), out_shape=jax.S...  5.82 us
    mul x16, other arithmetic, local(): values.append(value.astype(F32) * scales[spot])  4.27 us
    ppermute x2, starting transfers between devices, shift_expert(): lax.ppermute(value, 'expert', [(e, (e + k) % experts) for e in range(expe...  3.6 us
  transfers between devices with their start and end apart: 40, of which 20 were waited for; matrix products, arithmetic and copies ran while one was open for 9% of the time, Pallas kernels for 14%

profile of v6, /device:TPU:1, one launch (start us, length us, event | category | flops | bytes accessed | tf_op | source)
XLA Modules:
  0.0 120.3 jit_solution(965652602328807236)
XLA Ops:
  0.7 2.9 %dispatch.2.refs_0_ = bf16[192,1536]{1,0:T(8,128)(2,1)} custom-call(s32[2,512]{1,0:T(2,128)} %bitcast.40, f32[2,512]{1,0:T(2,128)} %bitcast.42, bf16[512,3072]{1,0:T(8,128)(2,1)} %grad_in.3), custom_call_target="tpu_custom_call" | custom-call | flops 4294967296 | tf_op jit(solution)/shard_map/dispatch/pallas_call | solution.py:80
  3.6 2.1 %collective-permute-start.1 = (bf16[192,1536]{1,0:T(8,128)(2,1)}, bf16[192,1536]{1,0:T(8,128)(2,1)S(1)}, u32[]{:S(2)}, u32[]{:S(2)}) collective-permute-start(bf16[192,1536]{1,0:T(8,128)(2,1)} %dispatch.2.refs_0_), channel_id=1, source_target_pairs={{0,1},{1,0},{2,3},{3,2},{4,5},{5,4},{6,7},{7,6},{8,9},{9,8},{10,11... | collective-permute-start | bytes 1769480 | tf_op jit(solution)/shard_map/ppermute | solution.py:220
  5.7 1.0 collective-permute-start.2
  6.7 0.7 multiply_bitcast_fusion
  7.5 1.3 %hidden_pieces.1 = (bf16[8,64,384]{2,1,0:T(8,128)(2,1)S(1)}, bf16[8,64,384]{2,1,0:T(8,128)(2,1)S(1)}) custom-call(s32[10]{0:T(128)S(1)} %pad_add_fusion.at, bf16[384,1024]{1,0:T(8,128)(2,1)S(1)} %bitcast.34, bf16[384,1024]{1,0:T(8,128)(2,1)S(1)} %bitcast.35), custom_call_target="tpu_custom_call" | custom-call | flops 8589934592 | tf_op jit(solution)/shard_map/hidden_pieces/pallas_call | solution.py:153
  8.8 2.9 %dispatch.3.refs_0_ = bf16[192,1536]{1,0:T(8,128)(2,1)} custom-call(s32[2,512]{1,0:T(2,128)} %bitcast.41, f32[2,512]{1,0:T(2,128)} %bitcast.43, bf16[512,3072]{1,0:T(8,128)(2,1)} %grad_in.3), custom_call_target="tpu_custom_call" | custom-call | flops 4294967296 | tf_op jit(solution)/shard_map/dispatch/pallas_call | solution.py:80
  11.8 7.2 %collective-permute-done.1.refs_1_ = bf16[192,1536]{1,0:T(8,128)(2,1)S(1)} collective-permute-done((bf16[192,1536]{1,0:T(8,128)(2,1)}, bf16[192,1536]{1,0:T(8,128)(2,1)S(1)}, u32[]{:S(2)}, u32[]{:S(2)}) %collective-permute-start.1) | collective-permute-done | bytes 589856 | tf_op jit(solution)/shard_map/ppermute | solution.py:220
  19.0 1.2 %collective-permute-start.3 = (bf16[192,1536]{1,0:T(8,128)(2,1)S(1)}, bf16[192,1536]{1,0:T(8,128)(2,1)S(1)}, u32[]{:S(2)}, u32[]{:S(2)}) collective-permute-start(bf16[192,1536]{1,0:T(8,128)(2,1)S(1)} %collective-permute-done.1.refs_1_), channel_id=1, source_target_pairs={{0,2},{2,0},{4,6},{6,4},{8,10},{10,8},{12,14},{14,12},{16,18},{18,... | collective-permute-start | bytes 1769480 | tf_op jit(solution)/shard_map/ppermute | solution.py:217
  20.2 1.5 %collective-permute-start.8 = (bf16[192,1536]{1,0:T(8,128)(2,1)}, bf16[192,1536]{1,0:T(8,128)(2,1)S(1)}, u32[]{:S(2)}, u32[]{:S(2)}) collective-permute-start(bf16[192,1536]{1,0:T(8,128)(2,1)} %dispatch.3.refs_0_), channel_id=1, source_target_pairs={{0,1},{1,0},{2,3},{3,2},{4,5},{5,4},{6,7},{7,6},{8,9},{9,8},{10,11... | collective-permute-start | bytes 1769480 | tf_op jit(solution)/shard_map/ppermute | solution.py:220
  21.9 1.4 %product.2 = f32[512,1536]{1,0:T(8,128)S(1)} custom-call(bf16[512,768]{1,0:T(8,128)(2,1)S(1)} %bitcast.32, bf16[192,1536]{1,0:T(8,128)(2,1)S(1)} %copy-done.1, bf16[192,1536]{1,0:T(8,128)(2,1)S(1)} %collective-permute-done.1.refs_1_, bf16[192,1536]{1,0:T(8,128)(2,1)S(1)} %collective-permute-done.2.refs_2_, bf16[192,1536]{1,0:T(8,128)(2,1)S(1)} %collective-permute-done.3.refs_3_), custom_call_target="tpu_custom_call" | custom-call | tf_op jit(solution)/shard_map/product/pallas_call | solution.py:177
  23.5 1.6 %collective-permute-start.4 = (f16[64,768]{1,0:T(8,128)(2,1)S(1)}, f16[64,768]{1,0:T(8,128)(2,1)S(1)}, u32[]{:S(2)}, u32[]{:S(2)}) collective-permute-start(f16[64,768]{1,0:T(8,128)(2,1)S(1)} %get-tuple-element.91), channel_id=1, source_target_pairs={{0,8},{2,10},{8,16},{10,18},{16,24},{18,26},{24,28},{26,30},{28,20... | collective-permute-start | bytes 294920 | tf_op jit(solution)/shard_map/ppermute | solution.py:214
  25.1 2.4 %collective-permute-done.4 = f16[64,768]{1,0:T(8,128)(2,1)S(1)} collective-permute-done((f16[64,768]{1,0:T(8,128)(2,1)S(1)}, f16[64,768]{1,0:T(8,128)(2,1)S(1)}, u32[]{:S(2)}, u32[]{:S(2)}) %collective-permute-start.4) | collective-permute-done | bytes 98336 | tf_op jit(solution)/shard_map/ppermute | solution.py:214
  27.6 1.3 %collective-permute-done.5 = f16[64,768]{1,0:T(8,128)(2,1)S(1)} collective-permute-done((f16[64,768]{1,0:T(8,128)(2,1)S(1)}, f16[64,768]{1,0:T(8,128)(2,1)S(1)}, u32[]{:S(2)}, u32[]{:S(2)}) %collective-permute-start.5) | collective-permute-done | bytes 98336 | tf_op jit(solution)/shard_map/ppermute | solution.py:214
  29.0 1.3 %collective-permute-start.6 = (f16[64,1536]{1,0:T(8,128)(2,1)S(1)}, f16[64,1536]{1,0:T(8,128)(2,1)S(1)}, u32[]{:S(2)}, u32[]{:S(2)}) collective-permute-start(f16[64,1536]{1,0:T(8,128)(2,1)S(1)} %pad_maximum_fusion.3), channel_id=1, source_target_pairs={{0,8},{2,10},{8,16},{10,18},{16,24},{18,26},{24,28},{26,30},{28,20... | collective-permute-start | bytes 589832 | tf_op jit(solution)/shard_map/ppermute | solution.py:214
  30.6 2.1 %collective-permute-start.11 = (bf16[192,1536]{1,0:T(8,128)(2,1)S(1)}, bf16[192,1536]{1,0:T(8,128)(2,1)S(1)}, u32[]{:S(2)}, u32[]{:S(2)}) collective-permute-start(bf16[192,1536]{1,0:T(8,128)(2,1)S(1)} %copy-done), channel_id=1, source_target_pairs={{0,2},{2,0},{4,6},{6,4},{8,10},{10,8},{12,14},{14,12},{16,18},{18,... | collective-permute-start | bytes 1769480 | tf_op jit(solution)/shard_map/ppermute | solution.py:217
  32.7 2.7 %collective-permute-done.8.refs_1_ = bf16[192,1536]{1,0:T(8,128)(2,1)S(1)} collective-permute-done((bf16[192,1536]{1,0:T(8,128)(2,1)}, bf16[192,1536]{1,0:T(8,128)(2,1)S(1)}, u32[]{:S(2)}, u32[]{:S(2)}) %collective-permute-start.8) | collective-permute-done | bytes 589856 | tf_op jit(solution)/shard_map/ppermute | solution.py:220
  35.5 2.5 %collective-permute-start.12 = (bf16[192,1536]{1,0:T(8,128)(2,1)S(1)}, bf16[192,1536]{1,0:T(8,128)(2,1)S(1)}, u32[]{:S(2)}, u32[]{:S(2)}) collective-permute-start(bf16[192,1536]{1,0:T(8,128)(2,1)S(1)} %collective-permute-done.8.refs_1_), channel_id=1, source_target_pairs={{0,2},{2,0},{4,6},{6,4},{8,10},{10,8},{12,14},{14,12},{16,18},{18,... | collective-permute-start | bytes 1769480 | tf_op jit(solution)/shard_map/ppermute | solution.py:217
  38.0 1.3 %collective-permute-start.9 = (f16[64,1536]{1,0:T(8,128)(2,1)S(1)}, f16[64,1536]{1,0:T(8,128)(2,1)S(1)}, u32[]{:S(2)}, u32[]{:S(2)}) collective-permute-start(f16[64,1536]{1,0:T(8,128)(2,1)S(1)} %get-tuple-element.81), channel_id=1, source_target_pairs={{0,8},{2,10},{8,16},{10,18},{16,24},{18,26},{24,28},{26,30},{28,20... | collective-permute-start | bytes 589832 | tf_op jit(solution)/shard_map/ppermute | solution.py:214
  39.7 1.4 %product.3 = f32[512,1536]{1,0:T(8,128)S(1)} custom-call(bf16[512,768]{1,0:T(8,128)(2,1)S(1)} %bitcast.33, bf16[192,1536]{1,0:T(8,128)(2,1)S(1)} %copy-done, bf16[192,1536]{1,0:T(8,128)(2,1)S(1)} %collective-permute-done.8.refs_1_, bf16[192,1536]{1,0:T(8,128)(2,1)S(1)} %collective-permute-done.11.refs_2_, bf16[192,1536]{1,0:T(8,128)(2,1)S(1)} %collective-permute-done.12.refs_3_), custom_call_target="tpu_custom_call" | custom-call | tf_op jit(solution)/shard_map/product/pallas_call | solution.py:177
  41.3 1.3 %collective-permute-start.15 = (f16[64,768]{1,0:T(8,128)(2,1)S(1)}, f16[64,768]{1,0:T(8,128)(2,1)S(1)}, u32[]{:S(2)}, u32[]{:S(2)}) collective-permute-start(f16[64,768]{1,0:T(8,128)(2,1)S(1)} %get-tuple-element.87), channel_id=1, source_target_pairs={{0,8},{2,10},{8,16},{10,18},{16,24},{18,26},{24,28},{26,30},{28,20... | collective-permute-start | bytes 294920 | tf_op jit(solution)/shard_map/ppermute | solution.py:214
  42.9 1.6 %collective-permute-done.9 = f16[64,1536]{1,0:T(8,128)(2,1)S(1)} collective-permute-done((f16[64,1536]{1,0:T(8,128)(2,1)S(1)}, f16[64,1536]{1,0:T(8,128)(2,1)S(1)}, u32[]{:S(2)}, u32[]{:S(2)}) %collective-permute-start.9) | collective-permute-done | bytes 196640 | tf_op jit(solution)/shard_map/ppermute | solution.py:214
  44.5 1.0 collective-permute-done.10
  46.6 1.0 collective-permute-done.16
  47.7 1.3 %collective-permute-start.17 = (f16[64,1536]{1,0:T(8,128)(2,1)S(1)}, f16[64,1536]{1,0:T(8,128)(2,1)S(1)}, u32[]{:S(2)}, u32[]{:S(2)}) collective-permute-start(f16[64,1536]{1,0:T(8,128)(2,1)S(1)} %pad_maximum_fusion.5), channel_id=1, source_target_pairs={{0,8},{2,10},{8,16},{10,18},{16,24},{18,26},{24,28},{26,30},{28,20... | collective-permute-start | bytes 589832 | tf_op jit(solution)/shard_map/ppermute | solution.py:214
  49.3 3.6 %collective-permute-done.17 = f16[64,1536]{1,0:T(8,128)(2,1)S(1)} collective-permute-done((f16[64,1536]{1,0:T(8,128)(2,1)S(1)}, f16[64,1536]{1,0:T(8,128)(2,1)S(1)}, u32[]{:S(2)}, u32[]{:S(2)}) %collective-permute-start.17) | collective-permute-done | bytes 196640 | tf_op jit(solution)/shard_map/ppermute | solution.py:214
  53.0 1.0 collective-permute-done.18
  54.1 0.5 collective-permute-start.19
  54.7 1.0 collective-permute-start.20
  55.8 0.5 collective-permute-start.13
  56.4 1.0 collective-permute-start.14
  57.4 1.4 %collective-permute-done.19 = f16[64,1536]{1,0:T(8,128)(2,1)S(1)} collective-permute-done((f16[64,1536]{1,0:T(8,128)(2,1)S(1)}, f16[64,1536]{1,0:T(8,128)(2,1)S(1)}, u32[]{:S(2)}, u32[]{:S(2)}) %collective-permute-start.19) | collective-permute-done | bytes 196640 | tf_op jit(solution)/shard_map/ppermute | solution.py:214
  58.7 0.5 collective-permute-done.20
  60.0 1.0 collective-permute-start.21
  61.2 0.6 collective-permute-start.22
  61.9 0.9 collective-permute-done.13
  63.8 3.7 %collective-permute-done.21 = s16[64,1664]{1,0:T(8,128)(2,1)S(1)} collective-permute-done((s16[64,1664]{1,0:T(8,128)(2,1)S(1)}, s16[64,1664]{1,0:T(8,128)(2,1)S(1)}, u32[]{:S(2)}, u32[]{:S(2)}) %collective-permute-start.21) | collective-permute-done | bytes 213024 | tf_op jit(solution)/shard_map/ppermute | solution.py:214
  67.4 1.0 collective-permute-done.22
  69.1 0.6 multiply_reduce_fusion
  69.8 1.4 %convert_multiply_fusion.13 = (f32[64,3072]{1,0:T(8,128)S(1)}, f16[64,3072]{1,0:T(8,128)(2,1)S(1)}, f32[1,64,3072]{2,1,0:T(8,128)}) fusion(f32[64]{0:T(128)S(1)} %get-tuple-element.97, f32[64]{0:T(128)S(1)} %get-tuple-element.96, f32[1,64,3072]{2,1,0:T(8,128)S(1)} %copy-done.4, f32[1,64,3072]{2,1,0:T(8,128)S(1)} %get-tuple-element.63, ...), kind=kLoop, calls=%fused_computation.19 | loop fusion | flops 1966080 | bytes 4326144 | tf_op jit(solution)/shard_map/mul | solution.py:326
  71.7 1.2 collective-permute-start.25
  73.0 4.6 %collective-permute-start.23 = (f16[64,3200]{1,0:T(8,128)(2,1)S(1)}, f16[64,3200]{1,0:T(8,128)(2,1)S(1)}, u32[]{:S(2)}, u32[]{:S(2)}) collective-permute-start(f16[64,3200]{1,0:T(8,128)(2,1)S(1)} %pad_maximum_fusion.2), channel_id=1, source_target_pairs={{0,2},{2,0},{4,6},{6,4},{8,10},{10,8},{12,14},{14,12},{16,18},{18,... | collective-permute-start | bytes 1228808 | tf_op jit(solution)/shard_map/ppermute | solution.py:217
  77.6 1.4 %put.6.refs_0_ = f32[1024,3072]{1,0:T(8,128)} custom-call(s32[16]{0:T(128)S(1)} %mul.416.starts, f32[64,3072]{1,0:T(8,128)S(1)} %get-tuple-element.58.refs_0_), custom_call_target="tpu_custom_call" | custom-call | flops 4294967296 | tf_op jit(solution)/shard_map/put/pallas_call | solution.py:118
  79.1 4.4 %collective-permute-start.26 = (f16[64,3200]{1,0:T(8,128)(2,1)}, f16[64,3200]{1,0:T(8,128)(2,1)S(1)}, u32[]{:S(2)}, u32[]{:S(2)}) collective-permute-start(f16[64,3200]{1,0:T(8,128)(2,1)} %collective-permute-done.24), channel_id=1, source_target_pairs={{0,2},{2,0},{4,6},{6,4},{8,10},{10,8},{12,14},{14,12},{16,18},{18,... | collective-permute-start | bytes 1228808 | tf_op jit(solution)/shard_map/ppermute | solution.py:217
  83.5 0.8 collective-permute-start.28
  84.3 0.7 collective-permute-start.29
  84.9 0.9 exponential_reduce_fusion.13
  86.4 1.1 convert_multiply_fusion.11.refs_2_
  87.6 2.0 %put.7.refs_0_ = f32[1024,3072]{1,0:T(8,128)} custom-call(s32[16]{0:T(128)S(1)} %mul.416.starts, f32[1024,3072]{1,0:T(8,128)} %put.6.refs_0_, f32[64,3072]{1,0:T(8,128)S(1)} %convert_multiply_fusion.12.refs_1_, f32[64,3072]{1,0:T(8,128)S(1)} %convert_multiply_fusion.11.refs_2_, ...), custom_call_target="tpu_custom_call", output_to_operand_aliasing={{}: (1, {})} | custom-call | flops 4294967296 | tf_op jit(solution)/shard_map/put/pallas_call | solution.py:118
  89.6 0.6 collective-permute-start.27
  90.2 4.5 %collective-permute-done.28 = f16[64,3200]{1,0:T(8,128)(2,1)S(1)} collective-permute-done((f16[64,3200]{1,0:T(8,128)(2,1)}, f16[64,3200]{1,0:T(8,128)(2,1)S(1)}, u32[]{:S(2)}, u32[]{:S(2)}) %collective-permute-start.28) | collective-permute-done | bytes 409632 | tf_op jit(solution)/shard_map/ppermute | solution.py:214
  94.8 0.8 collective-permute-start.30
  95.6 0.8 collective-permute-start.32
  96.4 0.7 collective-permute-start.33
  98.3 2.2 %put.8.refs_0_ = f32[1024,3072]{1,0:T(8,128)} custom-call(s32[16]{0:T(128)S(1)} %mul.416.starts, f32[1024,3072]{1,0:T(8,128)} %put.7.refs_0_, f32[64,3072]{1,0:T(8,128)S(1)} %convert_multiply_fusion.9.refs_1_, f32[64,3072]{1,0:T(8,128)S(1)} %convert_multiply_fusion.8.refs_2_, ...), custom_call_target="tpu_custom_call", output_to_operand_aliasing={{}: (1, {})} | custom-call | flops 4294967296 | tf_op jit(solution)/shard_map/put/pallas_call | solution.py:118
  100.6 0.6 collective-permute-start.31
  101.2 5.5 %collective-permute-done.32 = f16[64,3200]{1,0:T(8,128)(2,1)S(1)} collective-permute-done((f16[64,3200]{1,0:T(8,128)(2,1)S(1)}, f16[64,3200]{1,0:T(8,128)(2,1)S(1)}, u32[]{:S(2)}, u32[]{:S(2)}) %collective-permute-start.32) | collective-permute-done | bytes 409632 | tf_op jit(solution)/shard_map/ppermute | solution.py:214
  106.7 0.8 collective-permute-start.37
  107.6 0.7 collective-permute-start.36
  109.6 2.2 %put.9.refs_0_ = f32[1024,3072]{1,0:T(8,128)} custom-call(s32[16]{0:T(128)S(1)} %mul.416.starts, f32[1024,3072]{1,0:T(8,128)} %put.8.refs_0_, f32[64,3072]{1,0:T(8,128)S(1)} %convert_multiply_fusion.5.refs_1_, f32[64,3072]{1,0:T(8,128)S(1)} %convert_multiply_fusion.4.refs_2_, ...), custom_call_target="tpu_custom_call", output_to_operand_aliasing={{}: (1, {})} | custom-call | flops 4294967296 | tf_op jit(solution)/shard_map/put/pallas_call | solution.py:118
  111.9 1.4 %collective-permute-start.34 = (f16[64,3200]{1,0:T(8,128)(2,1)S(1)}, f16[64,3200]{1,0:T(8,128)(2,1)S(1)}, u32[]{:S(2)}, u32[]{:S(2)}) collective-permute-start(f16[64,3200]{1,0:T(8,128)(2,1)S(1)} %collective-permute-done.32), channel_id=1, source_target_pairs={{0,2},{2,0},{4,6},{6,4},{8,10},{10,8},{12,14},{14,12},{16,18},{18,... | collective-permute-start | bytes 1228808 | tf_op jit(solution)/shard_map/ppermute | solution.py:217
  113.4 0.7 collective-permute-start.39
  114.3 1.3 %collective-permute-start.38 = (f16[64,1664]{1,0:T(8,128)(2,1)S(1)}, f16[64,1664]{1,0:T(8,128)(2,1)S(1)}, u32[]{:S(2)}, u32[]{:S(2)}) collective-permute-start(f16[64,1664]{1,0:T(8,128)(2,1)S(1)} %collective-permute-done.36), channel_id=1, source_target_pairs={{0,2},{2,0},{4,6},{6,4},{8,10},{10,8},{12,14},{14,12},{16,18},{18,... | collective-permute-start | bytes 638984 | tf_op jit(solution)/shard_map/ppermute | solution.py:217
  116.4 2.0 %put.10.refs_0_ = f32[1024,3072]{1,0:T(8,128)} custom-call(s32[16]{0:T(128)S(1)} %mul.416.starts, f32[1024,3072]{1,0:T(8,128)} %put.9.refs_0_, f32[64,3072]{1,0:T(8,128)S(1)} %convert_multiply_fusion.1.refs_1_, f32[64,3072]{1,0:T(8,128)S(1)} %convert_multiply_fusion.refs_2_, ...), custom_call_target="tpu_custom_call", output_to_operand_aliasing={{}: (1, {})} | custom-call | flops 4294967296 | tf_op jit(solution)/shard_map/put/pallas_call | solution.py:118
  118.7 1.4 %put.11 = f32[1024,3072]{1,0:T(8,128)} custom-call(s32[16]{0:T(128)S(1)} %mul.416.starts, f32[1024,3072]{1,0:T(8,128)} %put.10.refs_0_, f32[64,1536]{1,0:T(8,128)S(1)} %get-tuple-element.93.refs_1_, f32[64,1536]{1,0:T(8,128)S(1)} %get-tuple-element.92.refs_2_), custom_call_target="tpu_custom_call", output_to_operand_aliasing={{}: (1, {})} | custom-call | flops 4294967296 | tf_op jit(solution)/shard_map/put/pallas_call | solution.py:118
  (128 shorter events, 11.7 us)
Async XLA Ops:
  0.6 6.8 %copy-start.2 = (bf16[384,1,1024]{2,0,1:T(8,128)(2,1)S(1)}, bf16[384,1,1024]{2,0,1:T(8,128)(2,1)}, u32[]{:S(2)}) copy-start(bf16[384,1,1024]{2,0,1:T(8,128)(2,1)} %param.13) | copy-start | bytes 2359300
  0.6 6.8 %copy-start.3 = (bf16[384,1,1024]{2,0,1:T(8,128)(2,1)S(1)}, bf16[384,1,1024]{2,0,1:T(8,128)(2,1)}, u32[]{:S(2)}) copy-start(bf16[384,1,1024]{2,0,1:T(8,128)(2,1)} %param.14) | copy-start | bytes 2359300
  3.6 15.4 %collective-permute-start.1 = (bf16[192,1536]{1,0:T(8,128)(2,1)}, bf16[192,1536]{1,0:T(8,128)(2,1)S(1)}, u32[]{:S(2)}, u32[]{:S(2)}) collective-permute-start(bf16[192,1536]{1,0:T(8,128)(2,1)} %dispatch.2.refs_0_), channel_id=1, source_target_pairs={{0,1},{1,0},{2,3},{3,2},{4,5},{5,4},{6,7},{7,6},{8,9},{9,8},{10,11... | collective-permute-start | bytes 1769480 | tf_op jit(solution)/shard_map/ppermute | solution.py:220
  5.7 16.0 %collective-permute-start.2 = (bf16[192,1536]{1,0:T(8,128)(2,1)}, bf16[192,1536]{1,0:T(8,128)(2,1)S(1)}, u32[]{:S(2)}, u32[]{:S(2)}) collective-permute-start(bf16[192,1536]{1,0:T(8,128)(2,1)} %dispatch.2.refs_0_), channel_id=1, source_target_pairs={{0,2},{2,0},{4,6},{6,4},{8,10},{10,8},{12,14},{14,12},{16,18},{18,... | collective-permute-start | bytes 1769480 | tf_op jit(solution)/shard_map/ppermute | solution.py:217
  8.8 13.1 %copy-start.1 = (bf16[192,1536]{1,0:T(8,128)(2,1)S(1)}, bf16[192,1536]{1,0:T(8,128)(2,1)}, u32[]{:S(2)}) copy-start(bf16[192,1536]{1,0:T(8,128)(2,1)} %dispatch.2.refs_0_) | copy-start | bytes 1769476
  8.8 3.0 %collective-permute-start = (bf16[8,64,384]{2,1,0:T(8,128)(2,1)S(1)}, bf16[8,64,384]{2,1,0:T(8,128)(2,1)S(1)}, u32[]{:S(2)}, u32[]{:S(2)}) collective-permute-start(bf16[8,64,384]{2,1,0:T(8,128)(2,1)S(1)} %get-tuple-element.30), channel_id=1, source_target_pairs={{0,2},{2,0},{4,6},{6,4},{8,10},{10,8},{12,14},{14,12},{16,18},{18,... | collective-permute-start | bytes 1179656 | tf_op jit(solution)/shard_map/ppermute | solution.py:217
  19.0 2.9 %collective-permute-start.3 = (bf16[192,1536]{1,0:T(8,128)(2,1)S(1)}, bf16[192,1536]{1,0:T(8,128)(2,1)S(1)}, u32[]{:S(2)}, u32[]{:S(2)}) collective-permute-start(bf16[192,1536]{1,0:T(8,128)(2,1)S(1)} %collective-permute-done.1.refs_1_), channel_id=1, source_target_pairs={{0,2},{2,0},{4,6},{6,4},{8,10},{10,8},{12,14},{14,12},{16,18},{18,... | collective-permute-start | bytes 1769480 | tf_op jit(solution)/shard_map/ppermute | solution.py:217
  20.2 15.2 %collective-permute-start.8 = (bf16[192,1536]{1,0:T(8,128)(2,1)}, bf16[192,1536]{1,0:T(8,128)(2,1)S(1)}, u32[]{:S(2)}, u32[]{:S(2)}) collective-permute-start(bf16[192,1536]{1,0:T(8,128)(2,1)} %dispatch.3.refs_0_), channel_id=1, source_target_pairs={{0,1},{1,0},{2,3},{3,2},{4,5},{5,4},{6,7},{7,6},{8,9},{9,8},{10,11... | collective-permute-start | bytes 1769480 | tf_op jit(solution)/shard_map/ppermute | solution.py:220
  23.2 7.3 %copy-start = (bf16[192,1536]{1,0:T(8,128)(2,1)S(1)}, bf16[192,1536]{1,0:T(8,128)(2,1)}, u32[]{:S(2)}) copy-start(bf16[192,1536]{1,0:T(8,128)(2,1)} %dispatch.3.refs_0_) | copy-start | bytes 1769476
  23.5 4.1 %collective-permute-start.4 = (f16[64,768]{1,0:T(8,128)(2,1)S(1)}, f16[64,768]{1,0:T(8,128)(2,1)S(1)}, u32[]{:S(2)}, u32[]{:S(2)}) collective-permute-start(f16[64,768]{1,0:T(8,128)(2,1)S(1)} %get-tuple-element.91), channel_id=1, source_target_pairs={{0,8},{2,10},{8,16},{10,18},{16,24},{18,26},{24,28},{26,30},{28,20... | collective-permute-start | bytes 294920 | tf_op jit(solution)/shard_map/ppermute | solution.py:214
  25.1 3.8 %collective-permute-start.5 = (f16[64,768]{1,0:T(8,128)(2,1)S(1)}, f16[64,768]{1,0:T(8,128)(2,1)S(1)}, u32[]{:S(2)}, u32[]{:S(2)}) collective-permute-start(f16[64,768]{1,0:T(8,128)(2,1)S(1)} %get-tuple-element.90), channel_id=1, source_target_pairs={{0,4},{2,6},{8,0},{10,2},{16,8},{18,10},{24,16},{26,18},{28,24},{3... | collective-permute-start | bytes 294920 | tf_op jit(solution)/shard_map/ppermute | solution.py:214
  29.0 6.4 %collective-permute-start.6 = (f16[64,1536]{1,0:T(8,128)(2,1)S(1)}, f16[64,1536]{1,0:T(8,128)(2,1)S(1)}, u32[]{:S(2)}, u32[]{:S(2)}) collective-permute-start(f16[64,1536]{1,0:T(8,128)(2,1)S(1)} %pad_maximum_fusion.3), channel_id=1, source_target_pairs={{0,8},{2,10},{8,16},{10,18},{16,24},{18,26},{24,28},{26,30},{28,20... | collective-permute-start | bytes 589832 | tf_op jit(solution)/shard_map/ppermute | solution.py:214
  30.4 5.0 %collective-permute-start.7 = (f16[64,1536]{1,0:T(8,128)(2,1)S(1)}, f16[64,1536]{1,0:T(8,128)(2,1)S(1)}, u32[]{:S(2)}, u32[]{:S(2)}) collective-permute-start(f16[64,1536]{1,0:T(8,128)(2,1)S(1)} %pad_maximum_fusion.4), channel_id=1, source_target_pairs={{0,4},{2,6},{8,0},{10,2},{16,8},{18,10},{24,16},{26,18},{28,24},{3... | collective-permute-start | bytes 589832 | tf_op jit(solution)/shard_map/ppermute | solution.py:214
  30.6 8.9 %collective-permute-start.11 = (bf16[192,1536]{1,0:T(8,128)(2,1)S(1)}, bf16[192,1536]{1,0:T(8,128)(2,1)S(1)}, u32[]{:S(2)}, u32[]{:S(2)}) collective-permute-start(bf16[192,1536]{1,0:T(8,128)(2,1)S(1)} %copy-done), channel_id=1, source_target_pairs={{0,2},{2,0},{4,6},{6,4},{8,10},{10,8},{12,14},{14,12},{16,18},{18,... | collective-permute-start | bytes 1769480 | tf_op jit(solution)/shard_map/ppermute | solution.py:217
  35.5 4.2 %collective-permute-start.12 = (bf16[192,1536]{1,0:T(8,128)(2,1)S(1)}, bf16[192,1536]{1,0:T(8,128)(2,1)S(1)}, u32[]{:S(2)}, u32[]{:S(2)}) collective-permute-start(bf16[192,1536]{1,0:T(8,128)(2,1)S(1)} %collective-permute-done.8.refs_1_), channel_id=1, source_target_pairs={{0,2},{2,0},{4,6},{6,4},{8,10},{10,8},{12,14},{14,12},{16,18},{18,... | collective-permute-start | bytes 1769480 | tf_op jit(solution)/shard_map/ppermute | solution.py:217
  38.0 6.5 %collective-permute-start.9 = (f16[64,1536]{1,0:T(8,128)(2,1)S(1)}, f16[64,1536]{1,0:T(8,128)(2,1)S(1)}, u32[]{:S(2)}, u32[]{:S(2)}) collective-permute-start(f16[64,1536]{1,0:T(8,128)(2,1)S(1)} %get-tuple-element.81), channel_id=1, source_target_pairs={{0,8},{2,10},{8,16},{10,18},{16,24},{18,26},{24,28},{26,30},{28,20... | collective-permute-start | bytes 589832 | tf_op jit(solution)/shard_map/ppermute | solution.py:214
  39.3 6.1 %collective-permute-start.10 = (f16[64,1536]{1,0:T(8,128)(2,1)S(1)}, f16[64,1536]{1,0:T(8,128)(2,1)S(1)}, u32[]{:S(2)}, u32[]{:S(2)}) collective-permute-start(f16[64,1536]{1,0:T(8,128)(2,1)S(1)} %get-tuple-element.80), channel_id=1, source_target_pairs={{0,4},{2,6},{8,0},{10,2},{16,8},{18,10},{24,16},{26,18},{28,24},{3... | collective-permute-start | bytes 589832 | tf_op jit(solution)/shard_map/ppermute | solution.py:214
  41.3 5.3 %collective-permute-start.15 = (f16[64,768]{1,0:T(8,128)(2,1)S(1)}, f16[64,768]{1,0:T(8,128)(2,1)S(1)}, u32[]{:S(2)}, u32[]{:S(2)}) collective-permute-start(f16[64,768]{1,0:T(8,128)(2,1)S(1)} %get-tuple-element.87), channel_id=1, source_target_pairs={{0,8},{2,10},{8,16},{10,18},{16,24},{18,26},{24,28},{26,30},{28,20... | collective-permute-start | bytes 294920 | tf_op jit(solution)/shard_map/ppermute | solution.py:214
  42.7 4.9 %collective-permute-start.16 = (f16[64,768]{1,0:T(8,128)(2,1)S(1)}, f16[64,768]{1,0:T(8,128)(2,1)S(1)}, u32[]{:S(2)}, u32[]{:S(2)}) collective-permute-start(f16[64,768]{1,0:T(8,128)(2,1)S(1)} %get-tuple-element.86), channel_id=1, source_target_pairs={{0,4},{2,6},{8,0},{10,2},{16,8},{18,10},{24,16},{26,18},{28,24},{3... | collective-permute-start | bytes 294920 | tf_op jit(solution)/shard_map/ppermute | solution.py:214
  45.7 10.0 %copy-start.4 = (f32[1,64,3072]{2,1,0:T(8,128)S(1)}, f32[1,64,3072]{2,1,0:T(8,128)}, u32[]{:S(2)}) copy-start(f32[1,64,3072]{2,1,0:T(8,128)} %param.15) | copy-start | bytes 2359300
  47.7 5.3 %collective-permute-start.17 = (f16[64,1536]{1,0:T(8,128)(2,1)S(1)}, f16[64,1536]{1,0:T(8,128)(2,1)S(1)}, u32[]{:S(2)}, u32[]{:S(2)}) collective-permute-start(f16[64,1536]{1,0:T(8,128)(2,1)S(1)} %pad_maximum_fusion.5), channel_id=1, source_target_pairs={{0,8},{2,10},{8,16},{10,18},{16,24},{18,26},{24,28},{26,30},{28,20... | collective-permute-start | bytes 589832 | tf_op jit(solution)/shard_map/ppermute | solution.py:214
  49.0 5.0 %collective-permute-start.18 = (f16[64,1536]{1,0:T(8,128)(2,1)S(1)}, f16[64,1536]{1,0:T(8,128)(2,1)S(1)}, u32[]{:S(2)}, u32[]{:S(2)}) collective-permute-start(f16[64,1536]{1,0:T(8,128)(2,1)S(1)} %pad_maximum_fusion.6), channel_id=1, source_target_pairs={{0,4},{2,6},{8,0},{10,2},{16,8},{18,10},{24,16},{26,18},{28,24},{3... | collective-permute-start | bytes 589832 | tf_op jit(solution)/shard_map/ppermute | solution.py:214
  54.1 4.6 %collective-permute-start.19 = (f16[64,1536]{1,0:T(8,128)(2,1)S(1)}, f16[64,1536]{1,0:T(8,128)(2,1)S(1)}, u32[]{:S(2)}, u32[]{:S(2)}) collective-permute-start(f16[64,1536]{1,0:T(8,128)(2,1)S(1)} %get-tuple-element.75), channel_id=1, source_target_pairs={{0,8},{2,10},{8,16},{10,18},{16,24},{18,26},{24,28},{26,30},{28,20... | collective-permute-start | bytes 589832 | tf_op jit(solution)/shard_map/ppermute | solution.py:214
  54.7 4.5 %collective-permute-start.20 = (f16[64,1536]{1,0:T(8,128)(2,1)S(1)}, f16[64,1536]{1,0:T(8,128)(2,1)S(1)}, u32[]{:S(2)}, u32[]{:S(2)}) collective-permute-start(f16[64,1536]{1,0:T(8,128)(2,1)S(1)} %get-tuple-element.74), channel_id=1, source_target_pairs={{0,4},{2,6},{8,0},{10,2},{16,8},{18,10},{24,16},{26,18},{28,24},{3... | collective-permute-start | bytes 589832 | tf_op jit(solution)/shard_map/ppermute | solution.py:214
  55.8 6.9 %collective-permute-start.13 = (s16[64,1664]{1,0:T(8,128)(2,1)S(1)}, s16[64,1664]{1,0:T(8,128)(2,1)S(1)}, u32[]{:S(2)}, u32[]{:S(2)}) collective-permute-start(s16[64,1664]{1,0:T(8,128)(2,1)S(1)} %fusion.2), channel_id=1, source_target_pairs={{0,8},{2,10},{8,16},{10,18},{16,24},{18,26},{24,28},{26,30},{28,20... | collective-permute-start | bytes 638984 | tf_op jit(solution)/shard_map/ppermute | solution.py:214
  56.4 6.8 %collective-permute-start.14 = (s16[64,1664]{1,0:T(8,128)(2,1)S(1)}, s16[64,1664]{1,0:T(8,128)(2,1)S(1)}, u32[]{:S(2)}, u32[]{:S(2)}) collective-permute-start(s16[64,1664]{1,0:T(8,128)(2,1)S(1)} %fusion.3), channel_id=1, source_target_pairs={{0,4},{2,6},{8,0},{10,2},{16,8},{18,10},{24,16},{26,18},{28,24},{3... | collective-permute-start | bytes 638984 | tf_op jit(solution)/shard_map/ppermute | solution.py:214
  59.5 9.6 %copy-start.7 = (f32[1,64,3072]{2,1,0:T(8,128)S(1)}, f32[1,64,3072]{2,1,0:T(8,128)}, u32[]{:S(2)}) copy-start(f32[1,64,3072]{2,1,0:T(8,128)} %param.16) | copy-start | bytes 2359300
  59.5 9.6 %copy-start.8 = (f32[1,64,3072]{2,1,0:T(8,128)S(1)}, f32[1,64,3072]{2,1,0:T(8,128)}, u32[]{:S(2)}) copy-start(f32[1,64,3072]{2,1,0:T(8,128)} %param.17) | copy-start | bytes 2359300
  60.0 7.4 %collective-permute-start.21 = (s16[64,1664]{1,0:T(8,128)(2,1)S(1)}, s16[64,1664]{1,0:T(8,128)(2,1)S(1)}, u32[]{:S(2)}, u32[]{:S(2)}) collective-permute-start(s16[64,1664]{1,0:T(8,128)(2,1)S(1)} %fusion.4), channel_id=1, source_target_pairs={{0,8},{2,10},{8,16},{10,18},{16,24},{18,26},{24,28},{26,30},{28,20... | collective-permute-start | bytes 638984 | tf_op jit(solution)/shard_map/ppermute | solution.py:214
  61.2 7.3 %collective-permute-start.22 = (s16[64,1664]{1,0:T(8,128)(2,1)S(1)}, s16[64,1664]{1,0:T(8,128)(2,1)S(1)}, u32[]{:S(2)}, u32[]{:S(2)}) collective-permute-start(s16[64,1664]{1,0:T(8,128)(2,1)S(1)} %fusion.5), channel_id=1, source_target_pairs={{0,4},{2,6},{8,0},{10,2},{16,8},{18,10},{24,16},{26,18},{28,24},{3... | collective-permute-start | bytes 638984 | tf_op jit(solution)/shard_map/ppermute | solution.py:214
  69.7 9.3 %copy-start.5 = (f32[1,64,3072]{2,1,0:T(8,128)}, f32[1,64,3072]{2,1,0:T(8,128)S(1)}, u32[]{:S(2)}) copy-start(f32[1,64,3072]{2,1,0:T(8,128)S(1)} %get-tuple-element.62) | copy-start | bytes 2359300
  69.7 9.3 %copy-start.6 = (f32[1,64,3072]{2,1,0:T(8,128)}, f32[1,64,3072]{2,1,0:T(8,128)S(1)}, u32[]{:S(2)}) copy-start(f32[1,64,3072]{2,1,0:T(8,128)S(1)} %get-tuple-element.63) | copy-start | bytes 2359300
  71.3 7.7 %collective-permute-start.24 = (f16[64,3200]{1,0:T(8,128)(2,1)S(1)}, f16[64,3200]{1,0:T(8,128)(2,1)}, u32[]{:S(2)}, u32[]{:S(2)}) collective-permute-start(f16[64,3200]{1,0:T(8,128)(2,1)S(1)} %pad_maximum_fusion.2), channel_id=1, source_target_pairs={{0,8},{2,10},{8,16},{10,18},{16,24},{18,26},{24,28},{26,30},{28,20... | collective-permute-start | bytes 1228808 | tf_op jit(solution)/shard_map/ppermute | solution.py:214
  71.7 12.6 %collective-permute-start.25 = (f16[64,3200]{1,0:T(8,128)(2,1)S(1)}, f16[64,3200]{1,0:T(8,128)(2,1)S(1)}, u32[]{:S(2)}, u32[]{:S(2)}) collective-permute-start(f16[64,3200]{1,0:T(8,128)(2,1)S(1)} %pad_maximum_fusion.2), channel_id=1, source_target_pairs={{0,4},{2,6},{8,0},{10,2},{16,8},{18,10},{24,16},{26,18},{28,24},{3... | collective-permute-start | bytes 1228808 | tf_op jit(solution)/shard_map/ppermute | solution.py:214
  73.0 13.0 %collective-permute-start.23 = (f16[64,3200]{1,0:T(8,128)(2,1)S(1)}, f16[64,3200]{1,0:T(8,128)(2,1)S(1)}, u32[]{:S(2)}, u32[]{:S(2)}) collective-permute-start(f16[64,3200]{1,0:T(8,128)(2,1)S(1)} %pad_maximum_fusion.2), channel_id=1, source_target_pairs={{0,2},{2,0},{4,6},{6,4},{8,10},{10,8},{12,14},{14,12},{16,18},{18,... | collective-permute-start | bytes 1228808 | tf_op jit(solution)/shard_map/ppermute | solution.py:217
  79.1 18.3 %collective-permute-start.26 = (f16[64,3200]{1,0:T(8,128)(2,1)}, f16[64,3200]{1,0:T(8,128)(2,1)S(1)}, u32[]{:S(2)}, u32[]{:S(2)}) collective-permute-start(f16[64,3200]{1,0:T(8,128)(2,1)} %collective-permute-done.24), channel_id=1, source_target_pairs={{0,2},{2,0},{4,6},{6,4},{8,10},{10,8},{12,14},{14,12},{16,18},{18,... | collective-permute-start | bytes 1228808 | tf_op jit(solution)/shard_map/ppermute | solution.py:217
  83.5 11.3 %collective-permute-start.28 = (f16[64,3200]{1,0:T(8,128)(2,1)}, f16[64,3200]{1,0:T(8,128)(2,1)S(1)}, u32[]{:S(2)}, u32[]{:S(2)}) collective-permute-start(f16[64,3200]{1,0:T(8,128)(2,1)} %collective-permute-done.24), channel_id=1, source_target_pairs={{0,8},{2,10},{8,16},{10,18},{16,24},{18,26},{24,28},{26,30},{28,20... | collective-permute-start | bytes 1228808 | tf_op jit(solution)/shard_map/ppermute | solution.py:214
  84.3 12.1 %collective-permute-start.29 = (f16[64,3200]{1,0:T(8,128)(2,1)S(1)}, f16[64,3200]{1,0:T(8,128)(2,1)S(1)}, u32[]{:S(2)}, u32[]{:S(2)}) collective-permute-start(f16[64,3200]{1,0:T(8,128)(2,1)S(1)} %collective-permute-done.25), channel_id=1, source_target_pairs={{0,4},{2,6},{8,0},{10,2},{16,8},{18,10},{24,16},{26,18},{28,24},{3... | collective-permute-start | bytes 1228808 | tf_op jit(solution)/shard_map/ppermute | solution.py:214
  89.6 8.1 %collective-permute-start.27 = (f16[64,3200]{1,0:T(8,128)(2,1)S(1)}, f16[64,3200]{1,0:T(8,128)(2,1)S(1)}, u32[]{:S(2)}, u32[]{:S(2)}) collective-permute-start(f16[64,3200]{1,0:T(8,128)(2,1)S(1)} %collective-permute-done.25), channel_id=1, source_target_pairs={{0,2},{2,0},{4,6},{6,4},{8,10},{10,8},{12,14},{14,12},{16,18},{18,... | collective-permute-start | bytes 1228808 | tf_op jit(solution)/shard_map/ppermute | solution.py:217
  94.8 13.9 %collective-permute-start.30 = (f16[64,3200]{1,0:T(8,128)(2,1)S(1)}, f16[64,3200]{1,0:T(8,128)(2,1)S(1)}, u32[]{:S(2)}, u32[]{:S(2)}) collective-permute-start(f16[64,3200]{1,0:T(8,128)(2,1)S(1)} %collective-permute-done.28), channel_id=1, source_target_pairs={{0,2},{2,0},{4,6},{6,4},{8,10},{10,8},{12,14},{14,12},{16,18},{18,... | collective-permute-start | bytes 1228808 | tf_op jit(solution)/shard_map/ppermute | solution.py:217
  95.6 11.1 %collective-permute-start.32 = (f16[64,3200]{1,0:T(8,128)(2,1)S(1)}, f16[64,3200]{1,0:T(8,128)(2,1)S(1)}, u32[]{:S(2)}, u32[]{:S(2)}) collective-permute-start(f16[64,3200]{1,0:T(8,128)(2,1)S(1)} %collective-permute-done.28), channel_id=1, source_target_pairs={{0,8},{2,10},{8,16},{10,18},{16,24},{18,26},{24,28},{26,30},{28,20... | collective-permute-start | bytes 1228808 | tf_op jit(solution)/shard_map/ppermute | solution.py:214
  96.4 11.2 %collective-permute-start.33 = (f16[64,3200]{1,0:T(8,128)(2,1)S(1)}, f16[64,3200]{1,0:T(8,128)(2,1)S(1)}, u32[]{:S(2)}, u32[]{:S(2)}) collective-permute-start(f16[64,3200]{1,0:T(8,128)(2,1)S(1)} %collective-permute-done.29), channel_id=1, source_target_pairs={{0,4},{2,6},{8,0},{10,2},{16,8},{18,10},{24,16},{26,18},{28,24},{3... | collective-permute-start | bytes 1228808 | tf_op jit(solution)/shard_map/ppermute | solution.py:214
  100.6 8.5 %collective-permute-start.31 = (f16[64,3200]{1,0:T(8,128)(2,1)S(1)}, f16[64,3200]{1,0:T(8,128)(2,1)S(1)}, u32[]{:S(2)}, u32[]{:S(2)}) collective-permute-start(f16[64,3200]{1,0:T(8,128)(2,1)S(1)} %collective-permute-done.29), channel_id=1, source_target_pairs={{0,2},{2,0},{4,6},{6,4},{8,10},{10,8},{12,14},{14,12},{16,18},{18,... | collective-permute-start | bytes 1228808 | tf_op jit(solution)/shard_map/ppermute | solution.py:217
  106.7 6.7 %collective-permute-start.37 = (f16[64,1536]{1,0:T(8,128)(2,1)S(1)}, f16[64,1536]{1,0:T(8,128)(2,1)S(1)}, u32[]{:S(2)}, u32[]{:S(2)}) collective-permute-start(f16[64,1536]{1,0:T(8,128)(2,1)S(1)} %slice.334), channel_id=1, source_target_pairs={{0,8},{2,10},{8,16},{10,18},{16,24},{18,26},{24,28},{26,30},{28,20... | collective-permute-start | bytes 589832 | tf_op jit(solution)/shard_map/ppermute | solution.py:214
  107.6 6.5 %collective-permute-start.36 = (f16[64,1664]{1,0:T(8,128)(2,1)S(1)}, f16[64,1664]{1,0:T(8,128)(2,1)S(1)}, u32[]{:S(2)}, u32[]{:S(2)}) collective-permute-start(f16[64,1664]{1,0:T(8,128)(2,1)S(1)} %slice.331), channel_id=1, source_target_pairs={{0,4},{2,6},{8,0},{10,2},{16,8},{18,10},{24,16},{26,18},{28,24},{3... | collective-permute-start | bytes 638984 | tf_op jit(solution)/shard_map/ppermute | solution.py:214
  111.9 3.8 %collective-permute-start.34 = (f16[64,3200]{1,0:T(8,128)(2,1)S(1)}, f16[64,3200]{1,0:T(8,128)(2,1)S(1)}, u32[]{:S(2)}, u32[]{:S(2)}) collective-permute-start(f16[64,3200]{1,0:T(8,128)(2,1)S(1)} %collective-permute-done.32), channel_id=1, source_target_pairs={{0,2},{2,0},{4,6},{6,4},{8,10},{10,8},{12,14},{14,12},{16,18},{18,... | collective-permute-start | bytes 1228808 | tf_op jit(solution)/shard_map/ppermute | solution.py:217
  113.3 2.8 %collective-permute-start.35 = (f16[64,3200]{1,0:T(8,128)(2,1)S(1)}, f16[64,3200]{1,0:T(8,128)(2,1)S(1)}, u32[]{:S(2)}, u32[]{:S(2)}) collective-permute-start(f16[64,3200]{1,0:T(8,128)(2,1)S(1)} %collective-permute-done.33), channel_id=1, source_target_pairs={{0,2},{2,0},{4,6},{6,4},{8,10},{10,8},{12,14},{14,12},{16,18},{18,... | collective-permute-start | bytes 1228808 | tf_op jit(solution)/shard_map/ppermute | solution.py:217
  113.4 5.2 %collective-permute-start.39 = (f16[64,1536]{1,0:T(8,128)(2,1)S(1)}, f16[64,1536]{1,0:T(8,128)(2,1)S(1)}, u32[]{:S(2)}, u32[]{:S(2)}) collective-permute-start(f16[64,1536]{1,0:T(8,128)(2,1)S(1)} %collective-permute-done.37), channel_id=1, source_target_pairs={{0,2},{2,0},{4,6},{6,4},{8,10},{10,8},{12,14},{14,12},{16,18},{18,... | collective-permute-start | bytes 589832 | tf_op jit(solution)/shard_map/ppermute | solution.py:217
  114.3 4.1 %collective-permute-start.38 = (f16[64,1664]{1,0:T(8,128)(2,1)S(1)}, f16[64,1664]{1,0:T(8,128)(2,1)S(1)}, u32[]{:S(2)}, u32[]{:S(2)}) collective-permute-start(f16[64,1664]{1,0:T(8,128)(2,1)S(1)} %collective-permute-done.36), channel_id=1, source_target_pairs={{0,2},{2,0},{4,6},{6,4},{8,10},{10,8},{12,14},{14,12},{16,18},{18,... | collective-permute-start | bytes 638984 | tf_op jit(solution)/shard_map/ppermute | solution.py:217

commit v7 on v6

--- a/solution.py
+++ b/solution.py
@@ -15,7 +15,7 @@
 SPLIT = 1
 HIDDEN_FLOPS = 8 << 30
 OFFSET = 3
-FINE = 1
+FINE = 2
 DISPATCH_FLOPS = 4 << 30
 DISPATCH_VMEM = 56
 

time: 121 us -> 123 us (1.017)
  other arithmetic: 13.4 us -> 16.1 us
  waiting for transfers between devices: 40.3 us -> 38.8 us
    ppermute x24, waiting for transfers between devices: 30 us -> 28.5 us  [step_ring(): lax.ppermute(value, 'dp', [(place(*x, c), place(*y, c)) for x, y in pairs...]
  transfers between devices with their start and end apart: 40 -> 40, of which waited for: 20 -> 18; matrix products, arithmetic and copies ran while one was open for 9% -> 11% of each run, Pallas kernels for 14% -> 14%
where the time goes in v7:
time: 123 us
  starting transfers between devices  44 us (36%)
  waiting for transfers between devices  38.8 us (32%)
  Pallas kernels  21.1 us (17%)
  other arithmetic  16.1 us (13%)
  between operations  1.56 us (1%)
    ppermute x24, waiting for transfers between devices, step_ring(): lax.ppermute(value, 'dp', [(place(*x, c), place(*y, c)) for x, y in pairs...  28.5 us
    ppermute x14, starting transfers between devices, swap_core(): lax.ppermute(value, 'dp', [(place(a, b, c), place(a, b, c + 1)) for a, b,...  21.9 us
    ppermute x24, starting transfers between devices, step_ring(): lax.ppermute(value, 'dp', [(place(*x, c), place(*y, c)) for x, y in pairs...  18.5 us
    pallas_call x6, Pallas kernels, put(): pl.pallas_call(functools.partial(put_kernel, tuple(marks), aliased), out_...  11.3 us
    ppermute x2, waiting for transfers between devices, shift_expert(): lax.ppermute(value, 'expert', [(e, (e + k) % experts) for e in range(expe...  9.92 us
    pallas_call x2, Pallas kernels, dispatch(): pl.pallas_call(functools.partial(dispatch_kernel, first), out_shape=jax.S...  5.82 us
    mul x16, other arithmetic, local(): values.append(value.astype(F32) * scales[spot])  4.27 us
    ppermute x2, starting transfers between devices, shift_expert(): lax.ppermute(value, 'expert', [(e, (e + k) % experts) for e in range(expe...  3.6 us
  transfers between devices with their start and end apart: 40, of which 18 were waited for; matrix products, arithmetic and copies ran while one was open for 11% of the time, Pallas kernels for 14%

profile of v7, /device:TPU:1, one launch (start us, length us, event | category | flops | bytes accessed | tf_op | source)
XLA Modules:
  0.0 122.6 jit_solution(13537534766093161300)
XLA Ops:
  0.7 2.9 %dispatch.2.refs_0_ = bf16[192,1536]{1,0:T(8,128)(2,1)} custom-call(s32[2,512]{1,0:T(2,128)} %bitcast.40, f32[2,512]{1,0:T(2,128)} %bitcast.42, bf16[512,3072]{1,0:T(8,128)(2,1)} %grad_in.3), custom_call_target="tpu_custom_call" | custom-call | flops 4294967296 | tf_op jit(solution)/shard_map/dispatch/pallas_call | solution.py:80
  3.6 2.1 %collective-permute-start.1 = (bf16[192,1536]{1,0:T(8,128)(2,1)}, bf16[192,1536]{1,0:T(8,128)(2,1)S(1)}, u32[]{:S(2)}, u32[]{:S(2)}) collective-permute-start(bf16[192,1536]{1,0:T(8,128)(2,1)} %dispatch.2.refs_0_), channel_id=1, source_target_pairs={{0,1},{1,0},{2,3},{3,2},{4,5},{5,4},{6,7},{7,6},{8,9},{9,8},{10,11... | collective-permute-start | bytes 1769480 | tf_op jit(solution)/shard_map/ppermute | solution.py:220
  5.7 1.0 collective-permute-start.2
  6.7 0.7 multiply_bitcast_fusion
  7.5 1.3 %hidden_pieces.1 = (bf16[8,64,384]{2,1,0:T(8,128)(2,1)S(1)}, bf16[8,64,384]{2,1,0:T(8,128)(2,1)S(1)}) custom-call(s32[10]{0:T(128)S(1)} %pad_add_fusion.at, bf16[384,1024]{1,0:T(8,128)(2,1)S(1)} %bitcast.34, bf16[384,1024]{1,0:T(8,128)(2,1)S(1)} %bitcast.35), custom_call_target="tpu_custom_call" | custom-call | flops 8589934592 | tf_op jit(solution)/shard_map/hidden_pieces/pallas_call | solution.py:153
  8.8 2.9 %dispatch.3.refs_0_ = bf16[192,1536]{1,0:T(8,128)(2,1)} custom-call(s32[2,512]{1,0:T(2,128)} %bitcast.41, f32[2,512]{1,0:T(2,128)} %bitcast.43, bf16[512,3072]{1,0:T(8,128)(2,1)} %grad_in.3), custom_call_target="tpu_custom_call" | custom-call | flops 4294967296 | tf_op jit(solution)/shard_map/dispatch/pallas_call | solution.py:80
  11.8 7.2 %collective-permute-done.1.refs_1_ = bf16[192,1536]{1,0:T(8,128)(2,1)S(1)} collective-permute-done((bf16[192,1536]{1,0:T(8,128)(2,1)}, bf16[192,1536]{1,0:T(8,128)(2,1)S(1)}, u32[]{:S(2)}, u32[]{:S(2)}) %collective-permute-start.1) | collective-permute-done | bytes 589856 | tf_op jit(solution)/shard_map/ppermute | solution.py:220
  19.0 1.2 %collective-permute-start.3 = (bf16[192,1536]{1,0:T(8,128)(2,1)S(1)}, bf16[192,1536]{1,0:T(8,128)(2,1)S(1)}, u32[]{:S(2)}, u32[]{:S(2)}) collective-permute-start(bf16[192,1536]{1,0:T(8,128)(2,1)S(1)} %collective-permute-done.1.refs_1_), channel_id=1, source_target_pairs={{0,2},{2,0},{4,6},{6,4},{8,10},{10,8},{12,14},{14,12},{16,18},{18,... | collective-permute-start | bytes 1769480 | tf_op jit(solution)/shard_map/ppermute | solution.py:217
  20.2 1.5 %collective-permute-start.8 = (bf16[192,1536]{1,0:T(8,128)(2,1)}, bf16[192,1536]{1,0:T(8,128)(2,1)S(1)}, u32[]{:S(2)}, u32[]{:S(2)}) collective-permute-start(bf16[192,1536]{1,0:T(8,128)(2,1)} %dispatch.3.refs_0_), channel_id=1, source_target_pairs={{0,1},{1,0},{2,3},{3,2},{4,5},{5,4},{6,7},{7,6},{8,9},{9,8},{10,11... | collective-permute-start | bytes 1769480 | tf_op jit(solution)/shard_map/ppermute | solution.py:220
  21.9 1.4 %product.2 = f32[512,1536]{1,0:T(8,128)S(1)} custom-call(bf16[512,768]{1,0:T(8,128)(2,1)S(1)} %bitcast.32, bf16[192,1536]{1,0:T(8,128)(2,1)S(1)} %copy-done.1, bf16[192,1536]{1,0:T(8,128)(2,1)S(1)} %collective-permute-done.1.refs_1_, bf16[192,1536]{1,0:T(8,128)(2,1)S(1)} %collective-permute-done.2.refs_2_, bf16[192,1536]{1,0:T(8,128)(2,1)S(1)} %collective-permute-done.3.refs_3_), custom_call_target="tpu_custom_call" | custom-call | tf_op jit(solution)/shard_map/product/pallas_call | solution.py:177
  23.5 1.6 %collective-permute-start.4 = (f16[64,768]{1,0:T(8,128)(2,1)S(1)}, f16[64,768]{1,0:T(8,128)(2,1)S(1)}, u32[]{:S(2)}, u32[]{:S(2)}) collective-permute-start(f16[64,768]{1,0:T(8,128)(2,1)S(1)} %get-tuple-element.103), channel_id=1, source_target_pairs={{0,8},{2,10},{8,16},{10,18},{16,24},{18,26},{24,28},{26,30},{28,20... | collective-permute-start | bytes 294920 | tf_op jit(solution)/shard_map/ppermute | solution.py:214
  25.1 2.4 %collective-permute-done.4 = f16[64,768]{1,0:T(8,128)(2,1)S(1)} collective-permute-done((f16[64,768]{1,0:T(8,128)(2,1)S(1)}, f16[64,768]{1,0:T(8,128)(2,1)S(1)}, u32[]{:S(2)}, u32[]{:S(2)}) %collective-permute-start.4) | collective-permute-done | bytes 98336 | tf_op jit(solution)/shard_map/ppermute | solution.py:214
  27.6 1.3 %collective-permute-done.5 = f16[64,768]{1,0:T(8,128)(2,1)S(1)} collective-permute-done((f16[64,768]{1,0:T(8,128)(2,1)S(1)}, f16[64,768]{1,0:T(8,128)(2,1)S(1)}, u32[]{:S(2)}, u32[]{:S(2)}) %collective-permute-start.5) | collective-permute-done | bytes 98336 | tf_op jit(solution)/shard_map/ppermute | solution.py:214
  29.0 1.3 %collective-permute-start.6 = (f16[64,1536]{1,0:T(8,128)(2,1)S(1)}, f16[64,1536]{1,0:T(8,128)(2,1)S(1)}, u32[]{:S(2)}, u32[]{:S(2)}) collective-permute-start(f16[64,1536]{1,0:T(8,128)(2,1)S(1)} %pad_maximum_fusion.3), channel_id=1, source_target_pairs={{0,8},{2,10},{8,16},{10,18},{16,24},{18,26},{24,28},{26,30},{28,20... | collective-permute-start | bytes 589832 | tf_op jit(solution)/shard_map/ppermute | solution.py:214
  30.6 2.1 %collective-permute-start.11 = (bf16[192,1536]{1,0:T(8,128)(2,1)S(1)}, bf16[192,1536]{1,0:T(8,128)(2,1)S(1)}, u32[]{:S(2)}, u32[]{:S(2)}) collective-permute-start(bf16[192,1536]{1,0:T(8,128)(2,1)S(1)} %copy-done), channel_id=1, source_target_pairs={{0,2},{2,0},{4,6},{6,4},{8,10},{10,8},{12,14},{14,12},{16,18},{18,... | collective-permute-start | bytes 1769480 | tf_op jit(solution)/shard_map/ppermute | solution.py:217
  32.7 2.7 %collective-permute-done.8.refs_1_ = bf16[192,1536]{1,0:T(8,128)(2,1)S(1)} collective-permute-done((bf16[192,1536]{1,0:T(8,128)(2,1)}, bf16[192,1536]{1,0:T(8,128)(2,1)S(1)}, u32[]{:S(2)}, u32[]{:S(2)}) %collective-permute-start.8) | collective-permute-done | bytes 589856 | tf_op jit(solution)/shard_map/ppermute | solution.py:220
  35.6 0.4 negate_select_fusion.6
  36.3 2.5 %collective-permute-start.12 = (bf16[192,1536]{1,0:T(8,128)(2,1)S(1)}, bf16[192,1536]{1,0:T(8,128)(2,1)S(1)}, u32[]{:S(2)}, u32[]{:S(2)}) collective-permute-start(bf16[192,1536]{1,0:T(8,128)(2,1)S(1)} %collective-permute-done.8.refs_1_), channel_id=1, source_target_pairs={{0,2},{2,0},{4,6},{6,4},{8,10},{10,8},{12,14},{14,12},{16,18},{18,... | collective-permute-start | bytes 1769480 | tf_op jit(solution)/shard_map/ppermute | solution.py:217
  38.9 1.3 %collective-permute-start.9 = (s16[64,1664]{1,0:T(8,128)(2,1)S(1)}, s16[64,1664]{1,0:T(8,128)(2,1)S(1)}, u32[]{:S(2)}, u32[]{:S(2)}) collective-permute-start(s16[64,1664]{1,0:T(8,128)(2,1)S(1)} %fusion.2), channel_id=1, source_target_pairs={{0,8},{2,10},{8,16},{10,18},{16,24},{18,26},{24,28},{26,30},{28,20... | collective-permute-start | bytes 638984 | tf_op jit(solution)/shard_map/ppermute | solution.py:214
  40.5 1.4 %product.3 = f32[512,1536]{1,0:T(8,128)S(1)} custom-call(bf16[512,768]{1,0:T(8,128)(2,1)S(1)} %bitcast.33, bf16[192,1536]{1,0:T(8,128)(2,1)S(1)} %copy-done, bf16[192,1536]{1,0:T(8,128)(2,1)S(1)} %collective-permute-done.8.refs_1_, bf16[192,1536]{1,0:T(8,128)(2,1)S(1)} %collective-permute-done.11.refs_2_, bf16[192,1536]{1,0:T(8,128)(2,1)S(1)} %collective-permute-done.12.refs_3_), custom_call_target="tpu_custom_call" | custom-call | tf_op jit(solution)/shard_map/product/pallas_call | solution.py:177
  42.2 1.3 %collective-permute-start.15 = (f16[64,768]{1,0:T(8,128)(2,1)S(1)}, f16[64,768]{1,0:T(8,128)(2,1)S(1)}, u32[]{:S(2)}, u32[]{:S(2)}) collective-permute-start(f16[64,768]{1,0:T(8,128)(2,1)S(1)} %get-tuple-element.99), channel_id=1, source_target_pairs={{0,8},{2,10},{8,16},{10,18},{16,24},{18,26},{24,28},{26,30},{28,20... | collective-permute-start | bytes 294920 | tf_op jit(solution)/shard_map/ppermute | solution.py:214
  43.7 2.0 %collective-permute-done.9 = s16[64,1664]{1,0:T(8,128)(2,1)S(1)} collective-permute-done((s16[64,1664]{1,0:T(8,128)(2,1)S(1)}, s16[64,1664]{1,0:T(8,128)(2,1)S(1)}, u32[]{:S(2)}, u32[]{:S(2)}) %collective-permute-start.9) | collective-permute-done | bytes 213024 | tf_op jit(solution)/shard_map/ppermute | solution.py:214
  45.7 1.0 collective-permute-done.10
  47.4 0.6 negate_select_fusion.4
  48.3 0.5 collective-permute-done.16
  48.9 1.3 %collective-permute-start.17 = (f16[64,1536]{1,0:T(8,128)(2,1)S(1)}, f16[64,1536]{1,0:T(8,128)(2,1)S(1)}, u32[]{:S(2)}, u32[]{:S(2)}) collective-permute-start(f16[64,1536]{1,0:T(8,128)(2,1)S(1)} %pad_maximum_fusion.5), channel_id=1, source_target_pairs={{0,8},{2,10},{8,16},{10,18},{16,24},{18,26},{24,28},{26,30},{28,20... | collective-permute-start | bytes 589832 | tf_op jit(solution)/shard_map/ppermute | solution.py:214
  50.5 3.3 %collective-permute-done.17 = f16[64,1536]{1,0:T(8,128)(2,1)S(1)} collective-permute-done((f16[64,1536]{1,0:T(8,128)(2,1)S(1)}, f16[64,1536]{1,0:T(8,128)(2,1)S(1)}, u32[]{:S(2)}, u32[]{:S(2)}) %collective-permute-start.17) | collective-permute-done | bytes 196640 | tf_op jit(solution)/shard_map/ppermute | solution.py:214
  53.8 1.2 %collective-permute-done.18 = f16[64,1536]{1,0:T(8,128)(2,1)S(1)} collective-permute-done((f16[64,1536]{1,0:T(8,128)(2,1)S(1)}, f16[64,1536]{1,0:T(8,128)(2,1)S(1)}, u32[]{:S(2)}, u32[]{:S(2)}) %collective-permute-start.18) | collective-permute-done | bytes 196640 | tf_op jit(solution)/shard_map/ppermute | solution.py:214
  55.3 0.4 negate_select_fusion.2
  55.9 0.4 collective-permute-start.19
  56.4 1.2 collective-permute-start.20
  58.1 1.1 collective-permute-start.14
  59.3 1.4 %collective-permute-done.19 = s16[64,1664]{1,0:T(8,128)(2,1)S(1)} collective-permute-done((s16[64,1664]{1,0:T(8,128)(2,1)S(1)}, s16[64,1664]{1,0:T(8,128)(2,1)S(1)}, u32[]{:S(2)}, u32[]{:S(2)}) %collective-permute-start.19) | collective-permute-done | bytes 213024 | tf_op jit(solution)/shard_map/ppermute | solution.py:214
  60.6 0.5 collective-permute-done.20
  62.0 0.6 negate_select_fusion
  62.7 1.1 collective-permute-start.21
  63.9 0.6 collective-permute-start.22
  65.6 4.4 %collective-permute-done.21 = s16[64,1664]{1,0:T(8,128)(2,1)S(1)} collective-permute-done((s16[64,1664]{1,0:T(8,128)(2,1)S(1)}, s16[64,1664]{1,0:T(8,128)(2,1)S(1)}, u32[]{:S(2)}, u32[]{:S(2)}) %collective-permute-start.21) | collective-permute-done | bytes 213024 | tf_op jit(solution)/shard_map/ppermute | solution.py:214
  70.9 0.6 multiply_reduce_fusion
  71.6 1.4 %convert_multiply_fusion.13 = (f32[64,3072]{1,0:T(8,128)S(1)}, f16[64,3072]{1,0:T(8,128)(2,1)S(1)}, f32[1,64,3072]{2,1,0:T(8,128)}) fusion(f32[64]{0:T(128)S(1)} %get-tuple-element.109, f32[64]{0:T(128)S(1)} %get-tuple-element.108, f32[1,64,3072]{2,1,0:T(8,128)S(1)} %copy-done.4, f32[1,64,3072]{2,1,0:T(8,128)S(1)} %get-tuple-element.67, ...), kind=kLoop, calls=%fused_computation.19 | loop fusion | flops 1966080 | bytes 4326144 | tf_op jit(solution)/shard_map/mul | solution.py:326
  73.2 1.0 collective-permute-start.24
  74.1 0.6 collective-permute-start.25
  74.8 5.5 %collective-permute-start.23 = (f16[64,3200]{1,0:T(8,128)(2,1)S(1)}, f16[64,3200]{1,0:T(8,128)(2,1)S(1)}, u32[]{:S(2)}, u32[]{:S(2)}) collective-permute-start(f16[64,3200]{1,0:T(8,128)(2,1)S(1)} %pad_maximum_fusion.2), channel_id=1, source_target_pairs={{0,2},{2,0},{4,6},{6,4},{8,10},{10,8},{12,14},{14,12},{16,18},{18,... | collective-permute-start | bytes 1228808 | tf_op jit(solution)/shard_map/ppermute | solution.py:217
  80.4 1.4 %put.6.refs_0_ = f32[1024,3072]{1,0:T(8,128)} custom-call(s32[16]{0:T(128)S(1)} %mul.524.starts, f32[64,3072]{1,0:T(8,128)S(1)} %get-tuple-element.62.refs_0_), custom_call_target="tpu_custom_call" | custom-call | flops 4294967296 | tf_op jit(solution)/shard_map/put/pallas_call | solution.py:118
  81.8 4.4 %collective-permute-start.26 = (f16[64,3200]{1,0:T(8,128)(2,1)}, f16[64,3200]{1,0:T(8,128)(2,1)S(1)}, u32[]{:S(2)}, u32[]{:S(2)}) collective-permute-start(f16[64,3200]{1,0:T(8,128)(2,1)} %collective-permute-done.24), channel_id=1, source_target_pairs={{0,2},{2,0},{4,6},{6,4},{8,10},{10,8},{12,14},{14,12},{16,18},{18,... | collective-permute-start | bytes 1228808 | tf_op jit(solution)/shard_map/ppermute | solution.py:217
  86.6 1.1 collective-permute-start.29
  87.7 0.9 exponential_reduce_fusion.13
  89.2 1.1 convert_multiply_fusion.11.refs_2_
  90.4 2.0 %put.7.refs_0_ = f32[1024,3072]{1,0:T(8,128)} custom-call(s32[16]{0:T(128)S(1)} %mul.524.starts, f32[1024,3072]{1,0:T(8,128)} %put.6.refs_0_, f32[64,3072]{1,0:T(8,128)S(1)} %convert_multiply_fusion.12.refs_1_, f32[64,3072]{1,0:T(8,128)S(1)} %convert_multiply_fusion.11.refs_2_, ...), custom_call_target="tpu_custom_call", output_to_operand_aliasing={{}: (1, {})} | custom-call | flops 4294967296 | tf_op jit(solution)/shard_map/put/pallas_call | solution.py:118
  92.4 0.6 collective-permute-start.27
  93.0 4.5 %collective-permute-done.28 = f16[64,3200]{1,0:T(8,128)(2,1)S(1)} collective-permute-done((f16[64,3200]{1,0:T(8,128)(2,1)}, f16[64,3200]{1,0:T(8,128)(2,1)S(1)}, u32[]{:S(2)}, u32[]{:S(2)}) %collective-permute-start.28) | collective-permute-done | bytes 409632 | tf_op jit(solution)/shard_map/ppermute | solution.py:214
  97.6 0.8 collective-permute-start.30
  98.7 1.1 collective-permute-start.33
  101.1 2.2 %put.8.refs_0_ = f32[1024,3072]{1,0:T(8,128)} custom-call(s32[16]{0:T(128)S(1)} %mul.524.starts, f32[1024,3072]{1,0:T(8,128)} %put.7.refs_0_, f32[64,3072]{1,0:T(8,128)S(1)} %convert_multiply_fusion.9.refs_1_, f32[64,3072]{1,0:T(8,128)S(1)} %convert_multiply_fusion.8.refs_2_, ...), custom_call_target="tpu_custom_call", output_to_operand_aliasing={{}: (1, {})} | custom-call | flops 4294967296 | tf_op jit(solution)/shard_map/put/pallas_call | solution.py:118
  103.4 0.6 collective-permute-start.31
  104.0 5.5 %collective-permute-done.32 = f16[64,3200]{1,0:T(8,128)(2,1)S(1)} collective-permute-done((f16[64,3200]{1,0:T(8,128)(2,1)S(1)}, f16[64,3200]{1,0:T(8,128)(2,1)S(1)}, u32[]{:S(2)}, u32[]{:S(2)}) %collective-permute-start.32) | collective-permute-done | bytes 409632 | tf_op jit(solution)/shard_map/ppermute | solution.py:214
  109.5 0.4 collective-permute-start.37
  109.9 1.2 collective-permute-start.36
  112.4 2.2 %put.9.refs_0_ = f32[1024,3072]{1,0:T(8,128)} custom-call(s32[16]{0:T(128)S(1)} %mul.524.starts, f32[1024,3072]{1,0:T(8,128)} %put.8.refs_0_, f32[64,3072]{1,0:T(8,128)S(1)} %convert_multiply_fusion.5.refs_1_, f32[64,3072]{1,0:T(8,128)S(1)} %convert_multiply_fusion.4.refs_2_, ...), custom_call_target="tpu_custom_call", output_to_operand_aliasing={{}: (1, {})} | custom-call | flops 4294967296 | tf_op jit(solution)/shard_map/put/pallas_call | solution.py:118
  114.6 1.4 %collective-permute-start.34 = (f16[64,3200]{1,0:T(8,128)(2,1)S(1)}, f16[64,3200]{1,0:T(8,128)(2,1)S(1)}, u32[]{:S(2)}, u32[]{:S(2)}) collective-permute-start(f16[64,3200]{1,0:T(8,128)(2,1)S(1)} %collective-permute-done.32), channel_id=1, source_target_pairs={{0,2},{2,0},{4,6},{6,4},{8,10},{10,8},{12,14},{14,12},{16,18},{18,... | collective-permute-start | bytes 1228808 | tf_op jit(solution)/shard_map/ppermute | solution.py:217
  116.1 0.7 collective-permute-start.39
  117.0 0.8 collective-permute-start.38
  118.7 2.0 %put.10.refs_0_ = f32[1024,3072]{1,0:T(8,128)} custom-call(s32[16]{0:T(128)S(1)} %mul.524.starts, f32[1024,3072]{1,0:T(8,128)} %put.9.refs_0_, f32[64,3072]{1,0:T(8,128)S(1)} %convert_multiply_fusion.1.refs_1_, f32[64,3072]{1,0:T(8,128)S(1)} %convert_multiply_fusion.refs_2_, ...), custom_call_target="tpu_custom_call", output_to_operand_aliasing={{}: (1, {})} | custom-call | flops 4294967296 | tf_op jit(solution)/shard_map/put/pallas_call | solution.py:118
  121.0 1.4 %put.11 = f32[1024,3072]{1,0:T(8,128)} custom-call(s32[16]{0:T(128)S(1)} %mul.524.starts, f32[1024,3072]{1,0:T(8,128)} %put.10.refs_0_, f32[64,1536]{1,0:T(8,128)S(1)} %get-tuple-element.105.refs_1_, f32[64,1536]{1,0:T(8,128)S(1)} %get-tuple-element.104.refs_2_), custom_call_target="tpu_custom_call", output_to_operand_aliasing={{}: (1, {})} | custom-call | flops 4294967296 | tf_op jit(solution)/shard_map/put/pallas_call | solution.py:118
  (146 shorter events, 13.3 us)
Async XLA Ops:
  0.6 6.8 %copy-start.2 = (bf16[384,1,1024]{2,0,1:T(8,128)(2,1)S(1)}, bf16[384,1,1024]{2,0,1:T(8,128)(2,1)}, u32[]{:S(2)}) copy-start(bf16[384,1,1024]{2,0,1:T(8,128)(2,1)} %param.13) | copy-start | bytes 2359300
  0.6 6.8 %copy-start.3 = (bf16[384,1,1024]{2,0,1:T(8,128)(2,1)S(1)}, bf16[384,1,1024]{2,0,1:T(8,128)(2,1)}, u32[]{:S(2)}) copy-start(bf16[384,1,1024]{2,0,1:T(8,128)(2,1)} %param.14) | copy-start | bytes 2359300
  3.6 15.4 %collective-permute-start.1 = (bf16[192,1536]{1,0:T(8,128)(2,1)}, bf16[192,1536]{1,0:T(8,128)(2,1)S(1)}, u32[]{:S(2)}, u32[]{:S(2)}) collective-permute-start(bf16[192,1536]{1,0:T(8,128)(2,1)} %dispatch.2.refs_0_), channel_id=1, source_target_pairs={{0,1},{1,0},{2,3},{3,2},{4,5},{5,4},{6,7},{7,6},{8,9},{9,8},{10,11... | collective-permute-start | bytes 1769480 | tf_op jit(solution)/shard_map/ppermute | solution.py:220
  5.7 16.0 %collective-permute-start.2 = (bf16[192,1536]{1,0:T(8,128)(2,1)}, bf16[192,1536]{1,0:T(8,128)(2,1)S(1)}, u32[]{:S(2)}, u32[]{:S(2)}) collective-permute-start(bf16[192,1536]{1,0:T(8,128)(2,1)} %dispatch.2.refs_0_), channel_id=1, source_target_pairs={{0,2},{2,0},{4,6},{6,4},{8,10},{10,8},{12,14},{14,12},{16,18},{18,... | collective-permute-start | bytes 1769480 | tf_op jit(solution)/shard_map/ppermute | solution.py:217
  8.8 13.1 %copy-start.1 = (bf16[192,1536]{1,0:T(8,128)(2,1)S(1)}, bf16[192,1536]{1,0:T(8,128)(2,1)}, u32[]{:S(2)}) copy-start(bf16[192,1536]{1,0:T(8,128)(2,1)} %dispatch.2.refs_0_) | copy-start | bytes 1769476
  8.8 3.0 %collective-permute-start = (bf16[8,64,384]{2,1,0:T(8,128)(2,1)S(1)}, bf16[8,64,384]{2,1,0:T(8,128)(2,1)S(1)}, u32[]{:S(2)}, u32[]{:S(2)}) collective-permute-start(bf16[8,64,384]{2,1,0:T(8,128)(2,1)S(1)} %get-tuple-element.30), channel_id=1, source_target_pairs={{0,2},{2,0},{4,6},{6,4},{8,10},{10,8},{12,14},{14,12},{16,18},{18,... | collective-permute-start | bytes 1179656 | tf_op jit(solution)/shard_map/ppermute | solution.py:217
  19.0 2.9 %collective-permute-start.3 = (bf16[192,1536]{1,0:T(8,128)(2,1)S(1)}, bf16[192,1536]{1,0:T(8,128)(2,1)S(1)}, u32[]{:S(2)}, u32[]{:S(2)}) collective-permute-start(bf16[192,1536]{1,0:T(8,128)(2,1)S(1)} %collective-permute-done.1.refs_1_), channel_id=1, source_target_pairs={{0,2},{2,0},{4,6},{6,4},{8,10},{10,8},{12,14},{14,12},{16,18},{18,... | collective-permute-start | bytes 1769480 | tf_op jit(solution)/shard_map/ppermute | solution.py:217
  20.2 15.2 %collective-permute-start.8 = (bf16[192,1536]{1,0:T(8,128)(2,1)}, bf16[192,1536]{1,0:T(8,128)(2,1)S(1)}, u32[]{:S(2)}, u32[]{:S(2)}) collective-permute-start(bf16[192,1536]{1,0:T(8,128)(2,1)} %dispatch.3.refs_0_), channel_id=1, source_target_pairs={{0,1},{1,0},{2,3},{3,2},{4,5},{5,4},{6,7},{7,6},{8,9},{9,8},{10,11... | collective-permute-start | bytes 1769480 | tf_op jit(solution)/shard_map/ppermute | solution.py:220
  23.2 7.3 %copy-start = (bf16[192,1536]{1,0:T(8,128)(2,1)S(1)}, bf16[192,1536]{1,0:T(8,128)(2,1)}, u32[]{:S(2)}) copy-start(bf16[192,1536]{1,0:T(8,128)(2,1)} %dispatch.3.refs_0_) | copy-start | bytes 1769476
  23.5 4.1 %collective-permute-start.4 = (f16[64,768]{1,0:T(8,128)(2,1)S(1)}, f16[64,768]{1,0:T(8,128)(2,1)S(1)}, u32[]{:S(2)}, u32[]{:S(2)}) collective-permute-start(f16[64,768]{1,0:T(8,128)(2,1)S(1)} %get-tuple-element.103), channel_id=1, source_target_pairs={{0,8},{2,10},{8,16},{10,18},{16,24},{18,26},{24,28},{26,30},{28,20... | collective-permute-start | bytes 294920 | tf_op jit(solution)/shard_map/ppermute | solution.py:214
  25.1 3.8 %collective-permute-start.5 = (f16[64,768]{1,0:T(8,128)(2,1)S(1)}, f16[64,768]{1,0:T(8,128)(2,1)S(1)}, u32[]{:S(2)}, u32[]{:S(2)}) collective-permute-start(f16[64,768]{1,0:T(8,128)(2,1)S(1)} %get-tuple-element.102), channel_id=1, source_target_pairs={{0,4},{2,6},{8,0},{10,2},{16,8},{18,10},{24,16},{26,18},{28,24},{3... | collective-permute-start | bytes 294920 | tf_op jit(solution)/shard_map/ppermute | solution.py:214
  29.0 6.4 %collective-permute-start.6 = (f16[64,1536]{1,0:T(8,128)(2,1)S(1)}, f16[64,1536]{1,0:T(8,128)(2,1)S(1)}, u32[]{:S(2)}, u32[]{:S(2)}) collective-permute-start(f16[64,1536]{1,0:T(8,128)(2,1)S(1)} %pad_maximum_fusion.3), channel_id=1, source_target_pairs={{0,8},{2,10},{8,16},{10,18},{16,24},{18,26},{24,28},{26,30},{28,20... | collective-permute-start | bytes 589832 | tf_op jit(solution)/shard_map/ppermute | solution.py:214
  30.4 5.0 %collective-permute-start.7 = (f16[64,1536]{1,0:T(8,128)(2,1)S(1)}, f16[64,1536]{1,0:T(8,128)(2,1)S(1)}, u32[]{:S(2)}, u32[]{:S(2)}) collective-permute-start(f16[64,1536]{1,0:T(8,128)(2,1)S(1)} %pad_maximum_fusion.4), channel_id=1, source_target_pairs={{0,4},{2,6},{8,0},{10,2},{16,8},{18,10},{24,16},{26,18},{28,24},{3... | collective-permute-start | bytes 589832 | tf_op jit(solution)/shard_map/ppermute | solution.py:214
  30.6 9.7 %collective-permute-start.11 = (bf16[192,1536]{1,0:T(8,128)(2,1)S(1)}, bf16[192,1536]{1,0:T(8,128)(2,1)S(1)}, u32[]{:S(2)}, u32[]{:S(2)}) collective-permute-start(bf16[192,1536]{1,0:T(8,128)(2,1)S(1)} %copy-done), channel_id=1, source_target_pairs={{0,2},{2,0},{4,6},{6,4},{8,10},{10,8},{12,14},{14,12},{16,18},{18,... | collective-permute-start | bytes 1769480 | tf_op jit(solution)/shard_map/ppermute | solution.py:217
  36.3 4.2 %collective-permute-start.12 = (bf16[192,1536]{1,0:T(8,128)(2,1)S(1)}, bf16[192,1536]{1,0:T(8,128)(2,1)S(1)}, u32[]{:S(2)}, u32[]{:S(2)}) collective-permute-start(bf16[192,1536]{1,0:T(8,128)(2,1)S(1)} %collective-permute-done.8.refs_1_), channel_id=1, source_target_pairs={{0,2},{2,0},{4,6},{6,4},{8,10},{10,8},{12,14},{14,12},{16,18},{18,... | collective-permute-start | bytes 1769480 | tf_op jit(solution)/shard_map/ppermute | solution.py:217
  38.9 6.8 %collective-permute-start.9 = (s16[64,1664]{1,0:T(8,128)(2,1)S(1)}, s16[64,1664]{1,0:T(8,128)(2,1)S(1)}, u32[]{:S(2)}, u32[]{:S(2)}) collective-permute-start(s16[64,1664]{1,0:T(8,128)(2,1)S(1)} %fusion.2), channel_id=1, source_target_pairs={{0,8},{2,10},{8,16},{10,18},{16,24},{18,26},{24,28},{26,30},{28,20... | collective-permute-start | bytes 638984 | tf_op jit(solution)/shard_map/ppermute | solution.py:214
  40.2 6.5 %collective-permute-start.10 = (s16[64,1664]{1,0:T(8,128)(2,1)S(1)}, s16[64,1664]{1,0:T(8,128)(2,1)S(1)}, u32[]{:S(2)}, u32[]{:S(2)}) collective-permute-start(s16[64,1664]{1,0:T(8,128)(2,1)S(1)} %fusion.3), channel_id=1, source_target_pairs={{0,4},{2,6},{8,0},{10,2},{16,8},{18,10},{24,16},{26,18},{28,24},{3... | collective-permute-start | bytes 638984 | tf_op jit(solution)/shard_map/ppermute | solution.py:214
  42.2 6.2 %collective-permute-start.15 = (f16[64,768]{1,0:T(8,128)(2,1)S(1)}, f16[64,768]{1,0:T(8,128)(2,1)S(1)}, u32[]{:S(2)}, u32[]{:S(2)}) collective-permute-start(f16[64,768]{1,0:T(8,128)(2,1)S(1)} %get-tuple-element.99), channel_id=1, source_target_pairs={{0,8},{2,10},{8,16},{10,18},{16,24},{18,26},{24,28},{26,30},{28,20... | collective-permute-start | bytes 294920 | tf_op jit(solution)/shard_map/ppermute | solution.py:214
  43.5 5.3 %collective-permute-start.16 = (f16[64,768]{1,0:T(8,128)(2,1)S(1)}, f16[64,768]{1,0:T(8,128)(2,1)S(1)}, u32[]{:S(2)}, u32[]{:S(2)}) collective-permute-start(f16[64,768]{1,0:T(8,128)(2,1)S(1)} %get-tuple-element.98), channel_id=1, source_target_pairs={{0,4},{2,6},{8,0},{10,2},{16,8},{18,10},{24,16},{26,18},{28,24},{3... | collective-permute-start | bytes 294920 | tf_op jit(solution)/shard_map/ppermute | solution.py:214
  48.3 9.3 %copy-start.4 = (f32[1,64,3072]{2,1,0:T(8,128)S(1)}, f32[1,64,3072]{2,1,0:T(8,128)}, u32[]{:S(2)}) copy-start(f32[1,64,3072]{2,1,0:T(8,128)} %param.15) | copy-start | bytes 2359300
  48.9 4.9 %collective-permute-start.17 = (f16[64,1536]{1,0:T(8,128)(2,1)S(1)}, f16[64,1536]{1,0:T(8,128)(2,1)S(1)}, u32[]{:S(2)}, u32[]{:S(2)}) collective-permute-start(f16[64,1536]{1,0:T(8,128)(2,1)S(1)} %pad_maximum_fusion.5), channel_id=1, source_target_pairs={{0,8},{2,10},{8,16},{10,18},{16,24},{18,26},{24,28},{26,30},{28,20... | collective-permute-start | bytes 589832 | tf_op jit(solution)/shard_map/ppermute | solution.py:214
  50.2 4.9 %collective-permute-start.18 = (f16[64,1536]{1,0:T(8,128)(2,1)S(1)}, f16[64,1536]{1,0:T(8,128)(2,1)S(1)}, u32[]{:S(2)}, u32[]{:S(2)}) collective-permute-start(f16[64,1536]{1,0:T(8,128)(2,1)S(1)} %pad_maximum_fusion.6), channel_id=1, source_target_pairs={{0,4},{2,6},{8,0},{10,2},{16,8},{18,10},{24,16},{26,18},{28,24},{3... | collective-permute-start | bytes 589832 | tf_op jit(solution)/shard_map/ppermute | solution.py:214
  55.9 4.7 %collective-permute-start.19 = (s16[64,1664]{1,0:T(8,128)(2,1)S(1)}, s16[64,1664]{1,0:T(8,128)(2,1)S(1)}, u32[]{:S(2)}, u32[]{:S(2)}) collective-permute-start(s16[64,1664]{1,0:T(8,128)(2,1)S(1)} %fusion.6), channel_id=1, source_target_pairs={{0,8},{2,10},{8,16},{10,18},{16,24},{18,26},{24,28},{26,30},{28,20... | collective-permute-start | bytes 638984 | tf_op jit(solution)/shard_map/ppermute | solution.py:214
  56.4 4.7 %collective-permute-start.20 = (s16[64,1664]{1,0:T(8,128)(2,1)S(1)}, s16[64,1664]{1,0:T(8,128)(2,1)S(1)}, u32[]{:S(2)}, u32[]{:S(2)}) collective-permute-start(s16[64,1664]{1,0:T(8,128)(2,1)S(1)} %fusion.7), channel_id=1, source_target_pairs={{0,4},{2,6},{8,0},{10,2},{16,8},{18,10},{24,16},{26,18},{28,24},{3... | collective-permute-start | bytes 638984 | tf_op jit(solution)/shard_map/ppermute | solution.py:214
  57.8 6.9 %collective-permute-start.13 = (s16[64,1664]{1,0:T(8,128)(2,1)S(1)}, s16[64,1664]{1,0:T(8,128)(2,1)S(1)}, u32[]{:S(2)}, u32[]{:S(2)}) collective-permute-start(s16[64,1664]{1,0:T(8,128)(2,1)S(1)} %fusion.4), channel_id=1, source_target_pairs={{0,8},{2,10},{8,16},{10,18},{16,24},{18,26},{24,28},{26,30},{28,20... | collective-permute-start | bytes 638984 | tf_op jit(solution)/shard_map/ppermute | solution.py:214
  58.1 6.8 %collective-permute-start.14 = (s16[64,1664]{1,0:T(8,128)(2,1)S(1)}, s16[64,1664]{1,0:T(8,128)(2,1)S(1)}, u32[]{:S(2)}, u32[]{:S(2)}) collective-permute-start(s16[64,1664]{1,0:T(8,128)(2,1)S(1)} %fusion.5), channel_id=1, source_target_pairs={{0,4},{2,6},{8,0},{10,2},{16,8},{18,10},{24,16},{26,18},{28,24},{3... | collective-permute-start | bytes 638984 | tf_op jit(solution)/shard_map/ppermute | solution.py:214
  61.9 9.0 %copy-start.7 = (f32[1,64,3072]{2,1,0:T(8,128)S(1)}, f32[1,64,3072]{2,1,0:T(8,128)}, u32[]{:S(2)}) copy-start(f32[1,64,3072]{2,1,0:T(8,128)} %param.16) | copy-start | bytes 2359300
  61.9 9.0 %copy-start.8 = (f32[1,64,3072]{2,1,0:T(8,128)S(1)}, f32[1,64,3072]{2,1,0:T(8,128)}, u32[]{:S(2)}) copy-start(f32[1,64,3072]{2,1,0:T(8,128)} %param.17) | copy-start | bytes 2359300
  62.7 7.4 %collective-permute-start.21 = (s16[64,1664]{1,0:T(8,128)(2,1)S(1)}, s16[64,1664]{1,0:T(8,128)(2,1)S(1)}, u32[]{:S(2)}, u32[]{:S(2)}) collective-permute-start(s16[64,1664]{1,0:T(8,128)(2,1)S(1)} %fusion.8), channel_id=1, source_target_pairs={{0,8},{2,10},{8,16},{10,18},{16,24},{18,26},{24,28},{26,30},{28,20... | collective-permute-start | bytes 638984 | tf_op jit(solution)/shard_map/ppermute | solution.py:214
  63.9 6.3 %collective-permute-start.22 = (s16[64,1664]{1,0:T(8,128)(2,1)S(1)}, s16[64,1664]{1,0:T(8,128)(2,1)S(1)}, u32[]{:S(2)}, u32[]{:S(2)}) collective-permute-start(s16[64,1664]{1,0:T(8,128)(2,1)S(1)} %fusion.9), channel_id=1, source_target_pairs={{0,4},{2,6},{8,0},{10,2},{16,8},{18,10},{24,16},{26,18},{28,24},{3... | collective-permute-start | bytes 638984 | tf_op jit(solution)/shard_map/ppermute | solution.py:214
  71.6 10.3 %copy-start.5 = (f32[1,64,3072]{2,1,0:T(8,128)}, f32[1,64,3072]{2,1,0:T(8,128)S(1)}, u32[]{:S(2)}) copy-start(f32[1,64,3072]{2,1,0:T(8,128)S(1)} %get-tuple-element.66) | copy-start | bytes 2359300
  71.6 10.3 %copy-start.6 = (f32[1,64,3072]{2,1,0:T(8,128)}, f32[1,64,3072]{2,1,0:T(8,128)S(1)}, u32[]{:S(2)}) copy-start(f32[1,64,3072]{2,1,0:T(8,128)S(1)} %get-tuple-element.67) | copy-start | bytes 2359300
  73.2 8.7 %collective-permute-start.24 = (f16[64,3200]{1,0:T(8,128)(2,1)S(1)}, f16[64,3200]{1,0:T(8,128)(2,1)}, u32[]{:S(2)}, u32[]{:S(2)}) collective-permute-start(f16[64,3200]{1,0:T(8,128)(2,1)S(1)} %pad_maximum_fusion.2), channel_id=1, source_target_pairs={{0,8},{2,10},{8,16},{10,18},{16,24},{18,26},{24,28},{26,30},{28,20... | collective-permute-start | bytes 1228808 | tf_op jit(solution)/shard_map/ppermute | solution.py:214
  74.1 12.5 %collective-permute-start.25 = (f16[64,3200]{1,0:T(8,128)(2,1)S(1)}, f16[64,3200]{1,0:T(8,128)(2,1)S(1)}, u32[]{:S(2)}, u32[]{:S(2)}) collective-permute-start(f16[64,3200]{1,0:T(8,128)(2,1)S(1)} %pad_maximum_fusion.2), channel_id=1, source_target_pairs={{0,4},{2,6},{8,0},{10,2},{16,8},{18,10},{24,16},{26,18},{28,24},{3... | collective-permute-start | bytes 1228808 | tf_op jit(solution)/shard_map/ppermute | solution.py:214
  74.8 14.0 %collective-permute-start.23 = (f16[64,3200]{1,0:T(8,128)(2,1)S(1)}, f16[64,3200]{1,0:T(8,128)(2,1)S(1)}, u32[]{:S(2)}, u32[]{:S(2)}) collective-permute-start(f16[64,3200]{1,0:T(8,128)(2,1)S(1)} %pad_maximum_fusion.2), channel_id=1, source_target_pairs={{0,2},{2,0},{4,6},{6,4},{8,10},{10,8},{12,14},{14,12},{16,18},{18,... | collective-permute-start | bytes 1228808 | tf_op jit(solution)/shard_map/ppermute | solution.py:217
  81.8 18.3 %collective-permute-start.26 = (f16[64,3200]{1,0:T(8,128)(2,1)}, f16[64,3200]{1,0:T(8,128)(2,1)S(1)}, u32[]{:S(2)}, u32[]{:S(2)}) collective-permute-start(f16[64,3200]{1,0:T(8,128)(2,1)} %collective-permute-done.24), channel_id=1, source_target_pairs={{0,2},{2,0},{4,6},{6,4},{8,10},{10,8},{12,14},{14,12},{16,18},{18,... | collective-permute-start | bytes 1228808 | tf_op jit(solution)/shard_map/ppermute | solution.py:217
  86.3 11.3 %collective-permute-start.28 = (f16[64,3200]{1,0:T(8,128)(2,1)}, f16[64,3200]{1,0:T(8,128)(2,1)S(1)}, u32[]{:S(2)}, u32[]{:S(2)}) collective-permute-start(f16[64,3200]{1,0:T(8,128)(2,1)} %collective-permute-done.24), channel_id=1, source_target_pairs={{0,8},{2,10},{8,16},{10,18},{16,24},{18,26},{24,28},{26,30},{28,20... | collective-permute-start | bytes 1228808 | tf_op jit(solution)/shard_map/ppermute | solution.py:214
  86.6 12.1 %collective-permute-start.29 = (f16[64,3200]{1,0:T(8,128)(2,1)S(1)}, f16[64,3200]{1,0:T(8,128)(2,1)S(1)}, u32[]{:S(2)}, u32[]{:S(2)}) collective-permute-start(f16[64,3200]{1,0:T(8,128)(2,1)S(1)} %collective-permute-done.25), channel_id=1, source_target_pairs={{0,4},{2,6},{8,0},{10,2},{16,8},{18,10},{24,16},{26,18},{28,24},{3... | collective-permute-start | bytes 1228808 | tf_op jit(solution)/shard_map/ppermute | solution.py:214
  92.4 8.1 %collective-permute-start.27 = (f16[64,3200]{1,0:T(8,128)(2,1)S(1)}, f16[64,3200]{1,0:T(8,128)(2,1)S(1)}, u32[]{:S(2)}, u32[]{:S(2)}) collective-permute-start(f16[64,3200]{1,0:T(8,128)(2,1)S(1)} %collective-permute-done.25), channel_id=1, source_target_pairs={{0,2},{2,0},{4,6},{6,4},{8,10},{10,8},{12,14},{14,12},{16,18},{18,... | collective-permute-start | bytes 1228808 | tf_op jit(solution)/shard_map/ppermute | solution.py:217
  97.6 13.9 %collective-permute-start.30 = (f16[64,3200]{1,0:T(8,128)(2,1)S(1)}, f16[64,3200]{1,0:T(8,128)(2,1)S(1)}, u32[]{:S(2)}, u32[]{:S(2)}) collective-permute-start(f16[64,3200]{1,0:T(8,128)(2,1)S(1)} %collective-permute-done.28), channel_id=1, source_target_pairs={{0,2},{2,0},{4,6},{6,4},{8,10},{10,8},{12,14},{14,12},{16,18},{18,... | collective-permute-start | bytes 1228808 | tf_op jit(solution)/shard_map/ppermute | solution.py:217
  98.3 11.1 %collective-permute-start.32 = (f16[64,3200]{1,0:T(8,128)(2,1)S(1)}, f16[64,3200]{1,0:T(8,128)(2,1)S(1)}, u32[]{:S(2)}, u32[]{:S(2)}) collective-permute-start(f16[64,3200]{1,0:T(8,128)(2,1)S(1)} %collective-permute-done.28), channel_id=1, source_target_pairs={{0,8},{2,10},{8,16},{10,18},{16,24},{18,26},{24,28},{26,30},{28,20... | collective-permute-start | bytes 1228808 | tf_op jit(solution)/shard_map/ppermute | solution.py:214
  98.7 11.2 %collective-permute-start.33 = (f16[64,3200]{1,0:T(8,128)(2,1)S(1)}, f16[64,3200]{1,0:T(8,128)(2,1)S(1)}, u32[]{:S(2)}, u32[]{:S(2)}) collective-permute-start(f16[64,3200]{1,0:T(8,128)(2,1)S(1)} %collective-permute-done.29), channel_id=1, source_target_pairs={{0,4},{2,6},{8,0},{10,2},{16,8},{18,10},{24,16},{26,18},{28,24},{3... | collective-permute-start | bytes 1228808 | tf_op jit(solution)/shard_map/ppermute | solution.py:214
  103.4 8.5 %collective-permute-start.31 = (f16[64,3200]{1,0:T(8,128)(2,1)S(1)}, f16[64,3200]{1,0:T(8,128)(2,1)S(1)}, u32[]{:S(2)}, u32[]{:S(2)}) collective-permute-start(f16[64,3200]{1,0:T(8,128)(2,1)S(1)} %collective-permute-done.29), channel_id=1, source_target_pairs={{0,2},{2,0},{4,6},{6,4},{8,10},{10,8},{12,14},{14,12},{16,18},{18,... | collective-permute-start | bytes 1228808 | tf_op jit(solution)/shard_map/ppermute | solution.py:217
  109.5 6.7 %collective-permute-start.37 = (f16[64,1536]{1,0:T(8,128)(2,1)S(1)}, f16[64,1536]{1,0:T(8,128)(2,1)S(1)}, u32[]{:S(2)}, u32[]{:S(2)}) collective-permute-start(f16[64,1536]{1,0:T(8,128)(2,1)S(1)} %slice.366), channel_id=1, source_target_pairs={{0,8},{2,10},{8,16},{10,18},{16,24},{18,26},{24,28},{26,30},{28,20... | collective-permute-start | bytes 589832 | tf_op jit(solution)/shard_map/ppermute | solution.py:214
  109.9 6.9 %collective-permute-start.36 = (f16[64,1664]{1,0:T(8,128)(2,1)S(1)}, f16[64,1664]{1,0:T(8,128)(2,1)S(1)}, u32[]{:S(2)}, u32[]{:S(2)}) collective-permute-start(f16[64,1664]{1,0:T(8,128)(2,1)S(1)} %slice.363), channel_id=1, source_target_pairs={{0,4},{2,6},{8,0},{10,2},{16,8},{18,10},{24,16},{26,18},{28,24},{3... | collective-permute-start | bytes 638984 | tf_op jit(solution)/shard_map/ppermute | solution.py:214
  114.6 3.4 %collective-permute-start.34 = (f16[64,3200]{1,0:T(8,128)(2,1)S(1)}, f16[64,3200]{1,0:T(8,128)(2,1)S(1)}, u32[]{:S(2)}, u32[]{:S(2)}) collective-permute-start(f16[64,3200]{1,0:T(8,128)(2,1)S(1)} %collective-permute-done.32), channel_id=1, source_target_pairs={{0,2},{2,0},{4,6},{6,4},{8,10},{10,8},{12,14},{14,12},{16,18},{18,... | collective-permute-start | bytes 1228808 | tf_op jit(solution)/shard_map/ppermute | solution.py:217
  116.1 2.3 %collective-permute-start.35 = (f16[64,3200]{1,0:T(8,128)(2,1)S(1)}, f16[64,3200]{1,0:T(8,128)(2,1)S(1)}, u32[]{:S(2)}, u32[]{:S(2)}) collective-permute-start(f16[64,3200]{1,0:T(8,128)(2,1)S(1)} %collective-permute-done.33), channel_id=1, source_target_pairs={{0,2},{2,0},{4,6},{6,4},{8,10},{10,8},{12,14},{14,12},{16,18},{18,... | collective-permute-start | bytes 1228808 | tf_op jit(solution)/shard_map/ppermute | solution.py:217
  116.1 4.7 %collective-permute-start.39 = (f16[64,1536]{1,0:T(8,128)(2,1)S(1)}, f16[64,1536]{1,0:T(8,128)(2,1)S(1)}, u32[]{:S(2)}, u32[]{:S(2)}) collective-permute-start(f16[64,1536]{1,0:T(8,128)(2,1)S(1)} %collective-permute-done.37), channel_id=1, source_target_pairs={{0,2},{2,0},{4,6},{6,4},{8,10},{10,8},{12,14},{14,12},{16,18},{18,... | collective-permute-start | bytes 589832 | tf_op jit(solution)/shard_map/ppermute | solution.py:217
  117.0 3.6 %collective-permute-start.38 = (f16[64,1664]{1,0:T(8,128)(2,1)S(1)}, f16[64,1664]{1,0:T(8,128)(2,1)S(1)}, u32[]{:S(2)}, u32[]{:S(2)}) collective-permute-start(f16[64,1664]{1,0:T(8,128)(2,1)S(1)} %collective-permute-done.36), channel_id=1, source_target_pairs={{0,2},{2,0},{4,6},{6,4},{8,10},{10,8},{12,14},{14,12},{16,18},{18,... | collective-permute-start | bytes 638984 | tf_op jit(solution)/shard_map/ppermute | solution.py:217
